TPU v7x, 32 devices: a whole 2x2x4 slice. The times are simulated.
32 devices in a mesh: col: 8 (over z, y), disp: 4 (over x, core).
Axes of the slice: x: 2, y: 2, z: 4, core: 2. Of those that a mesh axis runs over, the one named last changes fastest.
Arguments:
- left: bfloat16 [320, 64, 128], P(None, 'col'), may hold values from -6 to 6
- right: bfloat16 [320, 64, 128], P(None, 'col'), may hold values from -6 to 6
- kernel: bfloat16 [3, 3, 3, 32, 40], replicated, may hold values from -0.1875 to 0.1875
- cotangent: bfloat16 [32, 48, 64, 128], P(None, 'disp', 'col'), may hold values from -14 to 14
Outputs:
- grad_left: bfloat16 [320, 64, 128], P('disp', 'col')
- grad_right: bfloat16 [320, 64, 128], P('disp', 'col')
- grad_kernel: float32 [3, 3, 3, 32, 40], replicated
All inputs are finite; a program needn't handle non-finite values.
Results may differ from a plain program's by a relative error of at most 0.0034.
The roundings to bfloat16 on the way count: a program that leaves them out, or rounds other values in their place, can miss the bound.
Values may be sent and summed in bfloat16 or wider, within the bound.
No kernel may reach another device: no remote copies, remote signals or barrier semaphores. Data moves between devices by JAX's collectives and lax.ppermute only.
A program may use at most 128 MiB of HBM per device.

v0:
```python
import functools
import math

import jax
import jax.numpy as jnp
import numpy as np
from jax import lax
from jax.experimental import pallas as pl
from jax.experimental.pallas import tpu as pltpu
from jax.sharding import PartitionSpec as P

C = 320
G = 40
D = 48
GROUP = C // G
HIGHEST = lax.Precision.HIGHEST


def shifted(value, axis, steps):
    count = lax.axis_size(axis)
    leading, last = (max(0, -steps), min(count, count - steps))
    return lax.ppermute(value, axis, [(source, source + steps) for source in range(leading, last)])


def conv_rows(outs, width):
    main = np.tile(np.arange(width), outs)
    return np.concatenate([main, np.full(outs, -1), np.full(outs, width)])


def toeplitz(kernel_local, width):
    outs, groups = kernel_local.shape[3:]
    row_col = conv_rows(outs, width)
    row_out = np.concatenate([np.repeat(np.arange(outs), width), np.tile(np.arange(outs), 2)])
    spread = np.zeros((outs, row_col.size), np.float32)
    spread[row_out, np.arange(row_col.size)] = 1
    taps = jnp.transpose(kernel_local[::-1], (1, 2, 4, 0, 3))
    wide = jnp.einsum(
        "qrgpo,ok->qrgpk", taps, jnp.asarray(spread, jnp.bfloat16),
        preferred_element_type=jnp.float32,
    ).astype(jnp.bfloat16)
    out_col = np.arange(width)
    column_tap = out_col[:, None] - row_col[None, :] + 1
    total = jnp.zeros((3, groups, width, 3, row_col.size), jnp.bfloat16)
    for tap in range(3):
        mask = jnp.asarray(column_tap == tap)[None, None, :, None, :]
        total = jnp.where(mask, wide[tap][:, :, None], total)
    return total.reshape(3 * groups * width, 3 * row_col.size)


def roll_zero(value, steps):
    size = value.shape[-1]
    lane = lax.broadcasted_iota(jnp.int32, value.shape, value.ndim - 1)
    moved = pltpu.roll(value, steps % size, value.ndim - 1)
    return jnp.where(lane == (0 if steps > 0 else size - 1), 0.0, moved)


def work(
    hops, places, left_ref, right_ref, cot_ref, halo_ref, weight_ref, fold_ref,
    grad_left_ref, own_ref, *rest
):
    sent_refs, (sums_ref, left_s, right_s, vol_s, cot_s, gv_s, grad_s, prod_s) = (
        rest[:hops], rest[hops:],
    )
    channels, width, rows = left_ref.shape
    groups = channels // GROUP
    blocks, outs, levels = cot_ref.shape[:3]
    main = outs * width
    span = main + 2 * outs
    reach = hops * width
    f32, bf16 = jnp.float32, jnp.bfloat16

    left_s[...] = left_ref[...].astype(f32)
    for hop in range(hops + 1):
        place = places[0] - hop
        block = right_ref[jnp.maximum(place, 0)].astype(f32)
        at = reach - hop * width
        right_s[:, at : at + width] = jnp.where(place >= 0, block, 0.0)

    def volume_step(group, carry):
        first = group * GROUP
        lefts = [left_s[first + k] for k in range(GROUP)]
        rows_at = pl.ds(pl.multiple_of(group * width, width), width)
        for d in range(D):
            total = lefts[0] * right_s[first, reach - d : reach - d + width]
            for k in range(1, GROUP):
                total = total + lefts[k] * right_s[first + k, reach - d : reach - d + width]
            value = (total * (1.0 / GROUP)).astype(bf16).astype(f32)
            vol_s[d, 0, rows_at] = roll_zero(value, 1)
            vol_s[d, 1, rows_at] = value
            vol_s[d, 2, rows_at] = roll_zero(value, -1)
        return carry

    lax.fori_loop(0, groups, volume_step, 0)

    cot_s[0] = jnp.zeros((span, rows), bf16)
    cot_s[D + 1] = jnp.zeros((span, rows), bf16)
    for block in range(blocks):

        def assemble(level, carry, block=block):
            at = block * levels + level + 1
            value = cot_ref[block, :, level].astype(f32).reshape(main, rows)
            cot_s[at, 0:main] = value.astype(bf16)
            cot_s[at, main:span] = halo_ref[block, level]
            return carry

        lax.fori_loop(0, levels, assemble, 0)

    def grad_volume_step(pair, carry):
        first = pair * 2
        near = cot_s[pl.ds(first, 3)].reshape(3 * span, rows)
        far = cot_s[pl.ds(first + 1, 3)].reshape(3 * span, rows)
        result = jnp.dot(
            weight_ref[...], jnp.concatenate([near, far], axis=1), preferred_element_type=f32
        )
        size = groups * width
        for half in range(2):
            part = result[:, half * rows : (half + 1) * rows]
            total = (
                part[size : 2 * size]
                + roll_zero(part[:size], -1)
                + roll_zero(part[2 * size :], 1)
            )
            gv_s[first + half] = total.astype(bf16).astype(f32)
        return carry

    lax.fori_loop(0, D // 2, grad_volume_step, 0)

    chunk = 4
    prod_s[...] = jnp.zeros(prod_s.shape, f32)

    def kernel_step(step, carry):
        first = step * chunk
        volume = jnp.concatenate(
            [vol_s[first + k].reshape(3 * groups * width, rows).astype(bf16) for k in range(chunk)],
            axis=1,
        )
        for tap in range(3):
            value = jnp.concatenate([cot_s[first + k + tap] for k in range(chunk)], axis=1)
            prod_s[tap] += lax.dot_general(
                value, volume, (((1,), (1,)), ((), ())), preferred_element_type=f32
            )
        return carry

    lax.fori_loop(0, D // chunk, kernel_step, 0)

    size = 3 * groups * width
    col_in = lax.broadcasted_iota(jnp.int32, (width, size), 0)
    col_out = lax.broadcasted_iota(jnp.int32, (width, size), 1) % width
    edge = lax.broadcasted_iota(jnp.int32, (outs, size), 1) % width
    for column_tap in range(3):
        mask = col_out - col_in + 1 == column_tap
        parts = []
        for tap in range(3):
            value = prod_s[tap, 0:main].reshape(outs, width, size)
            total = jnp.sum(jnp.where(mask[None], value, 0.0), axis=1)
            if column_tap == 2:
                total = total + jnp.where(edge == 0, prod_s[tap, main : main + outs], 0.0)
            if column_tap == 0:
                total = total + jnp.where(edge == width - 1, prod_s[tap, main + outs : span], 0.0)
            parts.append(total)
        gathered = jnp.concatenate(parts, axis=0)
        sums_ref[column_tap] = lax.dot_general(
            fold_ref[...], gathered, (((1,), (1,)), ((), ())),
            precision=HIGHEST, preferred_element_type=f32,
        )

    grad_s[...] = jnp.zeros(grad_s.shape, f32)

    def grads_step(group, carry):
        first = group * GROUP
        lefts = [left_s[first + k] for k in range(GROUP)]
        totals = [jnp.zeros((width, rows), f32) for k in range(GROUP)]
        rows_at = pl.ds(pl.multiple_of(group * width, width), width)
        for d in range(D):
            value = gv_s[d, rows_at]
            for k in range(GROUP):
                totals[k] = totals[k] + value * right_s[first + k, reach - d : reach - d + width]
                grad_s[first + k, reach - d : reach - d + width] += value * lefts[k]
        for k in range(GROUP):
            grad_left_ref[first + k] = (totals[k] * (1.0 / GROUP)).astype(bf16)
        return carry

    lax.fori_loop(0, groups, grads_step, 0)
    own_ref[...] = grad_s[:, reach : reach + width] * (1.0 / GROUP)
    for hop in range(1, hops + 1):
        at = reach - hop * width
        sent_refs[hop - 1][...] = (grad_s[:, at : at + width] * (1.0 / GROUP)).astype(bf16)


def run_work(place, left, right_blocks, cot_blocks, halo_blocks, weights, fold, hops):
    channels, width, rows = left.shape
    groups = channels // GROUP
    blocks, outs, levels = cot_blocks.shape[:3]
    span = outs * (width + 2)
    size = 3 * groups * width
    f32, bf16 = jnp.float32, jnp.bfloat16
    vmem = pl.BlockSpec(memory_space=pltpu.VMEM)
    return pl.pallas_call(
        functools.partial(work, hops),
        out_shape=[
            jax.ShapeDtypeStruct((channels, width, rows), bf16),
            jax.ShapeDtypeStruct((channels, width, rows), f32),
            *[jax.ShapeDtypeStruct((channels, width, rows), bf16)] * hops,
            jax.ShapeDtypeStruct((3, fold.shape[0], 3 * outs), f32),
        ],
        in_specs=[pl.BlockSpec(memory_space=pltpu.SMEM)] + [vmem] * 6,
        out_specs=[vmem] * (hops + 3),
        scratch_shapes=[
            pltpu.VMEM((channels, width, rows), f32),
            pltpu.VMEM((channels, (hops + 1) * width, rows), f32),
            pltpu.VMEM((D, 3, groups * width, rows), f32),
            pltpu.VMEM((D + 2, span, rows), bf16),
            pltpu.VMEM((D, groups * width, rows), f32),
            pltpu.VMEM((channels, (hops + 1) * width, rows), f32),
            pltpu.VMEM((3, span, size), f32),
        ],
        compiler_params=pltpu.CompilerParams(vmem_limit_bytes=48 * 1024 * 1024),
    )(place, left, right_blocks, cot_blocks, halo_blocks, weights, fold)


def body(left, right, kernel, cotangent):
    outs, levels, width, rows = cotangent.shape
    parts = lax.axis_size("disp")
    channels = C // parts
    groups = G // parts
    hops = (D + width - 2) // width
    part = lax.axis_index("disp")

    right_own = lax.dynamic_slice_in_dim(right, part * channels, channels, 0)
    right_blocks = lax.all_gather(right_own, "col")
    cot_blocks = lax.all_gather(cotangent, "disp")
    low = shifted(jnp.transpose(cotangent[:, :, width - 1], (1, 0, 2)), "col", 1)
    high = shifted(jnp.transpose(cotangent[:, :, 0], (1, 0, 2)), "col", -1)
    halo_blocks = lax.all_gather(jnp.concatenate([low, high], axis=1), "disp")

    left_own = lax.dynamic_slice_in_dim(left, part * channels, channels, 0)
    weights = toeplitz(lax.dynamic_slice_in_dim(kernel, part * groups, groups, 4), width)
    pad_rows = -(-3 * groups // 8) * 8
    fold = np.zeros((pad_rows, 3 * groups * width), np.float32)
    fold[np.arange(3 * groups * width) // width, np.arange(3 * groups * width)] = 1
    place = lax.axis_index("col").astype(jnp.int32)[None]
    results = run_work(
        place, left_own, right_blocks, cot_blocks, halo_blocks, weights, jnp.asarray(fold), hops
    )
    grad_left, own, sent, sums = results[0], results[1], results[2:-1], results[-1]

    sums = jnp.pad(sums, ((0, 0), (0, 0), (0, 128 - 3 * outs)))
    everyone = lax.all_gather(sums, ("col", "disp"))
    everyone = everyone.reshape(lax.axis_size("col"), parts, 3, pad_rows, 128)
    total = jnp.sum(everyone, axis=0)[:, :, : 3 * groups, : 3 * outs]
    total = total.reshape(parts, 3, 3, groups, 3, outs)
    cell_count = D * width * lax.axis_size("col") * rows
    grad_kernel = jnp.transpose(total, (4, 1, 2, 5, 0, 3))[::-1].reshape(3, 3, 3, outs, G)
    grad_kernel = grad_kernel * (1.0 / math.sqrt(cell_count))

    total_right = own
    for hop in range(1, hops + 1):
        total_right = total_right + shifted(sent[hop - 1], "col", -hop).astype(jnp.float32)
    return (grad_left, total_right.astype(jnp.bfloat16), grad_kernel)


def solution(mesh):
    return jax.shard_map(
        body,
        mesh=mesh,
        in_specs=(P(None, "col", None), P(None, "col", None), P(), P(None, "disp", "col", None)),
        out_specs=(P("disp", "col", None), P("disp", "col", None), P()),
        check_vma=False,
    )
```

profile of v0, /device:TPU:13, one launch (start us, length us, event | category | flops | bytes accessed | tf_op | source)
XLA Modules:
  0.0 184.7 jit_solution(2327142408044973415)
XLA Ops:
  7.2 1.0 copy-done
  8.3 0.7 constant_dynamic-slice_fusion.1
  9.0 0.7 all-gather.10.cloned.1.call-update
  9.8 1.7 fusion.1
  11.5 2.3 %collective-permute-start.1 = (bf16[12,32,128]{2,1,0:T(8,128)(2,1)S(1)}, bf16[12,32,128]{2,1,0:T(8,128)(2,1)S(1)}, u32[]{:S(2)}, u32[]{:S(2)}) collective-permute-start(bf16[12,32,128]{2,1,0:T(8,128)(2,1)S(1)} %bitcast.39), channel_id=1, source_target_pairs={{4,0},{8,4},{12,8},{16,12},{20,16},{24,20},{28,24},{5,1},{9,5},{13... | collective-permute-start | bytes 294920 | tf_op jit(solution)/shard_map/ppermute | solution.py:22
  13.8 4.0 %collective-permute-start = (bf16[12,32,128]{2,1,0:T(8,128)(2,1)S(1)}, bf16[12,32,128]{2,1,0:T(8,128)(2,1)S(1)}, u32[]{:S(2)}, u32[]{:S(2)}) collective-permute-start(bf16[12,32,128]{2,1,0:T(8,128)(2,1)S(1)} %bitcast.40), channel_id=1, source_target_pairs={{0,4},{4,8},{8,12},{12,16},{16,20},{20,24},{24,28},{1,5},{5,9},{9,... | collective-permute-start | bytes 294920 | tf_op jit(solution)/shard_map/ppermute | solution.py:22
  18.1 0.3 convolution_convert_fusion
  18.6 0.5 select_select_fusion
  19.1 0.5 select_n.30.weight_ref
  19.6 0.9 constant_dynamic-slice_fusion.2.left_ref
  20.6 0.3 collective-permute-done
  20.9 9.4 %all-gather.2 = bf16[48,64,128]{2,1,0:T(8,128)(2,1)S(1)} all-gather(bf16[12,64,128]{2,1,0:T(8,128)(2,1)S(1)} %pad_maximum_fusion), channel_id=4, replica_groups=mesh['col'=8,'disp'=4] {'disp'}, dimensions={0}, use_global_device_ids=true | all-gather | bytes 983040 | tf_op jit(solution)/shard_map/all_gather | solution.py:234
  30.3 21.4 %all-gather.8.cloned.1.call-done = bf16[640,8,128]{2,1,0:T(8,128)(2,1)} async-done(((bf16[80,8,128]{2,1,0:T(8,128)(2,1)}), bf16[640,8,128]{2,1,0:T(8,128)(2,1)}) %all-gather.8.cloned.1.call-update) | async-done | bytes 1310736 | tf_op jit(solution)/shard_map/all_gather | solution.py:230
  51.7 31.2 %all-gather.10.cloned.1.call-done = bf16[128,12,8,128]{3,2,1,0:T(8,128)(2,1)} async-done(((bf16[32,12,8,128]{3,2,1,0:T(8,128)(2,1)}), bf16[128,12,8,128]{3,2,1,0:T(8,128)(2,1)}) %all-gather.10.cloned.1.call-update) | async-done | bytes 3145744 | tf_op jit(solution)/shard_map/all_gather | solution.py:231
  82.9 1.3 copy-done.1
  84.3 24.5 %shard_map.112 = (bf16[80,8,128]{2,1,0:T(8,128)(2,1)}, f32[80,8,128]{2,1,0:T(8,128)S(1)}, bf16[80,8,128]{2,1,0:T(8,128)(2,1)S(1)}, bf16[80,8,128]{2,1,0:T(8,128)...) custom-call(s32[1]{0:T(128)} %bitcast.places, ...), custom_call_target="tpu_custom_call" | custom-call | tf_op jit(solution)/shard_map/pallas_call | solution.py:198
  108.8 0.6 pad.4
  109.5 2.2 %collective-permute-start.2 = (bf16[80,8,128]{2,1,0:T(8,128)(2,1)S(1)}, bf16[80,8,128]{2,1,0:T(8,128)(2,1)S(1)}, u32[]{:S(2)}, u32[]{:S(2)}) collective-permute-start(bf16[80,8,128]{2,1,0:T(8,128)(2,1)S(1)} %get-tuple-element.14), channel_id=1, source_target_pairs={{4,0},{8,4},{12,8},{16,12},{20,16},{24,20},{28,24},{5,1},{9,5},{13... | collective-permute-start | bytes 491528 | tf_op jit(solution)/shard_map/ppermute | solution.py:22
  111.6 2.2 %collective-permute-start.3 = (bf16[80,8,128]{2,1,0:T(8,128)(2,1)S(1)}, bf16[80,8,128]{2,1,0:T(8,128)(2,1)S(1)}, u32[]{:S(2)}, u32[]{:S(2)}) collective-permute-start(bf16[80,8,128]{2,1,0:T(8,128)(2,1)S(1)} %get-tuple-element.15), channel_id=1, source_target_pairs={{8,0},{12,4},{16,8},{20,12},{24,16},{28,20},{9,1},{13,5},{17,9},{2... | collective-permute-start | bytes 491528 | tf_op jit(solution)/shard_map/ppermute | solution.py:22
  113.8 1.9 %collective-permute-start.4 = (bf16[80,8,128]{2,1,0:T(8,128)(2,1)S(1)}, bf16[80,8,128]{2,1,0:T(8,128)(2,1)S(1)}, u32[]{:S(2)}, u32[]{:S(2)}) collective-permute-start(bf16[80,8,128]{2,1,0:T(8,128)(2,1)S(1)} %get-tuple-element.16), channel_id=1, source_target_pairs={{12,0},{16,4},{20,8},{24,12},{28,16},{13,1},{17,5},{21,9},{25,13},... | collective-permute-start | bytes 491528 | tf_op jit(solution)/shard_map/ppermute | solution.py:22
  115.7 1.3 collective-permute-start.5
  117.0 0.7 collective-permute-start.6
  117.8 0.7 collective-permute-start.7
  118.4 0.3 collective-permute-done.3
  118.7 7.7 %collective-permute-done.4 = bf16[80,8,128]{2,1,0:T(8,128)(2,1)S(1)} collective-permute-done((bf16[80,8,128]{2,1,0:T(8,128)(2,1)S(1)}, bf16[80,8,128]{2,1,0:T(8,128)(2,1)S(1)}, u32[]{:S(2)}, u32[]{:S(2)}) %collective-permute-start.4) | collective-permute-done | bytes 163872 | tf_op jit(solution)/shard_map/ppermute | solution.py:22
  126.4 1.3 collective-permute-done.5
  127.7 0.8 add_convert_fusion
  128.5 46.3 %all-gather.12.cloned.1.call-done = f32[96,32,128]{2,1,0:T(8,128)} async-done(((f32[3,32,128]{2,1,0:T(8,128)}), f32[96,32,128]{2,1,0:T(8,128)}) %all-gather.12.cloned.1.call-update) | async-done | bytes 1572880 | tf_op jit(solution)/shard_map/all_gather | solution.py:248
  174.8 1.6 reduce_sum.9
  176.4 0.3 reshape.40
  176.8 0.1 reverse_multiply_fusion
  177.2 1.0 copy.44
  (35 shorter events, 0.9 us)
Async XLA Ops:
  7.2 1.1 copy-start
  7.2 10.7 %copy-start.3 = (bf16[3,3,3,32,40]{4,3,2,1,0:T(8,128)(2,1)S(1)}, bf16[3,3,3,32,40]{4,3,2,1,0:T(8,128)(2,1)}, u32[]{:S(2)}) copy-start(bf16[3,3,3,32,40]{4,3,2,1,0:T(8,128)(2,1)} %param.11) | copy-start | bytes 207364
  7.2 44.5 %all-gather.8.cloned.1.call-start = ((), (), s32[]{:S(2)}) async-start(), calls=%async_computation | async-start | bytes 1474560 | tf_op jit(solution)/shard_map/all_gather | solution.py:230
  9.0 9.1 %copy-start.4 = (bf16[32,320,1,1,1]{1,0,4,3,2:T(8,128)(2,1)S(1)}, bf16[32,320,1,1,1]{1,0,4,3,2:T(8,128)(2,1)}, u32[]{:S(2)}) copy-start(bf16[32,320,1,1,1]{1,0,4,3,2:T(8,128)(2,1)} %constant.43) | copy-start | bytes 61444
  9.0 74.0 %all-gather.10.cloned.1.call-start = ((), (), s32[]{:S(2)}) async-start(), calls=%async_computation.1 | async-start | bytes 3932160 | tf_op jit(solution)/shard_map/all_gather | solution.py:231
  9.7 165.1 %all-gather.12.cloned.1.call-start = ((), (), s32[]{:S(2)}) async-start(), calls=%async_computation.2 | async-start | bytes 1622016 | tf_op jit(solution)/shard_map/all_gather | solution.py:248
  11.5 7.1 %copy-start.5 = (pred[8,320]{1,0:T(8,128)(4,1)S(1)}, pred[8,320]{1,0:T(8,128)(4,1)}, u32[]{:S(2)}) copy-start(pred[8,320]{1,0:T(8,128)(4,1)} %constant.39.clone) | copy-start | bytes 7684
  11.5 7.1 %copy-start.6 = (pred[8,320]{1,0:T(8,128)(4,1)S(1)}, pred[8,320]{1,0:T(8,128)(4,1)}, u32[]{:S(2)}) copy-start(pred[8,320]{1,0:T(8,128)(4,1)} %constant.38.clone) | copy-start | bytes 7684
  11.5 7.1 %copy-start.7 = (pred[8,320]{1,0:T(8,128)(4,1)S(1)}, pred[8,320]{1,0:T(8,128)(4,1)}, u32[]{:S(2)}) copy-start(pred[8,320]{1,0:T(8,128)(4,1)} %constant.37.clone) | copy-start | bytes 7684
  11.5 9.0 %collective-permute-start.1 = (bf16[12,32,128]{2,1,0:T(8,128)(2,1)S(1)}, bf16[12,32,128]{2,1,0:T(8,128)(2,1)S(1)}, u32[]{:S(2)}, u32[]{:S(2)}) collective-permute-start(bf16[12,32,128]{2,1,0:T(8,128)(2,1)S(1)} %bitcast.39), channel_id=1, source_target_pairs={{4,0},{8,4},{12,8},{16,12},{20,16},{24,20},{28,24},{5,1},{9,5},{13... | collective-permute-start | bytes 294920 | tf_op jit(solution)/shard_map/ppermute | solution.py:22
  13.8 7.1 %collective-permute-start = (bf16[12,32,128]{2,1,0:T(8,128)(2,1)S(1)}, bf16[12,32,128]{2,1,0:T(8,128)(2,1)S(1)}, u32[]{:S(2)}, u32[]{:S(2)}) collective-permute-start(bf16[12,32,128]{2,1,0:T(8,128)(2,1)S(1)} %bitcast.40), channel_id=1, source_target_pairs={{0,4},{4,8},{8,12},{12,16},{16,20},{20,24},{24,28},{1,5},{5,9},{9,... | collective-permute-start | bytes 294920 | tf_op jit(solution)/shard_map/ppermute | solution.py:22
  19.1 63.8 %copy-start.2 = (f32[32,240]{1,0:T(8,128)S(1)}, f32[32,240]{1,0:T(8,128)}, u32[]{:S(2)}) copy-start(f32[32,240]{1,0:T(8,128)} %constant.40.clone.fold_ref) | copy-start | bytes 92164
  82.9 1.3 copy-start.1
  109.5 8.3 %collective-permute-start.2 = (bf16[80,8,128]{2,1,0:T(8,128)(2,1)S(1)}, bf16[80,8,128]{2,1,0:T(8,128)(2,1)S(1)}, u32[]{:S(2)}, u32[]{:S(2)}) collective-permute-start(bf16[80,8,128]{2,1,0:T(8,128)(2,1)S(1)} %get-tuple-element.14), channel_id=1, source_target_pairs={{4,0},{8,4},{12,8},{16,12},{20,16},{24,20},{28,24},{5,1},{9,5},{13... | collective-permute-start | bytes 491528 | tf_op jit(solution)/shard_map/ppermute | solution.py:22
  111.6 7.1 %collective-permute-start.3 = (bf16[80,8,128]{2,1,0:T(8,128)(2,1)S(1)}, bf16[80,8,128]{2,1,0:T(8,128)(2,1)S(1)}, u32[]{:S(2)}, u32[]{:S(2)}) collective-permute-start(bf16[80,8,128]{2,1,0:T(8,128)(2,1)S(1)} %get-tuple-element.15), channel_id=1, source_target_pairs={{8,0},{12,4},{16,8},{20,12},{24,16},{28,20},{9,1},{13,5},{17,9},{2... | collective-permute-start | bytes 491528 | tf_op jit(solution)/shard_map/ppermute | solution.py:22
  113.8 12.6 %collective-permute-start.4 = (bf16[80,8,128]{2,1,0:T(8,128)(2,1)S(1)}, bf16[80,8,128]{2,1,0:T(8,128)(2,1)S(1)}, u32[]{:S(2)}, u32[]{:S(2)}) collective-permute-start(bf16[80,8,128]{2,1,0:T(8,128)(2,1)S(1)} %get-tuple-element.16), channel_id=1, source_target_pairs={{12,0},{16,4},{20,8},{24,12},{28,16},{13,1},{17,5},{21,9},{25,13},... | collective-permute-start | bytes 491528 | tf_op jit(solution)/shard_map/ppermute | solution.py:22
  115.7 12.0 %collective-permute-start.5 = (bf16[80,8,128]{2,1,0:T(8,128)(2,1)S(1)}, bf16[80,8,128]{2,1,0:T(8,128)(2,1)S(1)}, u32[]{:S(2)}, u32[]{:S(2)}) collective-permute-start(bf16[80,8,128]{2,1,0:T(8,128)(2,1)S(1)} %get-tuple-element.17), channel_id=1, source_target_pairs={{16,0},{20,4},{24,8},{28,12},{17,1},{21,5},{25,9},{29,13},{18,2},{... | collective-permute-start | bytes 491528 | tf_op jit(solution)/shard_map/ppermute | solution.py:22
  117.0 10.7 %collective-permute-start.6 = (bf16[80,8,128]{2,1,0:T(8,128)(2,1)S(1)}, bf16[80,8,128]{2,1,0:T(8,128)(2,1)S(1)}, u32[]{:S(2)}, u32[]{:S(2)}) collective-permute-start(bf16[80,8,128]{2,1,0:T(8,128)(2,1)S(1)} %get-tuple-element.18), channel_id=1, source_target_pairs={{20,0},{24,4},{28,8},{21,1},{25,5},{29,9},{22,2},{26,6},{30,10},{2... | collective-permute-start | bytes 491528 | tf_op jit(solution)/shard_map/ppermute | solution.py:22
  117.8 9.9 %collective-permute-start.7 = (bf16[80,8,128]{2,1,0:T(8,128)(2,1)S(1)}, bf16[80,8,128]{2,1,0:T(8,128)(2,1)S(1)}, u32[]{:S(2)}, u32[]{:S(2)}) collective-permute-start(bf16[80,8,128]{2,1,0:T(8,128)(2,1)S(1)} %get-tuple-element.19), channel_id=1, source_target_pairs={{24,0},{28,4},{25,1},{29,5},{26,2},{30,6},{27,3},{31,7}} | collective-permute-start | bytes 491528 | tf_op jit(solution)/shard_map/ppermute | solution.py:22
Sparse Core Ops, SparseCore 0:
  10.8 40.8 all-gather.7
  53.3 29.6 all-gather.9
  109.6 65.2 all-gather.11
where the time goes:
time: 187 us; the launch traced here: 185 us
  waiting for transfers between devices  109 us (58%)
  Pallas kernels  24.5 us (13%)
  starting transfers between devices  15.3 us (8%)
  between operations  14.1 us (8%)
  blocking collectives  9.39 us (5%)
  local copies, waits for them, and re-layouts  8.68 us (5%)
  other arithmetic  3.04 us (2%)
    all_gather x1, waiting for transfers between devices, body(): everyone = lax.all_gather(sums, ('col', 'disp'))  46.3 us
    all_gather x1, waiting for transfers between devices, body(): cot_blocks = lax.all_gather(cotangent, 'disp')  31.2 us
    pallas_call x1, Pallas kernels, run_work(): pl.pallas_call(functools.partial(work, hops), out_shape=[jax.ShapeDtypeSt...  24.5 us
    all_gather x1, waiting for transfers between devices, body(): right_blocks = lax.all_gather(right_own, 'col')  21.4 us
    ppermute x8, starting transfers between devices, shifted(): lax.ppermute(value, axis, [(source, source + steps) for source in range(l...  15.2 us
    ppermute x8, waiting for transfers between devices, shifted(): lax.ppermute(value, axis, [(source, source + steps) for source in range(l...  9.64 us
    all_gather x1, blocking collectives, body(): halo_blocks = lax.all_gather(jnp.concatenate([low, high], axis=1), 'disp')  9.39 us
  transfers between devices with their start and end apart: 11, of which 7 were waited for; matrix products, arithmetic and copies ran while one was open for 3% of the time, Pallas kernels for 0%

commit v1 on v0

v1 whole, which is shorter than its diff:
```python
import functools
import math

import jax
import jax.numpy as jnp
import numpy as np
from jax import lax
from jax.experimental import pallas as pl
from jax.experimental.pallas import tpu as pltpu
from jax.sharding import PartitionSpec as P

C = 320
G = 40
D = 48
GROUP = C // G
HIGHEST = lax.Precision.HIGHEST


def shifted(value, axis, steps):
    count = lax.axis_size(axis)
    leading, last = (max(0, -steps), min(count, count - steps))
    return lax.ppermute(value, axis, [(source, source + steps) for source in range(leading, last)])


def conv_rows(outs, width):
    main = np.tile(np.arange(width), outs)
    return np.concatenate([main, np.full(outs, -1), np.full(outs, width)])


def toeplitz(kernel_local, width):
    outs, groups = kernel_local.shape[3:]
    row_col = conv_rows(outs, width)
    row_out = np.concatenate([np.repeat(np.arange(outs), width), np.tile(np.arange(outs), 2)])
    spread = np.zeros((outs, row_col.size), np.float32)
    spread[row_out, np.arange(row_col.size)] = 1
    taps = jnp.transpose(kernel_local[::-1], (1, 2, 4, 0, 3))
    wide = jnp.einsum(
        "qrgpo,ok->qrgpk", taps, jnp.asarray(spread, jnp.bfloat16),
        preferred_element_type=jnp.float32,
    ).astype(jnp.bfloat16)
    out_col = np.arange(width)
    column_tap = out_col[:, None] - row_col[None, :] + 1
    total = jnp.zeros((3, groups, width, 3, row_col.size), jnp.bfloat16)
    for tap in range(3):
        mask = jnp.asarray(column_tap == tap)[None, None, :, None, :]
        total = jnp.where(mask, wide[tap][:, :, None], total)
    return total.reshape(3 * groups * width, 3 * row_col.size)


def roll_zero(value, steps):
    size = value.shape[-1]
    lane = lax.broadcasted_iota(jnp.int32, value.shape, value.ndim - 1)
    moved = pltpu.roll(value, steps % size, value.ndim - 1)
    return jnp.where(lane == (0 if steps > 0 else size - 1), 0.0, moved)


def spread_grad_volume(places, *refs):
    count = (len(refs) - 3) // 2
    cot_refs, halo_refs = refs[:count], refs[count : 2 * count]
    weight_ref, cot_s, gv_s = refs[2 * count :]
    outs, levels, width, rows = cot_refs[0].shape
    main = outs * width
    span = cot_s.shape[1]
    size = gv_s.shape[1]
    f32, bf16 = jnp.float32, jnp.bfloat16

    cot_s[0] = jnp.zeros((span, rows), bf16)
    cot_s[D + 1] = jnp.zeros((span, rows), bf16)
    for other in range(count):
        start = (places[0] ^ other) * levels + 1

        def assemble(level, carry, other=other, start=start):
            value = cot_refs[other][:, level].astype(f32).reshape(main, rows)
            cot_s[start + level, 0:main] = value.astype(bf16)
            cot_s[start + level, main:span] = halo_refs[other][level]
            return carry

        lax.fori_loop(0, levels, assemble, 0)

    def grad_volume_step(pair, carry):
        first = pair * 2
        near = cot_s[pl.ds(first, 3)].reshape(3 * span, rows)
        far = cot_s[pl.ds(first + 1, 3)].reshape(3 * span, rows)
        result = jnp.dot(
            weight_ref[...], jnp.concatenate([near, far], axis=1), preferred_element_type=f32
        )
        for half in range(2):
            part = result[:, half * rows : (half + 1) * rows]
            total = (
                part[size : 2 * size]
                + roll_zero(part[:size], -1)
                + roll_zero(part[2 * size :], 1)
            )
            gv_s[first + half] = total.astype(bf16).astype(f32)
        return carry

    lax.fori_loop(0, D // 2, grad_volume_step, 0)


def load_right(places, right_ref, right_s, hops, width):
    reach = hops * width
    for hop in range(hops + 1):
        place = places[1] - hop
        block = right_ref[jnp.maximum(place, 0)].astype(jnp.float32)
        at = reach - hop * width
        right_s[:, at : at + width] = jnp.where(place >= 0, block, 0.0)


def feature_grads(hops, places, left_ref, right_ref, gv_s, grad_left_ref, own_ref, *rest):
    sent_refs, (right_out, right_s, grad_s) = rest[:hops], rest[hops:]
    channels, width, rows = left_ref.shape
    groups = channels // GROUP
    reach = hops * width
    f32, bf16 = jnp.float32, jnp.bfloat16
    load_right(places, right_ref, right_s, hops, width)
    grad_s[...] = jnp.zeros(grad_s.shape, f32)

    def grads_step(group, carry):
        first = group * GROUP
        lefts = [left_ref[first + k].astype(f32) for k in range(GROUP)]
        totals = [jnp.zeros((width, rows), f32) for k in range(GROUP)]
        rows_at = pl.ds(pl.multiple_of(group * width, width), width)
        for d in range(D):
            value = gv_s[d, rows_at]
            for k in range(GROUP):
                totals[k] = totals[k] + value * right_s[first + k, reach - d : reach - d + width]
                grad_s[first + k, reach - d : reach - d + width] += value * lefts[k]
        for k in range(GROUP):
            grad_left_ref[first + k] = (totals[k] * (1.0 / GROUP)).astype(bf16)
        return carry

    lax.fori_loop(0, groups, grads_step, 0)
    right_out[...] = right_s[...]
    own_ref[...] = grad_s[:, reach : reach + width] * (1.0 / GROUP)
    for hop in range(1, hops + 1):
        at = reach - hop * width
        sent_refs[hop - 1][...] = (grad_s[:, at : at + width] * (1.0 / GROUP)).astype(bf16)


def kernel_sums(left_ref, right_s, cot_s, fold_ref, sums_ref, vol_s, prod_s):
    channels, width, rows = left_ref.shape
    groups = channels // GROUP
    span = cot_s.shape[1]
    outs = span // (width + 2)
    main = outs * width
    reach = right_s.shape[1] - width
    f32, bf16 = jnp.float32, jnp.bfloat16

    def volume_step(group, carry):
        first = group * GROUP
        lefts = [left_ref[first + k].astype(f32) for k in range(GROUP)]
        rows_at = pl.ds(pl.multiple_of(group * width, width), width)
        for d in range(D):
            total = lefts[0] * right_s[first, reach - d : reach - d + width]
            for k in range(1, GROUP):
                total = total + lefts[k] * right_s[first + k, reach - d : reach - d + width]
            value = (total * (1.0 / GROUP)).astype(bf16).astype(f32)
            vol_s[d, 0, rows_at] = roll_zero(value, 1)
            vol_s[d, 1, rows_at] = value
            vol_s[d, 2, rows_at] = roll_zero(value, -1)
        return carry

    lax.fori_loop(0, groups, volume_step, 0)

    chunk = 4
    size = 3 * groups * width
    prod_s[...] = jnp.zeros(prod_s.shape, f32)

    def kernel_step(step, carry):
        first = step * chunk
        volume = jnp.concatenate(
            [vol_s[first + k].reshape(size, rows).astype(bf16) for k in range(chunk)], axis=1
        )
        for tap in range(3):
            value = jnp.concatenate([cot_s[first + k + tap] for k in range(chunk)], axis=1)
            prod_s[tap] += lax.dot_general(
                value, volume, (((1,), (1,)), ((), ())), preferred_element_type=f32
            )
        return carry

    lax.fori_loop(0, D // chunk, kernel_step, 0)

    col_in = lax.broadcasted_iota(jnp.int32, (width, size), 0)
    col_out = lax.broadcasted_iota(jnp.int32, (width, size), 1) % width
    edge = lax.broadcasted_iota(jnp.int32, (outs, size), 1) % width
    for column_tap in range(3):
        mask = col_out - col_in + 1 == column_tap
        parts = []
        for tap in range(3):
            value = prod_s[tap, 0:main].reshape(outs, width, size)
            total = jnp.sum(jnp.where(mask[None], value, 0.0), axis=1)
            if column_tap == 2:
                total = total + jnp.where(edge == 0, prod_s[tap, main : main + outs], 0.0)
            if column_tap == 0:
                total = total + jnp.where(edge == width - 1, prod_s[tap, main + outs : span], 0.0)
            parts.append(total)
        gathered = jnp.concatenate(parts, axis=0)
        sums_ref[column_tap] = lax.dot_general(
            fold_ref[...], gathered, (((1,), (1,)), ((), ())),
            precision=HIGHEST, preferred_element_type=f32,
        )


VMEM = pl.BlockSpec(memory_space=pltpu.VMEM)
SMEM = pl.BlockSpec(memory_space=pltpu.SMEM)
PARAMS = pltpu.CompilerParams(vmem_limit_bytes=40 * 1024 * 1024)


def run_grad_volume(places, cots, halos, weights):
    outs, levels, width, rows = cots[0].shape
    return pl.pallas_call(
        spread_grad_volume,
        out_shape=[
            jax.ShapeDtypeStruct((D + 2, outs * (width + 2), rows), jnp.bfloat16),
            jax.ShapeDtypeStruct((D, weights.shape[0] // 3, rows), jnp.float32),
        ],
        in_specs=[SMEM] + [VMEM] * (2 * len(cots) + 1),
        out_specs=[VMEM] * 2,
        compiler_params=PARAMS,
        cost_estimate=pl.CostEstimate(flops=4000000000, bytes_accessed=10000000, transcendentals=0),
    )(places, *cots, *halos, weights)


def run_feature_grads(places, left, right_blocks, grad_volume, hops):
    channels, width, rows = left.shape
    f32, bf16 = jnp.float32, jnp.bfloat16
    wide = (channels, (hops + 1) * width, rows)
    return pl.pallas_call(
        functools.partial(feature_grads, hops),
        out_shape=[
            jax.ShapeDtypeStruct((channels, width, rows), bf16),
            jax.ShapeDtypeStruct((channels, width, rows), f32),
            *[jax.ShapeDtypeStruct((channels, width, rows), bf16)] * hops,
            jax.ShapeDtypeStruct(wide, f32),
        ],
        in_specs=[SMEM] + [VMEM] * 3,
        out_specs=[VMEM] * (hops + 3),
        scratch_shapes=[pltpu.VMEM(wide, f32), pltpu.VMEM(wide, f32)],
        compiler_params=PARAMS,
        cost_estimate=pl.CostEstimate(flops=4000000000, bytes_accessed=10000000, transcendentals=0),
    )(places, left, right_blocks, grad_volume)


def run_kernel_sums(left, right_wide, cot_wide, fold):
    channels, width, rows = left.shape
    size = fold.shape[1]
    span = cot_wide.shape[1]
    f32 = jnp.float32
    return pl.pallas_call(
        kernel_sums,
        out_shape=jax.ShapeDtypeStruct((3, fold.shape[0], 3 * span // (width + 2)), f32),
        in_specs=[VMEM] * 4,
        out_specs=VMEM,
        scratch_shapes=[pltpu.VMEM((D, 3, size // 3, rows), f32), pltpu.VMEM((3, span, size), f32)],
        compiler_params=PARAMS,
        cost_estimate=pl.CostEstimate(flops=4000000000, bytes_accessed=10000000, transcendentals=0),
    )(left, right_wide, cot_wide, fold)


def swapped(value, axis, bit):
    count = lax.axis_size(axis)
    return lax.ppermute(value, axis, [(source, source ^ bit) for source in range(count)])


def gather_swapping(value, axis):
    held = {0: value}
    bit = lax.axis_size(axis) // 2
    while bit:
        held.update({key | bit: swapped(item, axis, bit) for key, item in list(held.items())})
        bit //= 2
    return [held[key] for key in range(len(held))]


def body(left, right, kernel, cotangent):
    outs, levels, width, rows = cotangent.shape
    parts = lax.axis_size("disp")
    channels = C // parts
    groups = G // parts
    hops = (D + width - 2) // width
    part = lax.axis_index("disp")
    places = jnp.stack([part, lax.axis_index("col")]).astype(jnp.int32)

    cots = gather_swapping(cotangent, "disp")
    right_own = lax.dynamic_slice_in_dim(right, part * channels, channels, 0)
    right_blocks = lax.all_gather(right_own, "col")
    low = shifted(jnp.transpose(cotangent[:, :, width - 1], (1, 0, 2)), "col", 1)
    high = shifted(jnp.transpose(cotangent[:, :, 0], (1, 0, 2)), "col", -1)
    halos = gather_swapping(jnp.concatenate([low, high], axis=1), "disp")

    left_own = lax.dynamic_slice_in_dim(left, part * channels, channels, 0)
    weights = toeplitz(lax.dynamic_slice_in_dim(kernel, part * groups, groups, 4), width)
    pad_rows = -(-3 * groups // 8) * 8
    fold = np.zeros((pad_rows, 3 * groups * width), np.float32)
    fold[np.arange(3 * groups * width) // width, np.arange(3 * groups * width)] = 1

    cot_wide, grad_volume = run_grad_volume(places, cots, halos, weights)
    results = run_feature_grads(places, left_own, right_blocks, grad_volume, hops)
    grad_left, own, sent, right_wide = results[0], results[1], results[2:-1], results[-1]
    sums = run_kernel_sums(left_own, right_wide, cot_wide, jnp.asarray(fold))

    sums = jnp.pad(sums, ((0, 0), (0, 0), (0, 128 - 3 * outs)))
    total = jnp.sum(lax.all_gather(sums, "col"), axis=0)
    total = lax.all_gather(total, "disp")[:, :, : 3 * groups, : 3 * outs]
    total = total.reshape(parts, 3, 3, groups, 3, outs)
    cell_count = D * width * lax.axis_size("col") * rows
    grad_kernel = jnp.transpose(total, (4, 1, 2, 5, 0, 3))[::-1].reshape(3, 3, 3, outs, G)
    grad_kernel = grad_kernel * (1.0 / math.sqrt(cell_count))

    total_right = own
    for hop in range(hops, 0, -1):
        total_right = total_right + shifted(sent[hop - 1], "col", -hop).astype(jnp.float32)
    return (grad_left, total_right.astype(jnp.bfloat16), grad_kernel)


def solution(mesh):
    return jax.shard_map(
        body,
        mesh=mesh,
        in_specs=(P(None, "col", None), P(None, "col", None), P(), P(None, "disp", "col", None)),
        out_specs=(P("disp", "col", None), P("disp", "col", None), P()),
        check_vma=False,
    )
```

time: 187 us -> 134 us (0.72)
  the two profiles are of different devices: /device:TPU:13 before, /device:TPU:11 now
where the time goes in v1:
time: 134 us
  blocking collectives  40.3 us (30%)
  Pallas kernels  24.7 us (18%)
  starting transfers between devices  24.1 us (18%)
  local copies, waits for them, and re-layouts  15 us (11%)
  between operations  14.4 us (11%)
  waiting for transfers between devices  11.4 us (9%)
  other arithmetic  3.69 us (3%)
    all_gather x1, blocking collectives, body(): total = jnp.sum(lax.all_gather(sums, 'col'), axis=0)  26.7 us
    ppermute x8, starting transfers between devices, shifted(): lax.ppermute(value, axis, [(source, source + steps) for source in range(l...  19.9 us
    all_gather x1, blocking collectives, body(): total = lax.all_gather(total, 'disp')[:, :, :3 * groups, :3 * outs]  13.7 us
    pallas_call x1, Pallas kernels, run_grad_volume(): pl.pallas_call(spread_grad_volume, out_shape=[jax.ShapeDtypeStruct((D + 2...  11.1 us
    ppermute x6, waiting for transfers between devices, swapped(): lax.ppermute(value, axis, [(source, source ^ bit) for source in range(cou...  11.1 us
    pallas_call x1, Pallas kernels, run_kernel_sums(): pl.pallas_call(kernel_sums, out_shape=jax.ShapeDtypeStruct((3, fold.shape...  8.37 us
    unnamed x28, local copies, waits for them, and re-layouts  8.17 us
    pallas_call x1, Pallas kernels, run_feature_grads(): pl.pallas_call(functools.partial(feature_grads, hops), out_shape=[jax.Sha...  5.27 us
  transfers between devices with their start and end apart: 15, of which 4 were waited for; matrix products, arithmetic and copies ran while one was open for 7% of the time, Pallas kernels for 15%

profile of v1, /device:TPU:11, one launch (start us, length us, event | category | flops | bytes accessed | tf_op | source)
XLA Modules:
  0.0 133.9 jit_solution(11158911307503758173)
XLA Ops:
  7.2 1.0 copy-done
  8.3 0.7 constant_dynamic-slice_fusion.1
  9.3 1.0 collective-permute-start
  10.3 1.7 %fusion.1 = (bf16[32,12,1,128]{3,2,1,0:T(2,128)(2,1)S(1)}, bf16[32,12,1,128]{3,2,1,0:T(2,128)(2,1)S(1)}) fusion(bf16[32,12,8,128]{3,2,1,0:T(8,128)(2,1)} %refs_0_.1), kind=kLoop, calls=%fused_computation.18 | loop fusion | bytes 393216 | tf_op jit(solution)/shard_map/slice | solution.py:287
  12.0 3.1 %collective-permute-start.3 = (bf16[12,32,128]{2,1,0:T(8,128)(2,1)S(1)}, bf16[12,32,128]{2,1,0:T(8,128)(2,1)S(1)}, u32[]{:S(2)}, u32[]{:S(2)}) collective-permute-start(bf16[12,32,128]{2,1,0:T(8,128)(2,1)S(1)} %bitcast.37), channel_id=1, source_target_pairs={{0,4},{4,8},{8,12},{12,16},{16,20},{20,24},{24,28},{1,5},{5,9},{9,... | collective-permute-start | bytes 294920 | tf_op jit(solution)/shard_map/ppermute | solution.py:22
  15.2 3.0 %collective-permute-start.4 = (bf16[12,32,128]{2,1,0:T(8,128)(2,1)S(1)}, bf16[12,32,128]{2,1,0:T(8,128)(2,1)S(1)}, u32[]{:S(2)}, u32[]{:S(2)}) collective-permute-start(bf16[12,32,128]{2,1,0:T(8,128)(2,1)S(1)} %bitcast.38), channel_id=1, source_target_pairs={{4,0},{8,4},{12,8},{16,12},{20,16},{24,20},{28,24},{5,1},{9,5},{13... | collective-permute-start | bytes 294920 | tf_op jit(solution)/shard_map/ppermute | solution.py:22
  18.2 1.1 constant_dynamic-slice_fusion
  19.6 8.2 %collective-permute-done.1.refs_2_ = bf16[32,12,8,128]{3,2,1,0:T(8,128)(2,1)S(1)} collective-permute-done((bf16[32,12,8,128]{3,2,1,0:T(8,128)(2,1)}, bf16[32,12,8,128]{3,2,1,0:T(8,128)(2,1)S(1)}, u32[]{:S(2)}, u32[]{:S(2)}) %collective-permute-start.1) | collective-permute-done | bytes 786464 | tf_op jit(solution)/shard_map/ppermute | solution.py:262
  27.8 1.4 %collective-permute-start.2 = (bf16[32,12,8,128]{3,2,1,0:T(8,128)(2,1)S(1)}, bf16[32,12,8,128]{3,2,1,0:T(8,128)(2,1)}, u32[]{:S(2)}, u32[]{:S(2)}) collective-permute-start(bf16[32,12,8,128]{3,2,1,0:T(8,128)(2,1)S(1)} %collective-permute-done.1.refs_2_), channel_id=1, source_target_pairs={{0,1},{1,0},{2,3},{3,2},{4,5},{5,4},{6,7},{7,6},{8,9},{9,8},{10,11... | collective-permute-start | bytes 2359304 | tf_op jit(solution)/shard_map/ppermute | solution.py:262
  29.8 1.4 %select_select_fusion = bf16[3,10,8,3,320]{4,3,2,1,0:T(4,128)(2,1)} fusion(pred[8,320]{1,0:T(8,128)(4,1)S(1)} %copy-done.11, pred[8,320]{1,0:T(8,128)(4,1)S(1)} %copy-done.10, pred[8,320]{1,0:T(8,128)(4,1)S(1)} %copy-done.9, bf16[3,10,3,320]{3,2,1,0:T(4,128)(2,1)S(1)} %copy.49, bf16[3,10,3,320]{3,2,1,0:T(4,128)(2,1)S(1)} %copy.48, ...), kind=kLoop, calls=%fused_computation.1 | loop fusion | flops 691200 | bytes 641280 | tf_op jit(solution)/shard_map/jit(_where)/select_n | solution.py:46
  31.2 1.7 %select_n.30.refs_8_ = bf16[240,960]{1,0:T(8,128)(2,1)S(1)} reshape(bf16[3,10,8,3,320]{4,3,2,1,0:T(4,128)(2,1)} %select_select_fusion) | data formatting | bytes 921600 | tf_op jit(solution)/shard_map/jit(_where)/select_n | solution.py:46
  32.9 0.3 collective-permute-start.5
  33.2 2.8 %collective-permute-done.6.refs_6_ = bf16[12,64,128]{2,1,0:T(8,128)(2,1)S(1)} collective-permute-done((bf16[12,64,128]{2,1,0:T(8,128)(2,1)S(1)}, bf16[12,64,128]{2,1,0:T(8,128)(2,1)S(1)}, u32[]{:S(2)}, u32[]{:S(2)}) %collective-permute-start.6) | collective-permute-done | bytes 196640 | tf_op jit(solution)/shard_map/ppermute | solution.py:262
  36.1 0.8 collective-permute-start.7
  36.9 0.9 constant_dynamic-slice_fusion.2.left_ref
  37.9 11.1 %shard_map.112 = (bf16[50,320,128]{2,1,0:T(8,128)(2,1)S(1)}, f32[48,80,128]{2,1,0:T(8,128)S(1)}) custom-call(s32[2]{0:T(128)S(1)} %pad_add_fusion.places, bf16[32,12,8,128]{3,2,1,0:T(8,128)(2,1)S(1)} %copy-done.1, bf16[32,12,8,128]{3,2,1,0:T(8,128)(2,1)} %collective-permute-done.refs_1_, bf16[32,12,8,128]{3,2,1,0:T(8,128)(2,1)S(1)} %collective-permute-done.1.refs_2_, ...), custom_call_target="tpu_custom_call" | custom-call | flops 4000000000 | bytes 10000000 | tf_op jit(solution)/shard_map/pallas_call | solution.py:211
  49.1 1.9 %copy-done.4 = bf16[50,320,128]{2,1,0:T(8,128)(2,1)} copy-done((bf16[50,320,128]{2,1,0:T(8,128)(2,1)}, bf16[50,320,128]{2,1,0:T(8,128)(2,1)S(1)}, u32[]{:S(2)}) %copy-start.4) | copy-done | bytes 4096024
  51.0 1.3 copy-done.6
  52.5 1.3 copy-done.2
  53.9 1.5 %copy-done.7 = f32[48,80,128]{2,1,0:T(8,128)S(1)} copy-done((f32[48,80,128]{2,1,0:T(8,128)S(1)}, f32[48,80,128]{2,1,0:T(8,128)}, u32[]{:S(2)}) %copy-start.7) | copy-done | bytes 1966104
  55.4 5.3 %shard_map.113 = (bf16[80,8,128]{2,1,0:T(8,128)(2,1)}, f32[80,8,128]{2,1,0:T(8,128)S(1)}, bf16[80,8,128]{2,1,0:T(8,128)(2,1)S(1)}, bf16[80,8,128]{2,1,0:T(8,128)...) custom-call(s32[2]{0:T(128)S(1)} %pad_add_fusion.places, ...), custom_call_target="tpu_custom_call" | custom-call | flops 4000000000 | bytes 10000000 | tf_op jit(solution)/shard_map/pallas_call | solution.py:228
  60.7 0.7 collective-permute-start.8
  61.3 1.3 collective-permute-start.9
  62.6 1.3 collective-permute-start.10
  63.9 1.3 collective-permute-start.11
  65.2 3.8 %collective-permute-start.12 = (bf16[80,8,128]{2,1,0:T(8,128)(2,1)S(1)}, bf16[80,8,128]{2,1,0:T(8,128)(2,1)}, u32[]{:S(2)}, u32[]{:S(2)}) collective-permute-start(bf16[80,8,128]{2,1,0:T(8,128)(2,1)S(1)} %get-tuple-element.21), channel_id=1, source_target_pairs={{8,0},{12,4},{16,8},{20,12},{24,16},{28,20},{9,1},{13,5},{17,9},{2... | collective-permute-start | bytes 491528 | tf_op jit(solution)/shard_map/ppermute | solution.py:22
  69.1 8.4 %shard_map.114 = f32[3,32,96]{2,1,0:T(8,128)S(1)} custom-call(bf16[80,8,128]{2,1,0:T(8,128)(2,1)S(1)} %constant_dynamic-slice_fusion.2.left_ref, f32[80,56,128]{2,1,0:T(8,128)S(1)} %get-tuple-element.23.right_s, bf16[50,320,128]{2,1,0:T(8,128)(2,1)S(1)} %copy-done.5, f32[32,240]{1,0:T(8,128)S(1)} %copy-done.3), custom_call_target="tpu_custom_call" | custom-call | flops 4000000000 | bytes 10000000 | tf_op jit(solution)/shard_map/pallas_call | solution.py:249
  77.5 26.7 %all-gather.1 = f32[24,32,128]{2,1,0:T(8,128)S(1)} all-gather(f32[3,32,128]{2,1,0:T(8,128)S(1)} %pad.4), channel_id=3, replica_groups=mesh['col'=8,'disp'=4] {'col'}, dimensions={0}, use_global_device_ids=true | all-gather | bytes 442368 | tf_op jit(solution)/shard_map/all_gather | solution.py:302
  104.2 5.3 %collective-permute-start.13 = (bf16[80,8,128]{2,1,0:T(8,128)(2,1)S(1)}, bf16[80,8,128]{2,1,0:T(8,128)(2,1)}, u32[]{:S(2)}, u32[]{:S(2)}) collective-permute-start(bf16[80,8,128]{2,1,0:T(8,128)(2,1)S(1)} %get-tuple-element.22), channel_id=1, source_target_pairs={{4,0},{8,4},{12,8},{16,12},{20,16},{24,20},{28,24},{5,1},{9,5},{13... | collective-permute-start | bytes 491528 | tf_op jit(solution)/shard_map/ppermute | solution.py:22
  109.5 13.7 %all-gather.2 = f32[12,32,128]{2,1,0:T(8,128)S(1)} all-gather(f32[3,32,128]{2,1,0:T(8,128)S(1)} %reduce_sum.9), channel_id=4, replica_groups=mesh['col'=8,'disp'=4] {'disp'}, dimensions={0}, use_global_device_ids=true | all-gather | bytes 245760 | tf_op jit(solution)/shard_map/all_gather | solution.py:303
  124.0 1.0 copy.53
  125.0 2.0 %add_convert_fusion = bf16[80,8,128]{2,1,0:T(8,128)(2,1)} fusion(bf16[80,8,128]{2,1,0:T(8,128)(2,1)} %collective-permute-done.13, bf16[80,8,128]{2,1,0:T(8,128)(2,1)} %collective-permute-done.12, bf16[80,8,128]{2,1,0:T(8,128)(2,1)} %collective-permute-done.11, bf16[80,8,128]{2,1,0:T(8,128)(2,1)} %collective-permute-done.10, ...), kind=kLoop, calls=%fused_computation.4 | loop fusion | flops 1064960 | bytes 1474560 | tf_op jit(solution)/shard_map/convert_element_type | solution.py:312
  (54 shorter events, 2.5 us)
Async XLA Ops:
  7.2 1.1 copy-start
  7.2 12.1 %copy-start.8 = (bf16[32,320,1,1,1]{1,0,4,3,2:T(8,128)(2,1)S(1)}, bf16[32,320,1,1,1]{1,0,4,3,2:T(8,128)(2,1)}, u32[]{:S(2)}) copy-start(bf16[32,320,1,1,1]{1,0,4,3,2:T(8,128)(2,1)} %constant.43) | copy-start | bytes 61444
  7.2 45.4 %all-gather.5.cloned.1.call-start = ((), (), s32[]{:S(2)}) async-start(), calls=%async_computation | async-start | bytes 1474560 | tf_op jit(solution)/shard_map/all_gather | solution.py:285
  9.0 20.8 %copy-start.9 = (pred[8,320]{1,0:T(8,128)(4,1)S(1)}, pred[8,320]{1,0:T(8,128)(4,1)}, u32[]{:S(2)}) copy-start(pred[8,320]{1,0:T(8,128)(4,1)} %constant.39.clone) | copy-start | bytes 7684
  9.0 20.8 %copy-start.10 = (pred[8,320]{1,0:T(8,128)(4,1)S(1)}, pred[8,320]{1,0:T(8,128)(4,1)}, u32[]{:S(2)}) copy-start(pred[8,320]{1,0:T(8,128)(4,1)} %constant.38.clone) | copy-start | bytes 7684
  9.0 20.8 %copy-start.11 = (pred[8,320]{1,0:T(8,128)(4,1)S(1)}, pred[8,320]{1,0:T(8,128)(4,1)}, u32[]{:S(2)}) copy-start(pred[8,320]{1,0:T(8,128)(4,1)} %constant.37.clone) | copy-start | bytes 7684
  9.0 18.8 %collective-permute-start.1 = (bf16[32,12,8,128]{3,2,1,0:T(8,128)(2,1)}, bf16[32,12,8,128]{3,2,1,0:T(8,128)(2,1)S(1)}, u32[]{:S(2)}, u32[]{:S(2)}) collective-permute-start(bf16[32,12,8,128]{3,2,1,0:T(8,128)(2,1)} %refs_0_.1), channel_id=1, source_target_pairs={{0,2},{1,3},{2,0},{3,1},{4,6},{5,7},{6,4},{7,5},{8,10},{9,11},{10,... | collective-permute-start | bytes 2359304 | tf_op jit(solution)/shard_map/ppermute | solution.py:262
  9.3 28.6 %collective-permute-start = (bf16[32,12,8,128]{3,2,1,0:T(8,128)(2,1)}, bf16[32,12,8,128]{3,2,1,0:T(8,128)(2,1)}, u32[]{:S(2)}, u32[]{:S(2)}) collective-permute-start(bf16[32,12,8,128]{3,2,1,0:T(8,128)(2,1)} %refs_0_.1), channel_id=1, source_target_pairs={{0,1},{1,0},{2,3},{3,2},{4,5},{5,4},{6,7},{7,6},{8,9},{9,8},{10,11... | collective-permute-start | bytes 2359304 | tf_op jit(solution)/shard_map/ppermute | solution.py:262
  12.0 17.4 %collective-permute-start.3 = (bf16[12,32,128]{2,1,0:T(8,128)(2,1)S(1)}, bf16[12,32,128]{2,1,0:T(8,128)(2,1)S(1)}, u32[]{:S(2)}, u32[]{:S(2)}) collective-permute-start(bf16[12,32,128]{2,1,0:T(8,128)(2,1)S(1)} %bitcast.37), channel_id=1, source_target_pairs={{0,4},{4,8},{8,12},{12,16},{16,20},{20,24},{24,28},{1,5},{5,9},{9,... | collective-permute-start | bytes 294920 | tf_op jit(solution)/shard_map/ppermute | solution.py:22
  15.2 14.3 %collective-permute-start.4 = (bf16[12,32,128]{2,1,0:T(8,128)(2,1)S(1)}, bf16[12,32,128]{2,1,0:T(8,128)(2,1)S(1)}, u32[]{:S(2)}, u32[]{:S(2)}) collective-permute-start(bf16[12,32,128]{2,1,0:T(8,128)(2,1)S(1)} %bitcast.38), channel_id=1, source_target_pairs={{4,0},{8,4},{12,8},{16,12},{20,16},{24,20},{28,24},{5,1},{9,5},{13... | collective-permute-start | bytes 294920 | tf_op jit(solution)/shard_map/ppermute | solution.py:22
  19.3 18.6 %copy-start.1 = (bf16[32,12,8,128]{3,2,1,0:T(8,128)(2,1)S(1)}, bf16[32,12,8,128]{3,2,1,0:T(8,128)(2,1)}, u32[]{:S(2)}) copy-start(bf16[32,12,8,128]{3,2,1,0:T(8,128)(2,1)} %refs_0_.1) | copy-start | bytes 2359300
  27.8 10.1 %collective-permute-start.2 = (bf16[32,12,8,128]{3,2,1,0:T(8,128)(2,1)S(1)}, bf16[32,12,8,128]{3,2,1,0:T(8,128)(2,1)}, u32[]{:S(2)}, u32[]{:S(2)}) collective-permute-start(bf16[32,12,8,128]{3,2,1,0:T(8,128)(2,1)S(1)} %collective-permute-done.1.refs_2_), channel_id=1, source_target_pairs={{0,1},{1,0},{2,3},{3,2},{4,5},{5,4},{6,7},{7,6},{8,9},{9,8},{10,11... | collective-permute-start | bytes 2359304 | tf_op jit(solution)/shard_map/ppermute | solution.py:262
  29.5 6.6 %collective-permute-start.6 = (bf16[12,64,128]{2,1,0:T(8,128)(2,1)S(1)}, bf16[12,64,128]{2,1,0:T(8,128)(2,1)S(1)}, u32[]{:S(2)}, u32[]{:S(2)}) collective-permute-start(bf16[12,64,128]{2,1,0:T(8,128)(2,1)S(1)} %constant_dynamic-update-slice_fusion.refs_4_), channel_id=1, source_target_pairs={{0,2},{1,3},{2,0},{3,1},{4,6},{5,7},{6,4},{7,5},{8,10},{9,11},{10,... | collective-permute-start | bytes 589832 | tf_op jit(solution)/shard_map/ppermute | solution.py:262
  32.9 5.0 %collective-permute-start.5 = (bf16[12,64,128]{2,1,0:T(8,128)(2,1)S(1)}, bf16[12,64,128]{2,1,0:T(8,128)(2,1)S(1)}, u32[]{:S(2)}, u32[]{:S(2)}) collective-permute-start(bf16[12,64,128]{2,1,0:T(8,128)(2,1)S(1)} %constant_dynamic-update-slice_fusion.refs_4_), channel_id=1, source_target_pairs={{0,1},{1,0},{2,3},{3,2},{4,5},{5,4},{6,7},{7,6},{8,9},{9,8},{10,11... | collective-permute-start | bytes 589832 | tf_op jit(solution)/shard_map/ppermute | solution.py:262
  36.1 1.9 %collective-permute-start.7 = (bf16[12,64,128]{2,1,0:T(8,128)(2,1)S(1)}, bf16[12,64,128]{2,1,0:T(8,128)(2,1)S(1)}, u32[]{:S(2)}, u32[]{:S(2)}) collective-permute-start(bf16[12,64,128]{2,1,0:T(8,128)(2,1)S(1)} %collective-permute-done.6.refs_6_), channel_id=1, source_target_pairs={{0,1},{1,0},{2,3},{3,2},{4,5},{5,4},{6,7},{7,6},{8,9},{9,8},{10,11... | collective-permute-start | bytes 589832 | tf_op jit(solution)/shard_map/ppermute | solution.py:262
  49.0 1.9 %copy-start.4 = (bf16[50,320,128]{2,1,0:T(8,128)(2,1)}, bf16[50,320,128]{2,1,0:T(8,128)(2,1)S(1)}, u32[]{:S(2)}) copy-start(bf16[50,320,128]{2,1,0:T(8,128)(2,1)S(1)} %get-tuple-element.24.cot_s) | copy-start | bytes 12288004
  51.0 1.3 copy-start.6
  52.5 1.3 copy-start.2
  53.9 1.5 %copy-start.7 = (f32[48,80,128]{2,1,0:T(8,128)S(1)}, f32[48,80,128]{2,1,0:T(8,128)}, u32[]{:S(2)}) copy-start(f32[48,80,128]{2,1,0:T(8,128)} %copy-done.6) | copy-start | bytes 5898244
  55.4 13.7 %copy-start.3 = (f32[32,240]{1,0:T(8,128)S(1)}, f32[32,240]{1,0:T(8,128)}, u32[]{:S(2)}) copy-start(f32[32,240]{1,0:T(8,128)} %constant.40.clone.fold_ref) | copy-start | bytes 92164
  55.4 13.7 %copy-start.5 = (bf16[50,320,128]{2,1,0:T(8,128)(2,1)S(1)}, bf16[50,320,128]{2,1,0:T(8,128)(2,1)}, u32[]{:S(2)}) copy-start(bf16[50,320,128]{2,1,0:T(8,128)(2,1)} %copy-done.4) | copy-start | bytes 12288004
  60.7 43.5 %collective-permute-start.8 = (bf16[80,8,128]{2,1,0:T(8,128)(2,1)S(1)}, bf16[80,8,128]{2,1,0:T(8,128)(2,1)S(1)}, u32[]{:S(2)}, u32[]{:S(2)}) collective-permute-start(bf16[80,8,128]{2,1,0:T(8,128)(2,1)S(1)} %get-tuple-element.17), channel_id=1, source_target_pairs={{24,0},{28,4},{25,1},{29,5},{26,2},{30,6},{27,3},{31,7}} | collective-permute-start | bytes 491528 | tf_op jit(solution)/shard_map/ppermute | solution.py:22
  61.3 63.6 %collective-permute-start.9 = (bf16[80,8,128]{2,1,0:T(8,128)(2,1)S(1)}, bf16[80,8,128]{2,1,0:T(8,128)(2,1)}, u32[]{:S(2)}, u32[]{:S(2)}) collective-permute-start(bf16[80,8,128]{2,1,0:T(8,128)(2,1)S(1)} %get-tuple-element.18), channel_id=1, source_target_pairs={{20,0},{24,4},{28,8},{21,1},{25,5},{29,9},{22,2},{26,6},{30,10},{2... | collective-permute-start | bytes 491528 | tf_op jit(solution)/shard_map/ppermute | solution.py:22
  62.6 62.3 %collective-permute-start.10 = (bf16[80,8,128]{2,1,0:T(8,128)(2,1)S(1)}, bf16[80,8,128]{2,1,0:T(8,128)(2,1)}, u32[]{:S(2)}, u32[]{:S(2)}) collective-permute-start(bf16[80,8,128]{2,1,0:T(8,128)(2,1)S(1)} %get-tuple-element.19), channel_id=1, source_target_pairs={{16,0},{20,4},{24,8},{28,12},{17,1},{21,5},{25,9},{29,13},{18,2},{... | collective-permute-start | bytes 491528 | tf_op jit(solution)/shard_map/ppermute | solution.py:22
  63.9 61.0 %collective-permute-start.11 = (bf16[80,8,128]{2,1,0:T(8,128)(2,1)S(1)}, bf16[80,8,128]{2,1,0:T(8,128)(2,1)}, u32[]{:S(2)}, u32[]{:S(2)}) collective-permute-start(bf16[80,8,128]{2,1,0:T(8,128)(2,1)S(1)} %get-tuple-element.20), channel_id=1, source_target_pairs={{12,0},{16,4},{20,8},{24,12},{28,16},{13,1},{17,5},{21,9},{25,13},... | collective-permute-start | bytes 491528 | tf_op jit(solution)/shard_map/ppermute | solution.py:22
  65.2 59.7 %collective-permute-start.12 = (bf16[80,8,128]{2,1,0:T(8,128)(2,1)S(1)}, bf16[80,8,128]{2,1,0:T(8,128)(2,1)}, u32[]{:S(2)}, u32[]{:S(2)}) collective-permute-start(bf16[80,8,128]{2,1,0:T(8,128)(2,1)S(1)} %get-tuple-element.21), channel_id=1, source_target_pairs={{8,0},{12,4},{16,8},{20,12},{24,16},{28,20},{9,1},{13,5},{17,9},{2... | collective-permute-start | bytes 491528 | tf_op jit(solution)/shard_map/ppermute | solution.py:22
  104.2 20.8 %collective-permute-start.13 = (bf16[80,8,128]{2,1,0:T(8,128)(2,1)S(1)}, bf16[80,8,128]{2,1,0:T(8,128)(2,1)}, u32[]{:S(2)}, u32[]{:S(2)}) collective-permute-start(bf16[80,8,128]{2,1,0:T(8,128)(2,1)S(1)} %get-tuple-element.22), channel_id=1, source_target_pairs={{4,0},{8,4},{12,8},{16,12},{20,16},{24,20},{28,24},{5,1},{9,5},{13... | collective-permute-start | bytes 491528 | tf_op jit(solution)/shard_map/ppermute | solution.py:22
Sparse Core Ops, SparseCore 0:
  10.8 41.7 all-gather.4

commit v2 on v1

v2 whole, which is shorter than its diff:
```python
import functools
import math

import jax
import jax.numpy as jnp
import numpy as np
from jax import lax
from jax.experimental import pallas as pl
from jax.experimental.pallas import tpu as pltpu
from jax.sharding import PartitionSpec as P

C = 320
G = 40
D = 48
GROUP = C // G
HIGHEST = lax.Precision.HIGHEST


def shifted(value, axis, steps):
    count = lax.axis_size(axis)
    leading, last = (max(0, -steps), min(count, count - steps))
    return lax.ppermute(value, axis, [(source, source + steps) for source in range(leading, last)])


def conv_rows(outs, width):
    main = np.tile(np.arange(width), outs)
    return np.concatenate([main, np.full(outs, -1), np.full(outs, width)])


def toeplitz(kernel_local, width):
    outs, groups = kernel_local.shape[3:]
    row_col = conv_rows(outs, width)
    row_out = np.concatenate([np.repeat(np.arange(outs), width), np.tile(np.arange(outs), 2)])
    spread = np.zeros((outs, row_col.size), np.float32)
    spread[row_out, np.arange(row_col.size)] = 1
    taps = jnp.transpose(kernel_local[::-1], (1, 2, 4, 0, 3))
    wide = jnp.einsum(
        "qrgpo,ok->qrgpk", taps, jnp.asarray(spread, jnp.bfloat16),
        preferred_element_type=jnp.float32,
    ).astype(jnp.bfloat16)
    out_col = np.arange(width)
    column_tap = out_col[:, None] - row_col[None, :] + 1
    total = jnp.zeros((3, groups, width, 3, row_col.size), jnp.bfloat16)
    for tap in range(3):
        mask = jnp.asarray(column_tap == tap)[None, None, :, None, :]
        total = jnp.where(mask, wide[tap][:, :, None], total)
    return total.reshape(3 * groups * width, 3 * row_col.size)


def roll_zero(value, steps):
    size = value.shape[-1]
    lane = lax.broadcasted_iota(jnp.int32, value.shape, value.ndim - 1)
    moved = pltpu.roll(value, steps % size, value.ndim - 1)
    return jnp.where(lane == (0 if steps > 0 else size - 1), 0.0, moved)


def convolution_grads(parts, hops, places, *refs):
    cot_refs, halo_refs, refs = refs[:parts], refs[parts : 2 * parts], refs[2 * parts :]
    right_refs, refs = refs[: hops + 1], refs[hops + 1 :]
    left_ref, weight_ref, fold_ref, right_s, gv_s, sums_ref, cot_s, vol_s, prod_s = refs
    channels, width, rows = left_ref.shape
    groups = channels // GROUP
    outs, levels = cot_refs[0].shape[:2]
    main = outs * width
    span = main + 2 * outs
    size = groups * width
    reach = hops * width
    f32, bf16 = jnp.float32, jnp.bfloat16

    cot_s[0] = jnp.zeros((span, rows), bf16)
    cot_s[D + 1] = jnp.zeros((span, rows), bf16)
    for other in range(parts):
        start = (places[0] ^ other) * levels + 1

        def assemble(level, carry, other=other, start=start):
            value = cot_refs[other][:, level].reshape(main, rows)
            cot_s[start + level, 0:main] = value
            cot_s[start + level, main:span] = halo_refs[other][level]
            return carry

        lax.fori_loop(0, levels, assemble, 0)

    def grad_volume_step(pair, carry):
        first = pair * 2
        near = cot_s[pl.ds(first, 3)].reshape(3 * span, rows)
        far = cot_s[pl.ds(first + 1, 3)].reshape(3 * span, rows)
        result = jnp.dot(
            weight_ref[...], jnp.concatenate([near, far], axis=1), preferred_element_type=f32
        )
        for half in range(2):
            part = result[:, half * rows : (half + 1) * rows]
            total = (
                part[size : 2 * size]
                + roll_zero(part[:size], -1)
                + roll_zero(part[2 * size :], 1)
            )
            gv_s[first + half] = total.astype(bf16).astype(f32)
        return carry

    lax.fori_loop(0, D // 2, grad_volume_step, 0)

    for hop in range(hops + 1):
        at = reach - hop * width
        right_s[:, at : at + width] = right_refs[hop][...].astype(f32)

    def volume_step(group, carry):
        first = group * GROUP
        lefts = [left_ref[first + k].astype(f32) for k in range(GROUP)]
        rows_at = pl.ds(pl.multiple_of(group * width, width), width)
        for d in range(D):
            total = lefts[0] * right_s[first, reach - d : reach - d + width]
            for k in range(1, GROUP):
                total = total + lefts[k] * right_s[first + k, reach - d : reach - d + width]
            value = (total * (1.0 / GROUP)).astype(bf16).astype(f32)
            vol_s[d, 0, rows_at] = roll_zero(value, 1)
            vol_s[d, 1, rows_at] = value
            vol_s[d, 2, rows_at] = roll_zero(value, -1)
        return carry

    lax.fori_loop(0, groups, volume_step, 0)

    chunk = 4
    prod_s[...] = jnp.zeros(prod_s.shape, f32)

    def kernel_step(step, carry):
        first = step * chunk
        volume = jnp.concatenate(
            [vol_s[first + k].reshape(3 * size, rows).astype(bf16) for k in range(chunk)], axis=1
        )
        for tap in range(3):
            value = jnp.concatenate([cot_s[first + k + tap] for k in range(chunk)], axis=1)
            prod_s[tap] += lax.dot_general(
                value, volume, (((1,), (1,)), ((), ())), preferred_element_type=f32
            )
        return carry

    lax.fori_loop(0, D // chunk, kernel_step, 0)

    col_in = lax.broadcasted_iota(jnp.int32, (width, 3 * size), 0)
    col_out = lax.broadcasted_iota(jnp.int32, (width, 3 * size), 1) % width
    edge = lax.broadcasted_iota(jnp.int32, (outs, 3 * size), 1) % width
    for column_tap in range(3):
        mask = col_out - col_in + 1 == column_tap
        taps = []
        for tap in range(3):
            value = prod_s[tap, 0:main].reshape(outs, width, 3 * size)
            total = jnp.sum(jnp.where(mask[None], value, 0.0), axis=1)
            if column_tap == 2:
                total = total + jnp.where(edge == 0, prod_s[tap, main : main + outs], 0.0)
            if column_tap == 0:
                total = total + jnp.where(edge == width - 1, prod_s[tap, main + outs : span], 0.0)
            taps.append(total)
        gathered = jnp.concatenate(taps, axis=0)
        sums_ref[column_tap] = lax.dot_general(
            fold_ref[...], gathered, (((1,), (1,)), ((), ())),
            precision=HIGHEST, preferred_element_type=f32,
        )


def feature_grads(hops, left_ref, right_s, gv_s, grad_left_ref, own_ref, *rest):
    sent_refs, (grad_s,) = rest[:hops], rest[hops:]
    channels, width, rows = left_ref.shape
    groups = channels // GROUP
    reach = hops * width
    f32, bf16 = jnp.float32, jnp.bfloat16
    grad_s[...] = jnp.zeros(grad_s.shape, f32)

    def grads_step(group, carry):
        first = group * GROUP
        lefts = [left_ref[first + k].astype(f32) for k in range(GROUP)]
        totals = [jnp.zeros((width, rows), f32) for k in range(GROUP)]
        rows_at = pl.ds(pl.multiple_of(group * width, width), width)
        for d in range(D):
            value = gv_s[d, rows_at]
            for k in range(GROUP):
                totals[k] = totals[k] + value * right_s[first + k, reach - d : reach - d + width]
                grad_s[first + k, reach - d : reach - d + width] += value * lefts[k]
        for k in range(GROUP):
            grad_left_ref[first + k] = (totals[k] * (1.0 / GROUP)).astype(bf16)
        return carry

    lax.fori_loop(0, groups, grads_step, 0)
    own_ref[...] = grad_s[:, reach : reach + width] * (1.0 / GROUP)
    for hop in range(1, hops + 1):
        at = reach - hop * width
        sent_refs[hop - 1][...] = (grad_s[:, at : at + width] * (1.0 / GROUP)).astype(bf16)


VMEM = pl.BlockSpec(memory_space=pltpu.VMEM)
SMEM = pl.BlockSpec(memory_space=pltpu.SMEM)
MIB = 1024 * 1024


def run_convolution_grads(places, cots, halos, rights, left, weights, fold):
    outs, levels, width, rows = cots[0].shape
    channels = left.shape[0]
    size = fold.shape[1]
    span = outs * (width + 2)
    f32 = jnp.float32
    return pl.pallas_call(
        functools.partial(convolution_grads, len(cots), len(rights) - 1),
        out_shape=[
            jax.ShapeDtypeStruct((channels, len(rights) * width, rows), f32),
            jax.ShapeDtypeStruct((D, size // 3, rows), f32),
            jax.ShapeDtypeStruct((3, fold.shape[0], 3 * outs), f32),
        ],
        in_specs=[SMEM] + [VMEM] * (2 * len(cots) + len(rights) + 3),
        out_specs=[VMEM] * 3,
        scratch_shapes=[
            pltpu.VMEM((D + 2, span, rows), jnp.bfloat16),
            pltpu.VMEM((D, 3, size // 3, rows), f32),
            pltpu.VMEM((3, span, size), f32),
        ],
        compiler_params=pltpu.CompilerParams(vmem_limit_bytes=24 * MIB),
        cost_estimate=pl.CostEstimate(flops=8000000000, bytes_accessed=20000000, transcendentals=0),
    )(places, *cots, *halos, *rights, left, weights, fold)


def run_feature_grads(left, right_wide, grad_volume, hops):
    channels, width, rows = left.shape
    f32, bf16 = jnp.float32, jnp.bfloat16
    return pl.pallas_call(
        functools.partial(feature_grads, hops),
        out_shape=[
            jax.ShapeDtypeStruct((channels, width, rows), bf16),
            jax.ShapeDtypeStruct((channels, width, rows), f32),
            *[jax.ShapeDtypeStruct((channels, width, rows), bf16)] * hops,
        ],
        in_specs=[VMEM] * 3,
        out_specs=[VMEM] * (hops + 2),
        scratch_shapes=[pltpu.VMEM((channels, (hops + 1) * width, rows), f32)],
        compiler_params=pltpu.CompilerParams(vmem_limit_bytes=12 * MIB),
        cost_estimate=pl.CostEstimate(flops=4000000000, bytes_accessed=10000000, transcendentals=0),
    )(left, right_wide, grad_volume)


def swapped(value, axis, bit):
    count = lax.axis_size(axis)
    return lax.ppermute(value, axis, [(source, source ^ bit) for source in range(count)])


def gather_swapping(value, axis):
    held = {0: value}
    bit = lax.axis_size(axis) // 2
    while bit:
        held.update({key | bit: swapped(item, axis, bit) for key, item in list(held.items())})
        bit //= 2
    return [held[key] for key in range(len(held))]


def total_swapping(value, axis):
    bit = lax.axis_size(axis) // 2
    while bit:
        value = value + swapped(value, axis, bit)
        bit //= 2
    return value


def body(left, right, kernel, cotangent):
    outs, levels, width, rows = cotangent.shape
    parts = lax.axis_size("disp")
    channels = C // parts
    groups = G // parts
    hops = (D + width - 2) // width
    part = lax.axis_index("disp")
    places = part.astype(jnp.int32)[None]

    cots = gather_swapping(cotangent, "disp")
    low = shifted(jnp.transpose(cotangent[:, :, width - 1], (1, 0, 2)), "col", 1)
    high = shifted(jnp.transpose(cotangent[:, :, 0], (1, 0, 2)), "col", -1)
    halos = gather_swapping(jnp.concatenate([low, high], axis=1), "disp")
    right_own = lax.dynamic_slice_in_dim(right, part * channels, channels, 0)
    rights = [right_own] + [shifted(right_own, "col", hop) for hop in range(1, hops + 1)]

    left_own = lax.dynamic_slice_in_dim(left, part * channels, channels, 0)
    weights = toeplitz(lax.dynamic_slice_in_dim(kernel, part * groups, groups, 4), width)
    pad_rows = -(-3 * groups // 8) * 8
    fold = np.zeros((pad_rows, 3 * groups * width), np.float32)
    fold[np.arange(3 * groups * width) // width, np.arange(3 * groups * width)] = 1

    right_wide, grad_volume, sums = run_convolution_grads(
        places, cots, halos, rights, left_own, weights, jnp.asarray(fold)
    )
    results = run_feature_grads(left_own, right_wide, grad_volume, hops)
    grad_left, own, sent = results[0], results[1], results[2:]

    total = total_swapping(sums, "col")
    pieces = jnp.stack(gather_swapping(total, "disp"))
    pieces = pieces[jnp.arange(parts) ^ part][:, :, : 3 * groups]
    total = pieces.reshape(parts, 3, 3, groups, 3, outs)
    cell_count = D * width * lax.axis_size("col") * rows
    grad_kernel = jnp.transpose(total, (4, 1, 2, 5, 0, 3))[::-1].reshape(3, 3, 3, outs, G)
    grad_kernel = grad_kernel * (1.0 / math.sqrt(cell_count))

    total_right = own
    for hop in range(hops, 0, -1):
        total_right = total_right + shifted(sent[hop - 1], "col", -hop).astype(jnp.float32)
    return (grad_left, total_right.astype(jnp.bfloat16), grad_kernel)


def solution(mesh):
    return jax.shard_map(
        body,
        mesh=mesh,
        in_specs=(P(None, "col", None), P(None, "col", None), P(), P(None, "disp", "col", None)),
        out_specs=(P("disp", "col", None), P("disp", "col", None), P()),
        check_vma=False,
    )
```

time: 134 us -> 124 us (0.925)
  the two profiles are of different devices: /device:TPU:11 before, /device:TPU:13 now
where the time goes in v2:
time: 124 us; the launch traced here: 123 us
  starting transfers between devices  46.7 us (38%)
  waiting for transfers between devices  34.7 us (28%)
  Pallas kernels  24.5 us (20%)
  local copies, waits for them, and re-layouts  13.7 us (11%)
  other arithmetic  2.39 us (2%)
    ppermute x14, starting transfers between devices, shifted(): lax.ppermute(value, axis, [(source, source + steps) for source in range(l...  28.9 us
    ppermute x14, waiting for transfers between devices, shifted(): lax.ppermute(value, axis, [(source, source + steps) for source in range(l...  23.9 us
    pallas_call x1, Pallas kernels, run_convolution_grads(): pl.pallas_call(functools.partial(convolution_grads, len(cots), len(rights...  19.8 us
    ppermute x12, starting transfers between devices, swapped(): lax.ppermute(value, axis, [(source, source ^ bit) for source in range(cou...  17.8 us
    ppermute x12, waiting for transfers between devices, swapped(): lax.ppermute(value, axis, [(source, source ^ bit) for source in range(cou...  10.7 us
    unnamed x38, local copies, waits for them, and re-layouts  6.96 us
    pallas_call x1, Pallas kernels, run_feature_grads(): pl.pallas_call(functools.partial(feature_grads, hops), out_shape=[jax.Sha...  4.73 us
  transfers between devices with their start and end apart: 26, of which 7 were waited for; matrix products, arithmetic and copies ran while one was open for 7% of the time, Pallas kernels for 0%

profile of v2, /device:TPU:13, one launch (start us, length us, event | category | flops | bytes accessed | tf_op | source)
XLA Modules:
  0.0 123.4 jit_solution(16256064846597359082)
XLA Ops:
  0.7 1.3 %collective-permute-start.1 = (bf16[32,12,8,128]{3,2,1,0:T(8,128)(2,1)}, bf16[32,12,8,128]{3,2,1,0:T(8,128)(2,1)S(1)}, u32[]{:S(2)}, u32[]{:S(2)}) collective-permute-start(bf16[32,12,8,128]{3,2,1,0:T(8,128)(2,1)} %refs_0_.1), channel_id=1, source_target_pairs={{0,2},{1,3},{2,0},{3,1},{4,6},{5,7},{6,4},{7,5},{8,10},{9,11},{10,... | collective-permute-start | bytes 2359304 | tf_op jit(solution)/shard_map/ppermute | solution.py:239
  2.0 4.3 %collective-permute-start.10 = (bf16[80,8,128]{2,1,0:T(8,128)(2,1)S(1)}, bf16[80,8,128]{2,1,0:T(8,128)(2,1)S(1)}, u32[]{:S(2)}, u32[]{:S(2)}) collective-permute-start(bf16[80,8,128]{2,1,0:T(8,128)(2,1)S(1)} %constant_dynamic-slice_fusion.1.refs_8_), channel_id=1, source_target_pairs={{0,12},{4,16},{8,20},{12,24},{16,28},{1,13},{5,17},{9,21},{13,25},... | collective-permute-start | bytes 491528 | tf_op jit(solution)/shard_map/ppermute | solution.py:22
  6.3 1.4 %collective-permute-start.11 = (bf16[80,8,128]{2,1,0:T(8,128)(2,1)S(1)}, bf16[80,8,128]{2,1,0:T(8,128)(2,1)S(1)}, u32[]{:S(2)}, u32[]{:S(2)}) collective-permute-start(bf16[80,8,128]{2,1,0:T(8,128)(2,1)S(1)} %constant_dynamic-slice_fusion.1.refs_8_), channel_id=1, source_target_pairs={{0,16},{4,20},{8,24},{12,28},{1,17},{5,21},{9,25},{13,29},{2,18},{... | collective-permute-start | bytes 491528 | tf_op jit(solution)/shard_map/ppermute | solution.py:22
  7.7 1.7 %fusion.2 = (bf16[32,12,1,128]{3,2,1,0:T(2,128)(2,1)S(1)}, bf16[32,12,1,128]{3,2,1,0:T(2,128)(2,1)S(1)}) fusion(bf16[32,12,8,128]{3,2,1,0:T(8,128)(2,1)} %refs_0_.1), kind=kLoop, calls=%fused_computation.22 | loop fusion | bytes 393216 | tf_op jit(solution)/shard_map/slice | solution.py:270
  9.4 3.1 %collective-permute-start.3 = (bf16[12,32,128]{2,1,0:T(8,128)(2,1)S(1)}, bf16[12,32,128]{2,1,0:T(8,128)(2,1)S(1)}, u32[]{:S(2)}, u32[]{:S(2)}) collective-permute-start(bf16[12,32,128]{2,1,0:T(8,128)(2,1)S(1)} %bitcast.39), channel_id=1, source_target_pairs={{0,4},{4,8},{8,12},{12,16},{16,20},{20,24},{24,28},{1,5},{5,9},{9,... | collective-permute-start | bytes 294920 | tf_op jit(solution)/shard_map/ppermute | solution.py:22
  12.5 2.2 %collective-permute-start.4 = (bf16[12,32,128]{2,1,0:T(8,128)(2,1)S(1)}, bf16[12,32,128]{2,1,0:T(8,128)(2,1)S(1)}, u32[]{:S(2)}, u32[]{:S(2)}) collective-permute-start(bf16[12,32,128]{2,1,0:T(8,128)(2,1)S(1)} %bitcast.38), channel_id=1, source_target_pairs={{4,0},{8,4},{12,8},{16,12},{20,16},{24,20},{28,24},{5,1},{9,5},{13... | collective-permute-start | bytes 294920 | tf_op jit(solution)/shard_map/ppermute | solution.py:22
  14.7 1.1 constant_dynamic-slice_fusion
  16.2 10.1 %collective-permute-done.3 = bf16[12,32,128]{2,1,0:T(8,128)(2,1)S(1)} collective-permute-done((bf16[12,32,128]{2,1,0:T(8,128)(2,1)S(1)}, bf16[12,32,128]{2,1,0:T(8,128)(2,1)S(1)}, u32[]{:S(2)}, u32[]{:S(2)}) %collective-permute-start.3) | collective-permute-done | bytes 98336 | tf_op jit(solution)/shard_map/ppermute | solution.py:22
  28.3 5.0 %collective-permute-start.8 = (bf16[80,8,128]{2,1,0:T(8,128)(2,1)S(1)}, bf16[80,8,128]{2,1,0:T(8,128)(2,1)S(1)}, u32[]{:S(2)}, u32[]{:S(2)}) collective-permute-start(bf16[80,8,128]{2,1,0:T(8,128)(2,1)S(1)} %constant_dynamic-slice_fusion.1.refs_8_), channel_id=1, source_target_pairs={{0,4},{4,8},{8,12},{12,16},{16,20},{20,24},{24,28},{1,5},{5,9},{9,... | collective-permute-start | bytes 491528 | tf_op jit(solution)/shard_map/ppermute | solution.py:22
  33.4 1.1 collective-permute-start.6
  35.2 1.9 %collective-permute-start.9 = (bf16[80,8,128]{2,1,0:T(8,128)(2,1)S(1)}, bf16[80,8,128]{2,1,0:T(8,128)(2,1)}, u32[]{:S(2)}, u32[]{:S(2)}) collective-permute-start(bf16[80,8,128]{2,1,0:T(8,128)(2,1)S(1)} %constant_dynamic-slice_fusion.1.refs_8_), channel_id=1, source_target_pairs={{0,8},{4,12},{8,16},{12,20},{16,24},{20,28},{1,9},{5,13},{9,17},{1... | collective-permute-start | bytes 491528 | tf_op jit(solution)/shard_map/ppermute | solution.py:22
  37.8 1.0 collective-permute-start.5
  39.2 1.6 %collective-permute-start.7 = (bf16[12,64,128]{2,1,0:T(8,128)(2,1)S(1)}, bf16[12,64,128]{2,1,0:T(8,128)(2,1)}, u32[]{:S(2)}, u32[]{:S(2)}) collective-permute-start(bf16[12,64,128]{2,1,0:T(8,128)(2,1)S(1)} %collective-permute-done.6.refs_6_), channel_id=1, source_target_pairs={{0,1},{1,0},{2,3},{3,2},{4,5},{5,4},{6,7},{7,6},{8,9},{9,8},{10,11... | collective-permute-start | bytes 589832 | tf_op jit(solution)/shard_map/ppermute | solution.py:239
  40.8 1.4 %select_select_fusion = bf16[3,10,8,3,320]{4,3,2,1,0:T(4,128)(2,1)} fusion(pred[8,320]{1,0:T(8,128)(4,1)S(1)} %copy-done.14, pred[8,320]{1,0:T(8,128)(4,1)S(1)} %copy-done.15, pred[8,320]{1,0:T(8,128)(4,1)S(1)} %copy-done.16, bf16[3,10,3,320]{3,2,1,0:T(4,128)(2,1)S(1)} %copy.33, bf16[3,10,3,320]{3,2,1,0:T(4,128)(2,1)S(1)} %copy.32, ...), kind=kLoop, calls=%fused_computation.2 | loop fusion | flops 691200 | bytes 641280 | tf_op jit(solution)/shard_map/jit(_where)/select_n | solution.py:46
  42.2 1.7 %select_n.40.refs_16_ = bf16[240,960]{1,0:T(8,128)(2,1)S(1)} reshape(bf16[3,10,8,3,320]{4,3,2,1,0:T(4,128)(2,1)} %select_select_fusion) | data formatting | bytes 921600 | tf_op jit(solution)/shard_map/jit(_where)/select_n | solution.py:46
  43.8 0.9 constant_dynamic-slice_fusion.2.refs_15_.left_ref
  46.7 0.9 copy-done.7
  49.4 19.8 %shard_map.112 = (f32[80,56,128]{2,1,0:T(8,128)S(1)}, f32[48,80,128]{2,1,0:T(8,128)S(1)}, f32[3,32,96]{2,1,0:T(8,128)S(1)}) custom-call(s32[1]{0:T(128)} %bitcast.places, bf16[32,12,8,128]{3,2,1,0:T(8,128)(2,1)S(1)} %copy-done.1, bf16[32,12,8,128]{3,2,1,0:T(8,128)(2,1)} %collective-permute-done.refs_1_, ...), custom_call_target="tpu_custom_call" | custom-call | flops 8000000000 | bytes 20000000 | tf_op jit(solution)/shard_map/pallas_call | solution.py:200
  69.2 4.7 %shard_map.113 = (bf16[80,8,128]{2,1,0:T(8,128)(2,1)}, f32[80,8,128]{2,1,0:T(8,128)S(1)}, bf16[80,8,128]{2,1,0:T(8,128)(2,1)S(1)}, bf16[80,8,128]{2,1,0:T(8,128)...) custom-call(bf16[80,8,128]{2,1,0:T(8,128)(2,1)S(1)} %constant_dynami, ...), custom_call_target="tpu_custom_call" | custom-call | flops 4000000000 | bytes 10000000 | tf_op jit(solution)/shard_map/pallas_call | solution.py:222
  74.6 3.9 %collective-permute-start.20 = (f32[3,32,96]{2,1,0:T(8,128)S(1)}, f32[3,32,96]{2,1,0:T(8,128)S(1)}, u32[]{:S(2)}, u32[]{:S(2)}) collective-permute-start(f32[3,32,96]{2,1,0:T(8,128)S(1)} %get-tuple-element.24), channel_id=1, source_target_pairs={{0,16},{4,20},{8,24},{12,28},{16,0},{20,4},{24,8},{28,12},{1,17},{... | collective-permute-start | bytes 110600 | tf_op jit(solution)/shard_map/ppermute | solution.py:239
  78.5 4.5 %collective-permute-done.20 = f32[3,32,96]{2,1,0:T(8,128)S(1)} collective-permute-done((f32[3,32,96]{2,1,0:T(8,128)S(1)}, f32[3,32,96]{2,1,0:T(8,128)S(1)}, u32[]{:S(2)}, u32[]{:S(2)}) %collective-permute-start.20) | collective-permute-done | bytes 36896 | tf_op jit(solution)/shard_map/ppermute | solution.py:239
  83.1 2.9 %collective-permute-done.21 = f32[3,32,96]{2,1,0:T(8,128)S(1)} collective-permute-done((f32[3,32,96]{2,1,0:T(8,128)S(1)}, f32[3,32,96]{2,1,0:T(8,128)S(1)}, u32[]{:S(2)}, u32[]{:S(2)}) %collective-permute-start.21) | collective-permute-done | bytes 36896 | tf_op jit(solution)/shard_map/ppermute | solution.py:239
  86.1 2.9 %collective-permute-done.22 = f32[3,32,96]{2,1,0:T(8,128)S(1)} collective-permute-done((f32[3,32,96]{2,1,0:T(8,128)S(1)}, f32[3,32,96]{2,1,0:T(8,128)S(1)}, u32[]{:S(2)}, u32[]{:S(2)}) %collective-permute-start.22) | collective-permute-done | bytes 36896 | tf_op jit(solution)/shard_map/ppermute | solution.py:239
  90.3 1.3 %collective-permute-start.16 = (bf16[80,8,128]{2,1,0:T(8,128)(2,1)S(1)}, bf16[80,8,128]{2,1,0:T(8,128)(2,1)S(1)}, u32[]{:S(2)}, u32[]{:S(2)}) collective-permute-start(bf16[80,8,128]{2,1,0:T(8,128)(2,1)S(1)} %get-tuple-element.20), channel_id=1, source_target_pairs={{16,0},{20,4},{24,8},{28,12},{17,1},{21,5},{25,9},{29,13},{18,2},{... | collective-permute-start | bytes 491528 | tf_op jit(solution)/shard_map/ppermute | solution.py:22
  91.6 3.2 %collective-permute-start.17 = (bf16[80,8,128]{2,1,0:T(8,128)(2,1)S(1)}, bf16[80,8,128]{2,1,0:T(8,128)(2,1)S(1)}, u32[]{:S(2)}, u32[]{:S(2)}) collective-permute-start(bf16[80,8,128]{2,1,0:T(8,128)(2,1)S(1)} %get-tuple-element.21), channel_id=1, source_target_pairs={{12,0},{16,4},{20,8},{24,12},{28,16},{13,1},{17,5},{21,9},{25,13},... | collective-permute-start | bytes 491528 | tf_op jit(solution)/shard_map/ppermute | solution.py:22
  94.8 1.9 %collective-permute-start.18 = (bf16[80,8,128]{2,1,0:T(8,128)(2,1)S(1)}, bf16[80,8,128]{2,1,0:T(8,128)(2,1)S(1)}, u32[]{:S(2)}, u32[]{:S(2)}) collective-permute-start(bf16[80,8,128]{2,1,0:T(8,128)(2,1)S(1)} %get-tuple-element.22), channel_id=1, source_target_pairs={{8,0},{12,4},{16,8},{20,12},{24,16},{28,20},{9,1},{13,5},{17,9},{2... | collective-permute-start | bytes 491528 | tf_op jit(solution)/shard_map/ppermute | solution.py:22
  96.8 1.9 %collective-permute-start.19 = (bf16[80,8,128]{2,1,0:T(8,128)(2,1)S(1)}, bf16[80,8,128]{2,1,0:T(8,128)(2,1)S(1)}, u32[]{:S(2)}, u32[]{:S(2)}) collective-permute-start(bf16[80,8,128]{2,1,0:T(8,128)(2,1)S(1)} %get-tuple-element.23), channel_id=1, source_target_pairs={{4,0},{8,4},{12,8},{16,12},{20,16},{24,20},{28,24},{5,1},{9,5},{13... | collective-permute-start | bytes 491528 | tf_op jit(solution)/shard_map/ppermute | solution.py:22
  98.7 3.7 %collective-permute-start.23 = (f32[3,32,96]{2,1,0:T(8,128)S(1)}, f32[3,32,96]{2,1,0:T(8,128)S(1)}, u32[]{:S(2)}, u32[]{:S(2)}) collective-permute-start(f32[3,32,96]{2,1,0:T(8,128)S(1)} %add.54), channel_id=1, source_target_pairs={{0,1},{1,0},{2,3},{3,2},{4,5},{5,4},{6,7},{7,6},{8,9},{9,8},{10,11... | collective-permute-start | bytes 110600 | tf_op jit(solution)/shard_map/ppermute | solution.py:239
  102.5 4.0 %collective-permute-start.25 = (f32[3,32,96]{2,1,0:T(8,128)S(1)}, f32[3,32,96]{2,1,0:T(8,128)S(1)}, u32[]{:S(2)}, u32[]{:S(2)}) collective-permute-start(f32[3,32,96]{2,1,0:T(8,128)S(1)} %collective-permute-done.24), channel_id=1, source_target_pairs={{0,1},{1,0},{2,3},{3,2},{4,5},{5,4},{6,7},{7,6},{8,9},{9,8},{10,11... | collective-permute-start | bytes 110600 | tf_op jit(solution)/shard_map/ppermute | solution.py:239
  106.4 8.9 %collective-permute-done.18 = bf16[80,8,128]{2,1,0:T(8,128)(2,1)S(1)} collective-permute-done((bf16[80,8,128]{2,1,0:T(8,128)(2,1)S(1)}, bf16[80,8,128]{2,1,0:T(8,128)(2,1)S(1)}, u32[]{:S(2)}, u32[]{:S(2)}) %collective-permute-start.18) | collective-permute-done | bytes 163872 | tf_op jit(solution)/shard_map/ppermute | solution.py:22
  115.3 5.0 %collective-permute-done.19 = bf16[80,8,128]{2,1,0:T(8,128)(2,1)S(1)} collective-permute-done((bf16[80,8,128]{2,1,0:T(8,128)(2,1)S(1)}, bf16[80,8,128]{2,1,0:T(8,128)(2,1)S(1)}, u32[]{:S(2)}, u32[]{:S(2)}) %collective-permute-start.19) | collective-permute-done | bytes 163872 | tf_op jit(solution)/shard_map/ppermute | solution.py:22
  122.5 1.0 copy.37
  (86 shorter events, 12.1 us)
Async XLA Ops:
  0.6 15.2 %copy-start.13 = (bf16[32,320,1,1,1]{1,0,4,3,2:T(8,128)(2,1)S(1)}, bf16[32,320,1,1,1]{1,0,4,3,2:T(8,128)(2,1)}, u32[]{:S(2)}) copy-start(bf16[32,320,1,1,1]{1,0,4,3,2:T(8,128)(2,1)} %constant.36) | copy-start | bytes 61444
  0.7 26.3 %copy-start.1 = (bf16[32,12,8,128]{3,2,1,0:T(8,128)(2,1)S(1)}, bf16[32,12,8,128]{3,2,1,0:T(8,128)(2,1)}, u32[]{:S(2)}) copy-start(bf16[32,12,8,128]{3,2,1,0:T(8,128)(2,1)} %refs_0_.1) | copy-start | bytes 2359300
  0.7 26.8 %collective-permute-start.1 = (bf16[32,12,8,128]{3,2,1,0:T(8,128)(2,1)}, bf16[32,12,8,128]{3,2,1,0:T(8,128)(2,1)S(1)}, u32[]{:S(2)}, u32[]{:S(2)}) collective-permute-start(bf16[32,12,8,128]{3,2,1,0:T(8,128)(2,1)} %refs_0_.1), channel_id=1, source_target_pairs={{0,2},{1,3},{2,0},{3,1},{4,6},{5,7},{6,4},{7,5},{8,10},{9,11},{10,... | collective-permute-start | bytes 2359304 | tf_op jit(solution)/shard_map/ppermute | solution.py:239
  2.0 38.8 %copy-start.14 = (pred[8,320]{1,0:T(8,128)(4,1)S(1)}, pred[8,320]{1,0:T(8,128)(4,1)}, u32[]{:S(2)}) copy-start(pred[8,320]{1,0:T(8,128)(4,1)} %constant.32.clone) | copy-start | bytes 7684
  2.0 38.8 %copy-start.15 = (pred[8,320]{1,0:T(8,128)(4,1)S(1)}, pred[8,320]{1,0:T(8,128)(4,1)}, u32[]{:S(2)}) copy-start(pred[8,320]{1,0:T(8,128)(4,1)} %constant.33.clone) | copy-start | bytes 7684
  2.0 38.8 %copy-start.16 = (pred[8,320]{1,0:T(8,128)(4,1)S(1)}, pred[8,320]{1,0:T(8,128)(4,1)}, u32[]{:S(2)}) copy-start(pred[8,320]{1,0:T(8,128)(4,1)} %constant.34.clone) | copy-start | bytes 7684
  2.0 25.6 %collective-permute-start.10 = (bf16[80,8,128]{2,1,0:T(8,128)(2,1)S(1)}, bf16[80,8,128]{2,1,0:T(8,128)(2,1)S(1)}, u32[]{:S(2)}, u32[]{:S(2)}) collective-permute-start(bf16[80,8,128]{2,1,0:T(8,128)(2,1)S(1)} %constant_dynamic-slice_fusion.1.refs_8_), channel_id=1, source_target_pairs={{0,12},{4,16},{8,20},{12,24},{16,28},{1,13},{5,17},{9,21},{13,25},... | collective-permute-start | bytes 491528 | tf_op jit(solution)/shard_map/ppermute | solution.py:22
  6.3 22.0 %collective-permute-start.11 = (bf16[80,8,128]{2,1,0:T(8,128)(2,1)S(1)}, bf16[80,8,128]{2,1,0:T(8,128)(2,1)S(1)}, u32[]{:S(2)}, u32[]{:S(2)}) collective-permute-start(bf16[80,8,128]{2,1,0:T(8,128)(2,1)S(1)} %constant_dynamic-slice_fusion.1.refs_8_), channel_id=1, source_target_pairs={{0,16},{4,20},{8,24},{12,28},{1,17},{5,21},{9,25},{13,29},{2,18},{... | collective-permute-start | bytes 491528 | tf_op jit(solution)/shard_map/ppermute | solution.py:22
  9.4 16.8 %collective-permute-start.3 = (bf16[12,32,128]{2,1,0:T(8,128)(2,1)S(1)}, bf16[12,32,128]{2,1,0:T(8,128)(2,1)S(1)}, u32[]{:S(2)}, u32[]{:S(2)}) collective-permute-start(bf16[12,32,128]{2,1,0:T(8,128)(2,1)S(1)} %bitcast.39), channel_id=1, source_target_pairs={{0,4},{4,8},{8,12},{12,16},{16,20},{20,24},{24,28},{1,5},{5,9},{9,... | collective-permute-start | bytes 294920 | tf_op jit(solution)/shard_map/ppermute | solution.py:22
  12.5 14.4 %collective-permute-start.4 = (bf16[12,32,128]{2,1,0:T(8,128)(2,1)S(1)}, bf16[12,32,128]{2,1,0:T(8,128)(2,1)S(1)}, u32[]{:S(2)}, u32[]{:S(2)}) collective-permute-start(bf16[12,32,128]{2,1,0:T(8,128)(2,1)S(1)} %bitcast.38), channel_id=1, source_target_pairs={{4,0},{8,4},{12,8},{16,12},{20,16},{24,20},{28,24},{5,1},{9,5},{13... | collective-permute-start | bytes 294920 | tf_op jit(solution)/shard_map/ppermute | solution.py:22
  15.9 29.0 %copy-start.12 = (f32[32,240]{1,0:T(8,128)S(1)}, f32[32,240]{1,0:T(8,128)}, u32[]{:S(2)}) copy-start(f32[32,240]{1,0:T(8,128)} %constant.35.clone.refs_17_) | copy-start | bytes 92164
  26.2 7.1 %collective-permute-start.12 = (bf16[80,8,128]{2,1,0:T(8,128)(2,1)S(1)}, bf16[80,8,128]{2,1,0:T(8,128)(2,1)S(1)}, u32[]{:S(2)}, u32[]{:S(2)}) collective-permute-start(bf16[80,8,128]{2,1,0:T(8,128)(2,1)S(1)} %constant_dynamic-slice_fusion.1.refs_8_), channel_id=1, source_target_pairs={{0,20},{4,24},{8,28},{1,21},{5,25},{9,29},{2,22},{6,26},{10,30},{3... | collective-permute-start | bytes 491528 | tf_op jit(solution)/shard_map/ppermute | solution.py:22
  26.9 17.9 %collective-permute-start = (bf16[32,12,8,128]{3,2,1,0:T(8,128)(2,1)S(1)}, bf16[32,12,8,128]{3,2,1,0:T(8,128)(2,1)}, u32[]{:S(2)}, u32[]{:S(2)}) collective-permute-start(bf16[32,12,8,128]{3,2,1,0:T(8,128)(2,1)S(1)} %copy-done.1), channel_id=1, source_target_pairs={{0,1},{1,0},{2,3},{3,2},{4,5},{5,4},{6,7},{7,6},{8,9},{9,8},{10,11... | collective-permute-start | bytes 2359304 | tf_op jit(solution)/shard_map/ppermute | solution.py:239
  27.5 17.3 %collective-permute-start.2 = (bf16[32,12,8,128]{3,2,1,0:T(8,128)(2,1)S(1)}, bf16[32,12,8,128]{3,2,1,0:T(8,128)(2,1)}, u32[]{:S(2)}, u32[]{:S(2)}) collective-permute-start(bf16[32,12,8,128]{3,2,1,0:T(8,128)(2,1)S(1)} %collective-permute-done.1.refs_2_), channel_id=1, source_target_pairs={{0,1},{1,0},{2,3},{3,2},{4,5},{5,4},{6,7},{7,6},{8,9},{9,8},{10,11... | collective-permute-start | bytes 2359304 | tf_op jit(solution)/shard_map/ppermute | solution.py:239
  27.6 7.0 %collective-permute-start.13 = (bf16[80,8,128]{2,1,0:T(8,128)(2,1)S(1)}, bf16[80,8,128]{2,1,0:T(8,128)(2,1)S(1)}, u32[]{:S(2)}, u32[]{:S(2)}) collective-permute-start(bf16[80,8,128]{2,1,0:T(8,128)(2,1)S(1)} %constant_dynamic-slice_fusion.1.refs_8_), channel_id=1, source_target_pairs={{0,24},{4,28},{1,25},{5,29},{2,26},{6,30},{3,27},{7,31}} | collective-permute-start | bytes 491528 | tf_op jit(solution)/shard_map/ppermute | solution.py:22
  28.3 8.8 %collective-permute-start.8 = (bf16[80,8,128]{2,1,0:T(8,128)(2,1)S(1)}, bf16[80,8,128]{2,1,0:T(8,128)(2,1)S(1)}, u32[]{:S(2)}, u32[]{:S(2)}) collective-permute-start(bf16[80,8,128]{2,1,0:T(8,128)(2,1)S(1)} %constant_dynamic-slice_fusion.1.refs_8_), channel_id=1, source_target_pairs={{0,4},{4,8},{8,12},{12,16},{16,20},{20,24},{24,28},{1,5},{5,9},{9,... | collective-permute-start | bytes 491528 | tf_op jit(solution)/shard_map/ppermute | solution.py:22
  33.4 5.8 %collective-permute-start.6 = (bf16[12,64,128]{2,1,0:T(8,128)(2,1)S(1)}, bf16[12,64,128]{2,1,0:T(8,128)(2,1)S(1)}, u32[]{:S(2)}, u32[]{:S(2)}) collective-permute-start(bf16[12,64,128]{2,1,0:T(8,128)(2,1)S(1)} %constant_dynamic-update-slice_fusion.refs_4_), channel_id=1, source_target_pairs={{0,2},{1,3},{2,0},{3,1},{4,6},{5,7},{6,4},{7,5},{8,10},{9,11},{10,... | collective-permute-start | bytes 589832 | tf_op jit(solution)/shard_map/ppermute | solution.py:239
  35.2 9.5 %collective-permute-start.9 = (bf16[80,8,128]{2,1,0:T(8,128)(2,1)S(1)}, bf16[80,8,128]{2,1,0:T(8,128)(2,1)}, u32[]{:S(2)}, u32[]{:S(2)}) collective-permute-start(bf16[80,8,128]{2,1,0:T(8,128)(2,1)S(1)} %constant_dynamic-slice_fusion.1.refs_8_), channel_id=1, source_target_pairs={{0,8},{4,12},{8,16},{12,20},{16,24},{20,28},{1,9},{5,13},{9,17},{1... | collective-permute-start | bytes 491528 | tf_op jit(solution)/shard_map/ppermute | solution.py:22
  37.8 6.9 %collective-permute-start.5 = (bf16[12,64,128]{2,1,0:T(8,128)(2,1)S(1)}, bf16[12,64,128]{2,1,0:T(8,128)(2,1)S(1)}, u32[]{:S(2)}, u32[]{:S(2)}) collective-permute-start(bf16[12,64,128]{2,1,0:T(8,128)(2,1)S(1)} %constant_dynamic-update-slice_fusion.refs_4_), channel_id=1, source_target_pairs={{0,1},{1,0},{2,3},{3,2},{4,5},{5,4},{6,7},{7,6},{8,9},{9,8},{10,11... | collective-permute-start | bytes 589832 | tf_op jit(solution)/shard_map/ppermute | solution.py:239
  39.2 5.6 %collective-permute-start.7 = (bf16[12,64,128]{2,1,0:T(8,128)(2,1)S(1)}, bf16[12,64,128]{2,1,0:T(8,128)(2,1)}, u32[]{:S(2)}, u32[]{:S(2)}) collective-permute-start(bf16[12,64,128]{2,1,0:T(8,128)(2,1)S(1)} %collective-permute-done.6.refs_6_), channel_id=1, source_target_pairs={{0,1},{1,0},{2,3},{3,2},{4,5},{5,4},{6,7},{7,6},{8,9},{9,8},{10,11... | collective-permute-start | bytes 589832 | tf_op jit(solution)/shard_map/ppermute | solution.py:239
  73.9 22.8 %collective-permute-start.14 = (bf16[80,8,128]{2,1,0:T(8,128)(2,1)S(1)}, bf16[80,8,128]{2,1,0:T(8,128)(2,1)S(1)}, u32[]{:S(2)}, u32[]{:S(2)}) collective-permute-start(bf16[80,8,128]{2,1,0:T(8,128)(2,1)S(1)} %get-tuple-element.18), channel_id=1, source_target_pairs={{24,0},{28,4},{25,1},{29,5},{26,2},{30,6},{27,3},{31,7}} | collective-permute-start | bytes 491528 | tf_op jit(solution)/shard_map/ppermute | solution.py:22
  74.6 8.4 %collective-permute-start.20 = (f32[3,32,96]{2,1,0:T(8,128)S(1)}, f32[3,32,96]{2,1,0:T(8,128)S(1)}, u32[]{:S(2)}, u32[]{:S(2)}) collective-permute-start(f32[3,32,96]{2,1,0:T(8,128)S(1)} %get-tuple-element.24), channel_id=1, source_target_pairs={{0,16},{4,20},{8,24},{12,28},{16,0},{20,4},{24,8},{28,12},{1,17},{... | collective-permute-start | bytes 110600 | tf_op jit(solution)/shard_map/ppermute | solution.py:239
  83.0 3.0 %collective-permute-start.21 = (f32[3,32,96]{2,1,0:T(8,128)S(1)}, f32[3,32,96]{2,1,0:T(8,128)S(1)}, u32[]{:S(2)}, u32[]{:S(2)}) collective-permute-start(f32[3,32,96]{2,1,0:T(8,128)S(1)} %add.52), channel_id=1, source_target_pairs={{0,8},{4,12},{8,0},{12,4},{16,24},{20,28},{24,16},{28,20},{1,9},{5... | collective-permute-start | bytes 110600 | tf_op jit(solution)/shard_map/ppermute | solution.py:239
  86.1 3.0 %collective-permute-start.22 = (f32[3,32,96]{2,1,0:T(8,128)S(1)}, f32[3,32,96]{2,1,0:T(8,128)S(1)}, u32[]{:S(2)}, u32[]{:S(2)}) collective-permute-start(f32[3,32,96]{2,1,0:T(8,128)S(1)} %add.53), channel_id=1, source_target_pairs={{0,4},{4,0},{8,12},{12,8},{16,20},{20,16},{24,28},{28,24},{1,5},{5... | collective-permute-start | bytes 110600 | tf_op jit(solution)/shard_map/ppermute | solution.py:239
  89.1 5.7 %collective-permute-start.24 = (f32[3,32,96]{2,1,0:T(8,128)S(1)}, f32[3,32,96]{2,1,0:T(8,128)S(1)}, u32[]{:S(2)}, u32[]{:S(2)}) collective-permute-start(f32[3,32,96]{2,1,0:T(8,128)S(1)} %add.54), channel_id=1, source_target_pairs={{0,2},{1,3},{2,0},{3,1},{4,6},{5,7},{6,4},{7,5},{8,10},{9,11},{10,... | collective-permute-start | bytes 110600 | tf_op jit(solution)/shard_map/ppermute | solution.py:239
  89.6 9.1 %collective-permute-start.15 = (bf16[80,8,128]{2,1,0:T(8,128)(2,1)S(1)}, bf16[80,8,128]{2,1,0:T(8,128)(2,1)S(1)}, u32[]{:S(2)}, u32[]{:S(2)}) collective-permute-start(bf16[80,8,128]{2,1,0:T(8,128)(2,1)S(1)} %get-tuple-element.19), channel_id=1, source_target_pairs={{20,0},{24,4},{28,8},{21,1},{25,5},{29,9},{22,2},{26,6},{30,10},{2... | collective-permute-start | bytes 491528 | tf_op jit(solution)/shard_map/ppermute | solution.py:22
  90.3 12.2 %collective-permute-start.16 = (bf16[80,8,128]{2,1,0:T(8,128)(2,1)S(1)}, bf16[80,8,128]{2,1,0:T(8,128)(2,1)S(1)}, u32[]{:S(2)}, u32[]{:S(2)}) collective-permute-start(bf16[80,8,128]{2,1,0:T(8,128)(2,1)S(1)} %get-tuple-element.20), channel_id=1, source_target_pairs={{16,0},{20,4},{24,8},{28,12},{17,1},{21,5},{25,9},{29,13},{18,2},{... | collective-permute-start | bytes 491528 | tf_op jit(solution)/shard_map/ppermute | solution.py:22
  91.6 14.9 %collective-permute-start.17 = (bf16[80,8,128]{2,1,0:T(8,128)(2,1)S(1)}, bf16[80,8,128]{2,1,0:T(8,128)(2,1)S(1)}, u32[]{:S(2)}, u32[]{:S(2)}) collective-permute-start(bf16[80,8,128]{2,1,0:T(8,128)(2,1)S(1)} %get-tuple-element.21), channel_id=1, source_target_pairs={{12,0},{16,4},{20,8},{24,12},{28,16},{13,1},{17,5},{21,9},{25,13},... | collective-permute-start | bytes 491528 | tf_op jit(solution)/shard_map/ppermute | solution.py:22
  94.8 20.5 %collective-permute-start.18 = (bf16[80,8,128]{2,1,0:T(8,128)(2,1)S(1)}, bf16[80,8,128]{2,1,0:T(8,128)(2,1)S(1)}, u32[]{:S(2)}, u32[]{:S(2)}) collective-permute-start(bf16[80,8,128]{2,1,0:T(8,128)(2,1)S(1)} %get-tuple-element.22), channel_id=1, source_target_pairs={{8,0},{12,4},{16,8},{20,12},{24,16},{28,20},{9,1},{13,5},{17,9},{2... | collective-permute-start | bytes 491528 | tf_op jit(solution)/shard_map/ppermute | solution.py:22
  96.8 23.5 %collective-permute-start.19 = (bf16[80,8,128]{2,1,0:T(8,128)(2,1)S(1)}, bf16[80,8,128]{2,1,0:T(8,128)(2,1)S(1)}, u32[]{:S(2)}, u32[]{:S(2)}) collective-permute-start(bf16[80,8,128]{2,1,0:T(8,128)(2,1)S(1)} %get-tuple-element.23), channel_id=1, source_target_pairs={{4,0},{8,4},{12,8},{16,12},{20,16},{24,20},{28,24},{5,1},{9,5},{13... | collective-permute-start | bytes 491528 | tf_op jit(solution)/shard_map/ppermute | solution.py:22
  98.7 22.4 %collective-permute-start.23 = (f32[3,32,96]{2,1,0:T(8,128)S(1)}, f32[3,32,96]{2,1,0:T(8,128)S(1)}, u32[]{:S(2)}, u32[]{:S(2)}) collective-permute-start(f32[3,32,96]{2,1,0:T(8,128)S(1)} %add.54), channel_id=1, source_target_pairs={{0,1},{1,0},{2,3},{3,2},{4,5},{5,4},{6,7},{7,6},{8,9},{9,8},{10,11... | collective-permute-start | bytes 110600 | tf_op jit(solution)/shard_map/ppermute | solution.py:239
  102.5 18.6 %collective-permute-start.25 = (f32[3,32,96]{2,1,0:T(8,128)S(1)}, f32[3,32,96]{2,1,0:T(8,128)S(1)}, u32[]{:S(2)}, u32[]{:S(2)}) collective-permute-start(f32[3,32,96]{2,1,0:T(8,128)S(1)} %collective-permute-done.24), channel_id=1, source_target_pairs={{0,1},{1,0},{2,3},{3,2},{4,5},{5,4},{6,7},{7,6},{8,9},{9,8},{10,11... | collective-permute-start | bytes 110600 | tf_op jit(solution)/shard_map/ppermute | solution.py:239
  (11 other events, 40.2 us)

commit v3 on v2

v3 whole, which is shorter than its diff:
```python
import functools
import math

import jax
import jax.numpy as jnp
import numpy as np
from jax import lax
from jax.experimental import pallas as pl
from jax.experimental.pallas import tpu as pltpu
from jax.sharding import PartitionSpec as P

C = 320
G = 40
D = 48
GROUP = C // G
HIGHEST = lax.Precision.HIGHEST


def shifted(value, axis, steps):
    count = lax.axis_size(axis)
    leading, last = (max(0, -steps), min(count, count - steps))
    return lax.ppermute(value, axis, [(source, source + steps) for source in range(leading, last)])


def toeplitz(kernel_local, width, row_out, row_col):
    outs, groups = kernel_local.shape[3:]
    spread = np.zeros((outs, row_col.size), np.float32)
    spread[row_out, np.arange(row_col.size)] = 1
    taps = jnp.transpose(kernel_local[::-1], (1, 2, 4, 0, 3))
    wide = jnp.einsum(
        "qrgpo,ok->qrgpk", taps, jnp.asarray(spread, jnp.bfloat16),
        preferred_element_type=jnp.float32,
    ).astype(jnp.bfloat16)
    column_tap = np.arange(width)[:, None] - row_col[None, :] + 1
    total = jnp.zeros((3, groups, width, 3, row_col.size), jnp.bfloat16)
    for tap in range(3):
        mask = jnp.asarray(column_tap == tap)[None, None, :, None, :]
        total = jnp.where(mask, wide[tap][:, :, None], total)
    return total.reshape(3 * groups * width, 3 * row_col.size)


def roll_zero(value, steps):
    size = value.shape[-1]
    lane = lax.broadcasted_iota(jnp.int32, value.shape, value.ndim - 1)
    moved = pltpu.roll(value, steps % size, value.ndim - 1)
    return jnp.where(lane == (0 if steps > 0 else size - 1), 0.0, moved)


def sum_row_taps(part, size):
    return (
        part[size : 2 * size]
        + roll_zero(part[:size], -1)
        + roll_zero(part[2 * size :], 1)
    )


def segment_grad_volume(places, first_ref, second_ref, weight_ref, cot_s, gv_s, low_ref, high_ref):
    outs, levels, width, rows = first_ref.shape
    main = outs * width
    size = gv_s.shape[1]
    f32, bf16 = jnp.float32, jnp.bfloat16
    second_first = places[0] & 1
    for edge in (0, 1, 2 * levels + 2, 2 * levels + 3):
        cot_s[edge] = jnp.zeros((main, rows), bf16)
    for ref, start in (
        (first_ref, second_first * levels),
        (second_ref, (1 - second_first) * levels),
    ):

        def assemble(level, carry, ref=ref, start=start):
            value = ref[:, level]
            cot_s[start + level + 2] = value.reshape(main, rows)
            wide = value.astype(f32)
            low_ref[start + level] = wide[:, width - 1].astype(bf16)
            high_ref[start + level] = wide[:, 0].astype(bf16)
            return carry

        lax.fori_loop(0, levels, assemble, 0)

    def step(pair, carry):
        at = pair * 2
        near = cot_s[pl.ds(at, 3)].reshape(3 * main, rows)
        far = cot_s[pl.ds(at + 1, 3)].reshape(3 * main, rows)
        result = jnp.dot(
            weight_ref[...], jnp.concatenate([near, far], axis=1), preferred_element_type=f32
        )
        for half in range(2):
            gv_s[at + half] = sum_row_taps(result[:, half * rows : (half + 1) * rows], size)
        return carry

    lax.fori_loop(0, levels + 1, step, 0)


def segment_start(places, segment, levels):
    return ((places[0] ^ (2 * segment)) & ~1) * levels


def fold_columns(fold_ref, value):
    return lax.dot_general(
        fold_ref[...], value, (((1,), (1,)), ((), ())),
        precision=HIGHEST, preferred_element_type=jnp.float32,
    )


def main_kernel_sums(segments, hops, places, *refs):
    seg_refs, refs = refs[:segments], refs[segments:]
    right_refs, refs = refs[: hops + 1], refs[hops + 1 :]
    left_ref, fold_ref, right_s, vol_out, sums_ref, cot_s, vol_s, prod_s = refs
    channels, width, rows = left_ref.shape
    groups = channels // GROUP
    levels = seg_refs[0].shape[0] // 2 - 2
    main = cot_s.shape[1]
    outs = main // width
    size = groups * width
    reach = hops * width
    f32, bf16 = jnp.float32, jnp.bfloat16

    for hop in range(hops + 1):
        at = reach - hop * width
        right_s[:, at : at + width] = right_refs[hop][...].astype(f32)

    cot_s[0] = jnp.zeros((main, rows), bf16)
    cot_s[D + 1] = jnp.zeros((main, rows), bf16)
    for segment in range(segments):
        start = segment_start(places, segment, levels)

        def move(level, carry, segment=segment, start=start):
            cot_s[start + level + 1] = seg_refs[segment][level + 2]
            return carry

        lax.fori_loop(0, 2 * levels, move, 0)

    def volume_step(group, carry):
        first = group * GROUP
        lefts = [left_ref[first + k].astype(f32) for k in range(GROUP)]
        rows_at = pl.ds(pl.multiple_of(group * width, width), width)
        for d in range(D):
            total = lefts[0] * right_s[first, reach - d : reach - d + width]
            for k in range(1, GROUP):
                total = total + lefts[k] * right_s[first + k, reach - d : reach - d + width]
            value = (total * (1.0 / GROUP)).astype(bf16).astype(f32)
            vol_s[d, 0, rows_at] = roll_zero(value, 1)
            vol_s[d, 1, rows_at] = value
            vol_s[d, 2, rows_at] = roll_zero(value, -1)
        return carry

    lax.fori_loop(0, groups, volume_step, 0)

    chunk = 4
    prod_s[...] = jnp.zeros(prod_s.shape, f32)

    def kernel_step(step, carry):
        first = step * chunk
        volumes = [vol_s[first + k].reshape(3 * size, rows).astype(bf16) for k in range(chunk)]
        for k in range(chunk):
            vol_out[first + k] = volumes[k]
        volume = jnp.concatenate(volumes, axis=1)
        for tap in range(3):
            value = jnp.concatenate([cot_s[first + k + tap] for k in range(chunk)], axis=1)
            prod_s[tap] += lax.dot_general(
                value, volume, (((1,), (1,)), ((), ())), preferred_element_type=f32
            )
        return carry

    lax.fori_loop(0, D // chunk, kernel_step, 0)

    col_in = lax.broadcasted_iota(jnp.int32, (width, 3 * size), 0)
    col_out = lax.broadcasted_iota(jnp.int32, (width, 3 * size), 1) % width
    for column_tap in range(3):
        mask = col_out - col_in + 1 == column_tap
        taps = []
        for tap in range(3):
            value = prod_s[tap].reshape(outs, width, 3 * size)
            taps.append(jnp.sum(jnp.where(mask[None], value, 0.0), axis=1))
        sums_ref[column_tap] = fold_columns(fold_ref, jnp.concatenate(taps, axis=0))


def halo_kernel_sums(segments, width, places, *refs):
    low_refs, high_refs, refs = refs[:segments], refs[segments : 2 * segments], refs[2 * segments :]
    vol_ref, part_ref, fold_ref, sums_ref, halo_s, prod_s = refs
    levels, outs, rows = low_refs[0].shape
    size = vol_ref.shape[1]
    f32, bf16 = jnp.float32, jnp.bfloat16
    halo_s[0] = jnp.zeros((2 * outs, rows), bf16)
    halo_s[D + 1] = jnp.zeros((2 * outs, rows), bf16)
    for segment in range(segments):
        start = segment_start(places, segment, levels // 2)

        def move(level, carry, segment=segment, start=start):
            halo_s[start + level + 1, 0:outs] = low_refs[segment][level]
            halo_s[start + level + 1, outs : 2 * outs] = high_refs[segment][level]
            return carry

        lax.fori_loop(0, levels, move, 0)

    chunk = 4
    prod_s[...] = jnp.zeros(prod_s.shape, f32)

    def kernel_step(step, carry):
        first = step * chunk
        volume = jnp.concatenate([vol_ref[first + k] for k in range(chunk)], axis=1)
        value = jnp.concatenate(
            [
                jnp.concatenate([halo_s[first + k + tap] for k in range(chunk)], axis=1)
                for tap in range(3)
            ],
            axis=0,
        )
        prod_s[...] += lax.dot_general(
            value, volume, (((1,), (1,)), ((), ())), preferred_element_type=f32
        )
        return carry

    lax.fori_loop(0, D // chunk, kernel_step, 0)

    edge = lax.broadcasted_iota(jnp.int32, (3 * outs, size), 1) % width
    lows = [prod_s[2 * tap * outs : (2 * tap + 1) * outs] for tap in range(3)]
    highs = [prod_s[(2 * tap + 1) * outs : (2 * tap + 2) * outs] for tap in range(3)]
    low = jnp.where(edge == 0, jnp.concatenate(lows, axis=0), 0.0)
    high = jnp.where(edge == width - 1, jnp.concatenate(highs, axis=0), 0.0)
    sums_ref[0] = part_ref[0] + fold_columns(fold_ref, high)
    sums_ref[1] = part_ref[1]
    sums_ref[2] = part_ref[2] + fold_columns(fold_ref, low)


def total_grad_volume(segments, places, *refs):
    part_refs, (halo_ref, weight_ref, gv_ref, sum_s) = refs[:segments], refs[segments:]
    levels = part_refs[0].shape[0] // 2 - 1
    rows = halo_ref.shape[2]
    span = halo_ref.shape[1]
    size = gv_ref.shape[1]
    f32, bf16 = jnp.float32, jnp.bfloat16
    sum_s[...] = jnp.zeros(sum_s.shape, f32)
    for segment in range(segments):
        start = segment_start(places, segment, levels)

        def move(level, carry, segment=segment, start=start):
            sum_s[start + level] += part_refs[segment][level]
            return carry

        lax.fori_loop(0, 2 * levels + 2, move, 0)

    def step(pair, carry):
        at = pair * 2
        near = halo_ref[pl.ds(at, 3)].reshape(3 * span, rows)
        far = halo_ref[pl.ds(at + 1, 3)].reshape(3 * span, rows)
        result = jnp.dot(
            weight_ref[...], jnp.concatenate([near, far], axis=1), preferred_element_type=f32
        )
        for half in range(2):
            total = sum_row_taps(result[:, half * rows : (half + 1) * rows], size)
            gv_ref[at + half] = (total + sum_s[at + half + 1]).astype(bf16).astype(f32)
        return carry

    lax.fori_loop(0, D // 2, step, 0)


def feature_grads(hops, left_ref, right_s, gv_s, grad_left_ref, own_ref, *rest):
    sent_refs, (grad_s,) = rest[:hops], rest[hops:]
    channels, width, rows = left_ref.shape
    groups = channels // GROUP
    reach = hops * width
    f32, bf16 = jnp.float32, jnp.bfloat16
    grad_s[...] = jnp.zeros(grad_s.shape, f32)

    def grads_step(group, carry):
        first = group * GROUP
        lefts = [left_ref[first + k].astype(f32) for k in range(GROUP)]
        totals = [jnp.zeros((width, rows), f32) for k in range(GROUP)]
        rows_at = pl.ds(pl.multiple_of(group * width, width), width)
        for d in range(D):
            value = gv_s[d, rows_at]
            for k in range(GROUP):
                totals[k] = totals[k] + value * right_s[first + k, reach - d : reach - d + width]
                grad_s[first + k, reach - d : reach - d + width] += value * lefts[k]
        for k in range(GROUP):
            grad_left_ref[first + k] = (totals[k] * (1.0 / GROUP)).astype(bf16)
        return carry

    lax.fori_loop(0, groups, grads_step, 0)
    own_ref[...] = grad_s[:, reach : reach + width] * (1.0 / GROUP)
    for hop in range(1, hops + 1):
        at = reach - hop * width
        sent_refs[hop - 1][...] = (grad_s[:, at : at + width] * (1.0 / GROUP)).astype(bf16)


VMEM = pl.BlockSpec(memory_space=pltpu.VMEM)
SMEM = pl.BlockSpec(memory_space=pltpu.SMEM)
MIB = 1024 * 1024


def run(function, places, operands, outs, scratch, limit, flops):
    return pl.pallas_call(
        function,
        out_shape=[jax.ShapeDtypeStruct(shape, kind) for shape, kind in outs],
        in_specs=[SMEM] + [VMEM] * len(operands),
        out_specs=[VMEM] * len(outs),
        scratch_shapes=[pltpu.VMEM(shape, kind) for shape, kind in scratch],
        compiler_params=pltpu.CompilerParams(vmem_limit_bytes=limit * MIB),
        cost_estimate=pl.CostEstimate(flops=flops, bytes_accessed=4 * MIB, transcendentals=0),
    )(places, *operands)


def run_feature_grads(left, right_wide, grad_volume, hops):
    channels, width, rows = left.shape
    f32, bf16 = jnp.float32, jnp.bfloat16
    return pl.pallas_call(
        functools.partial(feature_grads, hops),
        out_shape=[
            jax.ShapeDtypeStruct((channels, width, rows), bf16),
            jax.ShapeDtypeStruct((channels, width, rows), f32),
            *[jax.ShapeDtypeStruct((channels, width, rows), bf16)] * hops,
        ],
        in_specs=[VMEM] * 3,
        out_specs=[VMEM] * (hops + 2),
        scratch_shapes=[pltpu.VMEM((channels, (hops + 1) * width, rows), f32)],
        compiler_params=pltpu.CompilerParams(vmem_limit_bytes=12 * MIB),
        cost_estimate=pl.CostEstimate(flops=4000000000, bytes_accessed=10000000, transcendentals=0),
    )(left, right_wide, grad_volume)


def swapped(value, axis, bit):
    count = lax.axis_size(axis)
    return lax.ppermute(value, axis, [(source, source ^ bit) for source in range(count)])


def gather_swapping(value, axis):
    held = {0: value}
    bit = lax.axis_size(axis) // 2
    while bit:
        held.update({key | bit: swapped(item, axis, bit) for key, item in list(held.items())})
        bit //= 2
    return [held[key] for key in range(len(held))]


def body(left, right, kernel, cotangent):
    outs, levels, width, rows = cotangent.shape
    parts = lax.axis_size("disp")
    channels = C // parts
    groups = G // parts
    hops = (D + width - 2) // width
    segments = parts // 2
    size = groups * width
    main = outs * width
    f32, bf16 = jnp.float32, jnp.bfloat16
    part = lax.axis_index("disp")
    places = part.astype(jnp.int32)[None]

    cots = gather_swapping(cotangent, "disp")
    right_own = lax.dynamic_slice_in_dim(right, part * channels, channels, 0)
    rights = [right_own] + [shifted(right_own, "col", hop) for hop in range(1, hops + 1)]

    left_own = lax.dynamic_slice_in_dim(left, part * channels, channels, 0)
    kernel_own = lax.dynamic_slice_in_dim(kernel, part * groups, groups, 4)
    channel = np.arange(outs)
    weights = toeplitz(
        kernel_own, width, np.repeat(channel, width), np.tile(np.arange(width), outs)
    )
    halo_weights = toeplitz(
        kernel_own, width, np.tile(channel, 2), np.repeat(np.array([-1, width]), outs)
    )
    pad_rows = -(-3 * groups // 8) * 8
    fold = np.zeros((pad_rows, 3 * size), np.float32)
    fold[np.arange(3 * size) // width, np.arange(3 * size)] = 1
    fold = jnp.asarray(fold)

    edge = ((2 * levels, outs, rows), bf16)
    spread = [
        run(
            segment_grad_volume, places, [cots[2 * k], cots[2 * k + 1], weights],
            [
                ((2 * levels + 4, main, rows), bf16),
                ((2 * levels + 2, size, rows), f32),
                edge, edge,
            ],
            [], 8, 2000000000,
        )
        for k in range(segments)
    ]
    lows = [shifted(item[2], "col", 1) for item in spread]
    highs = [shifted(item[3], "col", -1) for item in spread]

    right_wide, volume, main_sums = run(
        functools.partial(main_kernel_sums, segments, hops), places,
        [item[0] for item in spread] + rights + [left_own, fold],
        [
            ((channels, (hops + 1) * width, rows), f32),
            ((D, 3 * size, rows), bf16),
            ((3, pad_rows, 3 * outs), f32),
        ],
        [
            ((D + 2, main, rows), bf16),
            ((D, 3, size, rows), f32),
            ((3, main, 3 * size), f32),
        ],
        16, 4000000000,
    )
    sums, halo_wide = run(
        functools.partial(halo_kernel_sums, segments, width), places,
        lows + highs + [volume, main_sums, fold],
        [((3, pad_rows, 3 * outs), f32), ((D + 2, 2 * outs, rows), bf16)],
        [((6 * outs, 3 * size), f32)],
        8, 1000000000,
    )
    (grad_volume,) = run(
        functools.partial(total_grad_volume, segments), places,
        [item[1] for item in spread] + [halo_wide, halo_weights],
        [((D, size, rows), f32)], [((D + 2, size, rows), f32)], 8, 1000000000,
    )

    bit = lax.axis_size("col") // 2
    total = sums + swapped(sums, "col", bit)
    grad_volume, total = lax.optimization_barrier((grad_volume, total))
    bit //= 2
    results = run_feature_grads(left_own, right_wide, grad_volume, hops)
    grad_left, own, sent = results[0], results[1], results[2:]
    total = total + swapped(total, "col", bit)
    bit //= 2
    arrived = {hop: shifted(sent[hop - 1], "col", -hop) for hop in range(1, hops + 1)}
    total, arrived[1] = lax.optimization_barrier((total, arrived[1]))
    while bit:
        total = total + swapped(total, "col", bit)
        bit //= 2
    pieces = jnp.stack(gather_swapping(total, "disp"))
    pieces = pieces[jnp.arange(parts) ^ part][:, :, : 3 * groups]
    total = pieces.reshape(parts, 3, 3, groups, 3, outs)
    cell_count = D * width * lax.axis_size("col") * rows
    grad_kernel = jnp.transpose(total, (4, 1, 2, 5, 0, 3))[::-1].reshape(3, 3, 3, outs, G)
    grad_kernel = grad_kernel * (1.0 / math.sqrt(cell_count))

    total_right = own
    for hop in range(1, hops + 1):
        total_right = total_right + arrived[hop].astype(f32)
    return (grad_left, total_right.astype(bf16), grad_kernel)


def solution(mesh):
    return jax.shard_map(
        body,
        mesh=mesh,
        in_specs=(P(None, "col", None), P(None, "col", None), P(), P(None, "disp", "col", None)),
        out_specs=(P("disp", "col", None), P("disp", "col", None), P()),
        check_vma=False,
    )
```

time: 124 us -> 132 us (1.065)
  the two profiles are of different devices: /device:TPU:13 before, /device:TPU:0 now
where the time goes in v3:
time: 132 us; the launch traced here: 131 us
  starting transfers between devices  43.9 us (33%)
  waiting for transfers between devices  38.9 us (29%)
  Pallas kernels  35.5 us (27%)
  local copies, waits for them, and re-layouts  7.78 us (6%)
  other arithmetic  2.82 us (2%)
    ppermute x16, starting transfers between devices, shifted(): lax.ppermute(value, axis, [(source, source + steps) for source in range(l...  35.8 us
    pallas_call x5, Pallas kernels, run(): pl.pallas_call(function, out_shape=[jax.ShapeDtypeStruct(shape, kind) for...  31.1 us
    ppermute x9, waiting for transfers between devices, swapped(): lax.ppermute(value, axis, [(source, source ^ bit) for source in range(cou...  23.3 us
    ppermute x16, waiting for transfers between devices, shifted(): lax.ppermute(value, axis, [(source, source + steps) for source in range(l...  15.6 us
    ppermute x9, starting transfers between devices, swapped(): lax.ppermute(value, axis, [(source, source ^ bit) for source in range(cou...  8.15 us
    pallas_call x1, Pallas kernels, run_feature_grads(): pl.pallas_call(functools.partial(feature_grads, hops), out_shape=[jax.Sha...  4.44 us
  transfers between devices with their start and end apart: 25, of which 7 were waited for; matrix products, arithmetic and copies ran while one was open for 6% of the time, Pallas kernels for 21%

profile of v3, /device:TPU:0, one launch (start us, length us, event | category | flops | bytes accessed | tf_op | source)
XLA Modules:
  0.0 131.3 jit_solution(2437016868236014701)
XLA Ops:
  1.7 7.0 %collective-permute-start.8 = (bf16[80,8,128]{2,1,0:T(8,128)(2,1)S(1)}, bf16[80,8,128]{2,1,0:T(8,128)(2,1)S(1)}, u32[]{:S(2)}, u32[]{:S(2)}) collective-permute-start(bf16[80,8,128]{2,1,0:T(8,128)(2,1)S(1)} %constant_dynamic-slice_fusion.refs_2_), channel_id=1, source_target_pairs={{0,24},{4,28},{1,25},{5,29},{2,26},{6,30},{3,27},{7,31}} | collective-permute-start | bytes 491528 | tf_op jit(solution)/shard_map/ppermute | solution.py:22
  8.7 2.0 %collective-permute-start.7 = (bf16[80,8,128]{2,1,0:T(8,128)(2,1)S(1)}, bf16[80,8,128]{2,1,0:T(8,128)(2,1)}, u32[]{:S(2)}, u32[]{:S(2)}) collective-permute-start(bf16[80,8,128]{2,1,0:T(8,128)(2,1)S(1)} %constant_dynamic-slice_fusion.refs_2_), channel_id=1, source_target_pairs={{0,20},{4,24},{8,28},{1,21},{5,25},{9,29},{2,22},{6,26},{10,30},{3... | collective-permute-start | bytes 491528 | tf_op jit(solution)/shard_map/ppermute | solution.py:22
  10.7 2.0 %collective-permute-start.6 = (bf16[80,8,128]{2,1,0:T(8,128)(2,1)S(1)}, bf16[80,8,128]{2,1,0:T(8,128)(2,1)}, u32[]{:S(2)}, u32[]{:S(2)}) collective-permute-start(bf16[80,8,128]{2,1,0:T(8,128)(2,1)S(1)} %constant_dynamic-slice_fusion.refs_2_), channel_id=1, source_target_pairs={{0,16},{4,20},{8,24},{12,28},{1,17},{5,21},{9,25},{13,29},{2,18},{... | collective-permute-start | bytes 491528 | tf_op jit(solution)/shard_map/ppermute | solution.py:22
  12.6 1.5 %collective-permute-start.1 = (bf16[32,12,8,128]{3,2,1,0:T(8,128)(2,1)}, bf16[32,12,8,128]{3,2,1,0:T(8,128)(2,1)S(1)}, u32[]{:S(2)}, u32[]{:S(2)}) collective-permute-start(bf16[32,12,8,128]{3,2,1,0:T(8,128)(2,1)} %first_ref.1), channel_id=1, source_target_pairs={{0,2},{1,3},{2,0},{3,1},{4,6},{5,7},{6,4},{7,5},{8,10},{9,11},{10,... | collective-permute-start | bytes 2359304 | tf_op jit(solution)/shard_map/ppermute | solution.py:324
  14.1 1.1 constant_dynamic-slice_fusion.1
  16.6 16.2 %collective-permute-done.1.first_ref = bf16[32,12,8,128]{3,2,1,0:T(8,128)(2,1)S(1)} collective-permute-done((bf16[32,12,8,128]{3,2,1,0:T(8,128)(2,1)}, bf16[32,12,8,128]{3,2,1,0:T(8,128)(2,1)S(1)}, u32[]{:S(2)}, u32[]{:S(2)}) %collective-permute-start.1) | collective-permute-done | bytes 786464 | tf_op jit(solution)/shard_map/ppermute | solution.py:324
  35.0 1.1 select_n.62.refs_3_
  38.1 2.8 %collective-permute-start.5 = (bf16[80,8,128]{2,1,0:T(8,128)(2,1)S(1)}, bf16[80,8,128]{2,1,0:T(8,128)(2,1)S(1)}, u32[]{:S(2)}, u32[]{:S(2)}) collective-permute-start(bf16[80,8,128]{2,1,0:T(8,128)(2,1)S(1)} %constant_dynamic-slice_fusion.refs_2_), channel_id=1, source_target_pairs={{0,12},{4,16},{8,20},{12,24},{16,28},{1,13},{5,17},{9,21},{13,25},... | collective-permute-start | bytes 491528 | tf_op jit(solution)/shard_map/ppermute | solution.py:22
  40.9 5.2 %shard_map.148 = (bf16[28,256,128]{2,1,0:T(8,128)(2,1)S(1)}, f32[26,80,128]{2,1,0:T(8,128)S(1)}, bf16[24,32,128]{2,1,0:T(8,128)(2,1)S(1)}, bf16[24,32,128]{2,1,0:T(8,128)(2,1)S(1)}) custom-call(s32[1]{0:T(128)} %bitcast.places, bf16[32,12,8,128]{3,2,1,0:T(8,128)(2,1)S(1)} %copy-done.2, bf16[32,12,8,128]{3,2,1,0:T(8,128)(2,1)S(1)} %collective-permute-done.second_ref, ...), custom_call_target="tpu_custom_call" | custom-call | flops 2000000000 | bytes 4194304 | tf_op jit(solution)/shard_map/pallas_call | solution.py:293
  46.1 2.0 %collective-permute-start.4 = (bf16[80,8,128]{2,1,0:T(8,128)(2,1)S(1)}, bf16[80,8,128]{2,1,0:T(8,128)(2,1)S(1)}, u32[]{:S(2)}, u32[]{:S(2)}) collective-permute-start(bf16[80,8,128]{2,1,0:T(8,128)(2,1)S(1)} %constant_dynamic-slice_fusion.refs_2_), channel_id=1, source_target_pairs={{0,8},{4,12},{8,16},{12,20},{16,24},{20,28},{1,9},{5,13},{9,17},{1... | collective-permute-start | bytes 491528 | tf_op jit(solution)/shard_map/ppermute | solution.py:22
  48.1 2.4 %collective-permute-start.3 = (bf16[80,8,128]{2,1,0:T(8,128)(2,1)S(1)}, bf16[80,8,128]{2,1,0:T(8,128)(2,1)S(1)}, u32[]{:S(2)}, u32[]{:S(2)}) collective-permute-start(bf16[80,8,128]{2,1,0:T(8,128)(2,1)S(1)} %constant_dynamic-slice_fusion.refs_2_), channel_id=1, source_target_pairs={{0,4},{4,8},{8,12},{12,16},{16,20},{20,24},{24,28},{1,5},{5,9},{9,... | collective-permute-start | bytes 491528 | tf_op jit(solution)/shard_map/ppermute | solution.py:22
  50.5 6.3 %shard_map.149 = (bf16[28,256,128]{2,1,0:T(8,128)(2,1)S(1)}, f32[26,80,128]{2,1,0:T(8,128)S(1)}, bf16[24,32,128]{2,1,0:T(8,128)(2,1)S(1)}, bf16[24,32,128]{2,1,0:T(8,128)(2,1)S(1)}) custom-call(s32[1]{0:T(128)} %bitcast.places, bf16[32,12,8,128]{3,2,1,0:T(8,128)(2,1)S(1)} %collective-permute-done.1.first_ref, ...), custom_call_target="tpu_custom_call" | custom-call | flops 2000000000 | bytes 4194304 | tf_op jit(solution)/shard_map/pallas_call | solution.py:293
  56.9 2.9 %collective-permute-start.9 = (bf16[24,32,128]{2,1,0:T(8,128)(2,1)S(1)}, bf16[24,32,128]{2,1,0:T(8,128)(2,1)S(1)}, u32[]{:S(2)}, u32[]{:S(2)}) collective-permute-start(bf16[24,32,128]{2,1,0:T(8,128)(2,1)S(1)} %get-tuple-element.33), channel_id=1, source_target_pairs={{0,4},{4,8},{8,12},{12,16},{16,20},{20,24},{24,28},{1,5},{5,9},{9,... | collective-permute-start | bytes 589832 | tf_op jit(solution)/shard_map/ppermute | solution.py:22
  59.7 1.3 collective-permute-start.11
  61.0 4.6 %collective-permute-start.10 = (bf16[24,32,128]{2,1,0:T(8,128)(2,1)S(1)}, bf16[24,32,128]{2,1,0:T(8,128)(2,1)S(1)}, u32[]{:S(2)}, u32[]{:S(2)}) collective-permute-start(bf16[24,32,128]{2,1,0:T(8,128)(2,1)S(1)} %get-tuple-element.34), channel_id=1, source_target_pairs={{0,4},{4,8},{8,12},{12,16},{16,20},{20,24},{24,28},{1,5},{5,9},{9,... | collective-permute-start | bytes 589832 | tf_op jit(solution)/shard_map/ppermute | solution.py:22
  65.6 1.3 collective-permute-start.12
  66.9 9.3 %shard_map.150 = (f32[80,56,128]{2,1,0:T(8,128)S(1)}, bf16[48,240,128]{2,1,0:T(8,128)(2,1)S(1)}, f32[3,32,96]{2,1,0:T(8,128)S(1)}) custom-call(s32[1]{0:T(128)} %bitcast.places, bf16[28,256,128]{2,1,0:T(8,128)(2,1)S(1)} %get-tuple-element.28.refs_0_, bf16[28,256,128]{2,1,0:T(8,128)(2,1)S(1)} %get-tuple-element.29.refs_1_, ...), custom_call_target="tpu_custom_call" | custom-call | flops 4000000000 | bytes 4194304 | tf_op jit(solution)/shard_map/pallas_call | solution.py:293
  76.9 3.5 %shard_map.151 = (f32[3,32,96]{2,1,0:T(8,128)S(1)}, bf16[50,64,128]{2,1,0:T(8,128)(2,1)S(1)}) custom-call(s32[1]{0:T(128)} %bitcast.places, bf16[24,32,128]{2,1,0:T(8,128)(2,1)S(1)} %collective-permute-done.9.refs_0_, bf16[24,32,128]{2,1,0:T(8,128)(2,1)S(1)} %collective-permute-done.10.refs_1_, bf16[24,32,128]{2,1,0:T(8,128)(2,1)S(1)} %collective-permute-done.11.refs_2_, ...), custom_call_target="tpu_custom_call" | custom-call | flops 1000000000 | bytes 4194304 | tf_op jit(solution)/shard_map/pallas_call | solution.py:293
  80.4 1.2 collective-permute-start.13
  81.6 6.8 %shard_map.152.gv_s = f32[48,80,128]{2,1,0:T(8,128)S(1)} custom-call(s32[1]{0:T(128)} %bitcast.places, f32[26,80,128]{2,1,0:T(8,128)S(1)} %get-tuple-element.31.refs_0_, f32[26,80,128]{2,1,0:T(8,128)S(1)} %get-tuple-element.32.refs_1_, bf16[50,64,128]{2,1,0:T(8,128)(2,1)S(1)} %get-tuple-element.39.refs_2_, bf16[240,192]{1,0:T(8,128)(2,1)S(1)} %select_n.62.refs_3_), custom_call_target="tpu_custom_call" | custom-call | flops 1000000000 | bytes 4194304 | tf_op jit(solution)/shard_map/pallas_call | solution.py:293
  88.4 4.4 %shard_map.153 = (bf16[80,8,128]{2,1,0:T(8,128)(2,1)}, f32[80,8,128]{2,1,0:T(8,128)S(1)}, bf16[80,8,128]{2,1,0:T(8,128)(2,1)S(1)}, bf16[80,8,128]{2,1,0:T(8,128)...) custom-call(bf16[80,8,128]{2,1,0:T(8,128)(2,1)S(1)} %constant_dynami, ...), custom_call_target="tpu_custom_call" | custom-call | flops 4000000000 | bytes 10000000 | tf_op jit(solution)/shard_map/pallas_call | solution.py:307
  92.9 1.3 collective-permute-start.15
  94.2 3.5 %collective-permute-start.14 = (f32[3,32,96]{2,1,0:T(8,128)S(1)}, f32[3,32,96]{2,1,0:T(8,128)S(1)}, u32[]{:S(2)}, u32[]{:S(2)}) collective-permute-start(f32[3,32,96]{2,1,0:T(8,128)S(1)} %add.46), channel_id=1, source_target_pairs={{0,8},{4,12},{8,0},{12,4},{16,24},{20,28},{24,16},{28,20},{1,9},{5... | collective-permute-start | bytes 110600 | tf_op jit(solution)/shard_map/ppermute | solution.py:324
  97.7 1.3 collective-permute-start.16
  99.0 4.2 %collective-permute-done.14 = f32[3,32,96]{2,1,0:T(8,128)S(1)} collective-permute-done((f32[3,32,96]{2,1,0:T(8,128)S(1)}, f32[3,32,96]{2,1,0:T(8,128)S(1)}, u32[]{:S(2)}, u32[]{:S(2)}) %collective-permute-start.14) | collective-permute-done | bytes 36896 | tf_op jit(solution)/shard_map/ppermute | solution.py:324
  103.6 1.3 collective-permute-start.17
  104.9 1.3 collective-permute-start.18
  106.2 1.3 collective-permute-start.19
  108.4 1.3 collective-permute-start.20
  109.7 1.6 %collective-permute-start.23 = (f32[3,32,96]{2,1,0:T(8,128)S(1)}, f32[3,32,96]{2,1,0:T(8,128)S(1)}, u32[]{:S(2)}, u32[]{:S(2)}) collective-permute-start(f32[3,32,96]{2,1,0:T(8,128)S(1)} %add.54), channel_id=1, source_target_pairs={{0,2},{1,3},{2,0},{3,1},{4,6},{5,7},{6,4},{7,5},{8,10},{9,11},{10,... | collective-permute-start | bytes 110600 | tf_op jit(solution)/shard_map/ppermute | solution.py:324
  112.0 1.9 %collective-permute-done.23 = f32[3,32,96]{2,1,0:T(8,128)S(1)} collective-permute-done((f32[3,32,96]{2,1,0:T(8,128)S(1)}, f32[3,32,96]{2,1,0:T(8,128)S(1)}, u32[]{:S(2)}, u32[]{:S(2)}) %collective-permute-start.23) | collective-permute-done | bytes 36896 | tf_op jit(solution)/shard_map/ppermute | solution.py:324
  113.9 14.2 %collective-permute-done.18 = bf16[80,8,128]{2,1,0:T(8,128)(2,1)S(1)} collective-permute-done((bf16[80,8,128]{2,1,0:T(8,128)(2,1)S(1)}, bf16[80,8,128]{2,1,0:T(8,128)(2,1)S(1)}, u32[]{:S(2)}, u32[]{:S(2)}) %collective-permute-start.18) | collective-permute-done | bytes 163872 | tf_op jit(solution)/shard_map/ppermute | solution.py:22
  (72 shorter events, 12.3 us)
Async XLA Ops:
  0.7 33.6 %copy-start.7 = (pred[8,64]{1,0:T(8,128)(4,1)S(1)}, pred[8,64]{1,0:T(8,128)(4,1)}, u32[]{:S(2)}) copy-start(pred[8,64]{1,0:T(8,128)(4,1)} %constant.47.clone) | copy-start | bytes 1540
  0.7 33.5 %copy-start.8 = (pred[8,64]{1,0:T(8,128)(4,1)S(1)}, pred[8,64]{1,0:T(8,128)(4,1)}, u32[]{:S(2)}) copy-start(pred[8,64]{1,0:T(8,128)(4,1)} %constant.45.clone) | copy-start | bytes 1540
  1.7 44.4 %collective-permute-start.8 = (bf16[80,8,128]{2,1,0:T(8,128)(2,1)S(1)}, bf16[80,8,128]{2,1,0:T(8,128)(2,1)S(1)}, u32[]{:S(2)}, u32[]{:S(2)}) collective-permute-start(bf16[80,8,128]{2,1,0:T(8,128)(2,1)S(1)} %constant_dynamic-slice_fusion.refs_2_), channel_id=1, source_target_pairs={{0,24},{4,28},{1,25},{5,29},{2,26},{6,30},{3,27},{7,31}} | collective-permute-start | bytes 491528 | tf_op jit(solution)/shard_map/ppermute | solution.py:22
  8.7 48.1 %collective-permute-start.7 = (bf16[80,8,128]{2,1,0:T(8,128)(2,1)S(1)}, bf16[80,8,128]{2,1,0:T(8,128)(2,1)}, u32[]{:S(2)}, u32[]{:S(2)}) collective-permute-start(bf16[80,8,128]{2,1,0:T(8,128)(2,1)S(1)} %constant_dynamic-slice_fusion.refs_2_), channel_id=1, source_target_pairs={{0,20},{4,24},{8,28},{1,21},{5,25},{9,29},{2,22},{6,26},{10,30},{3... | collective-permute-start | bytes 491528 | tf_op jit(solution)/shard_map/ppermute | solution.py:22
  10.7 49.0 %collective-permute-start.6 = (bf16[80,8,128]{2,1,0:T(8,128)(2,1)S(1)}, bf16[80,8,128]{2,1,0:T(8,128)(2,1)}, u32[]{:S(2)}, u32[]{:S(2)}) collective-permute-start(bf16[80,8,128]{2,1,0:T(8,128)(2,1)S(1)} %constant_dynamic-slice_fusion.refs_2_), channel_id=1, source_target_pairs={{0,16},{4,20},{8,24},{12,28},{1,17},{5,21},{9,25},{13,29},{2,18},{... | collective-permute-start | bytes 491528 | tf_op jit(solution)/shard_map/ppermute | solution.py:22
  12.6 25.5 %collective-permute-start = (bf16[32,12,8,128]{3,2,1,0:T(8,128)(2,1)}, bf16[32,12,8,128]{3,2,1,0:T(8,128)(2,1)S(1)}, u32[]{:S(2)}, u32[]{:S(2)}) collective-permute-start(bf16[32,12,8,128]{3,2,1,0:T(8,128)(2,1)} %first_ref.1), channel_id=1, source_target_pairs={{0,1},{1,0},{2,3},{3,2},{4,5},{5,4},{6,7},{7,6},{8,9},{9,8},{10,11... | collective-permute-start | bytes 2359304 | tf_op jit(solution)/shard_map/ppermute | solution.py:324
  12.6 20.2 %collective-permute-start.1 = (bf16[32,12,8,128]{3,2,1,0:T(8,128)(2,1)}, bf16[32,12,8,128]{3,2,1,0:T(8,128)(2,1)S(1)}, u32[]{:S(2)}, u32[]{:S(2)}) collective-permute-start(bf16[32,12,8,128]{3,2,1,0:T(8,128)(2,1)} %first_ref.1), channel_id=1, source_target_pairs={{0,2},{1,3},{2,0},{3,1},{4,6},{5,7},{6,4},{7,5},{8,10},{9,11},{10,... | collective-permute-start | bytes 2359304 | tf_op jit(solution)/shard_map/ppermute | solution.py:324
  14.1 23.0 %copy-start.4 = (pred[8,256]{1,0:T(8,128)(4,1)S(1)}, pred[8,256]{1,0:T(8,128)(4,1)}, u32[]{:S(2)}) copy-start(pred[8,256]{1,0:T(8,128)(4,1)} %constant.43.clone) | copy-start | bytes 6148
  14.1 23.0 %copy-start.5 = (pred[8,256]{1,0:T(8,128)(4,1)S(1)}, pred[8,256]{1,0:T(8,128)(4,1)}, u32[]{:S(2)}) copy-start(pred[8,256]{1,0:T(8,128)(4,1)} %constant.42.clone) | copy-start | bytes 6148
  14.1 23.0 %copy-start.6 = (pred[8,256]{1,0:T(8,128)(4,1)S(1)}, pred[8,256]{1,0:T(8,128)(4,1)}, u32[]{:S(2)}) copy-start(pred[8,256]{1,0:T(8,128)(4,1)} %constant.17.clone) | copy-start | bytes 6148
  15.3 25.6 %copy-start.2 = (bf16[32,12,8,128]{3,2,1,0:T(8,128)(2,1)S(1)}, bf16[32,12,8,128]{3,2,1,0:T(8,128)(2,1)}, u32[]{:S(2)}) copy-start(bf16[32,12,8,128]{3,2,1,0:T(8,128)(2,1)} %first_ref.1) | copy-start | bytes 2359300
  32.8 15.3 %collective-permute-start.2 = (bf16[32,12,8,128]{3,2,1,0:T(8,128)(2,1)S(1)}, bf16[32,12,8,128]{3,2,1,0:T(8,128)(2,1)}, u32[]{:S(2)}, u32[]{:S(2)}) collective-permute-start(bf16[32,12,8,128]{3,2,1,0:T(8,128)(2,1)S(1)} %collective-permute-done.1.first_ref), channel_id=1, source_target_pairs={{0,1},{1,0},{2,3},{3,2},{4,5},{5,4},{6,7},{7,6},{8,9},{9,8},{10,11... | collective-permute-start | bytes 2359304 | tf_op jit(solution)/shard_map/ppermute | solution.py:324
  38.1 22.9 %collective-permute-start.5 = (bf16[80,8,128]{2,1,0:T(8,128)(2,1)S(1)}, bf16[80,8,128]{2,1,0:T(8,128)(2,1)S(1)}, u32[]{:S(2)}, u32[]{:S(2)}) collective-permute-start(bf16[80,8,128]{2,1,0:T(8,128)(2,1)S(1)} %constant_dynamic-slice_fusion.refs_2_), channel_id=1, source_target_pairs={{0,12},{4,16},{8,20},{12,24},{16,28},{1,13},{5,17},{9,21},{13,25},... | collective-permute-start | bytes 491528 | tf_op jit(solution)/shard_map/ppermute | solution.py:22
  46.1 20.8 %copy-start.1 = (f32[32,240]{1,0:T(8,128)S(1)}, f32[32,240]{1,0:T(8,128)}, u32[]{:S(2)}) copy-start(f32[32,240]{1,0:T(8,128)} %constant.48.clone.refs_10_.refs_6_) | copy-start | bytes 92164
  46.1 19.5 %collective-permute-start.4 = (bf16[80,8,128]{2,1,0:T(8,128)(2,1)S(1)}, bf16[80,8,128]{2,1,0:T(8,128)(2,1)S(1)}, u32[]{:S(2)}, u32[]{:S(2)}) collective-permute-start(bf16[80,8,128]{2,1,0:T(8,128)(2,1)S(1)} %constant_dynamic-slice_fusion.refs_2_), channel_id=1, source_target_pairs={{0,8},{4,12},{8,16},{12,20},{16,24},{20,28},{1,9},{5,13},{9,17},{1... | collective-permute-start | bytes 491528 | tf_op jit(solution)/shard_map/ppermute | solution.py:22
  48.1 18.8 %collective-permute-start.3 = (bf16[80,8,128]{2,1,0:T(8,128)(2,1)S(1)}, bf16[80,8,128]{2,1,0:T(8,128)(2,1)S(1)}, u32[]{:S(2)}, u32[]{:S(2)}) collective-permute-start(bf16[80,8,128]{2,1,0:T(8,128)(2,1)S(1)} %constant_dynamic-slice_fusion.refs_2_), channel_id=1, source_target_pairs={{0,4},{4,8},{8,12},{12,16},{16,20},{20,24},{24,28},{1,5},{5,9},{9,... | collective-permute-start | bytes 491528 | tf_op jit(solution)/shard_map/ppermute | solution.py:22
  56.9 19.4 %collective-permute-start.9 = (bf16[24,32,128]{2,1,0:T(8,128)(2,1)S(1)}, bf16[24,32,128]{2,1,0:T(8,128)(2,1)S(1)}, u32[]{:S(2)}, u32[]{:S(2)}) collective-permute-start(bf16[24,32,128]{2,1,0:T(8,128)(2,1)S(1)} %get-tuple-element.33), channel_id=1, source_target_pairs={{0,4},{4,8},{8,12},{12,16},{16,20},{20,24},{24,28},{1,5},{5,9},{9,... | collective-permute-start | bytes 589832 | tf_op jit(solution)/shard_map/ppermute | solution.py:22
  59.7 16.5 %collective-permute-start.11 = (bf16[24,32,128]{2,1,0:T(8,128)(2,1)S(1)}, bf16[24,32,128]{2,1,0:T(8,128)(2,1)S(1)}, u32[]{:S(2)}, u32[]{:S(2)}) collective-permute-start(bf16[24,32,128]{2,1,0:T(8,128)(2,1)S(1)} %get-tuple-element.35), channel_id=1, source_target_pairs={{4,0},{8,4},{12,8},{16,12},{20,16},{24,20},{28,24},{5,1},{9,5},{13... | collective-permute-start | bytes 589832 | tf_op jit(solution)/shard_map/ppermute | solution.py:22
  61.0 15.8 %collective-permute-start.10 = (bf16[24,32,128]{2,1,0:T(8,128)(2,1)S(1)}, bf16[24,32,128]{2,1,0:T(8,128)(2,1)S(1)}, u32[]{:S(2)}, u32[]{:S(2)}) collective-permute-start(bf16[24,32,128]{2,1,0:T(8,128)(2,1)S(1)} %get-tuple-element.34), channel_id=1, source_target_pairs={{0,4},{4,8},{8,12},{12,16},{16,20},{20,24},{24,28},{1,5},{5,9},{9,... | collective-permute-start | bytes 589832 | tf_op jit(solution)/shard_map/ppermute | solution.py:22
  65.6 11.3 %collective-permute-start.12 = (bf16[24,32,128]{2,1,0:T(8,128)(2,1)S(1)}, bf16[24,32,128]{2,1,0:T(8,128)(2,1)S(1)}, u32[]{:S(2)}, u32[]{:S(2)}) collective-permute-start(bf16[24,32,128]{2,1,0:T(8,128)(2,1)S(1)} %get-tuple-element.36), channel_id=1, source_target_pairs={{4,0},{8,4},{12,8},{16,12},{20,16},{24,20},{28,24},{5,1},{9,5},{13... | collective-permute-start | bytes 589832 | tf_op jit(solution)/shard_map/ppermute | solution.py:22
  80.4 8.0 %collective-permute-start.13 = (f32[3,32,96]{2,1,0:T(8,128)S(1)}, f32[3,32,96]{2,1,0:T(8,128)S(1)}, u32[]{:S(2)}, u32[]{:S(2)}) collective-permute-start(f32[3,32,96]{2,1,0:T(8,128)S(1)} %get-tuple-element.40), channel_id=1, source_target_pairs={{0,16},{4,20},{8,24},{12,28},{16,0},{20,4},{24,8},{28,12},{1,17},{... | collective-permute-start | bytes 110600 | tf_op jit(solution)/shard_map/ppermute | solution.py:324
  92.9 10.3 %collective-permute-start.15 = (bf16[80,8,128]{2,1,0:T(8,128)(2,1)S(1)}, bf16[80,8,128]{2,1,0:T(8,128)(2,1)S(1)}, u32[]{:S(2)}, u32[]{:S(2)}) collective-permute-start(bf16[80,8,128]{2,1,0:T(8,128)(2,1)S(1)} %get-tuple-element.45), channel_id=1, source_target_pairs={{4,0},{8,4},{12,8},{16,12},{20,16},{24,20},{28,24},{5,1},{9,5},{13... | collective-permute-start | bytes 491528 | tf_op jit(solution)/shard_map/ppermute | solution.py:22
  94.2 9.0 %collective-permute-start.14 = (f32[3,32,96]{2,1,0:T(8,128)S(1)}, f32[3,32,96]{2,1,0:T(8,128)S(1)}, u32[]{:S(2)}, u32[]{:S(2)}) collective-permute-start(f32[3,32,96]{2,1,0:T(8,128)S(1)} %add.46), channel_id=1, source_target_pairs={{0,8},{4,12},{8,0},{12,4},{16,24},{20,28},{24,16},{28,20},{1,9},{5... | collective-permute-start | bytes 110600 | tf_op jit(solution)/shard_map/ppermute | solution.py:324
  97.7 12.0 %collective-permute-start.16 = (bf16[80,8,128]{2,1,0:T(8,128)(2,1)S(1)}, bf16[80,8,128]{2,1,0:T(8,128)(2,1)S(1)}, u32[]{:S(2)}, u32[]{:S(2)}) collective-permute-start(bf16[80,8,128]{2,1,0:T(8,128)(2,1)S(1)} %get-tuple-element.47), channel_id=1, source_target_pairs={{8,0},{12,4},{16,8},{20,12},{24,16},{28,20},{9,1},{13,5},{17,9},{2... | collective-permute-start | bytes 491528 | tf_op jit(solution)/shard_map/ppermute | solution.py:22
  103.2 5.2 %collective-permute-start.21 = (f32[3,32,96]{2,1,0:T(8,128)S(1)}, f32[3,32,96]{2,1,0:T(8,128)S(1)}, u32[]{:S(2)}, u32[]{:S(2)}) collective-permute-start(f32[3,32,96]{2,1,0:T(8,128)S(1)} %add.47), channel_id=1, source_target_pairs={{0,4},{4,0},{8,12},{12,8},{16,20},{20,16},{24,28},{28,24},{1,5},{5... | collective-permute-start | bytes 110600 | tf_op jit(solution)/shard_map/ppermute | solution.py:324
  103.6 8.4 %collective-permute-start.17 = (bf16[80,8,128]{2,1,0:T(8,128)(2,1)S(1)}, bf16[80,8,128]{2,1,0:T(8,128)(2,1)S(1)}, u32[]{:S(2)}, u32[]{:S(2)}) collective-permute-start(bf16[80,8,128]{2,1,0:T(8,128)(2,1)S(1)} %get-tuple-element.48), channel_id=1, source_target_pairs={{12,0},{16,4},{20,8},{24,12},{28,16},{13,1},{17,5},{21,9},{25,13},... | collective-permute-start | bytes 491528 | tf_op jit(solution)/shard_map/ppermute | solution.py:22
  104.9 23.2 %collective-permute-start.18 = (bf16[80,8,128]{2,1,0:T(8,128)(2,1)S(1)}, bf16[80,8,128]{2,1,0:T(8,128)(2,1)S(1)}, u32[]{:S(2)}, u32[]{:S(2)}) collective-permute-start(bf16[80,8,128]{2,1,0:T(8,128)(2,1)S(1)} %get-tuple-element.49), channel_id=1, source_target_pairs={{16,0},{20,4},{24,8},{28,12},{17,1},{21,5},{25,9},{29,13},{18,2},{... | collective-permute-start | bytes 491528 | tf_op jit(solution)/shard_map/ppermute | solution.py:22
  106.2 22.0 %collective-permute-start.19 = (bf16[80,8,128]{2,1,0:T(8,128)(2,1)S(1)}, bf16[80,8,128]{2,1,0:T(8,128)(2,1)S(1)}, u32[]{:S(2)}, u32[]{:S(2)}) collective-permute-start(bf16[80,8,128]{2,1,0:T(8,128)(2,1)S(1)} %get-tuple-element.50), channel_id=1, source_target_pairs={{20,0},{24,4},{28,8},{21,1},{25,5},{29,9},{22,2},{26,6},{30,10},{2... | collective-permute-start | bytes 491528 | tf_op jit(solution)/shard_map/ppermute | solution.py:22
  108.4 19.7 %collective-permute-start.20 = (bf16[80,8,128]{2,1,0:T(8,128)(2,1)S(1)}, bf16[80,8,128]{2,1,0:T(8,128)(2,1)S(1)}, u32[]{:S(2)}, u32[]{:S(2)}) collective-permute-start(bf16[80,8,128]{2,1,0:T(8,128)(2,1)S(1)} %get-tuple-element.51), channel_id=1, source_target_pairs={{24,0},{28,4},{25,1},{29,5},{26,2},{30,6},{27,3},{31,7}} | collective-permute-start | bytes 491528 | tf_op jit(solution)/shard_map/ppermute | solution.py:22
  109.7 4.2 %collective-permute-start.23 = (f32[3,32,96]{2,1,0:T(8,128)S(1)}, f32[3,32,96]{2,1,0:T(8,128)S(1)}, u32[]{:S(2)}, u32[]{:S(2)}) collective-permute-start(f32[3,32,96]{2,1,0:T(8,128)S(1)} %add.54), channel_id=1, source_target_pairs={{0,2},{1,3},{2,0},{3,1},{4,6},{5,7},{6,4},{7,5},{8,10},{9,11},{10,... | collective-permute-start | bytes 110600 | tf_op jit(solution)/shard_map/ppermute | solution.py:324
  112.0 17.0 %collective-permute-start.22 = (f32[3,32,96]{2,1,0:T(8,128)S(1)}, f32[3,32,96]{2,1,0:T(8,128)S(1)}, u32[]{:S(2)}, u32[]{:S(2)}) collective-permute-start(f32[3,32,96]{2,1,0:T(8,128)S(1)} %add.54), channel_id=1, source_target_pairs={{0,1},{1,0},{2,3},{3,2},{4,5},{5,4},{6,7},{7,6},{8,9},{9,8},{10,11... | collective-permute-start | bytes 110600 | tf_op jit(solution)/shard_map/ppermute | solution.py:324
  113.9 15.1 %collective-permute-start.24 = (f32[3,32,96]{2,1,0:T(8,128)S(1)}, f32[3,32,96]{2,1,0:T(8,128)S(1)}, u32[]{:S(2)}, u32[]{:S(2)}) collective-permute-start(f32[3,32,96]{2,1,0:T(8,128)S(1)} %collective-permute-done.23), channel_id=1, source_target_pairs={{0,1},{1,0},{2,3},{3,2},{4,5},{5,4},{6,7},{7,6},{8,9},{9,8},{10,11... | collective-permute-start | bytes 110600 | tf_op jit(solution)/shard_map/ppermute | solution.py:324
  (2 other events, 16.8 us)

commit v4 on v2

--- a/solution.py
+++ b/solution.py
@@ -18,8 +18,7 @@
 
 def shifted(value, axis, steps):
     count = lax.axis_size(axis)
-    leading, last = (max(0, -steps), min(count, count - steps))
-    return lax.ppermute(value, axis, [(source, source + steps) for source in range(leading, last)])
+    return lax.ppermute(value, axis, [(source, (source + steps) % count) for source in range(count)])
 
 
 def conv_rows(outs, width):
@@ -54,10 +53,11 @@
     return jnp.where(lane == (0 if steps > 0 else size - 1), 0.0, moved)
 
 
-def convolution_grads(parts, hops, places, *refs):
+def kernel_sums(parts, hops, places, *refs):
     cot_refs, halo_refs, refs = refs[:parts], refs[parts : 2 * parts], refs[2 * parts :]
     right_refs, refs = refs[: hops + 1], refs[hops + 1 :]
-    left_ref, weight_ref, fold_ref, right_s, gv_s, sums_ref, cot_s, vol_s, prod_s = refs
+    left_ref, fold_ref, cot_s, right_s, sums_ref = refs[:5]
+    cot_b, halo_b, right_b, vol_s, prod_s, sems = refs[5:]
     channels, width, rows = left_ref.shape
     groups = channels // GROUP
     outs, levels = cot_refs[0].shape[:2]
@@ -67,41 +67,22 @@
     reach = hops * width
     f32, bf16 = jnp.float32, jnp.bfloat16
 
+    copies = []
+    for buffer, sources in ((right_b, right_refs), (cot_b, cot_refs), (halo_b, halo_refs)):
+        for at, source in enumerate(sources):
+            copies.append(
+                pltpu.make_async_copy(source, buffer.at[at], sems.at[len(copies)])
+            )
+    for copy in copies:
+        copy.start()
+
     cot_s[0] = jnp.zeros((span, rows), bf16)
     cot_s[D + 1] = jnp.zeros((span, rows), bf16)
-    for other in range(parts):
-        start = (places[0] ^ other) * levels + 1
-
-        def assemble(level, carry, other=other, start=start):
-            value = cot_refs[other][:, level].reshape(main, rows)
-            cot_s[start + level, 0:main] = value
-            cot_s[start + level, main:span] = halo_refs[other][level]
-            return carry
-
-        lax.fori_loop(0, levels, assemble, 0)
-
-    def grad_volume_step(pair, carry):
-        first = pair * 2
-        near = cot_s[pl.ds(first, 3)].reshape(3 * span, rows)
-        far = cot_s[pl.ds(first + 1, 3)].reshape(3 * span, rows)
-        result = jnp.dot(
-            weight_ref[...], jnp.concatenate([near, far], axis=1), preferred_element_type=f32
-        )
-        for half in range(2):
-            part = result[:, half * rows : (half + 1) * rows]
-            total = (
-                part[size : 2 * size]
-                + roll_zero(part[:size], -1)
-                + roll_zero(part[2 * size :], 1)
-            )
-            gv_s[first + half] = total.astype(bf16).astype(f32)
-        return carry
-
-    lax.fori_loop(0, D // 2, grad_volume_step, 0)
-
     for hop in range(hops + 1):
+        copies[hop].wait()
         at = reach - hop * width
-        right_s[:, at : at + width] = right_refs[hop][...].astype(f32)
+        block = right_b[hop].astype(f32)
+        right_s[:, at : at + width] = jnp.where(places[1] >= hop, block, 0.0)
 
     def volume_step(group, carry):
         first = group * GROUP
@@ -118,6 +99,18 @@
         return carry
 
     lax.fori_loop(0, groups, volume_step, 0)
+
+    for copy in copies[hops + 1 :]:
+        copy.wait()
+    for other in range(parts):
+        start = (places[0] ^ other) * levels + 1
+
+        def assemble(level, carry, other=other, start=start):
+            cot_s[start + level, 0:main] = cot_b[other, :, level].reshape(main, rows)
+            cot_s[start + level, main:span] = halo_b[other, level]
+            return carry
+
+        lax.fori_loop(0, levels, assemble, 0)
 
     chunk = 4
     prod_s[...] = jnp.zeros(prod_s.shape, f32)
@@ -157,8 +150,35 @@
         )
 
 
-def feature_grads(hops, left_ref, right_s, gv_s, grad_left_ref, own_ref, *rest):
+def grad_volume_levels(first_level, cot_s, weight_ref, gv_s):
+    count, size, rows = gv_s.shape
+    span = cot_s.shape[1]
+
+    def step(pair, carry):
+        at = first_level + pair * 2
+        near = cot_s[pl.ds(at, 3)].reshape(3 * span, rows)
+        far = cot_s[pl.ds(at + 1, 3)].reshape(3 * span, rows)
+        result = jnp.dot(
+            weight_ref[...], jnp.concatenate([near, far], axis=1),
+            preferred_element_type=jnp.float32,
+        )
+        for half in range(2):
+            part = result[:, half * rows : (half + 1) * rows]
+            total = (
+                part[size : 2 * size]
+                + roll_zero(part[:size], -1)
+                + roll_zero(part[2 * size :], 1)
+            )
+            gv_s[pair * 2 + half] = total.astype(jnp.bfloat16).astype(jnp.float32)
+        return carry
+
+    lax.fori_loop(0, count // 2, step, 0)
+
+
+def feature_grads(hops, pieces, left_ref, right_s, *refs):
+    gv_refs, (grad_left_ref, own_ref, *rest) = refs[:pieces], refs[pieces:]
     sent_refs, (grad_s,) = rest[:hops], rest[hops:]
+    held = gv_refs[0].shape[0]
     channels, width, rows = left_ref.shape
     groups = channels // GROUP
     reach = hops * width
@@ -171,7 +191,7 @@
         totals = [jnp.zeros((width, rows), f32) for k in range(GROUP)]
         rows_at = pl.ds(pl.multiple_of(group * width, width), width)
         for d in range(D):
-            value = gv_s[d, rows_at]
+            value = gv_refs[d // held][d % held, rows_at]
             for k in range(GROUP):
                 totals[k] = totals[k] + value * right_s[first + k, reach - d : reach - d + width]
                 grad_s[first + k, reach - d : reach - d + width] += value * lefts[k]
@@ -188,50 +208,71 @@
 
 VMEM = pl.BlockSpec(memory_space=pltpu.VMEM)
 SMEM = pl.BlockSpec(memory_space=pltpu.SMEM)
+ANY = pl.BlockSpec(memory_space=pl.ANY)
 MIB = 1024 * 1024
 
 
-def run_convolution_grads(places, cots, halos, rights, left, weights, fold):
+def cost(flops):
+    return pl.CostEstimate(flops=flops, bytes_accessed=4 * MIB, transcendentals=0)
+
+
+def run_kernel_sums(places, cots, halos, rights, left, fold):
     outs, levels, width, rows = cots[0].shape
     channels = left.shape[0]
     size = fold.shape[1]
     span = outs * (width + 2)
-    f32 = jnp.float32
+    f32, bf16 = jnp.float32, jnp.bfloat16
+    moved = [*cots, *halos, *rights]
     return pl.pallas_call(
-        functools.partial(convolution_grads, len(cots), len(rights) - 1),
+        functools.partial(kernel_sums, len(cots), len(rights) - 1),
         out_shape=[
+            jax.ShapeDtypeStruct((D + 2, span, rows), bf16),
             jax.ShapeDtypeStruct((channels, len(rights) * width, rows), f32),
-            jax.ShapeDtypeStruct((D, size // 3, rows), f32),
             jax.ShapeDtypeStruct((3, fold.shape[0], 3 * outs), f32),
         ],
-        in_specs=[SMEM] + [VMEM] * (2 * len(cots) + len(rights) + 3),
+        in_specs=[SMEM] + [ANY] * len(moved) + [VMEM] * 2,
         out_specs=[VMEM] * 3,
         scratch_shapes=[
-            pltpu.VMEM((D + 2, span, rows), jnp.bfloat16),
+            pltpu.VMEM((len(cots), *cots[0].shape), bf16),
+            pltpu.VMEM((len(halos), *halos[0].shape), bf16),
+            pltpu.VMEM((len(rights), *rights[0].shape), bf16),
             pltpu.VMEM((D, 3, size // 3, rows), f32),
             pltpu.VMEM((3, span, size), f32),
+            pltpu.SemaphoreType.DMA((len(moved),)),
         ],
-        compiler_params=pltpu.CompilerParams(vmem_limit_bytes=24 * MIB),
-        cost_estimate=pl.CostEstimate(flops=8000000000, bytes_accessed=20000000, transcendentals=0),
-    )(places, *cots, *halos, *rights, left, weights, fold)
-
-
-def run_feature_grads(left, right_wide, grad_volume, hops):
+        compiler_params=pltpu.CompilerParams(vmem_limit_bytes=20 * MIB),
+        cost_estimate=cost(8000000000),
+    )(places, *moved, left, fold)
+
+
+def run_grad_volume(cot_wide, weights, first_level, count):
+    size, rows = weights.shape[0] // 3, cot_wide.shape[2]
+    return pl.pallas_call(
+        functools.partial(grad_volume_levels, first_level),
+        out_shape=jax.ShapeDtypeStruct((count, size, rows), jnp.float32),
+        in_specs=[VMEM] * 2,
+        out_specs=VMEM,
+        compiler_params=pltpu.CompilerParams(vmem_limit_bytes=8 * MIB),
+        cost_estimate=cost(4000000000),
+    )(cot_wide, weights)
+
+
+def run_feature_grads(left, right_wide, grad_volumes, hops):
     channels, width, rows = left.shape
     f32, bf16 = jnp.float32, jnp.bfloat16
     return pl.pallas_call(
-        functools.partial(feature_grads, hops),
+        functools.partial(feature_grads, hops, len(grad_volumes)),
         out_shape=[
             jax.ShapeDtypeStruct((channels, width, rows), bf16),
             jax.ShapeDtypeStruct((channels, width, rows), f32),
             *[jax.ShapeDtypeStruct((channels, width, rows), bf16)] * hops,
         ],
-        in_specs=[VMEM] * 3,
+        in_specs=[VMEM] * (2 + len(grad_volumes)),
         out_specs=[VMEM] * (hops + 2),
         scratch_shapes=[pltpu.VMEM((channels, (hops + 1) * width, rows), f32)],
-        compiler_params=pltpu.CompilerParams(vmem_limit_bytes=12 * MIB),
-        cost_estimate=pl.CostEstimate(flops=4000000000, bytes_accessed=10000000, transcendentals=0),
-    )(left, right_wide, grad_volume)
+        compiler_params=pltpu.CompilerParams(vmem_limit_bytes=8 * MIB),
+        cost_estimate=cost(4000000000),
+    )(left, right_wide, *grad_volumes)
 
 
 def swapped(value, axis, bit):
@@ -248,26 +289,26 @@
     return [held[key] for key in range(len(held))]
 
 
-def total_swapping(value, axis):
-    bit = lax.axis_size(axis) // 2
-    while bit:
-        value = value + swapped(value, axis, bit)
-        bit //= 2
-    return value
+def total_swapping(value, bit):
+    return value + swapped(value, "col", bit)
 
 
 def body(left, right, kernel, cotangent):
     outs, levels, width, rows = cotangent.shape
     parts = lax.axis_size("disp")
+    columns = lax.axis_size("col")
     channels = C // parts
     groups = G // parts
     hops = (D + width - 2) // width
-    part = lax.axis_index("disp")
-    places = part.astype(jnp.int32)[None]
+    part, column = lax.axis_index("disp"), lax.axis_index("col")
+    places = jnp.stack([part, column]).astype(jnp.int32)
+    f32, bf16 = jnp.float32, jnp.bfloat16
 
     cots = gather_swapping(cotangent, "disp")
     low = shifted(jnp.transpose(cotangent[:, :, width - 1], (1, 0, 2)), "col", 1)
     high = shifted(jnp.transpose(cotangent[:, :, 0], (1, 0, 2)), "col", -1)
+    low = jnp.where(column > 0, low, 0).astype(bf16)
+    high = jnp.where(column < columns - 1, high, 0).astype(bf16)
     halos = gather_swapping(jnp.concatenate([low, high], axis=1), "disp")
     right_own = lax.dynamic_slice_in_dim(right, part * channels, channels, 0)
     rights = [right_own] + [shifted(right_own, "col", hop) for hop in range(1, hops + 1)]
@@ -278,24 +319,34 @@
     fold = np.zeros((pad_rows, 3 * groups * width), np.float32)
     fold[np.arange(3 * groups * width) // width, np.arange(3 * groups * width)] = 1
 
-    right_wide, grad_volume, sums = run_convolution_grads(
-        places, cots, halos, rights, left_own, weights, jnp.asarray(fold)
+    cot_wide, right_wide, total = run_kernel_sums(
+        places, cots, halos, rights, left_own, jnp.asarray(fold)
     )
-    results = run_feature_grads(left_own, right_wide, grad_volume, hops)
+    bits = [1 << k for k in reversed(range(columns.bit_length() - 1))]
+    first_half = run_grad_volume(cot_wide, weights, 0, D // 2)
+    total = total_swapping(total, bits[0])
+    cot_wide, first_half, total = lax.optimization_barrier((cot_wide, first_half, total))
+    second_half = run_grad_volume(cot_wide, weights, D // 2, D // 2)
+    total = total_swapping(total, bits[1])
+    second_half, total = lax.optimization_barrier((second_half, total))
+    results = run_feature_grads(left_own, right_wide, [first_half, second_half], hops)
+    for bit in bits[2:]:
+        total = total_swapping(total, bit)
+    *results, total = lax.optimization_barrier((*results, total))
     grad_left, own, sent = results[0], results[1], results[2:]
 
-    total = total_swapping(sums, "col")
+    total_right = own
+    for hop in range(hops, 0, -1):
+        arrived = shifted(sent[hop - 1], "col", -hop).astype(f32)
+        total_right = total_right + jnp.where(column + hop < columns, arrived, 0.0)
+
     pieces = jnp.stack(gather_swapping(total, "disp"))
     pieces = pieces[jnp.arange(parts) ^ part][:, :, : 3 * groups]
     total = pieces.reshape(parts, 3, 3, groups, 3, outs)
-    cell_count = D * width * lax.axis_size("col") * rows
+    cell_count = D * width * columns * rows
     grad_kernel = jnp.transpose(total, (4, 1, 2, 5, 0, 3))[::-1].reshape(3, 3, 3, outs, G)
     grad_kernel = grad_kernel * (1.0 / math.sqrt(cell_count))
-
-    total_right = own
-    for hop in range(hops, 0, -1):
-        total_right = total_right + shifted(sent[hop - 1], "col", -hop).astype(jnp.float32)
-    return (grad_left, total_right.astype(jnp.bfloat16), grad_kernel)
+    return (grad_left, total_right.astype(bf16), grad_kernel)
 
 
 def solution(mesh):

time: 124 us -> 118 us (0.952)
  starting transfers between devices: 46.7 us -> 27.9 us
  local copies, waits for them, and re-layouts: 13.7 us -> 18.9 us
  waiting for transfers between devices: 34.7 us -> 37.7 us
  other arithmetic: 2.39 us -> 4.71 us
  Pallas kernels: 24.5 us -> 25.9 us
    ppermute x14, waiting for transfers between devices: 23.9 us -> 37.7 us  [shifted(): lax.ppermute(value, axis, [(source, (source + steps) % count) for source...]
    ppermute x14, starting transfers between devices: 28.9 us -> 15.1 us  [shifted(): lax.ppermute(value, axis, [(source, (source + steps) % count) for source...]
    ppermute x12, waiting for transfers between devices: 10.7 us -> 0.03 us  [swapped(): lax.ppermute(value, axis, [(source, source ^ bit) for source in range(cou...]
    ppermute x12, starting transfers between devices: 17.8 us -> 12.8 us  [swapped(): lax.ppermute(value, axis, [(source, source ^ bit) for source in range(cou...]
    broadcast_in_dim x4, local copies, waits for them, and re-layouts: 0.14 us -> 3.54 us  [toeplitz(): total = jnp.where(mask, wide[tap][:, :, None], total)]
    unnamed x38 -> x35, local copies, waits for them, and re-layouts: 6.96 us -> 8.85 us
    pallas_call x2 -> x4, Pallas kernels: 24.5 us -> 25.9 us  [the longest x1 12.3 us: run_kernel_sums(): pl.pallas_call(functools.partial(kernel_sums, len(cots), len(rights) - 1)...]
    convert_element_type x1, other arithmetic: 0.81 us -> 2.12 us  [body(): return (grad_left, total_right.astype(bf16), grad_kernel)]
  transfers between devices with their start and end apart: 26 -> 26, of which waited for: 7 -> 7; matrix products, arithmetic and copies ran while one was open for 7% -> 13% of each run, Pallas kernels for 0% -> 12%
where the time goes in v4:
time: 118 us; the launch traced here: 117 us
  waiting for transfers between devices  37.7 us (32%)
  starting transfers between devices  27.9 us (24%)
  Pallas kernels  25.9 us (22%)
  local copies, waits for them, and re-layouts  18.9 us (16%)
  other arithmetic  4.71 us (4%)
    ppermute x14, waiting for transfers between devices, shifted(): lax.ppermute(value, axis, [(source, (source + steps) % count) for source...  37.7 us
    ppermute x14, starting transfers between devices, shifted(): lax.ppermute(value, axis, [(source, (source + steps) % count) for source...  15.1 us
    ppermute x12, starting transfers between devices, swapped(): lax.ppermute(value, axis, [(source, source ^ bit) for source in range(cou...  12.8 us
    pallas_call x1, Pallas kernels, run_kernel_sums(): pl.pallas_call(functools.partial(kernel_sums, len(cots), len(rights) - 1)...  12.3 us
    pallas_call x2, Pallas kernels, run_grad_volume(): pl.pallas_call(functools.partial(grad_volume_levels, first_level), out_sh...  8.89 us
    unnamed x35, local copies, waits for them, and re-layouts  8.85 us
    pallas_call x1, Pallas kernels, run_feature_grads(): pl.pallas_call(functools.partial(feature_grads, hops, len(grad_volumes)),...  4.7 us
    broadcast_in_dim x4, local copies, waits for them, and re-layouts, toeplitz(): total = jnp.where(mask, wide[tap][:, :, None], total)  3.54 us
  transfers between devices with their start and end apart: 26, of which 7 were waited for; matrix products, arithmetic and copies ran while one was open for 13% of the time, Pallas kernels for 12%

profile of v4, /device:TPU:13, one launch (start us, length us, event | category | flops | bytes accessed | tf_op | source)
XLA Modules:
  0.0 117.2 jit_solution(728468058077979889)
XLA Ops:
  0.7 1.2 %copy-done = bf16[320,8,128]{2,1,0:T(8,128)(2,1)S(1)} copy-done((bf16[320,8,128]{2,1,0:T(8,128)(2,1)S(1)}, bf16[320,8,128]{2,1,0:T(8,128)(2,1)}, u32[]{:S(2)}) %copy-start) | copy-done | bytes 655384
  2.0 2.3 %collective-permute-start.10 = (bf16[80,8,128]{2,1,0:T(8,128)(2,1)S(1)}, bf16[80,8,128]{2,1,0:T(8,128)(2,1)S(1)}, u32[]{:S(2)}, u32[]{:S(2)}) collective-permute-start(bf16[80,8,128]{2,1,0:T(8,128)(2,1)S(1)} %constant_dynamic-slice_fusion.1.refs_8_), channel_id=1, source_target_pairs={{0,12},{4,16},{8,20},{12,24},{16,28},{20,0},{24,4},{28,8},{1,13},{... | collective-permute-start | bytes 491528 | tf_op jit(solution)/shard_map/ppermute | solution.py:21
  4.4 2.3 %collective-permute-start.12 = (bf16[80,8,128]{2,1,0:T(8,128)(2,1)S(1)}, bf16[80,8,128]{2,1,0:T(8,128)(2,1)S(1)}, u32[]{:S(2)}, u32[]{:S(2)}) collective-permute-start(bf16[80,8,128]{2,1,0:T(8,128)(2,1)S(1)} %constant_dynamic-slice_fusion.1.refs_8_), channel_id=1, source_target_pairs={{0,20},{4,24},{8,28},{12,0},{16,4},{20,8},{24,12},{28,16},{1,21},{... | collective-permute-start | bytes 491528 | tf_op jit(solution)/shard_map/ppermute | solution.py:21
  6.7 1.2 %collective-permute-start.1 = (bf16[32,12,8,128]{3,2,1,0:T(8,128)(2,1)}, bf16[32,12,8,128]{3,2,1,0:T(8,128)(2,1)S(1)}, u32[]{:S(2)}, u32[]{:S(2)}) collective-permute-start(bf16[32,12,8,128]{3,2,1,0:T(8,128)(2,1)} %refs_0_.1), channel_id=1, source_target_pairs={{0,2},{1,3},{2,0},{3,1},{4,6},{5,7},{6,4},{7,5},{8,10},{9,11},{10,... | collective-permute-start | bytes 2359304 | tf_op jit(solution)/shard_map/ppermute | solution.py:280
  7.9 1.7 %fusion.2 = (bf16[32,12,1,128]{3,2,1,0:T(2,128)(2,1)S(1)}, bf16[32,12,1,128]{3,2,1,0:T(2,128)(2,1)S(1)}) fusion(bf16[32,12,8,128]{3,2,1,0:T(8,128)(2,1)} %refs_0_.1), kind=kLoop, calls=%fused_computation.24 | loop fusion | bytes 393216 | tf_op jit(solution)/shard_map/slice | solution.py:308
  10.3 1.1 collective-permute-start.4
  11.4 1.1 constant_dynamic-slice_fusion
  12.5 1.0 convolution_convert_fusion
  17.1 9.0 %collective-permute-done.4 = bf16[12,32,128]{2,1,0:T(8,128)(2,1)} collective-permute-done((bf16[12,32,128]{2,1,0:T(8,128)(2,1)}, bf16[12,32,128]{2,1,0:T(8,128)(2,1)}, u32[]{:S(2)}, u32[]{:S(2)}) %collective-permute-start.4) | collective-permute-done | bytes 98336 | tf_op jit(solution)/shard_map/ppermute | solution.py:21
  27.0 3.0 %collective-permute-done.3 = bf16[12,32,128]{2,1,0:T(8,128)(2,1)S(1)} collective-permute-done((bf16[12,32,128]{2,1,0:T(8,128)(2,1)S(1)}, bf16[12,32,128]{2,1,0:T(8,128)(2,1)S(1)}, u32[]{:S(2)}, u32[]{:S(2)}) %collective-permute-start.3) | collective-permute-done | bytes 98336 | tf_op jit(solution)/shard_map/ppermute | solution.py:21
  30.0 1.3 %collective-permute-start = (bf16[32,12,8,128]{3,2,1,0:T(8,128)(2,1)S(1)}, bf16[32,12,8,128]{3,2,1,0:T(8,128)(2,1)}, u32[]{:S(2)}, u32[]{:S(2)}) collective-permute-start(bf16[32,12,8,128]{3,2,1,0:T(8,128)(2,1)S(1)} %copy-done.1), channel_id=1, source_target_pairs={{0,1},{1,0},{2,3},{3,2},{4,5},{5,4},{6,7},{7,6},{8,9},{9,8},{10,11... | collective-permute-start | bytes 2359304 | tf_op jit(solution)/shard_map/ppermute | solution.py:280
  32.5 1.2 collective-permute-start.6
  33.7 1.4 %select_select_fusion = bf16[3,10,8,3,320]{4,3,2,1,0:T(4,128)(2,1)} fusion(pred[8,320]{1,0:T(8,128)(4,1)S(1)} %copy-done.13, pred[8,320]{1,0:T(8,128)(4,1)S(1)} %copy-done.14, pred[8,320]{1,0:T(8,128)(4,1)S(1)} %copy-done.15, bf16[3,10,3,320]{3,2,1,0:T(4,128)(2,1)S(1)} %copy.33, bf16[3,10,3,320]{3,2,1,0:T(4,128)(2,1)S(1)} %copy.32, ...), kind=kLoop, calls=%fused_computation.2 | loop fusion | flops 691200 | bytes 641280 | tf_op jit(solution)/shard_map/jit(_where)/select_n | solution.py:45
  35.1 5.5 %collective-permute-done.13.refs_14_ = bf16[80,8,128]{2,1,0:T(8,128)(2,1)S(1)} collective-permute-done((bf16[80,8,128]{2,1,0:T(8,128)(2,1)S(1)}, bf16[80,8,128]{2,1,0:T(8,128)(2,1)S(1)}, u32[]{:S(2)}, u32[]{:S(2)}) %collective-permute-start.13) | collective-permute-done | bytes 163872 | tf_op jit(solution)/shard_map/ppermute | solution.py:21
  42.0 1.0 collective-permute-start.5
  43.1 1.7 %select_n.96.weight_ref = bf16[240,960]{1,0:T(8,128)(2,1)S(1)} reshape(bf16[3,10,8,3,320]{4,3,2,1,0:T(4,128)(2,1)} %select_select_fusion) | data formatting | bytes 921600 | tf_op jit(solution)/shard_map/jit(_where)/select_n | solution.py:45
  50.6 12.3 %shard_map.112 = (bf16[50,320,128]{2,1,0:T(8,128)(2,1)S(1)}, f32[80,56,128]{2,1,0:T(8,128)S(1)}, f32[3,32,96]{2,1,0:T(8,128)S(1)}) custom-call(s32[2]{0:T(128)S(1)} %pad_add_fusion.places, bf16[32,12,8,128]{3,2,1,0:T(8,128)(2,1)S(1)} %copy-done.1, bf16[32,12,8,128]{3,2,1,0:T(8,128)(2,1)} %collective-permute-done.refs_1_, ...), custom_call_target="tpu_custom_call" | custom-call | flops 8000000000 | bytes 4194304 | tf_op jit(solution)/shard_map/pallas_call | solution.py:226
  63.0 2.2 %collective-permute-start.14 = (f32[3,32,96]{2,1,0:T(8,128)S(1)}, f32[3,32,96]{2,1,0:T(8,128)S(1)}, u32[]{:S(2)}, u32[]{:S(2)}) collective-permute-start(f32[3,32,96]{2,1,0:T(8,128)S(1)} %get-tuple-element.30), channel_id=1, source_target_pairs={{0,16},{4,20},{8,24},{12,28},{16,0},{20,4},{24,8},{28,12},{1,17},{... | collective-permute-start | bytes 110600 | tf_op jit(solution)/shard_map/ppermute | solution.py:280
  65.1 4.4 %shard_map.113.refs_0_ = f32[24,80,128]{2,1,0:T(8,128)S(1)} custom-call(bf16[50,320,128]{2,1,0:T(8,128)(2,1)S(1)} %get-tuple-element.32.cot_s, bf16[240,960]{1,0:T(8,128)(2,1)S(1)} %select_n.96.weight_ref), custom_call_target="tpu_custom_call" | custom-call | flops 4000000000 | bytes 4194304 | tf_op jit(solution)/shard_map/pallas_call | solution.py:250
  69.7 4.5 %shard_map.114.refs_1_ = f32[24,80,128]{2,1,0:T(8,128)S(1)} custom-call(bf16[50,320,128]{2,1,0:T(8,128)(2,1)S(1)} %get-tuple-element.32.cot_s, bf16[240,960]{1,0:T(8,128)(2,1)S(1)} %select_n.96.weight_ref), custom_call_target="tpu_custom_call" | custom-call | flops 4000000000 | bytes 4194304 | tf_op jit(solution)/shard_map/pallas_call | solution.py:250
  74.3 4.7 %shard_map.115 = (bf16[80,8,128]{2,1,0:T(8,128)(2,1)}, f32[80,8,128]{2,1,0:T(8,128)S(1)}, bf16[80,8,128]{2,1,0:T(8,128)(2,1)S(1)}, bf16[80,8,128]{2,1,0:T(8,128)...) custom-call(bf16[80,8,128]{2,1,0:T(8,128)(2,1)S(1)} %constant_dynami, ...), custom_call_target="tpu_custom_call" | custom-call | flops 4000000000 | bytes 4194304 | tf_op jit(solution)/shard_map/pallas_call | solution.py:263
  79.0 1.2 %collective-permute-start.24 = (f32[3,32,96]{2,1,0:T(8,128)S(1)}, f32[3,32,96]{2,1,0:T(8,128)S(1)}, u32[]{:S(2)}, u32[]{:S(2)}) collective-permute-start(f32[3,32,96]{2,1,0:T(8,128)S(1)} %add.66), channel_id=1, source_target_pairs={{0,2},{1,3},{2,0},{3,1},{4,6},{5,7},{6,4},{7,5},{8,10},{9,11},{10,... | collective-permute-start | bytes 110600 | tf_op jit(solution)/shard_map/ppermute | solution.py:280
  80.2 1.1 collective-permute-start.17
  81.3 2.7 %collective-permute-start.23 = (f32[3,32,96]{2,1,0:T(8,128)S(1)}, f32[3,32,96]{2,1,0:T(8,128)S(1)}, u32[]{:S(2)}, u32[]{:S(2)}) collective-permute-start(f32[3,32,96]{2,1,0:T(8,128)S(1)} %add.66), channel_id=1, source_target_pairs={{0,1},{1,0},{2,3},{3,2},{4,5},{5,4},{6,7},{7,6},{8,9},{9,8},{10,11... | collective-permute-start | bytes 110600 | tf_op jit(solution)/shard_map/ppermute | solution.py:280
  84.0 1.7 %collective-permute-start.25 = (f32[3,32,96]{2,1,0:T(8,128)S(1)}, f32[3,32,96]{2,1,0:T(8,128)S(1)}, u32[]{:S(2)}, u32[]{:S(2)}) collective-permute-start(f32[3,32,96]{2,1,0:T(8,128)S(1)} %collective-permute-done.24), channel_id=1, source_target_pairs={{0,1},{1,0},{2,3},{3,2},{4,5},{5,4},{6,7},{7,6},{8,9},{9,8},{10,11... | collective-permute-start | bytes 110600 | tf_op jit(solution)/shard_map/ppermute | solution.py:280
  85.7 3.6 %collective-permute-start.18 = (bf16[80,8,128]{2,1,0:T(8,128)(2,1)S(1)}, bf16[80,8,128]{2,1,0:T(8,128)(2,1)}, u32[]{:S(2)}, u32[]{:S(2)}) collective-permute-start(bf16[80,8,128]{2,1,0:T(8,128)(2,1)S(1)} %get-tuple-element.47), channel_id=1, source_target_pairs={{0,12},{4,16},{8,20},{12,24},{16,28},{20,0},{24,4},{28,8},{1,13},{... | collective-permute-start | bytes 491528 | tf_op jit(solution)/shard_map/ppermute | solution.py:21
  90.9 2.0 %collective-permute-start.22 = (bf16[80,8,128]{2,1,0:T(8,128)(2,1)S(1)}, bf16[80,8,128]{2,1,0:T(8,128)(2,1)}, u32[]{:S(2)}, u32[]{:S(2)}) collective-permute-start(bf16[80,8,128]{2,1,0:T(8,128)(2,1)S(1)} %get-tuple-element.51), channel_id=1, source_target_pairs={{0,28},{4,0},{8,4},{12,8},{16,12},{20,16},{24,20},{28,24},{1,29},{... | collective-permute-start | bytes 491528 | tf_op jit(solution)/shard_map/ppermute | solution.py:21
  94.2 1.0 copy.37
  95.2 11.5 %collective-permute-done.18 = bf16[80,8,128]{2,1,0:T(8,128)(2,1)} collective-permute-done((bf16[80,8,128]{2,1,0:T(8,128)(2,1)S(1)}, bf16[80,8,128]{2,1,0:T(8,128)(2,1)}, u32[]{:S(2)}, u32[]{:S(2)}) %collective-permute-start.18) | collective-permute-done | bytes 163872 | tf_op jit(solution)/shard_map/ppermute | solution.py:21
  106.8 3.5 %collective-permute-done.19 = bf16[80,8,128]{2,1,0:T(8,128)(2,1)} collective-permute-done((bf16[80,8,128]{2,1,0:T(8,128)(2,1)S(1)}, bf16[80,8,128]{2,1,0:T(8,128)(2,1)}, u32[]{:S(2)}, u32[]{:S(2)}) %collective-permute-start.19) | collective-permute-done | bytes 163872 | tf_op jit(solution)/shard_map/ppermute | solution.py:21
  110.3 4.8 %collective-permute-done.22 = bf16[80,8,128]{2,1,0:T(8,128)(2,1)} collective-permute-done((bf16[80,8,128]{2,1,0:T(8,128)(2,1)S(1)}, bf16[80,8,128]{2,1,0:T(8,128)(2,1)}, u32[]{:S(2)}, u32[]{:S(2)}) %collective-permute-start.22) | collective-permute-done | bytes 163872 | tf_op jit(solution)/shard_map/ppermute | solution.py:21
  115.1 2.1 %add_convert_fusion = bf16[80,8,128]{2,1,0:T(8,128)(2,1)} fusion(bf16[80,8,128]{2,1,0:T(8,128)(2,1)} %collective-permute-done.22, bf16[80,8,128]{2,1,0:T(8,128)(2,1)} %collective-permute-done.21, bf16[80,8,128]{2,1,0:T(8,128)(2,1)} %collective-permute-done.20, bf16[80,8,128]{2,1,0:T(8,128)(2,1)} %collective-permute-done.19, ...), kind=kLoop, calls=%fused_computation.5 | loop fusion | flops 1556480 | bytes 1474566 | tf_op jit(solution)/shard_map/convert_element_type | solution.py:349
  (88 shorter events, 16.8 us)
Async XLA Ops:
  0.6 33.1 %copy-start.13 = (pred[8,320]{1,0:T(8,128)(4,1)S(1)}, pred[8,320]{1,0:T(8,128)(4,1)}, u32[]{:S(2)}) copy-start(pred[8,320]{1,0:T(8,128)(4,1)} %constant.55.clone) | copy-start | bytes 7684
  0.7 33.0 %copy-start.14 = (pred[8,320]{1,0:T(8,128)(4,1)S(1)}, pred[8,320]{1,0:T(8,128)(4,1)}, u32[]{:S(2)}) copy-start(pred[8,320]{1,0:T(8,128)(4,1)} %constant.56.clone) | copy-start | bytes 7684
  0.7 33.0 %copy-start.15 = (pred[8,320]{1,0:T(8,128)(4,1)S(1)}, pred[8,320]{1,0:T(8,128)(4,1)}, u32[]{:S(2)}) copy-start(pred[8,320]{1,0:T(8,128)(4,1)} %constant.57.clone) | copy-start | bytes 7684
  0.7 45.4 %copy-start.12 = (f32[32,240]{1,0:T(8,128)S(1)}, f32[32,240]{1,0:T(8,128)}, u32[]{:S(2)}) copy-start(f32[32,240]{1,0:T(8,128)} %constant.58.clone.refs_16_) | copy-start | bytes 92164
  0.7 29.3 %copy-start.1 = (bf16[32,12,8,128]{3,2,1,0:T(8,128)(2,1)S(1)}, bf16[32,12,8,128]{3,2,1,0:T(8,128)(2,1)}, u32[]{:S(2)}) copy-start(bf16[32,12,8,128]{3,2,1,0:T(8,128)(2,1)} %refs_0_.1) | copy-start | bytes 2359300
  2.0 29.5 %collective-permute-start.10 = (bf16[80,8,128]{2,1,0:T(8,128)(2,1)S(1)}, bf16[80,8,128]{2,1,0:T(8,128)(2,1)S(1)}, u32[]{:S(2)}, u32[]{:S(2)}) collective-permute-start(bf16[80,8,128]{2,1,0:T(8,128)(2,1)S(1)} %constant_dynamic-slice_fusion.1.refs_8_), channel_id=1, source_target_pairs={{0,12},{4,16},{8,20},{12,24},{16,28},{20,0},{24,4},{28,8},{1,13},{... | collective-permute-start | bytes 491528 | tf_op jit(solution)/shard_map/ppermute | solution.py:21
  4.3 27.3 %collective-permute-start.11 = (bf16[80,8,128]{2,1,0:T(8,128)(2,1)S(1)}, bf16[80,8,128]{2,1,0:T(8,128)(2,1)S(1)}, u32[]{:S(2)}, u32[]{:S(2)}) collective-permute-start(bf16[80,8,128]{2,1,0:T(8,128)(2,1)S(1)} %constant_dynamic-slice_fusion.1.refs_8_), channel_id=1, source_target_pairs={{0,16},{4,20},{8,24},{12,28},{16,0},{20,4},{24,8},{28,12},{1,17},{... | collective-permute-start | bytes 491528 | tf_op jit(solution)/shard_map/ppermute | solution.py:21
  4.4 28.1 %collective-permute-start.12 = (bf16[80,8,128]{2,1,0:T(8,128)(2,1)S(1)}, bf16[80,8,128]{2,1,0:T(8,128)(2,1)S(1)}, u32[]{:S(2)}, u32[]{:S(2)}) collective-permute-start(bf16[80,8,128]{2,1,0:T(8,128)(2,1)S(1)} %constant_dynamic-slice_fusion.1.refs_8_), channel_id=1, source_target_pairs={{0,20},{4,24},{8,28},{12,0},{16,4},{20,8},{24,12},{28,16},{1,21},{... | collective-permute-start | bytes 491528 | tf_op jit(solution)/shard_map/ppermute | solution.py:21
  6.7 24.6 %collective-permute-start.1 = (bf16[32,12,8,128]{3,2,1,0:T(8,128)(2,1)}, bf16[32,12,8,128]{3,2,1,0:T(8,128)(2,1)S(1)}, u32[]{:S(2)}, u32[]{:S(2)}) collective-permute-start(bf16[32,12,8,128]{3,2,1,0:T(8,128)(2,1)} %refs_0_.1), channel_id=1, source_target_pairs={{0,2},{1,3},{2,0},{3,1},{4,6},{5,7},{6,4},{7,5},{8,10},{9,11},{10,... | collective-permute-start | bytes 2359304 | tf_op jit(solution)/shard_map/ppermute | solution.py:280
  10.3 15.8 %collective-permute-start.4 = (bf16[12,32,128]{2,1,0:T(8,128)(2,1)}, bf16[12,32,128]{2,1,0:T(8,128)(2,1)}, u32[]{:S(2)}, u32[]{:S(2)}) collective-permute-start(bf16[12,32,128]{2,1,0:T(8,128)(2,1)} %bitcast.33), channel_id=1, source_target_pairs={{0,28},{4,0},{8,4},{12,8},{16,12},{20,16},{24,20},{28,24},{1,29},{... | collective-permute-start | bytes 294920 | tf_op jit(solution)/shard_map/ppermute | solution.py:21
  26.1 3.9 %collective-permute-start.3 = (bf16[12,32,128]{2,1,0:T(8,128)(2,1)S(1)}, bf16[12,32,128]{2,1,0:T(8,128)(2,1)S(1)}, u32[]{:S(2)}, u32[]{:S(2)}) collective-permute-start(bf16[12,32,128]{2,1,0:T(8,128)(2,1)S(1)} %bitcast.39), channel_id=1, source_target_pairs={{0,4},{4,8},{8,12},{12,16},{16,20},{20,24},{24,28},{28,0},{1,5},{5... | collective-permute-start | bytes 294920 | tf_op jit(solution)/shard_map/ppermute | solution.py:21
  30.0 16.0 %collective-permute-start = (bf16[32,12,8,128]{3,2,1,0:T(8,128)(2,1)S(1)}, bf16[32,12,8,128]{3,2,1,0:T(8,128)(2,1)}, u32[]{:S(2)}, u32[]{:S(2)}) collective-permute-start(bf16[32,12,8,128]{3,2,1,0:T(8,128)(2,1)S(1)} %copy-done.1), channel_id=1, source_target_pairs={{0,1},{1,0},{2,3},{3,2},{4,5},{5,4},{6,7},{7,6},{8,9},{9,8},{10,11... | collective-permute-start | bytes 2359304 | tf_op jit(solution)/shard_map/ppermute | solution.py:280
  31.3 14.7 %collective-permute-start.2 = (bf16[32,12,8,128]{3,2,1,0:T(8,128)(2,1)S(1)}, bf16[32,12,8,128]{3,2,1,0:T(8,128)(2,1)}, u32[]{:S(2)}, u32[]{:S(2)}) collective-permute-start(bf16[32,12,8,128]{3,2,1,0:T(8,128)(2,1)S(1)} %collective-permute-done.1.refs_2_), channel_id=1, source_target_pairs={{0,1},{1,0},{2,3},{3,2},{4,5},{5,4},{6,7},{7,6},{8,9},{9,8},{10,11... | collective-permute-start | bytes 2359304 | tf_op jit(solution)/shard_map/ppermute | solution.py:280
  31.5 11.5 %copy-start.2 = (bf16[80,8,128]{2,1,0:T(8,128)(2,1)}, bf16[80,8,128]{2,1,0:T(8,128)(2,1)S(1)}, u32[]{:S(2)}) copy-start(bf16[80,8,128]{2,1,0:T(8,128)(2,1)S(1)} %collective-permute-done.10.refs_11_) | copy-start | bytes 491524
  31.5 9.1 %collective-permute-start.13 = (bf16[80,8,128]{2,1,0:T(8,128)(2,1)S(1)}, bf16[80,8,128]{2,1,0:T(8,128)(2,1)S(1)}, u32[]{:S(2)}, u32[]{:S(2)}) collective-permute-start(bf16[80,8,128]{2,1,0:T(8,128)(2,1)S(1)} %constant_dynamic-slice_fusion.1.refs_8_), channel_id=1, source_target_pairs={{0,24},{4,28},{8,0},{12,4},{16,8},{20,12},{24,16},{28,20},{1,25},{... | collective-permute-start | bytes 491528 | tf_op jit(solution)/shard_map/ppermute | solution.py:21
  31.6 9.7 %collective-permute-start.8 = (bf16[80,8,128]{2,1,0:T(8,128)(2,1)S(1)}, bf16[80,8,128]{2,1,0:T(8,128)(2,1)S(1)}, u32[]{:S(2)}, u32[]{:S(2)}) collective-permute-start(bf16[80,8,128]{2,1,0:T(8,128)(2,1)S(1)} %constant_dynamic-slice_fusion.1.refs_8_), channel_id=1, source_target_pairs={{0,4},{4,8},{8,12},{12,16},{16,20},{20,24},{24,28},{28,0},{1,5},{5... | collective-permute-start | bytes 491528 | tf_op jit(solution)/shard_map/ppermute | solution.py:21
  32.5 10.5 %collective-permute-start.6 = (bf16[12,64,128]{2,1,0:T(8,128)(2,1)S(1)}, bf16[12,64,128]{2,1,0:T(8,128)(2,1)S(1)}, u32[]{:S(2)}, u32[]{:S(2)}) collective-permute-start(bf16[12,64,128]{2,1,0:T(8,128)(2,1)S(1)} %pad_maximum_fusion.refs_4_), channel_id=1, source_target_pairs={{0,2},{1,3},{2,0},{3,1},{4,6},{5,7},{6,4},{7,5},{8,10},{9,11},{10,... | collective-permute-start | bytes 589832 | tf_op jit(solution)/shard_map/ppermute | solution.py:280
  41.3 4.8 %collective-permute-start.9 = (bf16[80,8,128]{2,1,0:T(8,128)(2,1)S(1)}, bf16[80,8,128]{2,1,0:T(8,128)(2,1)}, u32[]{:S(2)}, u32[]{:S(2)}) collective-permute-start(bf16[80,8,128]{2,1,0:T(8,128)(2,1)S(1)} %constant_dynamic-slice_fusion.1.refs_8_), channel_id=1, source_target_pairs={{0,8},{4,12},{8,16},{12,20},{16,24},{20,28},{24,0},{28,4},{1,9},{5... | collective-permute-start | bytes 491528 | tf_op jit(solution)/shard_map/ppermute | solution.py:21
  42.0 4.1 %collective-permute-start.5 = (bf16[12,64,128]{2,1,0:T(8,128)(2,1)S(1)}, bf16[12,64,128]{2,1,0:T(8,128)(2,1)S(1)}, u32[]{:S(2)}, u32[]{:S(2)}) collective-permute-start(bf16[12,64,128]{2,1,0:T(8,128)(2,1)S(1)} %pad_maximum_fusion.refs_4_), channel_id=1, source_target_pairs={{0,1},{1,0},{2,3},{3,2},{4,5},{5,4},{6,7},{7,6},{8,9},{9,8},{10,11... | collective-permute-start | bytes 589832 | tf_op jit(solution)/shard_map/ppermute | solution.py:280
  43.0 3.0 %collective-permute-start.7 = (bf16[12,64,128]{2,1,0:T(8,128)(2,1)S(1)}, bf16[12,64,128]{2,1,0:T(8,128)(2,1)}, u32[]{:S(2)}, u32[]{:S(2)}) collective-permute-start(bf16[12,64,128]{2,1,0:T(8,128)(2,1)S(1)} %collective-permute-done.6.refs_6_), channel_id=1, source_target_pairs={{0,1},{1,0},{2,3},{3,2},{4,5},{5,4},{6,7},{7,6},{8,9},{9,8},{10,11... | collective-permute-start | bytes 589832 | tf_op jit(solution)/shard_map/ppermute | solution.py:280
  63.0 6.6 %collective-permute-start.14 = (f32[3,32,96]{2,1,0:T(8,128)S(1)}, f32[3,32,96]{2,1,0:T(8,128)S(1)}, u32[]{:S(2)}, u32[]{:S(2)}) collective-permute-start(f32[3,32,96]{2,1,0:T(8,128)S(1)} %get-tuple-element.30), channel_id=1, source_target_pairs={{0,16},{4,20},{8,24},{12,28},{16,0},{20,4},{24,8},{28,12},{1,17},{... | collective-permute-start | bytes 110600 | tf_op jit(solution)/shard_map/ppermute | solution.py:280
  69.6 4.5 %collective-permute-start.15 = (f32[3,32,96]{2,1,0:T(8,128)S(1)}, f32[3,32,96]{2,1,0:T(8,128)S(1)}, u32[]{:S(2)}, u32[]{:S(2)}) collective-permute-start(f32[3,32,96]{2,1,0:T(8,128)S(1)} %add.64), channel_id=1, source_target_pairs={{0,8},{4,12},{8,0},{12,4},{16,24},{20,28},{24,16},{28,20},{1,9},{5... | collective-permute-start | bytes 110600 | tf_op jit(solution)/shard_map/ppermute | solution.py:280
  74.2 4.8 %collective-permute-start.16 = (f32[3,32,96]{2,1,0:T(8,128)S(1)}, f32[3,32,96]{2,1,0:T(8,128)S(1)}, u32[]{:S(2)}, u32[]{:S(2)}) collective-permute-start(f32[3,32,96]{2,1,0:T(8,128)S(1)} %add.65), channel_id=1, source_target_pairs={{0,4},{4,0},{8,12},{12,8},{16,20},{20,16},{24,28},{28,24},{1,5},{5... | collective-permute-start | bytes 110600 | tf_op jit(solution)/shard_map/ppermute | solution.py:280
  79.0 5.0 %collective-permute-start.24 = (f32[3,32,96]{2,1,0:T(8,128)S(1)}, f32[3,32,96]{2,1,0:T(8,128)S(1)}, u32[]{:S(2)}, u32[]{:S(2)}) collective-permute-start(f32[3,32,96]{2,1,0:T(8,128)S(1)} %add.66), channel_id=1, source_target_pairs={{0,2},{1,3},{2,0},{3,1},{4,6},{5,7},{6,4},{7,5},{8,10},{9,11},{10,... | collective-permute-start | bytes 110600 | tf_op jit(solution)/shard_map/ppermute | solution.py:280
  80.2 10.6 %collective-permute-start.17 = (bf16[80,8,128]{2,1,0:T(8,128)(2,1)S(1)}, bf16[80,8,128]{2,1,0:T(8,128)(2,1)S(1)}, u32[]{:S(2)}, u32[]{:S(2)}) collective-permute-start(bf16[80,8,128]{2,1,0:T(8,128)(2,1)S(1)} %get-tuple-element.46), channel_id=1, source_target_pairs={{0,8},{4,12},{8,16},{12,20},{16,24},{20,28},{24,0},{28,4},{1,9},{5... | collective-permute-start | bytes 491528 | tf_op jit(solution)/shard_map/ppermute | solution.py:21
  81.3 8.2 %collective-permute-start.23 = (f32[3,32,96]{2,1,0:T(8,128)S(1)}, f32[3,32,96]{2,1,0:T(8,128)S(1)}, u32[]{:S(2)}, u32[]{:S(2)}) collective-permute-start(f32[3,32,96]{2,1,0:T(8,128)S(1)} %add.66), channel_id=1, source_target_pairs={{0,1},{1,0},{2,3},{3,2},{4,5},{5,4},{6,7},{7,6},{8,9},{9,8},{10,11... | collective-permute-start | bytes 110600 | tf_op jit(solution)/shard_map/ppermute | solution.py:280
  84.0 6.2 %collective-permute-start.25 = (f32[3,32,96]{2,1,0:T(8,128)S(1)}, f32[3,32,96]{2,1,0:T(8,128)S(1)}, u32[]{:S(2)}, u32[]{:S(2)}) collective-permute-start(f32[3,32,96]{2,1,0:T(8,128)S(1)} %collective-permute-done.24), channel_id=1, source_target_pairs={{0,1},{1,0},{2,3},{3,2},{4,5},{5,4},{6,7},{7,6},{8,9},{9,8},{10,11... | collective-permute-start | bytes 110600 | tf_op jit(solution)/shard_map/ppermute | solution.py:280
  85.7 21.1 %collective-permute-start.18 = (bf16[80,8,128]{2,1,0:T(8,128)(2,1)S(1)}, bf16[80,8,128]{2,1,0:T(8,128)(2,1)}, u32[]{:S(2)}, u32[]{:S(2)}) collective-permute-start(bf16[80,8,128]{2,1,0:T(8,128)(2,1)S(1)} %get-tuple-element.47), channel_id=1, source_target_pairs={{0,12},{4,16},{8,20},{12,24},{16,28},{20,0},{24,4},{28,8},{1,13},{... | collective-permute-start | bytes 491528 | tf_op jit(solution)/shard_map/ppermute | solution.py:21
  89.3 21.0 %collective-permute-start.19 = (bf16[80,8,128]{2,1,0:T(8,128)(2,1)S(1)}, bf16[80,8,128]{2,1,0:T(8,128)(2,1)}, u32[]{:S(2)}, u32[]{:S(2)}) collective-permute-start(bf16[80,8,128]{2,1,0:T(8,128)(2,1)S(1)} %get-tuple-element.48), channel_id=1, source_target_pairs={{0,16},{4,20},{8,24},{12,28},{16,0},{20,4},{24,8},{28,12},{1,17},{... | collective-permute-start | bytes 491528 | tf_op jit(solution)/shard_map/ppermute | solution.py:21
  89.5 20.7 %collective-permute-start.20 = (bf16[80,8,128]{2,1,0:T(8,128)(2,1)S(1)}, bf16[80,8,128]{2,1,0:T(8,128)(2,1)}, u32[]{:S(2)}, u32[]{:S(2)}) collective-permute-start(bf16[80,8,128]{2,1,0:T(8,128)(2,1)S(1)} %get-tuple-element.49), channel_id=1, source_target_pairs={{0,20},{4,24},{8,28},{12,0},{16,4},{20,8},{24,12},{28,16},{1,21},{... | collective-permute-start | bytes 491528 | tf_op jit(solution)/shard_map/ppermute | solution.py:21
  90.2 20.1 %collective-permute-start.21 = (bf16[80,8,128]{2,1,0:T(8,128)(2,1)S(1)}, bf16[80,8,128]{2,1,0:T(8,128)(2,1)}, u32[]{:S(2)}, u32[]{:S(2)}) collective-permute-start(bf16[80,8,128]{2,1,0:T(8,128)(2,1)S(1)} %get-tuple-element.50), channel_id=1, source_target_pairs={{0,24},{4,28},{8,0},{12,4},{16,8},{20,12},{24,16},{28,20},{1,25},{... | collective-permute-start | bytes 491528 | tf_op jit(solution)/shard_map/ppermute | solution.py:21
  90.9 24.3 %collective-permute-start.22 = (bf16[80,8,128]{2,1,0:T(8,128)(2,1)S(1)}, bf16[80,8,128]{2,1,0:T(8,128)(2,1)}, u32[]{:S(2)}, u32[]{:S(2)}) collective-permute-start(bf16[80,8,128]{2,1,0:T(8,128)(2,1)S(1)} %get-tuple-element.51), channel_id=1, source_target_pairs={{0,28},{4,0},{8,4},{12,8},{16,12},{20,16},{24,20},{28,24},{1,29},{... | collective-permute-start | bytes 491528 | tf_op jit(solution)/shard_map/ppermute | solution.py:21
  (10 other events, 29.2 us)

commit v5 on v4

--- a/solution.py
+++ b/solution.py
@@ -53,8 +53,8 @@
     return jnp.where(lane == (0 if steps > 0 else size - 1), 0.0, moved)
 
 
-def kernel_sums(parts, hops, places, *refs):
-    cot_refs, halo_refs, refs = refs[:parts], refs[parts : 2 * parts], refs[2 * parts :]
+def kernel_sums(parts, hops, halo_order, places, *refs):
+    cot_refs, halo_ref, refs = refs[:parts], refs[parts], refs[parts + 1 :]
     right_refs, refs = refs[: hops + 1], refs[hops + 1 :]
     left_ref, fold_ref, cot_s, right_s, sums_ref = refs[:5]
     cot_b, halo_b, right_b, vol_s, prod_s, sems = refs[5:]
@@ -68,11 +68,12 @@
     f32, bf16 = jnp.float32, jnp.bfloat16
 
     copies = []
-    for buffer, sources in ((right_b, right_refs), (cot_b, cot_refs), (halo_b, halo_refs)):
+    for buffer, sources in ((right_b, right_refs), (cot_b, cot_refs)):
         for at, source in enumerate(sources):
             copies.append(
                 pltpu.make_async_copy(source, buffer.at[at], sems.at[len(copies)])
             )
+    copies.append(pltpu.make_async_copy(halo_ref, halo_b, sems.at[len(copies)]))
     for copy in copies:
         copy.start()
 
@@ -107,7 +108,7 @@
 
         def assemble(level, carry, other=other, start=start):
             cot_s[start + level, 0:main] = cot_b[other, :, level].reshape(main, rows)
-            cot_s[start + level, main:span] = halo_b[other, level]
+            cot_s[start + level, main:span] = halo_b[halo_order.index(other), level]
             return carry
 
         lax.fori_loop(0, levels, assemble, 0)
@@ -208,7 +209,7 @@
 
 VMEM = pl.BlockSpec(memory_space=pltpu.VMEM)
 SMEM = pl.BlockSpec(memory_space=pltpu.SMEM)
-ANY = pl.BlockSpec(memory_space=pl.ANY)
+HBM = pl.BlockSpec(memory_space=pltpu.HBM)
 MIB = 1024 * 1024
 
 
@@ -216,25 +217,25 @@
     return pl.CostEstimate(flops=flops, bytes_accessed=4 * MIB, transcendentals=0)
 
 
-def run_kernel_sums(places, cots, halos, rights, left, fold):
+def run_kernel_sums(places, cots, halos, halo_order, rights, left, fold):
     outs, levels, width, rows = cots[0].shape
     channels = left.shape[0]
     size = fold.shape[1]
     span = outs * (width + 2)
     f32, bf16 = jnp.float32, jnp.bfloat16
-    moved = [*cots, *halos, *rights]
+    moved = [*cots, halos, *rights]
     return pl.pallas_call(
-        functools.partial(kernel_sums, len(cots), len(rights) - 1),
+        functools.partial(kernel_sums, len(cots), len(rights) - 1, halo_order),
         out_shape=[
             jax.ShapeDtypeStruct((D + 2, span, rows), bf16),
             jax.ShapeDtypeStruct((channels, len(rights) * width, rows), f32),
             jax.ShapeDtypeStruct((3, fold.shape[0], 3 * outs), f32),
         ],
-        in_specs=[SMEM] + [ANY] * len(moved) + [VMEM] * 2,
+        in_specs=[SMEM] + [HBM] * len(moved) + [VMEM] * 2,
         out_specs=[VMEM] * 3,
         scratch_shapes=[
             pltpu.VMEM((len(cots), *cots[0].shape), bf16),
-            pltpu.VMEM((len(halos), *halos[0].shape), bf16),
+            pltpu.VMEM(halos.shape, bf16),
             pltpu.VMEM((len(rights), *rights[0].shape), bf16),
             pltpu.VMEM((D, 3, size // 3, rows), f32),
             pltpu.VMEM((3, span, size), f32),
@@ -280,13 +281,27 @@
     return lax.ppermute(value, axis, [(source, source ^ bit) for source in range(count)])
 
 
-def gather_swapping(value, axis):
+def gather_swapping(value, axis, others=()):
     held = {0: value}
     bit = lax.axis_size(axis) // 2
     while bit:
-        held.update({key | bit: swapped(item, axis, bit) for key, item in list(held.items())})
+        step = {key | bit: swapped(item, axis, bit) for key, item in held.items()}
+        if others and bit == lax.axis_size(axis) // 2:
+            (step[bit], *others) = lax.optimization_barrier((step[bit], *others))
+        held.update(step)
         bit //= 2
-    return [held[key] for key in range(len(held))]
+    return [held[key] for key in range(len(held))], others
+
+
+def gather_joining(value, axis):
+    count = lax.axis_size(axis)
+    held, order = value[None], [0]
+    bit = count // 2
+    while bit:
+        held = jnp.concatenate([held, swapped(held, axis, bit)], axis=0)
+        order = order + [key | bit for key in order]
+        bit //= 2
+    return held, order
 
 
 def total_swapping(value, bit):
@@ -304,14 +319,19 @@
     places = jnp.stack([part, column]).astype(jnp.int32)
     f32, bf16 = jnp.float32, jnp.bfloat16
 
-    cots = gather_swapping(cotangent, "disp")
-    low = shifted(jnp.transpose(cotangent[:, :, width - 1], (1, 0, 2)), "col", 1)
-    high = shifted(jnp.transpose(cotangent[:, :, 0], (1, 0, 2)), "col", -1)
+    low = jnp.transpose(cotangent[:, :, width - 1], (1, 0, 2))
+    high = jnp.transpose(cotangent[:, :, 0], (1, 0, 2))
+    low, high, right = lax.optimization_barrier((low, high, right))
+    low, high = shifted(low, "col", 1), shifted(high, "col", -1)
+    right_own = lax.dynamic_slice_in_dim(right, part * channels, channels, 0)
+    right_near, low, high = lax.optimization_barrier((right_own, low, high))
     low = jnp.where(column > 0, low, 0).astype(bf16)
     high = jnp.where(column < columns - 1, high, 0).astype(bf16)
-    halos = gather_swapping(jnp.concatenate([low, high], axis=1), "disp")
-    right_own = lax.dynamic_slice_in_dim(right, part * channels, channels, 0)
-    rights = [right_own] + [shifted(right_own, "col", hop) for hop in range(1, hops + 1)]
+    halos, halo_order = gather_joining(jnp.concatenate([low, high], axis=1), "disp")
+    rights = [right_own] + [
+        shifted(right_own if hop <= 2 else right_near, "col", hop) for hop in range(1, hops + 1)
+    ]
+    cots, rights = gather_swapping(cotangent, "disp", rights)
 
     left_own = lax.dynamic_slice_in_dim(left, part * channels, channels, 0)
     weights = toeplitz(lax.dynamic_slice_in_dim(kernel, part * groups, groups, 4), width)
@@ -320,7 +340,7 @@
     fold[np.arange(3 * groups * width) // width, np.arange(3 * groups * width)] = 1
 
     cot_wide, right_wide, total = run_kernel_sums(
-        places, cots, halos, rights, left_own, jnp.asarray(fold)
+        places, cots, halos, halo_order, rights, left_own, jnp.asarray(fold)
     )
     bits = [1 << k for k in reversed(range(columns.bit_length() - 1))]
     first_half = run_grad_volume(cot_wide, weights, 0, D // 2)
@@ -340,7 +360,7 @@
         arrived = shifted(sent[hop - 1], "col", -hop).astype(f32)
         total_right = total_right + jnp.where(column + hop < columns, arrived, 0.0)
 
-    pieces = jnp.stack(gather_swapping(total, "disp"))
+    pieces = jnp.stack(gather_swapping(total, "disp")[0])
     pieces = pieces[jnp.arange(parts) ^ part][:, :, : 3 * groups]
     total = pieces.reshape(parts, 3, 3, groups, 3, outs)
     cell_count = D * width * columns * rows

time: 118 us -> 119 us (level)
  local copies, waits for them, and re-layouts: 18.9 us -> 10.4 us
  starting transfers between devices: 27.9 us -> 33.3 us
  other arithmetic: 4.71 us -> 7.62 us
  waiting for transfers between devices: 37.7 us -> 40.5 us
    unnamed x35 -> x25, local copies, waits for them, and re-layouts: 8.85 us -> 3.61 us
    broadcast_in_dim x4, local copies, waits for them, and re-layouts: 3.54 us -> 0.14 us  [toeplitz(): total = jnp.where(mask, wide[tap][:, :, None], total)]
    ppermute x14, starting transfers between devices: 15.1 us -> 18.2 us  [shifted(): lax.ppermute(value, axis, [(source, (source + steps) % count) for source...]
    ppermute x12 -> x11, waiting for transfers between devices: 0.03 us -> 2.46 us  [swapped(): lax.ppermute(value, axis, [(source, source ^ bit) for source in range(cou...]
    ppermute x12 -> x11, starting transfers between devices: 12.8 us -> 15.2 us  [swapped(): lax.ppermute(value, axis, [(source, source ^ bit) for source in range(cou...]
    concatenate x1 -> x2, other arithmetic: 0.02 us -> 2.04 us  [gather_joining(): held = jnp.concatenate([held, swapped(held, axis, bit)], axis=0)]
  transfers between devices with their start and end apart: 26 -> 25, of which waited for: 7 -> 8; matrix products, arithmetic and copies ran while one was open for 13% -> 11% of each run, Pallas kernels for 12% -> 11%
where the time goes in v5:
time: 119 us
  waiting for transfers between devices  40.5 us (34%)
  starting transfers between devices  33.3 us (28%)
  Pallas kernels  25.1 us (21%)
  local copies, waits for them, and re-layouts  10.4 us (9%)
  other arithmetic  7.62 us (6%)
    ppermute x14, waiting for transfers between devices, shifted(): lax.ppermute(value, axis, [(source, (source + steps) % count) for source...  38 us
    ppermute x14, starting transfers between devices, shifted(): lax.ppermute(value, axis, [(source, (source + steps) % count) for source...  18.2 us
    ppermute x11, starting transfers between devices, swapped(): lax.ppermute(value, axis, [(source, source ^ bit) for source in range(cou...  15.2 us
    pallas_call x1, Pallas kernels, run_kernel_sums(): pl.pallas_call(functools.partial(kernel_sums, len(cots), len(rights) - 1,...  11.7 us
    pallas_call x2, Pallas kernels, run_grad_volume(): pl.pallas_call(functools.partial(grad_volume_levels, first_level), out_sh...  8.89 us
    pallas_call x1, Pallas kernels, run_feature_grads(): pl.pallas_call(functools.partial(feature_grads, hops, len(grad_volumes)),...  4.45 us
    unnamed x25, local copies, waits for them, and re-layouts  3.61 us
    ppermute x11, waiting for transfers between devices, swapped(): lax.ppermute(value, axis, [(source, source ^ bit) for source in range(cou...  2.46 us
  transfers between devices with their start and end apart: 25, of which 8 were waited for; matrix products, arithmetic and copies ran while one was open for 11% of the time, Pallas kernels for 11%

profile of v5, /device:TPU:13, one launch (start us, length us, event | category | flops | bytes accessed | tf_op | source)
XLA Modules:
  0.0 119.0 jit_solution(2103564277538654876)
XLA Ops:
  0.7 1.7 %fusion.2 = (bf16[32,12,1,128]{3,2,1,0:T(2,128)(2,1)S(1)}, bf16[32,12,1,128]{3,2,1,0:T(2,128)(2,1)S(1)}) fusion(bf16[32,12,8,128]{3,2,1,0:T(8,128)(2,1)} %refs_0_.1), kind=kLoop, calls=%fused_computation.26 | loop fusion | bytes 393216 | tf_op jit(solution)/shard_map/slice | solution.py:323
  2.5 1.3 %collective-permute-start.2 = (bf16[80,8,128]{2,1,0:T(8,128)(2,1)S(1)}, bf16[80,8,128]{2,1,0:T(8,128)(2,1)S(1)}, u32[]{:S(2)}, u32[]{:S(2)}) collective-permute-start(bf16[80,8,128]{2,1,0:T(8,128)(2,1)S(1)} %constant_dynamic-slice_fusion.1.refs_5_), channel_id=1, source_target_pairs={{0,4},{4,8},{8,12},{12,16},{16,20},{20,24},{24,28},{28,0},{1,5},{5... | collective-permute-start | bytes 491528 | tf_op jit(solution)/shard_map/ppermute | solution.py:21
  3.8 1.3 %collective-permute-start.3 = (bf16[80,8,128]{2,1,0:T(8,128)(2,1)S(1)}, bf16[80,8,128]{2,1,0:T(8,128)(2,1)S(1)}, u32[]{:S(2)}, u32[]{:S(2)}) collective-permute-start(bf16[80,8,128]{2,1,0:T(8,128)(2,1)S(1)} %constant_dynamic-slice_fusion.1.refs_5_), channel_id=1, source_target_pairs={{0,8},{4,12},{8,16},{12,20},{16,24},{20,28},{24,0},{28,4},{1,9},{5... | collective-permute-start | bytes 491528 | tf_op jit(solution)/shard_map/ppermute | solution.py:21
  5.1 1.2 %collective-permute-start.1 = (bf16[32,12,8,128]{3,2,1,0:T(8,128)(2,1)}, bf16[32,12,8,128]{3,2,1,0:T(8,128)(2,1)S(1)}, u32[]{:S(2)}, u32[]{:S(2)}) collective-permute-start(bf16[32,12,8,128]{3,2,1,0:T(8,128)(2,1)} %refs_0_.1), channel_id=1, source_target_pairs={{0,2},{1,3},{2,0},{3,1},{4,6},{5,7},{6,4},{7,5},{8,10},{9,11},{10,... | collective-permute-start | bytes 2359304 | tf_op jit(solution)/shard_map/ppermute | solution.py:281
  6.3 1.2 %collective-permute-start.4 = (bf16[12,32,128]{2,1,0:T(8,128)(2,1)S(1)}, bf16[12,32,128]{2,1,0:T(8,128)(2,1)}, u32[]{:S(2)}, u32[]{:S(2)}) collective-permute-start(bf16[12,32,128]{2,1,0:T(8,128)(2,1)S(1)} %get-tuple-element.43), channel_id=1, source_target_pairs={{0,4},{4,8},{8,12},{12,16},{16,20},{20,24},{24,28},{28,0},{1,5},{5... | collective-permute-start | bytes 294920 | tf_op jit(solution)/shard_map/ppermute | solution.py:21
  10.0 2.3 %collective-permute-done.4 = bf16[12,32,128]{2,1,0:T(8,128)(2,1)} collective-permute-done((bf16[12,32,128]{2,1,0:T(8,128)(2,1)S(1)}, bf16[12,32,128]{2,1,0:T(8,128)(2,1)}, u32[]{:S(2)}, u32[]{:S(2)}) %collective-permute-start.4) | collective-permute-done | bytes 98336 | tf_op jit(solution)/shard_map/ppermute | solution.py:21
  12.3 3.9 %collective-permute-start.6 = (bf16[80,8,128]{2,1,0:T(8,128)(2,1)S(1)}, bf16[80,8,128]{2,1,0:T(8,128)(2,1)S(1)}, u32[]{:S(2)}, u32[]{:S(2)}) collective-permute-start(bf16[80,8,128]{2,1,0:T(8,128)(2,1)S(1)} %constant_dynamic-slice_fusion.1.refs_5_), channel_id=1, source_target_pairs={{0,12},{4,16},{8,20},{12,24},{16,28},{20,0},{24,4},{28,8},{1,13},{... | collective-permute-start | bytes 491528 | tf_op jit(solution)/shard_map/ppermute | solution.py:21
  18.1 1.9 %collective-permute-start.9 = (bf16[80,8,128]{2,1,0:T(8,128)(2,1)S(1)}, bf16[80,8,128]{2,1,0:T(8,128)(2,1)S(1)}, u32[]{:S(2)}, u32[]{:S(2)}) collective-permute-start(bf16[80,8,128]{2,1,0:T(8,128)(2,1)S(1)} %constant_dynamic-slice_fusion.1.refs_5_), channel_id=1, source_target_pairs={{0,24},{4,28},{8,0},{12,4},{16,8},{20,12},{24,16},{28,20},{1,25},{... | collective-permute-start | bytes 491528 | tf_op jit(solution)/shard_map/ppermute | solution.py:21
  21.0 12.5 %collective-permute-done.6.refs_8_ = bf16[80,8,128]{2,1,0:T(8,128)(2,1)S(1)} collective-permute-done((bf16[80,8,128]{2,1,0:T(8,128)(2,1)S(1)}, bf16[80,8,128]{2,1,0:T(8,128)(2,1)S(1)}, u32[]{:S(2)}, u32[]{:S(2)}) %collective-permute-start.6) | collective-permute-done | bytes 163872 | tf_op jit(solution)/shard_map/ppermute | solution.py:21
  33.5 1.8 %collective-permute-start = (bf16[32,12,8,128]{3,2,1,0:T(8,128)(2,1)}, bf16[32,12,8,128]{3,2,1,0:T(8,128)(2,1)}, u32[]{:S(2)}, u32[]{:S(2)}) collective-permute-start(bf16[32,12,8,128]{3,2,1,0:T(8,128)(2,1)} %refs_0_.1), channel_id=1, source_target_pairs={{0,1},{1,0},{2,3},{3,2},{4,5},{5,4},{6,7},{7,6},{8,9},{9,8},{10,11... | collective-permute-start | bytes 2359304 | tf_op jit(solution)/shard_map/ppermute | solution.py:281
  35.3 1.7 %collective-permute-done.7.refs_9_ = bf16[80,8,128]{2,1,0:T(8,128)(2,1)S(1)} collective-permute-done((bf16[80,8,128]{2,1,0:T(8,128)(2,1)S(1)}, bf16[80,8,128]{2,1,0:T(8,128)(2,1)S(1)}, u32[]{:S(2)}, u32[]{:S(2)}) %collective-permute-start.7) | collective-permute-done | bytes 163872 | tf_op jit(solution)/shard_map/ppermute | solution.py:21
  38.2 1.5 %collective-permute-start.10 = (bf16[32,12,8,128]{3,2,1,0:T(8,128)(2,1)S(1)}, bf16[32,12,8,128]{3,2,1,0:T(8,128)(2,1)}, u32[]{:S(2)}, u32[]{:S(2)}) collective-permute-start(bf16[32,12,8,128]{3,2,1,0:T(8,128)(2,1)S(1)} %collective-permute-done.1.refs_2_), channel_id=1, source_target_pairs={{0,1},{1,0},{2,3},{3,2},{4,5},{5,4},{6,7},{7,6},{8,9},{9,8},{10,11... | collective-permute-start | bytes 2359304 | tf_op jit(solution)/shard_map/ppermute | solution.py:281
  39.8 2.4 %collective-permute-done.11 = bf16[1,12,64,128]{3,2,1,0:T(8,128)(2,1)S(1)} collective-permute-done((bf16[1,12,64,128]{3,2,1,0:T(8,128)(2,1)S(1)}, bf16[1,12,64,128]{3,2,1,0:T(8,128)(2,1)S(1)}, u32[]{:S(2)}, u32[]{:S(2)}) %collective-permute-start.11) | collective-permute-done | bytes 196640 | tf_op jit(solution)/shard_map/ppermute | solution.py:281
  43.1 2.0 %collective-permute-start.12 = (bf16[2,12,64,128]{3,2,1,0:T(8,128)(2,1)}, bf16[2,12,64,128]{3,2,1,0:T(8,128)(2,1)}, u32[]{:S(2)}, u32[]{:S(2)}) collective-permute-start(bf16[2,12,64,128]{3,2,1,0:T(8,128)(2,1)} %pad_maximum_fusion.1), channel_id=1, source_target_pairs={{0,1},{1,0},{2,3},{3,2},{4,5},{5,4},{6,7},{7,6},{8,9},{9,8},{10,11... | collective-permute-start | bytes 1179656 | tf_op jit(solution)/shard_map/ppermute | solution.py:281
  45.1 1.4 %select_select_fusion = bf16[3,10,8,3,320]{4,3,2,1,0:T(4,128)(2,1)} fusion(pred[8,320]{1,0:T(8,128)(4,1)S(1)} %copy-done.9, pred[8,320]{1,0:T(8,128)(4,1)S(1)} %copy-done.10, pred[8,320]{1,0:T(8,128)(4,1)S(1)} %copy-done.11, bf16[3,10,3,320]{3,2,1,0:T(4,128)(2,1)S(1)} %copy.33, bf16[3,10,3,320]{3,2,1,0:T(4,128)(2,1)S(1)} %copy.32, ...), kind=kLoop, calls=%fused_computation.3 | loop fusion | flops 691200 | bytes 641280 | tf_op jit(solution)/shard_map/jit(_where)/select_n | solution.py:45
  46.5 1.7 %select_n.96.weight_ref = bf16[240,960]{1,0:T(8,128)(2,1)S(1)} reshape(bf16[3,10,8,3,320]{4,3,2,1,0:T(4,128)(2,1)} %select_select_fusion) | data formatting | bytes 921600 | tf_op jit(solution)/shard_map/jit(_where)/select_n | solution.py:45
  49.2 1.2 %pad_maximum_fusion.refs_4_ = bf16[4,12,64,128]{3,2,1,0:T(8,128)(2,1)S(1)} fusion(bf16[2,12,64,128]{3,2,1,0:T(8,128)(2,1)} %collective-permute-done.12, bf16[1,12,64,128]{3,2,1,0:T(8,128)(2,1)} %copy-done.8, bf16[1,12,64,128]{3,2,1,0:T(8,128)(2,1)} %copy-done.7), kind=kLoop, calls=%fused_computation.2 | loop fusion | flops 786432 | bytes 1572864 | tf_op jit(solution)/shard_map/concatenate | solution.py:301
  53.0 11.7 %shard_map.112 = (bf16[50,320,128]{2,1,0:T(8,128)(2,1)S(1)}, f32[80,56,128]{2,1,0:T(8,128)S(1)}, f32[3,32,96]{2,1,0:T(8,128)S(1)}) custom-call(s32[2]{0:T(128)S(1)} %pad_add_fusion.places, bf16[32,12,8,128]{3,2,1,0:T(8,128)(2,1)S(1)} %copy-done.1, bf16[32,12,8,128]{3,2,1,0:T(8,128)(2,1)} %collective-permute-done.refs_1_, ...), custom_call_target="tpu_custom_call" | custom-call | flops 8000000000 | bytes 4194304 | tf_op jit(solution)/shard_map/pallas_call | solution.py:227
  64.8 3.2 %collective-permute-start.13 = (f32[3,32,96]{2,1,0:T(8,128)S(1)}, f32[3,32,96]{2,1,0:T(8,128)S(1)}, u32[]{:S(2)}, u32[]{:S(2)}) collective-permute-start(f32[3,32,96]{2,1,0:T(8,128)S(1)} %get-tuple-element.58), channel_id=1, source_target_pairs={{0,16},{4,20},{8,24},{12,28},{16,0},{20,4},{24,8},{28,12},{1,17},{... | collective-permute-start | bytes 110600 | tf_op jit(solution)/shard_map/ppermute | solution.py:281
  68.0 4.4 %shard_map.113.refs_0_ = f32[24,80,128]{2,1,0:T(8,128)S(1)} custom-call(bf16[50,320,128]{2,1,0:T(8,128)(2,1)S(1)} %get-tuple-element.60.cot_s, bf16[240,960]{1,0:T(8,128)(2,1)S(1)} %select_n.96.weight_ref), custom_call_target="tpu_custom_call" | custom-call | flops 4000000000 | bytes 4194304 | tf_op jit(solution)/shard_map/pallas_call | solution.py:251
  72.5 4.4 %shard_map.114.refs_1_ = f32[24,80,128]{2,1,0:T(8,128)S(1)} custom-call(bf16[50,320,128]{2,1,0:T(8,128)(2,1)S(1)} %get-tuple-element.60.cot_s, bf16[240,960]{1,0:T(8,128)(2,1)S(1)} %select_n.96.weight_ref), custom_call_target="tpu_custom_call" | custom-call | flops 4000000000 | bytes 4194304 | tf_op jit(solution)/shard_map/pallas_call | solution.py:251
  77.1 4.5 %shard_map.115 = (bf16[80,8,128]{2,1,0:T(8,128)(2,1)}, f32[80,8,128]{2,1,0:T(8,128)S(1)}, bf16[80,8,128]{2,1,0:T(8,128)(2,1)S(1)}, bf16[80,8,128]{2,1,0:T(8,128)...) custom-call(bf16[80,8,128]{2,1,0:T(8,128)(2,1)S(1)} %constant_dynami, ...), custom_call_target="tpu_custom_call" | custom-call | flops 4000000000 | bytes 4194304 | tf_op jit(solution)/shard_map/pallas_call | solution.py:264
  81.5 1.3 %collective-permute-start.23 = (f32[3,32,96]{2,1,0:T(8,128)S(1)}, f32[3,32,96]{2,1,0:T(8,128)S(1)}, u32[]{:S(2)}, u32[]{:S(2)}) collective-permute-start(f32[3,32,96]{2,1,0:T(8,128)S(1)} %add.66), channel_id=1, source_target_pairs={{0,2},{1,3},{2,0},{3,1},{4,6},{5,7},{6,4},{7,5},{8,10},{9,11},{10,... | collective-permute-start | bytes 110600 | tf_op jit(solution)/shard_map/ppermute | solution.py:281
  83.1 1.4 %collective-permute-start.22 = (f32[3,32,96]{2,1,0:T(8,128)S(1)}, f32[3,32,96]{2,1,0:T(8,128)S(1)}, u32[]{:S(2)}, u32[]{:S(2)}) collective-permute-start(f32[3,32,96]{2,1,0:T(8,128)S(1)} %add.66), channel_id=1, source_target_pairs={{0,1},{1,0},{2,3},{3,2},{4,5},{5,4},{6,7},{7,6},{8,9},{9,8},{10,11... | collective-permute-start | bytes 110600 | tf_op jit(solution)/shard_map/ppermute | solution.py:281
  84.5 1.5 %collective-permute-start.24 = (f32[3,32,96]{2,1,0:T(8,128)S(1)}, f32[3,32,96]{2,1,0:T(8,128)S(1)}, u32[]{:S(2)}, u32[]{:S(2)}) collective-permute-start(f32[3,32,96]{2,1,0:T(8,128)S(1)} %collective-permute-done.23), channel_id=1, source_target_pairs={{0,1},{1,0},{2,3},{3,2},{4,5},{5,4},{6,7},{7,6},{8,9},{9,8},{10,11... | collective-permute-start | bytes 110600 | tf_op jit(solution)/shard_map/ppermute | solution.py:281
  86.0 3.1 %collective-permute-start.17 = (bf16[80,8,128]{2,1,0:T(8,128)(2,1)S(1)}, bf16[80,8,128]{2,1,0:T(8,128)(2,1)}, u32[]{:S(2)}, u32[]{:S(2)}) collective-permute-start(bf16[80,8,128]{2,1,0:T(8,128)(2,1)S(1)} %get-tuple-element.75), channel_id=1, source_target_pairs={{0,12},{4,16},{8,20},{12,24},{16,28},{20,0},{24,4},{28,8},{1,13},{... | collective-permute-start | bytes 491528 | tf_op jit(solution)/shard_map/ppermute | solution.py:21
  90.0 1.9 %collective-permute-start.20 = (bf16[80,8,128]{2,1,0:T(8,128)(2,1)S(1)}, bf16[80,8,128]{2,1,0:T(8,128)(2,1)}, u32[]{:S(2)}, u32[]{:S(2)}) collective-permute-start(bf16[80,8,128]{2,1,0:T(8,128)(2,1)S(1)} %get-tuple-element.78), channel_id=1, source_target_pairs={{0,24},{4,28},{8,0},{12,4},{16,8},{20,12},{24,16},{28,20},{1,25},{... | collective-permute-start | bytes 491528 | tf_op jit(solution)/shard_map/ppermute | solution.py:21
  95.4 11.5 %collective-permute-done.17 = bf16[80,8,128]{2,1,0:T(8,128)(2,1)} collective-permute-done((bf16[80,8,128]{2,1,0:T(8,128)(2,1)S(1)}, bf16[80,8,128]{2,1,0:T(8,128)(2,1)}, u32[]{:S(2)}, u32[]{:S(2)}) %collective-permute-start.17) | collective-permute-done | bytes 163872 | tf_op jit(solution)/shard_map/ppermute | solution.py:21
  106.9 3.5 %collective-permute-done.18 = bf16[80,8,128]{2,1,0:T(8,128)(2,1)} collective-permute-done((bf16[80,8,128]{2,1,0:T(8,128)(2,1)S(1)}, bf16[80,8,128]{2,1,0:T(8,128)(2,1)}, u32[]{:S(2)}, u32[]{:S(2)}) %collective-permute-start.18) | collective-permute-done | bytes 163872 | tf_op jit(solution)/shard_map/ppermute | solution.py:21
  110.4 1.9 %collective-permute-done.20 = bf16[80,8,128]{2,1,0:T(8,128)(2,1)} collective-permute-done((bf16[80,8,128]{2,1,0:T(8,128)(2,1)S(1)}, bf16[80,8,128]{2,1,0:T(8,128)(2,1)}, u32[]{:S(2)}, u32[]{:S(2)}) %collective-permute-start.20) | collective-permute-done | bytes 163872 | tf_op jit(solution)/shard_map/ppermute | solution.py:21
  112.3 4.6 %collective-permute-done.21 = bf16[80,8,128]{2,1,0:T(8,128)(2,1)} collective-permute-done((bf16[80,8,128]{2,1,0:T(8,128)(2,1)S(1)}, bf16[80,8,128]{2,1,0:T(8,128)(2,1)}, u32[]{:S(2)}, u32[]{:S(2)}) %collective-permute-start.21) | collective-permute-done | bytes 163872 | tf_op jit(solution)/shard_map/ppermute | solution.py:21
  116.9 2.1 %add_convert_fusion = bf16[80,8,128]{2,1,0:T(8,128)(2,1)} fusion(bf16[80,8,128]{2,1,0:T(8,128)(2,1)} %collective-permute-done.21, bf16[80,8,128]{2,1,0:T(8,128)(2,1)} %collective-permute-done.20, bf16[80,8,128]{2,1,0:T(8,128)(2,1)} %collective-permute-done.19, bf16[80,8,128]{2,1,0:T(8,128)(2,1)} %collective-permute-done.18, ...), kind=kLoop, calls=%fused_computation.7 | loop fusion | flops 1556480 | bytes 1474566 | tf_op jit(solution)/shard_map/convert_element_type | solution.py:369
  (79 shorter events, 15.9 us)
Async XLA Ops:
  0.6 44.5 %copy-start.9 = (pred[8,320]{1,0:T(8,128)(4,1)S(1)}, pred[8,320]{1,0:T(8,128)(4,1)}, u32[]{:S(2)}) copy-start(pred[8,320]{1,0:T(8,128)(4,1)} %constant.55.clone) | copy-start | bytes 7684
  0.7 44.4 %copy-start.10 = (pred[8,320]{1,0:T(8,128)(4,1)S(1)}, pred[8,320]{1,0:T(8,128)(4,1)}, u32[]{:S(2)}) copy-start(pred[8,320]{1,0:T(8,128)(4,1)} %constant.56.clone) | copy-start | bytes 7684
  0.7 44.4 %copy-start.11 = (pred[8,320]{1,0:T(8,128)(4,1)S(1)}, pred[8,320]{1,0:T(8,128)(4,1)}, u32[]{:S(2)}) copy-start(pred[8,320]{1,0:T(8,128)(4,1)} %constant.57.clone) | copy-start | bytes 7684
  2.5 14.7 %collective-permute-start.2 = (bf16[80,8,128]{2,1,0:T(8,128)(2,1)S(1)}, bf16[80,8,128]{2,1,0:T(8,128)(2,1)S(1)}, u32[]{:S(2)}, u32[]{:S(2)}) collective-permute-start(bf16[80,8,128]{2,1,0:T(8,128)(2,1)S(1)} %constant_dynamic-slice_fusion.1.refs_5_), channel_id=1, source_target_pairs={{0,4},{4,8},{8,12},{12,16},{16,20},{20,24},{24,28},{28,0},{1,5},{5... | collective-permute-start | bytes 491528 | tf_op jit(solution)/shard_map/ppermute | solution.py:21
  3.8 14.3 %collective-permute-start.3 = (bf16[80,8,128]{2,1,0:T(8,128)(2,1)S(1)}, bf16[80,8,128]{2,1,0:T(8,128)(2,1)S(1)}, u32[]{:S(2)}, u32[]{:S(2)}) collective-permute-start(bf16[80,8,128]{2,1,0:T(8,128)(2,1)S(1)} %constant_dynamic-slice_fusion.1.refs_5_), channel_id=1, source_target_pairs={{0,8},{4,12},{8,16},{12,20},{16,24},{20,28},{24,0},{28,4},{1,9},{5... | collective-permute-start | bytes 491528 | tf_op jit(solution)/shard_map/ppermute | solution.py:21
  5.1 33.1 %collective-permute-start.1 = (bf16[32,12,8,128]{3,2,1,0:T(8,128)(2,1)}, bf16[32,12,8,128]{3,2,1,0:T(8,128)(2,1)S(1)}, u32[]{:S(2)}, u32[]{:S(2)}) collective-permute-start(bf16[32,12,8,128]{3,2,1,0:T(8,128)(2,1)} %refs_0_.1), channel_id=1, source_target_pairs={{0,2},{1,3},{2,0},{3,1},{4,6},{5,7},{6,4},{7,5},{8,10},{9,11},{10,... | collective-permute-start | bytes 2359304 | tf_op jit(solution)/shard_map/ppermute | solution.py:281
  6.3 6.0 %collective-permute-start.4 = (bf16[12,32,128]{2,1,0:T(8,128)(2,1)S(1)}, bf16[12,32,128]{2,1,0:T(8,128)(2,1)}, u32[]{:S(2)}, u32[]{:S(2)}) collective-permute-start(bf16[12,32,128]{2,1,0:T(8,128)(2,1)S(1)} %get-tuple-element.43), channel_id=1, source_target_pairs={{0,4},{4,8},{8,12},{12,16},{16,20},{20,24},{24,28},{28,0},{1,5},{5... | collective-permute-start | bytes 294920 | tf_op jit(solution)/shard_map/ppermute | solution.py:21
  7.6 4.7 %collective-permute-start.5 = (bf16[12,32,128]{2,1,0:T(8,128)(2,1)S(1)}, bf16[12,32,128]{2,1,0:T(8,128)(2,1)}, u32[]{:S(2)}, u32[]{:S(2)}) collective-permute-start(bf16[12,32,128]{2,1,0:T(8,128)(2,1)S(1)} %get-tuple-element.44), channel_id=1, source_target_pairs={{0,28},{4,0},{8,4},{12,8},{16,12},{20,16},{24,20},{28,24},{1,29},{... | collective-permute-start | bytes 294920 | tf_op jit(solution)/shard_map/ppermute | solution.py:21
  8.8 41.6 %copy-start.1 = (bf16[32,12,8,128]{3,2,1,0:T(8,128)(2,1)S(1)}, bf16[32,12,8,128]{3,2,1,0:T(8,128)(2,1)}, u32[]{:S(2)}) copy-start(bf16[32,12,8,128]{3,2,1,0:T(8,128)(2,1)} %refs_0_.1) | copy-start | bytes 2359300
  12.3 21.2 %collective-permute-start.6 = (bf16[80,8,128]{2,1,0:T(8,128)(2,1)S(1)}, bf16[80,8,128]{2,1,0:T(8,128)(2,1)S(1)}, u32[]{:S(2)}, u32[]{:S(2)}) collective-permute-start(bf16[80,8,128]{2,1,0:T(8,128)(2,1)S(1)} %constant_dynamic-slice_fusion.1.refs_5_), channel_id=1, source_target_pairs={{0,12},{4,16},{8,20},{12,24},{16,28},{20,0},{24,4},{28,8},{1,13},{... | collective-permute-start | bytes 491528 | tf_op jit(solution)/shard_map/ppermute | solution.py:21
  16.2 20.7 %collective-permute-start.7 = (bf16[80,8,128]{2,1,0:T(8,128)(2,1)S(1)}, bf16[80,8,128]{2,1,0:T(8,128)(2,1)S(1)}, u32[]{:S(2)}, u32[]{:S(2)}) collective-permute-start(bf16[80,8,128]{2,1,0:T(8,128)(2,1)S(1)} %constant_dynamic-slice_fusion.1.refs_5_), channel_id=1, source_target_pairs={{0,16},{4,20},{8,24},{12,28},{16,0},{20,4},{24,8},{28,12},{1,17},{... | collective-permute-start | bytes 491528 | tf_op jit(solution)/shard_map/ppermute | solution.py:21
  17.2 21.0 %collective-permute-start.8 = (bf16[80,8,128]{2,1,0:T(8,128)(2,1)S(1)}, bf16[80,8,128]{2,1,0:T(8,128)(2,1)S(1)}, u32[]{:S(2)}, u32[]{:S(2)}) collective-permute-start(bf16[80,8,128]{2,1,0:T(8,128)(2,1)S(1)} %constant_dynamic-slice_fusion.1.refs_5_), channel_id=1, source_target_pairs={{0,20},{4,24},{8,28},{12,0},{16,4},{20,8},{24,12},{28,16},{1,21},{... | collective-permute-start | bytes 491528 | tf_op jit(solution)/shard_map/ppermute | solution.py:21
  18.1 20.1 %collective-permute-start.9 = (bf16[80,8,128]{2,1,0:T(8,128)(2,1)S(1)}, bf16[80,8,128]{2,1,0:T(8,128)(2,1)S(1)}, u32[]{:S(2)}, u32[]{:S(2)}) collective-permute-start(bf16[80,8,128]{2,1,0:T(8,128)(2,1)S(1)} %constant_dynamic-slice_fusion.1.refs_5_), channel_id=1, source_target_pairs={{0,24},{4,28},{8,0},{12,4},{16,8},{20,12},{24,16},{28,20},{1,25},{... | collective-permute-start | bytes 491528 | tf_op jit(solution)/shard_map/ppermute | solution.py:21
  20.9 21.3 %copy-start.7 = (bf16[1,12,64,128]{3,2,1,0:T(8,128)(2,1)}, bf16[1,12,64,128]{3,2,1,0:T(8,128)(2,1)S(1)}, u32[]{:S(2)}) copy-start(bf16[1,12,64,128]{3,2,1,0:T(8,128)(2,1)S(1)} %maximum_bitcast_fusion) | copy-start | bytes 589828
  33.5 17.0 %collective-permute-start = (bf16[32,12,8,128]{3,2,1,0:T(8,128)(2,1)}, bf16[32,12,8,128]{3,2,1,0:T(8,128)(2,1)}, u32[]{:S(2)}, u32[]{:S(2)}) collective-permute-start(bf16[32,12,8,128]{3,2,1,0:T(8,128)(2,1)} %refs_0_.1), channel_id=1, source_target_pairs={{0,1},{1,0},{2,3},{3,2},{4,5},{5,4},{6,7},{7,6},{8,9},{9,8},{10,11... | collective-permute-start | bytes 2359304 | tf_op jit(solution)/shard_map/ppermute | solution.py:281
  37.0 5.3 %collective-permute-start.11 = (bf16[1,12,64,128]{3,2,1,0:T(8,128)(2,1)S(1)}, bf16[1,12,64,128]{3,2,1,0:T(8,128)(2,1)S(1)}, u32[]{:S(2)}, u32[]{:S(2)}) collective-permute-start(bf16[1,12,64,128]{3,2,1,0:T(8,128)(2,1)S(1)} %maximum_bitcast_fusion), channel_id=1, source_target_pairs={{0,2},{1,3},{2,0},{3,1},{4,6},{5,7},{6,4},{7,5},{8,10},{9,11},{10,... | collective-permute-start | bytes 589832 | tf_op jit(solution)/shard_map/ppermute | solution.py:281
  38.2 6.9 %copy-start.2 = (bf16[80,8,128]{2,1,0:T(8,128)(2,1)}, bf16[80,8,128]{2,1,0:T(8,128)(2,1)S(1)}, u32[]{:S(2)}) copy-start(bf16[80,8,128]{2,1,0:T(8,128)(2,1)S(1)} %collective-permute-done.8.refs_10_) | copy-start | bytes 491524
  38.2 6.9 %copy-start.4 = (bf16[80,8,128]{2,1,0:T(8,128)(2,1)}, bf16[80,8,128]{2,1,0:T(8,128)(2,1)S(1)}, u32[]{:S(2)}) copy-start(bf16[80,8,128]{2,1,0:T(8,128)(2,1)S(1)} %collective-permute-done.9.refs_11_) | copy-start | bytes 491524
  38.2 12.2 %collective-permute-start.10 = (bf16[32,12,8,128]{3,2,1,0:T(8,128)(2,1)S(1)}, bf16[32,12,8,128]{3,2,1,0:T(8,128)(2,1)}, u32[]{:S(2)}, u32[]{:S(2)}) collective-permute-start(bf16[32,12,8,128]{3,2,1,0:T(8,128)(2,1)S(1)} %collective-permute-done.1.refs_2_), channel_id=1, source_target_pairs={{0,1},{1,0},{2,3},{3,2},{4,5},{5,4},{6,7},{7,6},{8,9},{9,8},{10,11... | collective-permute-start | bytes 2359304 | tf_op jit(solution)/shard_map/ppermute | solution.py:281
  43.1 6.1 %collective-permute-start.12 = (bf16[2,12,64,128]{3,2,1,0:T(8,128)(2,1)}, bf16[2,12,64,128]{3,2,1,0:T(8,128)(2,1)}, u32[]{:S(2)}, u32[]{:S(2)}) collective-permute-start(bf16[2,12,64,128]{3,2,1,0:T(8,128)(2,1)} %pad_maximum_fusion.1), channel_id=1, source_target_pairs={{0,1},{1,0},{2,3},{3,2},{4,5},{5,4},{6,7},{7,6},{8,9},{9,8},{10,11... | collective-permute-start | bytes 1179656 | tf_op jit(solution)/shard_map/ppermute | solution.py:281
  64.8 7.6 %collective-permute-start.13 = (f32[3,32,96]{2,1,0:T(8,128)S(1)}, f32[3,32,96]{2,1,0:T(8,128)S(1)}, u32[]{:S(2)}, u32[]{:S(2)}) collective-permute-start(f32[3,32,96]{2,1,0:T(8,128)S(1)} %get-tuple-element.58), channel_id=1, source_target_pairs={{0,16},{4,20},{8,24},{12,28},{16,0},{20,4},{24,8},{28,12},{1,17},{... | collective-permute-start | bytes 110600 | tf_op jit(solution)/shard_map/ppermute | solution.py:281
  72.4 4.5 %collective-permute-start.14 = (f32[3,32,96]{2,1,0:T(8,128)S(1)}, f32[3,32,96]{2,1,0:T(8,128)S(1)}, u32[]{:S(2)}, u32[]{:S(2)}) collective-permute-start(f32[3,32,96]{2,1,0:T(8,128)S(1)} %add.64), channel_id=1, source_target_pairs={{0,8},{4,12},{8,0},{12,4},{16,24},{20,28},{24,16},{28,20},{1,9},{5... | collective-permute-start | bytes 110600 | tf_op jit(solution)/shard_map/ppermute | solution.py:281
  77.0 4.5 %collective-permute-start.15 = (f32[3,32,96]{2,1,0:T(8,128)S(1)}, f32[3,32,96]{2,1,0:T(8,128)S(1)}, u32[]{:S(2)}, u32[]{:S(2)}) collective-permute-start(f32[3,32,96]{2,1,0:T(8,128)S(1)} %add.65), channel_id=1, source_target_pairs={{0,4},{4,0},{8,12},{12,8},{16,20},{20,16},{24,28},{28,24},{1,5},{5... | collective-permute-start | bytes 110600 | tf_op jit(solution)/shard_map/ppermute | solution.py:281
  81.5 3.0 %collective-permute-start.23 = (f32[3,32,96]{2,1,0:T(8,128)S(1)}, f32[3,32,96]{2,1,0:T(8,128)S(1)}, u32[]{:S(2)}, u32[]{:S(2)}) collective-permute-start(f32[3,32,96]{2,1,0:T(8,128)S(1)} %add.66), channel_id=1, source_target_pairs={{0,2},{1,3},{2,0},{3,1},{4,6},{5,7},{6,4},{7,5},{8,10},{9,11},{10,... | collective-permute-start | bytes 110600 | tf_op jit(solution)/shard_map/ppermute | solution.py:281
  82.8 9.1 %collective-permute-start.16 = (bf16[80,8,128]{2,1,0:T(8,128)(2,1)S(1)}, bf16[80,8,128]{2,1,0:T(8,128)(2,1)S(1)}, u32[]{:S(2)}, u32[]{:S(2)}) collective-permute-start(bf16[80,8,128]{2,1,0:T(8,128)(2,1)S(1)} %get-tuple-element.74), channel_id=1, source_target_pairs={{0,8},{4,12},{8,16},{12,20},{16,24},{20,28},{24,0},{28,4},{1,9},{5... | collective-permute-start | bytes 491528 | tf_op jit(solution)/shard_map/ppermute | solution.py:21
  83.1 6.7 %collective-permute-start.22 = (f32[3,32,96]{2,1,0:T(8,128)S(1)}, f32[3,32,96]{2,1,0:T(8,128)S(1)}, u32[]{:S(2)}, u32[]{:S(2)}) collective-permute-start(f32[3,32,96]{2,1,0:T(8,128)S(1)} %add.66), channel_id=1, source_target_pairs={{0,1},{1,0},{2,3},{3,2},{4,5},{5,4},{6,7},{7,6},{8,9},{9,8},{10,11... | collective-permute-start | bytes 110600 | tf_op jit(solution)/shard_map/ppermute | solution.py:281
  84.5 5.4 %collective-permute-start.24 = (f32[3,32,96]{2,1,0:T(8,128)S(1)}, f32[3,32,96]{2,1,0:T(8,128)S(1)}, u32[]{:S(2)}, u32[]{:S(2)}) collective-permute-start(f32[3,32,96]{2,1,0:T(8,128)S(1)} %collective-permute-done.23), channel_id=1, source_target_pairs={{0,1},{1,0},{2,3},{3,2},{4,5},{5,4},{6,7},{7,6},{8,9},{9,8},{10,11... | collective-permute-start | bytes 110600 | tf_op jit(solution)/shard_map/ppermute | solution.py:281
  86.0 20.9 %collective-permute-start.17 = (bf16[80,8,128]{2,1,0:T(8,128)(2,1)S(1)}, bf16[80,8,128]{2,1,0:T(8,128)(2,1)}, u32[]{:S(2)}, u32[]{:S(2)}) collective-permute-start(bf16[80,8,128]{2,1,0:T(8,128)(2,1)S(1)} %get-tuple-element.75), channel_id=1, source_target_pairs={{0,12},{4,16},{8,20},{12,24},{16,28},{20,0},{24,4},{28,8},{1,13},{... | collective-permute-start | bytes 491528 | tf_op jit(solution)/shard_map/ppermute | solution.py:21
  89.1 21.3 %collective-permute-start.18 = (bf16[80,8,128]{2,1,0:T(8,128)(2,1)S(1)}, bf16[80,8,128]{2,1,0:T(8,128)(2,1)}, u32[]{:S(2)}, u32[]{:S(2)}) collective-permute-start(bf16[80,8,128]{2,1,0:T(8,128)(2,1)S(1)} %get-tuple-element.76), channel_id=1, source_target_pairs={{0,16},{4,20},{8,24},{12,28},{16,0},{20,4},{24,8},{28,12},{1,17},{... | collective-permute-start | bytes 491528 | tf_op jit(solution)/shard_map/ppermute | solution.py:21
  89.8 20.6 %collective-permute-start.19 = (bf16[80,8,128]{2,1,0:T(8,128)(2,1)S(1)}, bf16[80,8,128]{2,1,0:T(8,128)(2,1)}, u32[]{:S(2)}, u32[]{:S(2)}) collective-permute-start(bf16[80,8,128]{2,1,0:T(8,128)(2,1)S(1)} %get-tuple-element.77), channel_id=1, source_target_pairs={{0,20},{4,24},{8,28},{12,0},{16,4},{20,8},{24,12},{28,16},{1,21},{... | collective-permute-start | bytes 491528 | tf_op jit(solution)/shard_map/ppermute | solution.py:21
  90.0 22.3 %collective-permute-start.20 = (bf16[80,8,128]{2,1,0:T(8,128)(2,1)S(1)}, bf16[80,8,128]{2,1,0:T(8,128)(2,1)}, u32[]{:S(2)}, u32[]{:S(2)}) collective-permute-start(bf16[80,8,128]{2,1,0:T(8,128)(2,1)S(1)} %get-tuple-element.78), channel_id=1, source_target_pairs={{0,24},{4,28},{8,0},{12,4},{16,8},{20,12},{24,16},{28,20},{1,25},{... | collective-permute-start | bytes 491528 | tf_op jit(solution)/shard_map/ppermute | solution.py:21
  91.9 25.0 %collective-permute-start.21 = (bf16[80,8,128]{2,1,0:T(8,128)(2,1)S(1)}, bf16[80,8,128]{2,1,0:T(8,128)(2,1)}, u32[]{:S(2)}, u32[]{:S(2)}) collective-permute-start(bf16[80,8,128]{2,1,0:T(8,128)(2,1)S(1)} %get-tuple-element.79), channel_id=1, source_target_pairs={{0,28},{4,0},{8,4},{12,8},{16,12},{20,16},{24,20},{28,24},{1,29},{... | collective-permute-start | bytes 491528 | tf_op jit(solution)/shard_map/ppermute | solution.py:21
  (5 other events, 5.2 us)

commit v6 on v5

v6 whole, which is shorter than its diff:
```python
import functools
import math

import jax
import jax.numpy as jnp
import numpy as np
from jax import lax
from jax.experimental import pallas as pl
from jax.experimental.pallas import tpu as pltpu
from jax.sharding import PartitionSpec as P

C = 320
G = 40
D = 48
GROUP = C // G
HIGHEST = lax.Precision.HIGHEST


def shifted(value, axis, steps):
    count = lax.axis_size(axis)
    return lax.ppermute(value, axis, [(source, (source + steps) % count) for source in range(count)])


def conv_rows(outs, width):
    main = np.tile(np.arange(width), outs)
    return np.concatenate([main, np.full(outs, -1), np.full(outs, width)])


def toeplitz(kernel_local, width):
    outs, groups = kernel_local.shape[3:]
    row_col = conv_rows(outs, width)
    row_out = np.concatenate([np.repeat(np.arange(outs), width), np.tile(np.arange(outs), 2)])
    spread = np.zeros((outs, row_col.size), np.float32)
    spread[row_out, np.arange(row_col.size)] = 1
    taps = jnp.transpose(kernel_local[::-1], (1, 2, 4, 0, 3))
    wide = jnp.einsum(
        "qrgpo,ok->qrgpk", taps, jnp.asarray(spread, jnp.bfloat16),
        preferred_element_type=jnp.float32,
    ).astype(jnp.bfloat16)
    out_col = np.arange(width)
    column_tap = out_col[:, None] - row_col[None, :] + 1
    total = jnp.zeros((3, groups, width, 3, row_col.size), jnp.bfloat16)
    for tap in range(3):
        mask = jnp.asarray(column_tap == tap)[None, None, :, None, :]
        total = jnp.where(mask, wide[tap][:, :, None], total)
    return total.reshape(3 * groups * width, 3 * row_col.size)


def roll_zero(value, steps):
    size = value.shape[-1]
    lane = lax.broadcasted_iota(jnp.int32, value.shape, value.ndim - 1)
    moved = pltpu.roll(value, steps % size, value.ndim - 1)
    return jnp.where(lane == (0 if steps > 0 else size - 1), 0.0, moved)


def add_grads(first_level, count, cot_s, weight_ref, left_s, right_s, left_sum, grad_s):
    channels, width, rows = left_s.shape
    groups = channels // GROUP
    size = groups * width
    span = cot_s.shape[1]
    reach = right_s.shape[1] - width
    shift = right_s.shape[1] - grad_s.shape[1]
    f32, bf16 = jnp.float32, jnp.bfloat16

    def pair_values(at):
        near = cot_s[pl.ds(at, 3)].reshape(3 * span, rows)
        far = cot_s[pl.ds(at + 1, 3)].reshape(3 * span, rows)
        result = jnp.dot(
            weight_ref[...], jnp.concatenate([near, far], axis=1), preferred_element_type=f32
        )
        values = []
        for half in range(2):
            part = result[:, half * rows : (half + 1) * rows]
            total = (
                part[size : 2 * size]
                + roll_zero(part[:size], -1)
                + roll_zero(part[2 * size :], 1)
            )
            values.append(total.astype(bf16).astype(f32))
        return values

    def step(number, carry):
        level = first_level + number * width
        base = pl.multiple_of(reach - first_level - width - number * width, width)
        rights = right_s.at[:, pl.ds(base, 2 * width)]
        grads = grad_s.at[:, pl.ds(pl.multiple_of(base - shift, width), 2 * width)]

        def use(pair, values):
            at = width - 2 * pair
            for group in range(groups):
                ones = [value[group * width : (group + 1) * width] for value in values]
                for c in range(group * GROUP, (group + 1) * GROUP):
                    left = left_s[c]
                    left_sum[c] += (
                        ones[0] * rights[c, at : at + width]
                        + ones[1] * rights[c, at - 1 : at - 1 + width]
                    )
                    grads[c, at : at + width] += ones[0] * left
                    grads[c, at - 1 : at - 1 + width] += ones[1] * left

        waiting = pair_values(level)
        for pair in range(1, width // 2):
            later = pair_values(level + 2 * pair)
            use(pair - 1, waiting)
            waiting = later
        use(width // 2 - 1, waiting)
        return carry

    lax.fori_loop(0, count // width, step, 0)


def upper_grads(parts, hops, far, halo_order, places, *refs):
    cot_refs, halo_refs, refs = refs[:parts], refs[parts : parts + 2], refs[parts + 2 :]
    right_refs, refs = refs[: hops + 1], refs[hops + 1 :]
    left_ref, weight_ref, cot_s, right_s, left_sum, grad_out = refs[:6]
    sent_refs, refs = refs[6 : 6 + far], refs[6 + far :]
    cot_b, halo_b, right_b, left_s, grad_s, sems = refs
    channels, width, rows = left_ref.shape
    outs, levels = cot_refs[0].shape[:2]
    main = outs * width
    span = main + 2 * outs
    reach = hops * width
    f32, bf16 = jnp.float32, jnp.bfloat16

    copies = []
    for buffer, sources in ((right_b, right_refs), (cot_b, cot_refs)):
        for at, source in enumerate(sources):
            copies.append(
                pltpu.make_async_copy(source, buffer.at[at], sems.at[len(copies)])
            )
    half = halo_b.shape[0] // 2
    for at, source in enumerate(halo_refs):
        copies.append(
            pltpu.make_async_copy(source, halo_b.at[pl.ds(at * half, half)], sems.at[len(copies)])
        )
    for copy in copies:
        copy.start()

    left_s[...] = left_ref[...].astype(f32)
    left_sum[...] = jnp.zeros(left_sum.shape, f32)
    grad_s[...] = jnp.zeros(grad_s.shape, f32)
    cot_s[0] = jnp.zeros((span, rows), bf16)
    cot_s[D + 1] = jnp.zeros((span, rows), bf16)
    for hop in range(hops + 1):
        copies[hop].wait()
        at = reach - hop * width
        block = right_b[hop].astype(f32)
        right_s[:, at : at + width] = jnp.where(places[1] >= hop, block, 0.0)
    for copy in copies[hops + 1 :]:
        copy.wait()
    for other in range(parts):
        start = (places[0] ^ other) * levels + 1

        def assemble(level, carry, other=other, start=start):
            cot_s[start + level, 0:main] = cot_b[other, :, level].reshape(main, rows)
            cot_s[start + level, main:span] = halo_b[halo_order.index(other), level]
            return carry

        lax.fori_loop(0, levels, assemble, 0)

    add_grads(D // 2, D // 2, cot_s, weight_ref, left_s, right_s, left_sum, grad_s)
    grad_out[...] = grad_s[:, far * width :]
    for hop in range(hops, hops - far, -1):
        at = reach - hop * width
        sent_refs[hops - hop][...] = (grad_s[:, at : at + width] * (1.0 / GROUP)).astype(bf16)


def lower_grads(
    near, left_ref, weight_ref, cot_s, right_s, left_part, grad_part, grad_left_ref, own_ref, *rest
):
    sent_refs, (left_s, left_sum, grad_s) = rest[:near], rest[near:]
    channels, width, rows = left_ref.shape
    f32, bf16 = jnp.float32, jnp.bfloat16
    left_s[...] = left_ref[...].astype(f32)
    left_sum[...] = left_part[...]
    grad_s[...] = grad_part[...]
    add_grads(0, D // 2, cot_s, weight_ref, left_s, right_s, left_sum, grad_s)
    grad_left_ref[...] = (left_sum[...] * (1.0 / GROUP)).astype(bf16)
    own_ref[...] = grad_s[:, near * width :] * (1.0 / GROUP)
    for hop in range(near, 0, -1):
        at = (near - hop) * width
        sent_refs[near - hop][...] = (grad_s[:, at : at + width] * (1.0 / GROUP)).astype(bf16)


def kernel_sums(left_ref, cot_s, right_s, fold_ref, sums_ref, vol_s, prod_s):
    channels, width, rows = left_ref.shape
    groups = channels // GROUP
    span = cot_s.shape[1]
    outs = span // (width + 2)
    main = outs * width
    size = groups * width
    reach = right_s.shape[1] - width
    f32, bf16 = jnp.float32, jnp.bfloat16

    def volume_step(group, carry):
        first = group * GROUP
        lefts = [left_ref[first + k].astype(f32) for k in range(GROUP)]
        rows_at = pl.ds(pl.multiple_of(group * width, width), width)
        for d in range(D):
            total = lefts[0] * right_s[first, reach - d : reach - d + width]
            for k in range(1, GROUP):
                total = total + lefts[k] * right_s[first + k, reach - d : reach - d + width]
            value = (total * (1.0 / GROUP)).astype(bf16).astype(f32)
            vol_s[d, 0, rows_at] = roll_zero(value, 1)
            vol_s[d, 1, rows_at] = value
            vol_s[d, 2, rows_at] = roll_zero(value, -1)
        return carry

    lax.fori_loop(0, groups, volume_step, 0)

    chunk = 4
    prod_s[...] = jnp.zeros(prod_s.shape, f32)

    def kernel_step(step, carry):
        first = step * chunk
        volume = jnp.concatenate(
            [vol_s[first + k].reshape(3 * size, rows).astype(bf16) for k in range(chunk)], axis=1
        )
        for tap in range(3):
            value = jnp.concatenate([cot_s[first + k + tap] for k in range(chunk)], axis=1)
            prod_s[tap] += lax.dot_general(
                value, volume, (((1,), (1,)), ((), ())), preferred_element_type=f32
            )
        return carry

    lax.fori_loop(0, D // chunk, kernel_step, 0)

    col_in = lax.broadcasted_iota(jnp.int32, (width, 3 * size), 0)
    col_out = lax.broadcasted_iota(jnp.int32, (width, 3 * size), 1) % width
    edge = lax.broadcasted_iota(jnp.int32, (outs, 3 * size), 1) % width
    for column_tap in range(3):
        mask = col_out - col_in + 1 == column_tap
        taps = []
        for tap in range(3):
            value = prod_s[tap, 0:main].reshape(outs, width, 3 * size)
            total = jnp.sum(jnp.where(mask[None], value, 0.0), axis=1)
            if column_tap == 2:
                total = total + jnp.where(edge == 0, prod_s[tap, main : main + outs], 0.0)
            if column_tap == 0:
                total = total + jnp.where(edge == width - 1, prod_s[tap, main + outs : span], 0.0)
            taps.append(total)
        gathered = jnp.concatenate(taps, axis=0)
        sums_ref[column_tap] = lax.dot_general(
            fold_ref[...], gathered, (((1,), (1,)), ((), ())),
            precision=HIGHEST, preferred_element_type=f32,
        )


VMEM = pl.BlockSpec(memory_space=pltpu.VMEM)
SMEM = pl.BlockSpec(memory_space=pltpu.SMEM)
HBM = pl.BlockSpec(memory_space=pltpu.HBM)
MIB = 1024 * 1024


def run(function, operands, outs, scratch, limit, flops):
    return pl.pallas_call(
        function,
        out_shape=[jax.ShapeDtypeStruct(shape, kind) for shape, kind in outs],
        in_specs=[space for space, array in operands],
        out_specs=[VMEM] * len(outs),
        scratch_shapes=scratch,
        compiler_params=pltpu.CompilerParams(vmem_limit_bytes=limit * MIB),
        cost_estimate=pl.CostEstimate(flops=1024, bytes_accessed=1024, transcendentals=0),
    )(*[array for space, array in operands])


def swapped(value, axis, bit):
    count = lax.axis_size(axis)
    return lax.ppermute(value, axis, [(source, source ^ bit) for source in range(count)])


def gather_swapping(value, axis, others=()):
    held = {0: value}
    bit = lax.axis_size(axis) // 2
    while bit:
        step = {key | bit: swapped(item, axis, bit) for key, item in held.items()}
        if others and bit == lax.axis_size(axis) // 2:
            (step[bit], *others) = lax.optimization_barrier((step[bit], *others))
        held.update(step)
        bit //= 2
    return [held[key] for key in range(len(held))], others


def gather_joining(held, axis):
    bit = lax.axis_size(axis) // 2
    order = [0, bit]
    bit //= 2
    while bit:
        joined = jnp.concatenate(held, axis=0)
        held = [joined, swapped(joined, axis, bit)]
        order = order + [key | bit for key in order]
        bit //= 2
    return held, order


def total_swapping(value, bit):
    return value + swapped(value, "col", bit)


def body(left, right, kernel, cotangent):
    outs, levels, width, rows = cotangent.shape
    parts = lax.axis_size("disp")
    columns = lax.axis_size("col")
    channels = C // parts
    groups = G // parts
    size = groups * width
    span = outs * (width + 2)
    hops = (D + width - 2) // width
    far = D // 2 // width
    first = (hops // 2, hops // 2 + 1)
    near = hops - far
    part, column = lax.axis_index("disp"), lax.axis_index("col")
    places = jnp.stack([part, column]).astype(jnp.int32)
    f32, bf16 = jnp.float32, jnp.bfloat16

    low = jnp.transpose(cotangent[:, :, width - 1], (1, 0, 2))
    high = jnp.transpose(cotangent[:, :, 0], (1, 0, 2))
    low, high, right = lax.optimization_barrier((low, high, right))
    low, high = shifted(low, "col", 1), shifted(high, "col", -1)
    right_own = lax.dynamic_slice_in_dim(right, part * channels, channels, 0)
    left_own = lax.dynamic_slice_in_dim(left, part * channels, channels, 0)
    weights = toeplitz(lax.dynamic_slice_in_dim(kernel, part * groups, groups, 4), width)
    right_late, low, high, left_own, weights = lax.optimization_barrier(
        (right_own, low, high, left_own, weights)
    )
    low = jnp.where(column > 0, low, 0).astype(bf16)
    high = jnp.where(column < columns - 1, high, 0).astype(bf16)
    halo = jnp.concatenate([low, high], axis=1)[None]
    halo_across = swapped(halo, "disp", parts // 2)
    rights = [right_own] + [
        shifted(right_own if hop in first else right_late, "col", hop)
        for hop in range(1, hops + 1)
    ]
    cots, (halo_across, *rights[2:hops]) = gather_swapping(
        cotangent, "disp", [halo_across, *rights[2:hops]]
    )
    halos, halo_order = gather_joining([halo, halo_across], "disp")

    pad_rows = -(-3 * groups // 8) * 8
    fold = np.zeros((pad_rows, 3 * size), np.float32)
    fold[np.arange(3 * size) // width, np.arange(3 * size)] = 1

    block = (channels, width, rows)
    wide = (channels, (hops + 1) * width, rows)
    moved = [*cots, *halos, *rights]
    results = run(
        functools.partial(upper_grads, parts, hops, far, halo_order),
        [(SMEM, places)] + [(HBM, item) for item in moved] + [(VMEM, left_own), (VMEM, weights)],
        [
            ((D + 2, span, rows), bf16),
            (wide, f32),
            (block, f32),
            ((channels, (near + 1) * width, rows), f32),
            *[(block, bf16)] * far,
        ],
        [
            pltpu.VMEM((parts, *cotangent.shape), bf16),
            pltpu.VMEM((parts, levels, 2 * outs, rows), bf16),
            pltpu.VMEM((hops + 1, *block), bf16),
            pltpu.VMEM(block, f32),
            pltpu.VMEM(wide, f32),
            pltpu.SemaphoreType.DMA((len(moved),)),
        ],
        20, 8000000000,
    )
    cot_wide, right_wide, left_part, grad_part = results[:4]
    sent = dict(zip(range(hops, hops - far, -1), results[4:]))
    arrived = {hop: shifted(value, "col", -hop) for hop, value in sent.items()}

    (total,) = run(
        kernel_sums,
        [(VMEM, item) for item in (left_own, cot_wide, right_wide, jnp.asarray(fold))],
        [((3, pad_rows, 3 * outs), f32)],
        [pltpu.VMEM((D, 3, size, rows), f32), pltpu.VMEM((3, span, 3 * size), f32)],
        16, 8000000000,
    )
    grad_part, total = lax.optimization_barrier((grad_part, total))
    bits = [1 << k for k in reversed(range(columns.bit_length() - 1))]
    total = total_swapping(total, bits[0])
    results = run(
        functools.partial(lower_grads, near),
        [
            (VMEM, item)
            for item in (left_own, weights, cot_wide, right_wide, left_part, grad_part)
        ],
        [(block, bf16), (block, f32), *[(block, bf16)] * near],
        [
            pltpu.VMEM(block, f32),
            pltpu.VMEM(block, f32),
            pltpu.VMEM((channels, (near + 1) * width, rows), f32),
        ],
        16, 8000000000,
    )
    distant = sorted(arrived)
    *results, total = lax.optimization_barrier((*results, total, *[arrived[hop] for hop in distant]))
    results, held = results[: 2 + near], [*results[2 + near :], total]
    total, held = held[0], held[1:]
    arrived = dict(zip(distant, held))
    grad_left, own = results[:2]
    sent = dict(zip(range(near, 0, -1), results[2:]))
    arrived.update({hop: shifted(value, "col", -hop) for hop, value in sent.items()})
    for bit in bits[1:]:
        total = total_swapping(total, bit)

    total_right = own
    for hop in range(1, hops + 1):
        total_right = total_right + jnp.where(
            column + hop < columns, arrived[hop].astype(f32), 0.0
        )

    pieces = jnp.stack(gather_swapping(total, "disp")[0])
    pieces = pieces[jnp.arange(parts) ^ part][:, :, : 3 * groups]
    total = pieces.reshape(parts, 3, 3, groups, 3, outs)
    cell_count = D * width * columns * rows
    grad_kernel = jnp.transpose(total, (4, 1, 2, 5, 0, 3))[::-1].reshape(3, 3, 3, outs, G)
    grad_kernel = grad_kernel * (1.0 / math.sqrt(cell_count))
    return (grad_left, total_right.astype(bf16), grad_kernel)


def solution(mesh):
    return jax.shard_map(
        body,
        mesh=mesh,
        in_specs=(P(None, "col", None), P(None, "col", None), P(), P(None, "disp", "col", None)),
        out_specs=(P("disp", "col", None), P("disp", "col", None), P()),
        check_vma=False,
    )
```

time: 119 us -> 111 us (0.933)
  the two profiles are of different devices: /device:TPU:13 before, /device:TPU:29 now
where the time goes in v6:
time: 111 us
  waiting for transfers between devices  41.1 us (37%)
  starting transfers between devices  35.3 us (32%)
  Pallas kernels  21.5 us (19%)
  local copies, waits for them, and re-layouts  7.88 us (7%)
  other arithmetic  3.71 us (3%)
    ppermute x14, waiting for transfers between devices, shifted(): lax.ppermute(value, axis, [(source, (source + steps) % count) for source...  29.3 us
    ppermute x11, starting transfers between devices, swapped(): lax.ppermute(value, axis, [(source, source ^ bit) for source in range(cou...  22.3 us
    pallas_call x3, Pallas kernels, run(): pl.pallas_call(function, out_shape=[jax.ShapeDtypeStruct(shape, kind) for...  21.5 us
    ppermute x14, starting transfers between devices, shifted(): lax.ppermute(value, axis, [(source, (source + steps) % count) for source...  13 us
    ppermute x11, waiting for transfers between devices, swapped(): lax.ppermute(value, axis, [(source, source ^ bit) for source in range(cou...  11.8 us
  transfers between devices with their start and end apart: 25, of which 9 were waited for; matrix products, arithmetic and copies ran while one was open for 9% of the time, Pallas kernels for 12%

profile of v6, /device:TPU:29, one launch (start us, length us, event | category | flops | bytes accessed | tf_op | source)
XLA Modules:
  0.0 110.8 jit_solution(717359569418140424)
XLA Ops:
  0.7 1.3 %collective-permute-start.3 = (bf16[32,12,8,128]{3,2,1,0:T(8,128)(2,1)}, bf16[32,12,8,128]{3,2,1,0:T(8,128)(2,1)S(1)}, u32[]{:S(2)}, u32[]{:S(2)}) collective-permute-start(bf16[32,12,8,128]{3,2,1,0:T(8,128)(2,1)} %refs_0_.1), channel_id=1, source_target_pairs={{0,2},{1,3},{2,0},{3,1},{4,6},{5,7},{6,4},{7,5},{8,10},{9,11},{10,... | collective-permute-start | bytes 2359304 | tf_op jit(solution)/shard_map/ppermute | solution.py:269
  2.0 1.9 %fusion.2 = (bf16[32,12,1,128]{3,2,1,0:T(2,128)(2,1)S(1)}, bf16[32,12,1,128]{3,2,1,0:T(2,128)(2,1)S(1)}) fusion(bf16[32,12,8,128]{3,2,1,0:T(8,128)(2,1)} %refs_0_.1), kind=kLoop, calls=%fused_computation.25 | loop fusion | bytes 393216 | tf_op jit(solution)/shard_map/slice | solution.py:317
  3.9 1.5 %collective-permute-start.1 = (bf16[12,32,128]{2,1,0:T(8,128)(2,1)S(1)}, bf16[12,32,128]{2,1,0:T(8,128)(2,1)}, u32[]{:S(2)}, u32[]{:S(2)}) collective-permute-start(bf16[12,32,128]{2,1,0:T(8,128)(2,1)S(1)} %get-tuple-element.42), channel_id=1, source_target_pairs={{0,28},{4,0},{8,4},{12,8},{16,12},{20,16},{24,20},{28,24},{1,29},{... | collective-permute-start | bytes 294920 | tf_op jit(solution)/shard_map/ppermute | solution.py:21
  5.4 1.0 collective-permute-start.6
  6.4 1.1 constant_dynamic-slice_fusion
  8.0 1.4 %select_select_fusion = bf16[3,10,8,3,320]{4,3,2,1,0:T(4,128)(2,1)} fusion(pred[8,320]{1,0:T(8,128)(4,1)S(1)} %copy-done.4, pred[8,320]{1,0:T(8,128)(4,1)S(1)} %copy-done.5, pred[8,320]{1,0:T(8,128)(4,1)S(1)} %copy-done.6, bf16[3,10,3,320]{3,2,1,0:T(4,128)(2,1)S(1)} %copy.33, bf16[3,10,3,320]{3,2,1,0:T(4,128)(2,1)S(1)} %copy.32, ...), kind=kLoop, calls=%fused_computation.2 | loop fusion | flops 691200 | bytes 641280 | tf_op jit(solution)/shard_map/jit(_where)/select_n | solution.py:45
  9.4 0.9 constant_dynamic-slice_fusion.1.refs_13_.left_ref
  10.3 1.7 %select_n.92.refs_14_.weight_ref = bf16[240,960]{1,0:T(8,128)(2,1)S(1)} reshape(bf16[3,10,8,3,320]{4,3,2,1,0:T(4,128)(2,1)} %select_select_fusion) | data formatting | bytes 921600 | tf_op jit(solution)/shard_map/jit(_where)/select_n | solution.py:45
  12.4 3.2 %collective-permute-start.7 = (bf16[80,8,128]{2,1,0:T(8,128)(2,1)S(1)}, bf16[80,8,128]{2,1,0:T(8,128)(2,1)S(1)}, u32[]{:S(2)}, u32[]{:S(2)}) collective-permute-start(bf16[80,8,128]{2,1,0:T(8,128)(2,1)S(1)} %constant_dynamic-slice_fusion.2.refs_6_), channel_id=1, source_target_pairs={{0,16},{4,20},{8,24},{12,28},{16,0},{20,4},{24,8},{28,12},{1,17},{... | collective-permute-start | bytes 491528 | tf_op jit(solution)/shard_map/ppermute | solution.py:21
  15.6 1.9 %collective-permute-start.5 = (bf16[80,8,128]{2,1,0:T(8,128)(2,1)S(1)}, bf16[80,8,128]{2,1,0:T(8,128)(2,1)S(1)}, u32[]{:S(2)}, u32[]{:S(2)}) collective-permute-start(bf16[80,8,128]{2,1,0:T(8,128)(2,1)S(1)} %constant_dynamic-slice_fusion.2.refs_6_), channel_id=1, source_target_pairs={{0,8},{4,12},{8,16},{12,20},{16,24},{20,28},{24,0},{28,4},{1,9},{5... | collective-permute-start | bytes 491528 | tf_op jit(solution)/shard_map/ppermute | solution.py:21
  17.6 0.7 collective-permute-done.7.refs_10_
  18.4 9.4 %collective-permute-start.2 = (bf16[32,12,8,128]{3,2,1,0:T(8,128)(2,1)S(1)}, bf16[32,12,8,128]{3,2,1,0:T(8,128)(2,1)S(1)}, u32[]{:S(2)}, u32[]{:S(2)}) collective-permute-start(bf16[32,12,8,128]{3,2,1,0:T(8,128)(2,1)S(1)} %copy-done.1), channel_id=1, source_target_pairs={{0,1},{1,0},{2,3},{3,2},{4,5},{5,4},{6,7},{7,6},{8,9},{9,8},{10,11... | collective-permute-start | bytes 2359304 | tf_op jit(solution)/shard_map/ppermute | solution.py:269
  27.8 4.8 %collective-permute-done.8.refs_11_ = bf16[80,8,128]{2,1,0:T(8,128)(2,1)S(1)} collective-permute-done((bf16[80,8,128]{2,1,0:T(8,128)(2,1)S(1)}, bf16[80,8,128]{2,1,0:T(8,128)(2,1)S(1)}, u32[]{:S(2)}, u32[]{:S(2)}) %collective-permute-start.8) | collective-permute-done | bytes 163872 | tf_op jit(solution)/shard_map/ppermute | solution.py:21
  32.6 2.7 %collective-permute-start.9 = (bf16[32,12,8,128]{3,2,1,0:T(8,128)(2,1)S(1)}, bf16[32,12,8,128]{3,2,1,0:T(8,128)(2,1)S(1)}, u32[]{:S(2)}, u32[]{:S(2)}) collective-permute-start(bf16[32,12,8,128]{3,2,1,0:T(8,128)(2,1)S(1)} %collective-permute-done.3.refs_2_), channel_id=1, source_target_pairs={{0,1},{1,0},{2,3},{3,2},{4,5},{5,4},{6,7},{7,6},{8,9},{9,8},{10,11... | collective-permute-start | bytes 2359304 | tf_op jit(solution)/shard_map/ppermute | solution.py:269
  36.0 4.8 %collective-permute-done.11.refs_7_ = bf16[80,8,128]{2,1,0:T(8,128)(2,1)S(1)} collective-permute-done((bf16[80,8,128]{2,1,0:T(8,128)(2,1)S(1)}, bf16[80,8,128]{2,1,0:T(8,128)(2,1)S(1)}, u32[]{:S(2)}, u32[]{:S(2)}) %collective-permute-start.11) | collective-permute-done | bytes 163872 | tf_op jit(solution)/shard_map/ppermute | solution.py:21
  40.9 4.6 %collective-permute-done.12.refs_12_ = bf16[80,8,128]{2,1,0:T(8,128)(2,1)S(1)} collective-permute-done((bf16[80,8,128]{2,1,0:T(8,128)(2,1)S(1)}, bf16[80,8,128]{2,1,0:T(8,128)(2,1)S(1)}, u32[]{:S(2)}, u32[]{:S(2)}) %collective-permute-start.12) | collective-permute-done | bytes 163872 | tf_op jit(solution)/shard_map/ppermute | solution.py:21
  45.4 8.1 %shard_map.112 = (bf16[50,320,128]{2,1,0:T(8,128)(2,1)S(1)}, f32[80,56,128]{2,1,0:T(8,128)S(1)}, f32[80,8,128]{2,1,0:T(8,128)S(1)}, f32[80,32,128]{2,1,0:T(8,128...) custom-call(s32[2]{0:T(128)S(1)} %pad_add_fusion.places, ...), custom_call_target="tpu_custom_call" | custom-call | flops 1024 | bytes 1024 | tf_op jit(solution)/shard_map/pallas_call | solution.py:256
  54.1 1.6 %collective-permute-start.16 = (bf16[80,8,128]{2,1,0:T(8,128)(2,1)S(1)}, bf16[80,8,128]{2,1,0:T(8,128)(2,1)S(1)}, u32[]{:S(2)}, u32[]{:S(2)}) collective-permute-start(bf16[80,8,128]{2,1,0:T(8,128)(2,1)S(1)} %get-tuple-element.67), channel_id=1, source_target_pairs={{0,8},{4,12},{8,16},{12,20},{16,24},{20,28},{24,0},{28,4},{1,9},{5... | collective-permute-start | bytes 491528 | tf_op jit(solution)/shard_map/ppermute | solution.py:21
  55.6 8.4 %shard_map.113 = f32[3,32,96]{2,1,0:T(8,128)S(1)} custom-call(bf16[80,8,128]{2,1,0:T(8,128)(2,1)S(1)} %constant_dynamic-slice_fusion.1.refs_13_.left_ref, bf16[50,320,128]{2,1,0:T(8,128)(2,1)S(1)} %get-tuple-element.54.cot_s, f32[80,56,128]{2,1,0:T(8,128)S(1)} %get-tuple-element.55.right_s, f32[32,240]{1,0:T(8,128)S(1)} %copy-done.2), custom_call_target="tpu_custom_call" | custom-call | flops 1024 | bytes 1024 | tf_op jit(solution)/shard_map/pallas_call | solution.py:256
  64.0 1.3 %collective-permute-start.13 = (f32[3,32,96]{2,1,0:T(8,128)S(1)}, f32[3,32,96]{2,1,0:T(8,128)S(1)}, u32[]{:S(2)}, u32[]{:S(2)}) collective-permute-start(f32[3,32,96]{2,1,0:T(8,128)S(1)} %shard_map.113), channel_id=1, source_target_pairs={{0,16},{4,20},{8,24},{12,28},{16,0},{20,4},{24,8},{28,12},{1,17},{... | collective-permute-start | bytes 110600 | tf_op jit(solution)/shard_map/ppermute | solution.py:269
  65.4 5.1 %shard_map.114 = (bf16[80,8,128]{2,1,0:T(8,128)(2,1)}, f32[80,8,128]{2,1,0:T(8,128)S(1)}, bf16[80,8,128]{2,1,0:T(8,128)(2,1)S(1)}, bf16[80,8,128]{2,1,0:T(8,128)(2,1)S(1)}, bf16[80,8,128]{2,1,0:T(8,128)(2,1)S(1)}) custom-call(bf16[80,8,128]{2,1,0:T(8,128)(2,1)S(1)} %constant_dynamic-slice_fusion.1.refs_13_.left_ref, ...), custom_call_target="tpu_custom_call" | custom-call | flops 1024 | bytes 1024 | tf_op jit(solution)/shard_map/pallas_call | solution.py:256
  70.4 5.9 %collective-permute-done.13 = f32[3,32,96]{2,1,0:T(8,128)S(1)} collective-permute-done((f32[3,32,96]{2,1,0:T(8,128)S(1)}, f32[3,32,96]{2,1,0:T(8,128)S(1)}, u32[]{:S(2)}, u32[]{:S(2)}) %collective-permute-start.13) | collective-permute-done | bytes 36896 | tf_op jit(solution)/shard_map/ppermute | solution.py:269
  76.5 2.9 %collective-permute-done.20 = f32[3,32,96]{2,1,0:T(8,128)S(1)} collective-permute-done((f32[3,32,96]{2,1,0:T(8,128)S(1)}, f32[3,32,96]{2,1,0:T(8,128)S(1)}, u32[]{:S(2)}, u32[]{:S(2)}) %collective-permute-start.20) | collective-permute-done | bytes 36896 | tf_op jit(solution)/shard_map/ppermute | solution.py:269
  79.5 2.9 %collective-permute-done.21 = f32[3,32,96]{2,1,0:T(8,128)S(1)} collective-permute-done((f32[3,32,96]{2,1,0:T(8,128)S(1)}, f32[3,32,96]{2,1,0:T(8,128)S(1)}, u32[]{:S(2)}, u32[]{:S(2)}) %collective-permute-start.21) | collective-permute-done | bytes 36896 | tf_op jit(solution)/shard_map/ppermute | solution.py:269
  82.4 1.3 %collective-permute-start.23 = (f32[3,32,96]{2,1,0:T(8,128)S(1)}, f32[3,32,96]{2,1,0:T(8,128)S(1)}, u32[]{:S(2)}, u32[]{:S(2)}) collective-permute-start(f32[3,32,96]{2,1,0:T(8,128)S(1)} %add.78), channel_id=1, source_target_pairs={{0,2},{1,3},{2,0},{3,1},{4,6},{5,7},{6,4},{7,5},{8,10},{9,11},{10,... | collective-permute-start | bytes 110600 | tf_op jit(solution)/shard_map/ppermute | solution.py:269
  83.7 3.1 %collective-permute-start.22 = (f32[3,32,96]{2,1,0:T(8,128)S(1)}, f32[3,32,96]{2,1,0:T(8,128)S(1)}, u32[]{:S(2)}, u32[]{:S(2)}) collective-permute-start(f32[3,32,96]{2,1,0:T(8,128)S(1)} %add.78), channel_id=1, source_target_pairs={{0,1},{1,0},{2,3},{3,2},{4,5},{5,4},{6,7},{7,6},{8,9},{9,8},{10,11... | collective-permute-start | bytes 110600 | tf_op jit(solution)/shard_map/ppermute | solution.py:269
  86.8 2.6 %collective-permute-start.24 = (f32[3,32,96]{2,1,0:T(8,128)S(1)}, f32[3,32,96]{2,1,0:T(8,128)S(1)}, u32[]{:S(2)}, u32[]{:S(2)}) collective-permute-start(f32[3,32,96]{2,1,0:T(8,128)S(1)} %collective-permute-done.23), channel_id=1, source_target_pairs={{0,1},{1,0},{2,3},{3,2},{4,5},{5,4},{6,7},{7,6},{8,9},{9,8},{10,11... | collective-permute-start | bytes 110600 | tf_op jit(solution)/shard_map/ppermute | solution.py:269
  89.5 2.7 %collective-permute-start.19 = (bf16[80,8,128]{2,1,0:T(8,128)(2,1)S(1)}, bf16[80,8,128]{2,1,0:T(8,128)(2,1)}, u32[]{:S(2)}, u32[]{:S(2)}) collective-permute-start(bf16[80,8,128]{2,1,0:T(8,128)(2,1)S(1)} %get-tuple-element.72), channel_id=1, source_target_pairs={{0,20},{4,24},{8,28},{12,0},{16,4},{20,8},{24,12},{28,16},{1,21},{... | collective-permute-start | bytes 491528 | tf_op jit(solution)/shard_map/ppermute | solution.py:21
  93.5 1.0 copy.37
  94.5 3.5 %collective-permute-done.17 = bf16[80,8,128]{2,1,0:T(8,128)(2,1)} collective-permute-done((bf16[80,8,128]{2,1,0:T(8,128)(2,1)S(1)}, bf16[80,8,128]{2,1,0:T(8,128)(2,1)}, u32[]{:S(2)}, u32[]{:S(2)}) %collective-permute-start.17) | collective-permute-done | bytes 163872 | tf_op jit(solution)/shard_map/ppermute | solution.py:21
  98.0 10.9 %collective-permute-done.19 = bf16[80,8,128]{2,1,0:T(8,128)(2,1)} collective-permute-done((bf16[80,8,128]{2,1,0:T(8,128)(2,1)S(1)}, bf16[80,8,128]{2,1,0:T(8,128)(2,1)}, u32[]{:S(2)}, u32[]{:S(2)}) %collective-permute-start.19) | collective-permute-done | bytes 163872 | tf_op jit(solution)/shard_map/ppermute | solution.py:21
  108.9 1.9 %add_convert_fusion = bf16[80,8,128]{2,1,0:T(8,128)(2,1)} fusion(bf16[80,8,128]{2,1,0:T(8,128)(2,1)S(1)} %collective-permute-done.16, bf16[80,8,128]{2,1,0:T(8,128)(2,1)S(1)} %collective-permute-done.15, bf16[80,8,128]{2,1,0:T(8,128)(2,1)S(1)} %collective-permute-done.14, bf16[80,8,128]{2,1,0:T(8,128)(2,1)} %collective-permute-done.19, ...), kind=kLoop, calls=%fused_computation.6 | loop fusion | flops 1556480 | bytes 1474566 | tf_op jit(solution)/shard_map/convert_element_type | solution.py:417
  (67 shorter events, 3.8 us)
Async XLA Ops:
  0.6 4.8 %copy-start = (bf16[320,8,128]{2,1,0:T(8,128)(2,1)S(1)}, bf16[320,8,128]{2,1,0:T(8,128)(2,1)}, u32[]{:S(2)}) copy-start(bf16[320,8,128]{2,1,0:T(8,128)(2,1)} %param.10) | copy-start | bytes 1966084
  0.6 6.8 %copy-start.3 = (bf16[32,320,1,1,1]{1,0,4,3,2:T(8,128)(2,1)S(1)}, bf16[32,320,1,1,1]{1,0,4,3,2:T(8,128)(2,1)}, u32[]{:S(2)}) copy-start(bf16[32,320,1,1,1]{1,0,4,3,2:T(8,128)(2,1)} %constant.59) | copy-start | bytes 61444
  0.7 7.3 %copy-start.4 = (pred[8,320]{1,0:T(8,128)(4,1)S(1)}, pred[8,320]{1,0:T(8,128)(4,1)}, u32[]{:S(2)}) copy-start(pred[8,320]{1,0:T(8,128)(4,1)} %constant.55.clone) | copy-start | bytes 7684
  0.7 7.3 %copy-start.5 = (pred[8,320]{1,0:T(8,128)(4,1)S(1)}, pred[8,320]{1,0:T(8,128)(4,1)}, u32[]{:S(2)}) copy-start(pred[8,320]{1,0:T(8,128)(4,1)} %constant.56.clone) | copy-start | bytes 7684
  0.7 7.3 %copy-start.6 = (pred[8,320]{1,0:T(8,128)(4,1)S(1)}, pred[8,320]{1,0:T(8,128)(4,1)}, u32[]{:S(2)}) copy-start(pred[8,320]{1,0:T(8,128)(4,1)} %constant.57.clone) | copy-start | bytes 7684
  0.7 31.9 %collective-permute-start.3 = (bf16[32,12,8,128]{3,2,1,0:T(8,128)(2,1)}, bf16[32,12,8,128]{3,2,1,0:T(8,128)(2,1)S(1)}, u32[]{:S(2)}, u32[]{:S(2)}) collective-permute-start(bf16[32,12,8,128]{3,2,1,0:T(8,128)(2,1)} %refs_0_.1), channel_id=1, source_target_pairs={{0,2},{1,3},{2,0},{3,1},{4,6},{5,7},{6,4},{7,5},{8,10},{9,11},{10,... | collective-permute-start | bytes 2359304 | tf_op jit(solution)/shard_map/ppermute | solution.py:269
  3.9 8.1 %collective-permute-start = (bf16[12,32,128]{2,1,0:T(8,128)(2,1)S(1)}, bf16[12,32,128]{2,1,0:T(8,128)(2,1)S(1)}, u32[]{:S(2)}, u32[]{:S(2)}) collective-permute-start(bf16[12,32,128]{2,1,0:T(8,128)(2,1)S(1)} %get-tuple-element.41), channel_id=1, source_target_pairs={{0,4},{4,8},{8,12},{12,16},{16,20},{20,24},{24,28},{28,0},{1,5},{5... | collective-permute-start | bytes 294920 | tf_op jit(solution)/shard_map/ppermute | solution.py:21
  3.9 8.1 %collective-permute-start.1 = (bf16[12,32,128]{2,1,0:T(8,128)(2,1)S(1)}, bf16[12,32,128]{2,1,0:T(8,128)(2,1)}, u32[]{:S(2)}, u32[]{:S(2)}) collective-permute-start(bf16[12,32,128]{2,1,0:T(8,128)(2,1)S(1)} %get-tuple-element.42), channel_id=1, source_target_pairs={{0,28},{4,0},{8,4},{12,8},{16,12},{20,16},{24,20},{28,24},{1,29},{... | collective-permute-start | bytes 294920 | tf_op jit(solution)/shard_map/ppermute | solution.py:21
  5.4 12.1 %collective-permute-start.6 = (bf16[80,8,128]{2,1,0:T(8,128)(2,1)S(1)}, bf16[80,8,128]{2,1,0:T(8,128)(2,1)S(1)}, u32[]{:S(2)}, u32[]{:S(2)}) collective-permute-start(bf16[80,8,128]{2,1,0:T(8,128)(2,1)S(1)} %constant_dynamic-slice_fusion.2.refs_6_), channel_id=1, source_target_pairs={{0,12},{4,16},{8,20},{12,24},{16,28},{20,0},{24,4},{28,8},{1,13},{... | collective-permute-start | bytes 491528 | tf_op jit(solution)/shard_map/ppermute | solution.py:21
  7.8 10.6 %copy-start.1 = (bf16[32,12,8,128]{3,2,1,0:T(8,128)(2,1)S(1)}, bf16[32,12,8,128]{3,2,1,0:T(8,128)(2,1)}, u32[]{:S(2)}) copy-start(bf16[32,12,8,128]{3,2,1,0:T(8,128)(2,1)} %refs_0_.1) | copy-start | bytes 2359300
  12.1 20.5 %collective-permute-start.4 = (bf16[1,12,64,128]{3,2,1,0:T(8,128)(2,1)S(1)}, bf16[1,12,64,128]{3,2,1,0:T(8,128)(2,1)S(1)}, u32[]{:S(2)}, u32[]{:S(2)}) collective-permute-start(bf16[1,12,64,128]{3,2,1,0:T(8,128)(2,1)S(1)} %maximum_bitcast_fusion), channel_id=1, source_target_pairs={{0,2},{1,3},{2,0},{3,1},{4,6},{5,7},{6,4},{7,5},{8,10},{9,11},{10,... | collective-permute-start | bytes 589832 | tf_op jit(solution)/shard_map/ppermute | solution.py:269
  12.4 5.9 %collective-permute-start.7 = (bf16[80,8,128]{2,1,0:T(8,128)(2,1)S(1)}, bf16[80,8,128]{2,1,0:T(8,128)(2,1)S(1)}, u32[]{:S(2)}, u32[]{:S(2)}) collective-permute-start(bf16[80,8,128]{2,1,0:T(8,128)(2,1)S(1)} %constant_dynamic-slice_fusion.2.refs_6_), channel_id=1, source_target_pairs={{0,16},{4,20},{8,24},{12,28},{16,0},{20,4},{24,8},{28,12},{1,17},{... | collective-permute-start | bytes 491528 | tf_op jit(solution)/shard_map/ppermute | solution.py:21
  15.6 12.2 %collective-permute-start.5 = (bf16[80,8,128]{2,1,0:T(8,128)(2,1)S(1)}, bf16[80,8,128]{2,1,0:T(8,128)(2,1)S(1)}, u32[]{:S(2)}, u32[]{:S(2)}) collective-permute-start(bf16[80,8,128]{2,1,0:T(8,128)(2,1)S(1)} %constant_dynamic-slice_fusion.2.refs_6_), channel_id=1, source_target_pairs={{0,8},{4,12},{8,16},{12,20},{16,24},{20,28},{24,0},{28,4},{1,9},{5... | collective-permute-start | bytes 491528 | tf_op jit(solution)/shard_map/ppermute | solution.py:21
  17.5 15.1 %collective-permute-start.8 = (bf16[80,8,128]{2,1,0:T(8,128)(2,1)S(1)}, bf16[80,8,128]{2,1,0:T(8,128)(2,1)S(1)}, u32[]{:S(2)}, u32[]{:S(2)}) collective-permute-start(bf16[80,8,128]{2,1,0:T(8,128)(2,1)S(1)} %constant_dynamic-slice_fusion.2.refs_6_), channel_id=1, source_target_pairs={{0,20},{4,24},{8,28},{12,0},{16,4},{20,8},{24,12},{28,16},{1,21},{... | collective-permute-start | bytes 491528 | tf_op jit(solution)/shard_map/ppermute | solution.py:21
  18.4 27.1 %collective-permute-start.2 = (bf16[32,12,8,128]{3,2,1,0:T(8,128)(2,1)S(1)}, bf16[32,12,8,128]{3,2,1,0:T(8,128)(2,1)S(1)}, u32[]{:S(2)}, u32[]{:S(2)}) collective-permute-start(bf16[32,12,8,128]{3,2,1,0:T(8,128)(2,1)S(1)} %copy-done.1), channel_id=1, source_target_pairs={{0,1},{1,0},{2,3},{3,2},{4,5},{5,4},{6,7},{7,6},{8,9},{9,8},{10,11... | collective-permute-start | bytes 2359304 | tf_op jit(solution)/shard_map/ppermute | solution.py:269
  32.6 12.8 %collective-permute-start.9 = (bf16[32,12,8,128]{3,2,1,0:T(8,128)(2,1)S(1)}, bf16[32,12,8,128]{3,2,1,0:T(8,128)(2,1)S(1)}, u32[]{:S(2)}, u32[]{:S(2)}) collective-permute-start(bf16[32,12,8,128]{3,2,1,0:T(8,128)(2,1)S(1)} %collective-permute-done.3.refs_2_), channel_id=1, source_target_pairs={{0,1},{1,0},{2,3},{3,2},{4,5},{5,4},{6,7},{7,6},{8,9},{9,8},{10,11... | collective-permute-start | bytes 2359304 | tf_op jit(solution)/shard_map/ppermute | solution.py:269
  35.4 10.0 %collective-permute-start.10 = (bf16[2,12,64,128]{3,2,1,0:T(8,128)(2,1)S(1)}, bf16[2,12,64,128]{3,2,1,0:T(8,128)(2,1)S(1)}, u32[]{:S(2)}, u32[]{:S(2)}) collective-permute-start(bf16[2,12,64,128]{3,2,1,0:T(8,128)(2,1)S(1)} %pad_maximum_fusion.refs_4_), channel_id=1, source_target_pairs={{0,1},{1,0},{2,3},{3,2},{4,5},{5,4},{6,7},{7,6},{8,9},{9,8},{10,11... | collective-permute-start | bytes 1179656 | tf_op jit(solution)/shard_map/ppermute | solution.py:269
  35.5 5.4 %collective-permute-start.11 = (bf16[80,8,128]{2,1,0:T(8,128)(2,1)S(1)}, bf16[80,8,128]{2,1,0:T(8,128)(2,1)S(1)}, u32[]{:S(2)}, u32[]{:S(2)}) collective-permute-start(bf16[80,8,128]{2,1,0:T(8,128)(2,1)S(1)} %constant_dynamic-slice_fusion.2.refs_6_), channel_id=1, source_target_pairs={{0,4},{4,8},{8,12},{12,16},{16,20},{20,24},{24,28},{28,0},{1,5},{5... | collective-permute-start | bytes 491528 | tf_op jit(solution)/shard_map/ppermute | solution.py:21
  36.0 9.5 %collective-permute-start.12 = (bf16[80,8,128]{2,1,0:T(8,128)(2,1)S(1)}, bf16[80,8,128]{2,1,0:T(8,128)(2,1)S(1)}, u32[]{:S(2)}, u32[]{:S(2)}) collective-permute-start(bf16[80,8,128]{2,1,0:T(8,128)(2,1)S(1)} %constant_dynamic-slice_fusion.2.refs_6_), channel_id=1, source_target_pairs={{0,24},{4,28},{8,0},{12,4},{16,8},{20,12},{24,16},{28,20},{1,25},{... | collective-permute-start | bytes 491528 | tf_op jit(solution)/shard_map/ppermute | solution.py:21
  36.0 19.6 %copy-start.2 = (f32[32,240]{1,0:T(8,128)S(1)}, f32[32,240]{1,0:T(8,128)}, u32[]{:S(2)}) copy-start(f32[32,240]{1,0:T(8,128)} %constant.58.clone.fold_ref) | copy-start | bytes 92164
  53.5 22.9 %collective-permute-start.14 = (bf16[80,8,128]{2,1,0:T(8,128)(2,1)S(1)}, bf16[80,8,128]{2,1,0:T(8,128)(2,1)S(1)}, u32[]{:S(2)}, u32[]{:S(2)}) collective-permute-start(bf16[80,8,128]{2,1,0:T(8,128)(2,1)S(1)} %get-tuple-element.65), channel_id=1, source_target_pairs={{0,16},{4,20},{8,24},{12,28},{16,0},{20,4},{24,8},{28,12},{1,17},{... | collective-permute-start | bytes 491528 | tf_op jit(solution)/shard_map/ppermute | solution.py:21
  53.6 22.8 %collective-permute-start.15 = (bf16[80,8,128]{2,1,0:T(8,128)(2,1)S(1)}, bf16[80,8,128]{2,1,0:T(8,128)(2,1)S(1)}, u32[]{:S(2)}, u32[]{:S(2)}) collective-permute-start(bf16[80,8,128]{2,1,0:T(8,128)(2,1)S(1)} %get-tuple-element.66), channel_id=1, source_target_pairs={{0,12},{4,16},{8,20},{12,24},{16,28},{20,0},{24,4},{28,8},{1,13},{... | collective-permute-start | bytes 491528 | tf_op jit(solution)/shard_map/ppermute | solution.py:21
  54.1 22.3 %collective-permute-start.16 = (bf16[80,8,128]{2,1,0:T(8,128)(2,1)S(1)}, bf16[80,8,128]{2,1,0:T(8,128)(2,1)S(1)}, u32[]{:S(2)}, u32[]{:S(2)}) collective-permute-start(bf16[80,8,128]{2,1,0:T(8,128)(2,1)S(1)} %get-tuple-element.67), channel_id=1, source_target_pairs={{0,8},{4,12},{8,16},{12,20},{16,24},{20,28},{24,0},{28,4},{1,9},{5... | collective-permute-start | bytes 491528 | tf_op jit(solution)/shard_map/ppermute | solution.py:21
  64.0 12.3 %collective-permute-start.13 = (f32[3,32,96]{2,1,0:T(8,128)S(1)}, f32[3,32,96]{2,1,0:T(8,128)S(1)}, u32[]{:S(2)}, u32[]{:S(2)}) collective-permute-start(f32[3,32,96]{2,1,0:T(8,128)S(1)} %shard_map.113), channel_id=1, source_target_pairs={{0,16},{4,20},{8,24},{12,28},{16,0},{20,4},{24,8},{28,12},{1,17},{... | collective-permute-start | bytes 110600 | tf_op jit(solution)/shard_map/ppermute | solution.py:269
  76.4 3.0 %collective-permute-start.20 = (f32[3,32,96]{2,1,0:T(8,128)S(1)}, f32[3,32,96]{2,1,0:T(8,128)S(1)}, u32[]{:S(2)}, u32[]{:S(2)}) collective-permute-start(f32[3,32,96]{2,1,0:T(8,128)S(1)} %add.64), channel_id=1, source_target_pairs={{0,8},{4,12},{8,0},{12,4},{16,24},{20,28},{24,16},{28,20},{1,9},{5... | collective-permute-start | bytes 110600 | tf_op jit(solution)/shard_map/ppermute | solution.py:269
  79.4 3.0 %collective-permute-start.21 = (f32[3,32,96]{2,1,0:T(8,128)S(1)}, f32[3,32,96]{2,1,0:T(8,128)S(1)}, u32[]{:S(2)}, u32[]{:S(2)}) collective-permute-start(f32[3,32,96]{2,1,0:T(8,128)S(1)} %add.77), channel_id=1, source_target_pairs={{0,4},{4,0},{8,12},{12,8},{16,20},{20,16},{24,28},{28,24},{1,5},{5... | collective-permute-start | bytes 110600 | tf_op jit(solution)/shard_map/ppermute | solution.py:269
  82.4 4.4 %collective-permute-start.23 = (f32[3,32,96]{2,1,0:T(8,128)S(1)}, f32[3,32,96]{2,1,0:T(8,128)S(1)}, u32[]{:S(2)}, u32[]{:S(2)}) collective-permute-start(f32[3,32,96]{2,1,0:T(8,128)S(1)} %add.78), channel_id=1, source_target_pairs={{0,2},{1,3},{2,0},{3,1},{4,6},{5,7},{6,4},{7,5},{8,10},{9,11},{10,... | collective-permute-start | bytes 110600 | tf_op jit(solution)/shard_map/ppermute | solution.py:269
  83.7 8.5 %collective-permute-start.22 = (f32[3,32,96]{2,1,0:T(8,128)S(1)}, f32[3,32,96]{2,1,0:T(8,128)S(1)}, u32[]{:S(2)}, u32[]{:S(2)}) collective-permute-start(f32[3,32,96]{2,1,0:T(8,128)S(1)} %add.78), channel_id=1, source_target_pairs={{0,1},{1,0},{2,3},{3,2},{4,5},{5,4},{6,7},{7,6},{8,9},{9,8},{10,11... | collective-permute-start | bytes 110600 | tf_op jit(solution)/shard_map/ppermute | solution.py:269
  86.8 5.4 %collective-permute-start.24 = (f32[3,32,96]{2,1,0:T(8,128)S(1)}, f32[3,32,96]{2,1,0:T(8,128)S(1)}, u32[]{:S(2)}, u32[]{:S(2)}) collective-permute-start(f32[3,32,96]{2,1,0:T(8,128)S(1)} %collective-permute-done.23), channel_id=1, source_target_pairs={{0,1},{1,0},{2,3},{3,2},{4,5},{5,4},{6,7},{7,6},{8,9},{9,8},{10,11... | collective-permute-start | bytes 110600 | tf_op jit(solution)/shard_map/ppermute | solution.py:269
  89.4 8.6 %collective-permute-start.17 = (bf16[80,8,128]{2,1,0:T(8,128)(2,1)S(1)}, bf16[80,8,128]{2,1,0:T(8,128)(2,1)}, u32[]{:S(2)}, u32[]{:S(2)}) collective-permute-start(bf16[80,8,128]{2,1,0:T(8,128)(2,1)S(1)} %get-tuple-element.70), channel_id=1, source_target_pairs={{0,28},{4,0},{8,4},{12,8},{16,12},{20,16},{24,20},{28,24},{1,29},{... | collective-permute-start | bytes 491528 | tf_op jit(solution)/shard_map/ppermute | solution.py:21
  89.4 8.6 %collective-permute-start.18 = (bf16[80,8,128]{2,1,0:T(8,128)(2,1)S(1)}, bf16[80,8,128]{2,1,0:T(8,128)(2,1)}, u32[]{:S(2)}, u32[]{:S(2)}) collective-permute-start(bf16[80,8,128]{2,1,0:T(8,128)(2,1)S(1)} %get-tuple-element.71), channel_id=1, source_target_pairs={{0,24},{4,28},{8,0},{12,4},{16,8},{20,12},{24,16},{28,20},{1,25},{... | collective-permute-start | bytes 491528 | tf_op jit(solution)/shard_map/ppermute | solution.py:21
  89.5 19.4 %collective-permute-start.19 = (bf16[80,8,128]{2,1,0:T(8,128)(2,1)S(1)}, bf16[80,8,128]{2,1,0:T(8,128)(2,1)}, u32[]{:S(2)}, u32[]{:S(2)}) collective-permute-start(bf16[80,8,128]{2,1,0:T(8,128)(2,1)S(1)} %get-tuple-element.72), channel_id=1, source_target_pairs={{0,20},{4,24},{8,28},{12,0},{16,4},{20,8},{24,12},{28,16},{1,21},{... | collective-permute-start | bytes 491528 | tf_op jit(solution)/shard_map/ppermute | solution.py:21

commit v7 on v6

--- a/solution.py
+++ b/solution.py
@@ -109,60 +109,19 @@
     lax.fori_loop(0, count // width, step, 0)
 
 
-def upper_grads(parts, hops, far, halo_order, places, *refs):
-    cot_refs, halo_refs, refs = refs[:parts], refs[parts : parts + 2], refs[parts + 2 :]
-    right_refs, refs = refs[: hops + 1], refs[hops + 1 :]
-    left_ref, weight_ref, cot_s, right_s, left_sum, grad_out = refs[:6]
-    sent_refs, refs = refs[6 : 6 + far], refs[6 + far :]
-    cot_b, halo_b, right_b, left_s, grad_s, sems = refs
-    channels, width, rows = left_ref.shape
-    outs, levels = cot_refs[0].shape[:2]
-    main = outs * width
-    span = main + 2 * outs
-    reach = hops * width
+def upper_grads(far, left_ref, weight_ref, cot_s, right_s, left_sum, grad_out, *rest):
+    sent_refs, (left_s, grad_s) = rest[:far], rest[far:]
+    width = left_ref.shape[1]
     f32, bf16 = jnp.float32, jnp.bfloat16
-
-    copies = []
-    for buffer, sources in ((right_b, right_refs), (cot_b, cot_refs)):
-        for at, source in enumerate(sources):
-            copies.append(
-                pltpu.make_async_copy(source, buffer.at[at], sems.at[len(copies)])
-            )
-    half = halo_b.shape[0] // 2
-    for at, source in enumerate(halo_refs):
-        copies.append(
-            pltpu.make_async_copy(source, halo_b.at[pl.ds(at * half, half)], sems.at[len(copies)])
-        )
-    for copy in copies:
-        copy.start()
-
     left_s[...] = left_ref[...].astype(f32)
     left_sum[...] = jnp.zeros(left_sum.shape, f32)
     grad_s[...] = jnp.zeros(grad_s.shape, f32)
-    cot_s[0] = jnp.zeros((span, rows), bf16)
-    cot_s[D + 1] = jnp.zeros((span, rows), bf16)
-    for hop in range(hops + 1):
-        copies[hop].wait()
-        at = reach - hop * width
-        block = right_b[hop].astype(f32)
-        right_s[:, at : at + width] = jnp.where(places[1] >= hop, block, 0.0)
-    for copy in copies[hops + 1 :]:
-        copy.wait()
-    for other in range(parts):
-        start = (places[0] ^ other) * levels + 1
-
-        def assemble(level, carry, other=other, start=start):
-            cot_s[start + level, 0:main] = cot_b[other, :, level].reshape(main, rows)
-            cot_s[start + level, main:span] = halo_b[halo_order.index(other), level]
-            return carry
-
-        lax.fori_loop(0, levels, assemble, 0)
-
     add_grads(D // 2, D // 2, cot_s, weight_ref, left_s, right_s, left_sum, grad_s)
     grad_out[...] = grad_s[:, far * width :]
-    for hop in range(hops, hops - far, -1):
-        at = reach - hop * width
-        sent_refs[hops - hop][...] = (grad_s[:, at : at + width] * (1.0 / GROUP)).astype(bf16)
+    for at in range(far):
+        sent_refs[at][...] = (
+            grad_s[:, at * width : (at + 1) * width] * (1.0 / GROUP)
+        ).astype(bf16)
 
 
 def lower_grads(
@@ -182,15 +141,41 @@
         sent_refs[near - hop][...] = (grad_s[:, at : at + width] * (1.0 / GROUP)).astype(bf16)
 
 
-def kernel_sums(left_ref, cot_s, right_s, fold_ref, sums_ref, vol_s, prod_s):
+def kernel_sums(parts, hops, halo_order, places, *refs):
+    cot_refs, halo_refs, refs = refs[:parts], refs[parts : parts + 2], refs[parts + 2 :]
+    right_refs, refs = refs[: hops + 1], refs[hops + 1 :]
+    left_ref, fold_ref, cot_s, right_s, sums_ref = refs[:5]
+    cot_b, halo_b, right_b, vol_s, prod_s, sems = refs[5:]
     channels, width, rows = left_ref.shape
     groups = channels // GROUP
-    span = cot_s.shape[1]
-    outs = span // (width + 2)
+    outs, levels = cot_refs[0].shape[:2]
     main = outs * width
+    span = main + 2 * outs
     size = groups * width
-    reach = right_s.shape[1] - width
+    reach = hops * width
     f32, bf16 = jnp.float32, jnp.bfloat16
+
+    copies = []
+    for buffer, sources in ((right_b, right_refs), (cot_b, cot_refs)):
+        for at, source in enumerate(sources):
+            copies.append(
+                pltpu.make_async_copy(source, buffer.at[at], sems.at[len(copies)])
+            )
+    half = halo_b.shape[0] // 2
+    for at, source in enumerate(halo_refs):
+        copies.append(
+            pltpu.make_async_copy(source, halo_b.at[pl.ds(at * half, half)], sems.at[len(copies)])
+        )
+    for copy in copies:
+        copy.start()
+
+    cot_s[0] = jnp.zeros((span, rows), bf16)
+    cot_s[D + 1] = jnp.zeros((span, rows), bf16)
+    for hop in range(hops + 1):
+        copies[hop].wait()
+        at = reach - hop * width
+        block = right_b[hop].astype(f32)
+        right_s[:, at : at + width] = jnp.where(places[1] >= hop, block, 0.0)
 
     def volume_step(group, carry):
         first = group * GROUP
@@ -207,6 +192,18 @@
         return carry
 
     lax.fori_loop(0, groups, volume_step, 0)
+
+    for copy in copies[hops + 1 :]:
+        copy.wait()
+    for other in range(parts):
+        start = (places[0] ^ other) * levels + 1
+
+        def assemble(level, carry, other=other, start=start):
+            cot_s[start + level, 0:main] = cot_b[other, :, level].reshape(main, rows)
+            cot_s[start + level, main:span] = halo_b[halo_order.index(other), level]
+            return carry
+
+        lax.fori_loop(0, levels, assemble, 0)
 
     chunk = 4
     prod_s[...] = jnp.zeros(prod_s.shape, f32)
@@ -260,7 +257,7 @@
         out_specs=[VMEM] * len(outs),
         scratch_shapes=scratch,
         compiler_params=pltpu.CompilerParams(vmem_limit_bytes=limit * MIB),
-        cost_estimate=pl.CostEstimate(flops=1024, bytes_accessed=1024, transcendentals=0),
+        cost_estimate=pl.CostEstimate(flops=flops, bytes_accessed=1024, transcendentals=0),
     )(*[array for space, array in operands])
 
 
@@ -320,9 +317,7 @@
     right_own = lax.dynamic_slice_in_dim(right, part * channels, channels, 0)
     left_own = lax.dynamic_slice_in_dim(left, part * channels, channels, 0)
     weights = toeplitz(lax.dynamic_slice_in_dim(kernel, part * groups, groups, 4), width)
-    right_late, low, high, left_own, weights = lax.optimization_barrier(
-        (right_own, low, high, left_own, weights)
-    )
+    right_late, low, high = lax.optimization_barrier((right_own, low, high))
     low = jnp.where(column > 0, low, 0).astype(bf16)
     high = jnp.where(column < columns - 1, high, 0).astype(bf16)
     halo = jnp.concatenate([low, high], axis=1)[None]
@@ -343,41 +338,36 @@
     block = (channels, width, rows)
     wide = (channels, (hops + 1) * width, rows)
     moved = [*cots, *halos, *rights]
-    results = run(
-        functools.partial(upper_grads, parts, hops, far, halo_order),
-        [(SMEM, places)] + [(HBM, item) for item in moved] + [(VMEM, left_own), (VMEM, weights)],
-        [
-            ((D + 2, span, rows), bf16),
-            (wide, f32),
-            (block, f32),
-            ((channels, (near + 1) * width, rows), f32),
-            *[(block, bf16)] * far,
-        ],
+    cot_wide, right_wide, total = run(
+        functools.partial(kernel_sums, parts, hops, halo_order),
+        [(SMEM, places)]
+        + [(HBM, item) for item in moved]
+        + [(VMEM, left_own), (VMEM, jnp.asarray(fold))],
+        [((D + 2, span, rows), bf16), (wide, f32), ((3, pad_rows, 3 * outs), f32)],
         [
             pltpu.VMEM((parts, *cotangent.shape), bf16),
             pltpu.VMEM((parts, levels, 2 * outs, rows), bf16),
             pltpu.VMEM((hops + 1, *block), bf16),
-            pltpu.VMEM(block, f32),
-            pltpu.VMEM(wide, f32),
+            pltpu.VMEM((D, 3, size, rows), f32),
+            pltpu.VMEM((3, span, 3 * size), f32),
             pltpu.SemaphoreType.DMA((len(moved),)),
         ],
         20, 8000000000,
     )
-    cot_wide, right_wide, left_part, grad_part = results[:4]
-    sent = dict(zip(range(hops, hops - far, -1), results[4:]))
-    arrived = {hop: shifted(value, "col", -hop) for hop, value in sent.items()}
-
-    (total,) = run(
-        kernel_sums,
-        [(VMEM, item) for item in (left_own, cot_wide, right_wide, jnp.asarray(fold))],
-        [((3, pad_rows, 3 * outs), f32)],
-        [pltpu.VMEM((D, 3, size, rows), f32), pltpu.VMEM((3, span, 3 * size), f32)],
-        16, 8000000000,
-    )
-    grad_part, total = lax.optimization_barrier((grad_part, total))
     bits = [1 << k for k in reversed(range(columns.bit_length() - 1))]
+    left_part, grad_part, *sent = run(
+        functools.partial(upper_grads, far),
+        [(VMEM, item) for item in (left_own, weights, cot_wide, right_wide)],
+        [(block, f32), ((channels, (near + 1) * width, rows), f32), *[(block, bf16)] * far],
+        [pltpu.VMEM(block, f32), pltpu.VMEM(wide, f32)],
+        12, 8000000000,
+    )
     total = total_swapping(total, bits[0])
-    results = run(
+    *sent, grad_part, total = lax.optimization_barrier((*sent, grad_part, total))
+    arrived = {
+        hop: shifted(value, "col", -hop) for hop, value in zip(range(hops, near, -1), sent)
+    }
+    grad_left, own, *sent = run(
         functools.partial(lower_grads, near),
         [
             (VMEM, item)
@@ -389,18 +379,18 @@
             pltpu.VMEM(block, f32),
             pltpu.VMEM((channels, (near + 1) * width, rows), f32),
         ],
-        16, 8000000000,
-    )
-    distant = sorted(arrived)
-    *results, total = lax.optimization_barrier((*results, total, *[arrived[hop] for hop in distant]))
-    results, held = results[: 2 + near], [*results[2 + near :], total]
-    total, held = held[0], held[1:]
-    arrived = dict(zip(distant, held))
-    grad_left, own = results[:2]
-    sent = dict(zip(range(near, 0, -1), results[2:]))
-    arrived.update({hop: shifted(value, "col", -hop) for hop, value in sent.items()})
-    for bit in bits[1:]:
+        12, 8000000000,
+    )
+    total = total_swapping(total, bits[1])
+    sent, arrived[hops], arrived[hops - 1], total = lax.optimization_barrier(
+        (sent, arrived[hops], arrived[hops - 1], total)
+    )
+    arrived.update(
+        {hop: shifted(value, "col", -hop) for hop, value in zip(range(near, 0, -1), sent)}
+    )
+    for bit in bits[2:]:
         total = total_swapping(total, bit)
+    total, arrived[1] = lax.optimization_barrier((total, arrived[1]))
 
     total_right = own
     for hop in range(1, hops + 1):

time: 111 us -> 104 us (0.937)
  the two profiles are of different devices: /device:TPU:29 before, /device:TPU:6 now
where the time goes in v7:
time: 104 us
  waiting for transfers between devices  34.3 us (33%)
  starting transfers between devices  33.1 us (32%)
  Pallas kernels  21.7 us (21%)
  local copies, waits for them, and re-layouts  10.6 us (10%)
  other arithmetic  2.61 us (3%)
    ppermute x14, waiting for transfers between devices, shifted(): lax.ppermute(value, axis, [(source, (source + steps) % count) for source...  30.7 us
    ppermute x14, starting transfers between devices, shifted(): lax.ppermute(value, axis, [(source, (source + steps) % count) for source...  28.2 us
    pallas_call x3, Pallas kernels, run(): pl.pallas_call(function, out_shape=[jax.ShapeDtypeStruct(shape, kind) for...  21.7 us
    ppermute x11, starting transfers between devices, swapped(): lax.ppermute(value, axis, [(source, source ^ bit) for source in range(cou...  4.98 us
    unnamed x27, local copies, waits for them, and re-layouts  3.78 us
    ppermute x11, waiting for transfers between devices, swapped(): lax.ppermute(value, axis, [(source, source ^ bit) for source in range(cou...  3.57 us
  transfers between devices with their start and end apart: 25, of which 10 were waited for; matrix products, arithmetic and copies ran while one was open for 6% of the time, Pallas kernels for 9%

profile of v7, /device:TPU:6, one launch (start us, length us, event | category | flops | bytes accessed | tf_op | source)
XLA Modules:
  0.0 103.5 jit_solution(6379038444105728679)
XLA Ops:
  0.7 1.8 %fusion.2 = (bf16[32,12,1,128]{3,2,1,0:T(2,128)(2,1)S(1)}, bf16[32,12,1,128]{3,2,1,0:T(2,128)(2,1)S(1)}) fusion(bf16[32,12,8,128]{3,2,1,0:T(8,128)(2,1)} %refs_0_.1), kind=kLoop, calls=%fused_computation.25 | loop fusion | bytes 393216 | tf_op jit(solution)/shard_map/slice | solution.py:314
  2.6 2.6 %collective-permute-start.6 = (bf16[80,8,128]{2,1,0:T(8,128)(2,1)S(1)}, bf16[80,8,128]{2,1,0:T(8,128)(2,1)S(1)}, u32[]{:S(2)}, u32[]{:S(2)}) collective-permute-start(bf16[80,8,128]{2,1,0:T(8,128)(2,1)S(1)} %constant_dynamic-slice_fusion.refs_6_), channel_id=1, source_target_pairs={{0,12},{4,16},{8,20},{12,24},{16,28},{20,0},{24,4},{28,8},{1,13},{... | collective-permute-start | bytes 491528 | tf_op jit(solution)/shard_map/ppermute | solution.py:21
  5.8 2.6 %collective-permute-start.2 = (bf16[12,32,128]{2,1,0:T(8,128)(2,1)S(1)}, bf16[12,32,128]{2,1,0:T(8,128)(2,1)S(1)}, u32[]{:S(2)}, u32[]{:S(2)}) collective-permute-start(bf16[12,32,128]{2,1,0:T(8,128)(2,1)S(1)} %get-tuple-element.42), channel_id=1, source_target_pairs={{0,4},{4,8},{8,12},{12,16},{16,20},{20,24},{24,28},{28,0},{1,5},{5... | collective-permute-start | bytes 294920 | tf_op jit(solution)/shard_map/ppermute | solution.py:21
  8.8 1.1 %constant_dynamic-slice_fusion.1 = bf16[3,3,3,32,10]{4,3,2,1,0:T(8,128)(2,1)S(1)} fusion(bf16[3,3,3,32,40]{4,3,2,1,0:T(8,128)(2,1)} %param.11, s32[]{:T(128)S(6)} %select_n.88), kind=kLoop, calls=%fused_computation.21 | loop fusion | bytes 34564 | tf_op jit(solution)/shard_map/dynamic_slice | solution.py:319
  9.9 5.6 %collective-permute-done.2 = bf16[12,32,128]{2,1,0:T(8,128)(2,1)S(1)} collective-permute-done((bf16[12,32,128]{2,1,0:T(8,128)(2,1)S(1)}, bf16[12,32,128]{2,1,0:T(8,128)(2,1)S(1)}, u32[]{:S(2)}, u32[]{:S(2)}) %collective-permute-start.2) | collective-permute-done | bytes 98336 | tf_op jit(solution)/shard_map/ppermute | solution.py:21
  15.5 7.2 %collective-permute-start.5 = (bf16[80,8,128]{2,1,0:T(8,128)(2,1)S(1)}, bf16[80,8,128]{2,1,0:T(8,128)(2,1)S(1)}, u32[]{:S(2)}, u32[]{:S(2)}) collective-permute-start(bf16[80,8,128]{2,1,0:T(8,128)(2,1)S(1)} %constant_dynamic-slice_fusion.refs_6_), channel_id=1, source_target_pairs={{0,8},{4,12},{8,16},{12,20},{16,24},{20,28},{24,0},{28,4},{1,9},{5... | collective-permute-start | bytes 491528 | tf_op jit(solution)/shard_map/ppermute | solution.py:21
  23.8 1.9 %collective-permute-done.7.refs_10_ = bf16[80,8,128]{2,1,0:T(8,128)(2,1)S(1)} collective-permute-done((bf16[80,8,128]{2,1,0:T(8,128)(2,1)S(1)}, bf16[80,8,128]{2,1,0:T(8,128)(2,1)S(1)}, u32[]{:S(2)}, u32[]{:S(2)}) %collective-permute-start.7) | collective-permute-done | bytes 163872 | tf_op jit(solution)/shard_map/ppermute | solution.py:21
  25.7 1.7 %collective-permute-done.5.refs_8_ = bf16[80,8,128]{2,1,0:T(8,128)(2,1)S(1)} collective-permute-done((bf16[80,8,128]{2,1,0:T(8,128)(2,1)S(1)}, bf16[80,8,128]{2,1,0:T(8,128)(2,1)S(1)}, u32[]{:S(2)}, u32[]{:S(2)}) %collective-permute-start.5) | collective-permute-done | bytes 163872 | tf_op jit(solution)/shard_map/ppermute | solution.py:21
  27.4 6.3 %collective-permute-done.8.refs_11_ = bf16[80,8,128]{2,1,0:T(8,128)(2,1)S(1)} collective-permute-done((bf16[80,8,128]{2,1,0:T(8,128)(2,1)S(1)}, bf16[80,8,128]{2,1,0:T(8,128)(2,1)S(1)}, u32[]{:S(2)}, u32[]{:S(2)}) %collective-permute-start.8) | collective-permute-done | bytes 163872 | tf_op jit(solution)/shard_map/ppermute | solution.py:21
  34.5 1.4 %select_select_fusion = bf16[3,10,8,3,320]{4,3,2,1,0:T(4,128)(2,1)} fusion(pred[8,320]{1,0:T(8,128)(4,1)S(1)} %copy-done.10, pred[8,320]{1,0:T(8,128)(4,1)S(1)} %copy-done.11, pred[8,320]{1,0:T(8,128)(4,1)S(1)} %copy-done.12, bf16[3,10,3,320]{3,2,1,0:T(4,128)(2,1)S(1)} %copy.31, bf16[3,10,3,320]{3,2,1,0:T(4,128)(2,1)S(1)} %copy.30, ...), kind=kLoop, calls=%fused_computation.2 | loop fusion | flops 691200 | bytes 641280 | tf_op jit(solution)/shard_map/jit(_where)/select_n | solution.py:45
  35.9 2.5 %collective-permute-start.12 = (bf16[80,8,128]{2,1,0:T(8,128)(2,1)S(1)}, bf16[80,8,128]{2,1,0:T(8,128)(2,1)}, u32[]{:S(2)}, u32[]{:S(2)}) collective-permute-start(bf16[80,8,128]{2,1,0:T(8,128)(2,1)S(1)} %constant_dynamic-slice_fusion.refs_6_), channel_id=1, source_target_pairs={{0,24},{4,28},{8,0},{12,4},{16,8},{20,12},{24,16},{28,20},{1,25},{... | collective-permute-start | bytes 491528 | tf_op jit(solution)/shard_map/ppermute | solution.py:21
  38.5 1.7 %select_n.92.weight_ref = bf16[240,960]{1,0:T(8,128)(2,1)S(1)} reshape(bf16[3,10,8,3,320]{4,3,2,1,0:T(4,128)(2,1)} %select_select_fusion) | data formatting | bytes 921600 | tf_op jit(solution)/shard_map/jit(_where)/select_n | solution.py:45
  40.2 0.9 constant_dynamic-slice_fusion.2.refs_13_.left_ref
  41.1 1.1 %collective-permute-done.11.refs_7_ = bf16[80,8,128]{2,1,0:T(8,128)(2,1)} collective-permute-done((bf16[80,8,128]{2,1,0:T(8,128)(2,1)S(1)}, bf16[80,8,128]{2,1,0:T(8,128)(2,1)}, u32[]{:S(2)}, u32[]{:S(2)}) %collective-permute-start.11) | collective-permute-done | bytes 163872 | tf_op jit(solution)/shard_map/ppermute | solution.py:21
  42.2 3.5 %collective-permute-done.12.refs_12_ = bf16[80,8,128]{2,1,0:T(8,128)(2,1)} collective-permute-done((bf16[80,8,128]{2,1,0:T(8,128)(2,1)S(1)}, bf16[80,8,128]{2,1,0:T(8,128)(2,1)}, u32[]{:S(2)}, u32[]{:S(2)}) %collective-permute-start.12) | collective-permute-done | bytes 163872 | tf_op jit(solution)/shard_map/ppermute | solution.py:21
  45.7 0.9 copy-done.3
  46.6 0.9 copy-done.5
  47.5 0.9 copy-done.7
  48.4 12.0 %shard_map.112 = (bf16[50,320,128]{2,1,0:T(8,128)(2,1)S(1)}, f32[80,56,128]{2,1,0:T(8,128)S(1)}, f32[3,32,96]{2,1,0:T(8,128)S(1)}) custom-call(s32[2]{0:T(128)S(1)} %pad_add_fusion.places, bf16[32,12,8,128]{3,2,1,0:T(8,128)(2,1)S(1)} %copy-done.1, bf16[32,12,8,128]{3,2,1,0:T(8,128)(2,1)} %collective-permute-done.refs_1_, ...), custom_call_target="tpu_custom_call" | custom-call | flops 8000000000 | bytes 1024 | tf_op jit(solution)/shard_map/pallas_call | solution.py:253
  60.4 1.4 %collective-permute-start.13 = (f32[3,32,96]{2,1,0:T(8,128)S(1)}, f32[3,32,96]{2,1,0:T(8,128)S(1)}, u32[]{:S(2)}, u32[]{:S(2)}) collective-permute-start(f32[3,32,96]{2,1,0:T(8,128)S(1)} %get-tuple-element.60), channel_id=1, source_target_pairs={{0,16},{4,20},{8,24},{12,28},{16,0},{20,4},{24,8},{28,12},{1,17},{... | collective-permute-start | bytes 110600 | tf_op jit(solution)/shard_map/ppermute | solution.py:266
  61.8 4.5 %shard_map.113 = (f32[80,8,128]{2,1,0:T(8,128)S(1)}, f32[80,32,128]{2,1,0:T(8,128)S(1)}, bf16[80,8,128]{2,1,0:T(8,128)(2,1)S(1)}, bf16[80,8,128]{2,1,0:T(8,128)(2,1)S(1)}, bf16[80,8,128]{2,1,0:T(8,128)(2,1)S(1)}) custom-call(bf16[80,8,128]{2,1,0:T(8,128)(2,1)S(1)} %constant_dynamic-slice_fusion.2.refs_13_.left_ref, ...), custom_call_target="tpu_custom_call" | custom-call | flops 8000000000 | bytes 1024 | tf_op jit(solution)/shard_map/pallas_call | solution.py:253
  66.3 1.4 %collective-permute-start.16 = (f32[3,32,96]{2,1,0:T(8,128)S(1)}, f32[3,32,96]{2,1,0:T(8,128)S(1)}, u32[]{:S(2)}, u32[]{:S(2)}) collective-permute-start(f32[3,32,96]{2,1,0:T(8,128)S(1)} %add.64), channel_id=1, source_target_pairs={{0,8},{4,12},{8,0},{12,4},{16,24},{20,28},{24,16},{28,20},{1,9},{5... | collective-permute-start | bytes 110600 | tf_op jit(solution)/shard_map/ppermute | solution.py:266
  68.8 5.2 %shard_map.114 = (bf16[80,8,128]{2,1,0:T(8,128)(2,1)}, f32[80,8,128]{2,1,0:T(8,128)S(1)}, bf16[80,8,128]{2,1,0:T(8,128)(2,1)S(1)}, bf16[80,8,128]{2,1,0:T(8,128)(2,1)S(1)}, bf16[80,8,128]{2,1,0:T(8,128)(2,1)S(1)}) custom-call(bf16[80,8,128]{2,1,0:T(8,128)(2,1)S(1)} %constant_dynamic-slice_fusion.2.refs_13_.left_ref, ...), custom_call_target="tpu_custom_call" | custom-call | flops 8000000000 | bytes 1024 | tf_op jit(solution)/shard_map/pallas_call | solution.py:253
  74.0 2.7 %collective-permute-done.14 = bf16[80,8,128]{2,1,0:T(8,128)(2,1)S(1)} collective-permute-done((bf16[80,8,128]{2,1,0:T(8,128)(2,1)S(1)}, bf16[80,8,128]{2,1,0:T(8,128)(2,1)S(1)}, u32[]{:S(2)}, u32[]{:S(2)}) %collective-permute-start.14) | collective-permute-done | bytes 163872 | tf_op jit(solution)/shard_map/ppermute | solution.py:21
  76.7 0.9 collective-permute-done.15
  77.6 5.6 %collective-permute-start.18 = (bf16[80,8,128]{2,1,0:T(8,128)(2,1)S(1)}, bf16[80,8,128]{2,1,0:T(8,128)(2,1)S(1)}, u32[]{:S(2)}, u32[]{:S(2)}) collective-permute-start(bf16[80,8,128]{2,1,0:T(8,128)(2,1)S(1)} %get-tuple-element.71), channel_id=1, source_target_pairs={{0,28},{4,0},{8,4},{12,8},{16,12},{20,16},{24,20},{28,24},{1,29},{... | collective-permute-start | bytes 491528 | tf_op jit(solution)/shard_map/ppermute | solution.py:21
  83.3 1.1 %collective-permute-start.19 = (bf16[80,8,128]{2,1,0:T(8,128)(2,1)S(1)}, bf16[80,8,128]{2,1,0:T(8,128)(2,1)S(1)}, u32[]{:S(2)}, u32[]{:S(2)}) collective-permute-start(bf16[80,8,128]{2,1,0:T(8,128)(2,1)S(1)} %get-tuple-element.73), channel_id=1, source_target_pairs={{0,24},{4,28},{8,0},{12,4},{16,8},{20,12},{24,16},{28,20},{1,25},{... | collective-permute-start | bytes 491528 | tf_op jit(solution)/shard_map/ppermute | solution.py:21
  84.4 4.7 %collective-permute-start.20 = (bf16[80,8,128]{2,1,0:T(8,128)(2,1)S(1)}, bf16[80,8,128]{2,1,0:T(8,128)(2,1)S(1)}, u32[]{:S(2)}, u32[]{:S(2)}) collective-permute-start(bf16[80,8,128]{2,1,0:T(8,128)(2,1)S(1)} %get-tuple-element.74), channel_id=1, source_target_pairs={{0,20},{4,24},{8,28},{12,0},{16,4},{20,8},{24,12},{28,16},{1,21},{... | collective-permute-start | bytes 491528 | tf_op jit(solution)/shard_map/ppermute | solution.py:21
  89.8 3.5 %collective-permute-done.23 = f32[3,32,96]{2,1,0:T(8,128)S(1)} collective-permute-done((f32[3,32,96]{2,1,0:T(8,128)S(1)}, f32[3,32,96]{2,1,0:T(8,128)S(1)}, u32[]{:S(2)}, u32[]{:S(2)}) %collective-permute-start.23) | collective-permute-done | bytes 36896 | tf_op jit(solution)/shard_map/ppermute | solution.py:266
  93.3 7.0 %collective-permute-done.20 = bf16[80,8,128]{2,1,0:T(8,128)(2,1)S(1)} collective-permute-done((bf16[80,8,128]{2,1,0:T(8,128)(2,1)S(1)}, bf16[80,8,128]{2,1,0:T(8,128)(2,1)S(1)}, u32[]{:S(2)}, u32[]{:S(2)}) %collective-permute-start.20) | collective-permute-done | bytes 163872 | tf_op jit(solution)/shard_map/ppermute | solution.py:21
  100.3 0.9 add_convert_fusion
  102.6 1.0 copy.37
  (79 shorter events, 6.1 us)
Async XLA Ops:
  0.6 22.8 %copy-start.9 = (bf16[32,320,1,1,1]{1,0,4,3,2:T(8,128)(2,1)S(1)}, bf16[32,320,1,1,1]{1,0,4,3,2:T(8,128)(2,1)}, u32[]{:S(2)}) copy-start(bf16[32,320,1,1,1]{1,0,4,3,2:T(8,128)(2,1)} %constant.59) | copy-start | bytes 61444
  0.7 25.0 %copy-start.1 = (bf16[32,12,8,128]{3,2,1,0:T(8,128)(2,1)S(1)}, bf16[32,12,8,128]{3,2,1,0:T(8,128)(2,1)}, u32[]{:S(2)}) copy-start(bf16[32,12,8,128]{3,2,1,0:T(8,128)(2,1)} %refs_0_.1) | copy-start | bytes 2359300
  2.5 32.0 %copy-start.10 = (pred[8,320]{1,0:T(8,128)(4,1)S(1)}, pred[8,320]{1,0:T(8,128)(4,1)}, u32[]{:S(2)}) copy-start(pred[8,320]{1,0:T(8,128)(4,1)} %constant.55.clone) | copy-start | bytes 7684
  2.5 32.0 %copy-start.11 = (pred[8,320]{1,0:T(8,128)(4,1)S(1)}, pred[8,320]{1,0:T(8,128)(4,1)}, u32[]{:S(2)}) copy-start(pred[8,320]{1,0:T(8,128)(4,1)} %constant.56.clone) | copy-start | bytes 7684
  2.5 32.0 %copy-start.12 = (pred[8,320]{1,0:T(8,128)(4,1)S(1)}, pred[8,320]{1,0:T(8,128)(4,1)}, u32[]{:S(2)}) copy-start(pred[8,320]{1,0:T(8,128)(4,1)} %constant.57.clone) | copy-start | bytes 7684
  2.6 20.3 %collective-permute-start.6 = (bf16[80,8,128]{2,1,0:T(8,128)(2,1)S(1)}, bf16[80,8,128]{2,1,0:T(8,128)(2,1)S(1)}, u32[]{:S(2)}, u32[]{:S(2)}) collective-permute-start(bf16[80,8,128]{2,1,0:T(8,128)(2,1)S(1)} %constant_dynamic-slice_fusion.refs_6_), channel_id=1, source_target_pairs={{0,12},{4,16},{8,20},{12,24},{16,28},{20,0},{24,4},{28,8},{1,13},{... | collective-permute-start | bytes 491528 | tf_op jit(solution)/shard_map/ppermute | solution.py:21
  5.2 20.5 %collective-permute-start.7 = (bf16[80,8,128]{2,1,0:T(8,128)(2,1)S(1)}, bf16[80,8,128]{2,1,0:T(8,128)(2,1)S(1)}, u32[]{:S(2)}, u32[]{:S(2)}) collective-permute-start(bf16[80,8,128]{2,1,0:T(8,128)(2,1)S(1)} %constant_dynamic-slice_fusion.refs_6_), channel_id=1, source_target_pairs={{0,16},{4,20},{8,24},{12,28},{16,0},{20,4},{24,8},{28,12},{1,17},{... | collective-permute-start | bytes 491528 | tf_op jit(solution)/shard_map/ppermute | solution.py:21
  5.5 28.2 %collective-permute-start.1 = (bf16[32,12,8,128]{3,2,1,0:T(8,128)(2,1)}, bf16[32,12,8,128]{3,2,1,0:T(8,128)(2,1)S(1)}, u32[]{:S(2)}, u32[]{:S(2)}) collective-permute-start(bf16[32,12,8,128]{3,2,1,0:T(8,128)(2,1)} %refs_0_.1), channel_id=1, source_target_pairs={{0,2},{1,3},{2,0},{3,1},{4,6},{5,7},{6,4},{7,5},{8,10},{9,11},{10,... | collective-permute-start | bytes 2359304 | tf_op jit(solution)/shard_map/ppermute | solution.py:266
  5.8 9.7 %collective-permute-start.2 = (bf16[12,32,128]{2,1,0:T(8,128)(2,1)S(1)}, bf16[12,32,128]{2,1,0:T(8,128)(2,1)S(1)}, u32[]{:S(2)}, u32[]{:S(2)}) collective-permute-start(bf16[12,32,128]{2,1,0:T(8,128)(2,1)S(1)} %get-tuple-element.42), channel_id=1, source_target_pairs={{0,4},{4,8},{8,12},{12,16},{16,20},{20,24},{24,28},{28,0},{1,5},{5... | collective-permute-start | bytes 294920 | tf_op jit(solution)/shard_map/ppermute | solution.py:21
  8.5 7.1 %collective-permute-start.3 = (bf16[12,32,128]{2,1,0:T(8,128)(2,1)S(1)}, bf16[12,32,128]{2,1,0:T(8,128)(2,1)S(1)}, u32[]{:S(2)}, u32[]{:S(2)}) collective-permute-start(bf16[12,32,128]{2,1,0:T(8,128)(2,1)S(1)} %get-tuple-element.43), channel_id=1, source_target_pairs={{0,28},{4,0},{8,4},{12,8},{16,12},{20,16},{24,20},{28,24},{1,29},{... | collective-permute-start | bytes 294920 | tf_op jit(solution)/shard_map/ppermute | solution.py:21
  15.5 11.8 %collective-permute-start.5 = (bf16[80,8,128]{2,1,0:T(8,128)(2,1)S(1)}, bf16[80,8,128]{2,1,0:T(8,128)(2,1)S(1)}, u32[]{:S(2)}, u32[]{:S(2)}) collective-permute-start(bf16[80,8,128]{2,1,0:T(8,128)(2,1)S(1)} %constant_dynamic-slice_fusion.refs_6_), channel_id=1, source_target_pairs={{0,8},{4,12},{8,16},{12,20},{16,24},{20,28},{24,0},{28,4},{1,9},{5... | collective-permute-start | bytes 491528 | tf_op jit(solution)/shard_map/ppermute | solution.py:21
  22.8 10.9 %collective-permute-start.8 = (bf16[80,8,128]{2,1,0:T(8,128)(2,1)S(1)}, bf16[80,8,128]{2,1,0:T(8,128)(2,1)S(1)}, u32[]{:S(2)}, u32[]{:S(2)}) collective-permute-start(bf16[80,8,128]{2,1,0:T(8,128)(2,1)S(1)} %constant_dynamic-slice_fusion.refs_6_), channel_id=1, source_target_pairs={{0,20},{4,24},{8,28},{12,0},{16,4},{20,8},{24,12},{28,16},{1,21},{... | collective-permute-start | bytes 491528 | tf_op jit(solution)/shard_map/ppermute | solution.py:21
  22.8 10.8 %collective-permute-start.4 = (bf16[1,12,64,128]{3,2,1,0:T(8,128)(2,1)S(1)}, bf16[1,12,64,128]{3,2,1,0:T(8,128)(2,1)S(1)}, u32[]{:S(2)}, u32[]{:S(2)}) collective-permute-start(bf16[1,12,64,128]{3,2,1,0:T(8,128)(2,1)S(1)} %maximum_bitcast_fusion), channel_id=1, source_target_pairs={{0,2},{1,3},{2,0},{3,1},{4,6},{5,7},{6,4},{7,5},{8,10},{9,11},{10,... | collective-permute-start | bytes 589832 | tf_op jit(solution)/shard_map/ppermute | solution.py:266
  23.7 21.9 %copy-start.8 = (f32[32,240]{1,0:T(8,128)S(1)}, f32[32,240]{1,0:T(8,128)}, u32[]{:S(2)}) copy-start(f32[32,240]{1,0:T(8,128)} %constant.58.clone.refs_14_) | copy-start | bytes 92164
  25.7 12.7 %copy-start.2 = (bf16[80,8,128]{2,1,0:T(8,128)(2,1)}, bf16[80,8,128]{2,1,0:T(8,128)(2,1)S(1)}, u32[]{:S(2)}) copy-start(bf16[80,8,128]{2,1,0:T(8,128)(2,1)S(1)} %collective-permute-done.7.refs_10_) | copy-start | bytes 491524
  25.7 20.0 %collective-permute-start = (bf16[32,12,8,128]{3,2,1,0:T(8,128)(2,1)S(1)}, bf16[32,12,8,128]{3,2,1,0:T(8,128)(2,1)}, u32[]{:S(2)}, u32[]{:S(2)}) collective-permute-start(bf16[32,12,8,128]{3,2,1,0:T(8,128)(2,1)S(1)} %copy-done.1), channel_id=1, source_target_pairs={{0,1},{1,0},{2,3},{3,2},{4,5},{5,4},{6,7},{7,6},{8,9},{9,8},{10,11... | collective-permute-start | bytes 2359304 | tf_op jit(solution)/shard_map/ppermute | solution.py:266
  33.7 12.0 %collective-permute-start.9 = (bf16[32,12,8,128]{3,2,1,0:T(8,128)(2,1)S(1)}, bf16[32,12,8,128]{3,2,1,0:T(8,128)(2,1)}, u32[]{:S(2)}, u32[]{:S(2)}) collective-permute-start(bf16[32,12,8,128]{3,2,1,0:T(8,128)(2,1)S(1)} %collective-permute-done.1.refs_2_), channel_id=1, source_target_pairs={{0,1},{1,0},{2,3},{3,2},{4,5},{5,4},{6,7},{7,6},{8,9},{9,8},{10,11... | collective-permute-start | bytes 2359304 | tf_op jit(solution)/shard_map/ppermute | solution.py:266
  34.0 11.7 %collective-permute-start.10 = (bf16[2,12,64,128]{3,2,1,0:T(8,128)(2,1)S(1)}, bf16[2,12,64,128]{3,2,1,0:T(8,128)(2,1)}, u32[]{:S(2)}, u32[]{:S(2)}) collective-permute-start(bf16[2,12,64,128]{3,2,1,0:T(8,128)(2,1)S(1)} %pad_maximum_fusion.refs_4_), channel_id=1, source_target_pairs={{0,1},{1,0},{2,3},{3,2},{4,5},{5,4},{6,7},{7,6},{8,9},{9,8},{10,11... | collective-permute-start | bytes 1179656 | tf_op jit(solution)/shard_map/ppermute | solution.py:266
  35.9 6.2 %collective-permute-start.11 = (bf16[80,8,128]{2,1,0:T(8,128)(2,1)S(1)}, bf16[80,8,128]{2,1,0:T(8,128)(2,1)}, u32[]{:S(2)}, u32[]{:S(2)}) collective-permute-start(bf16[80,8,128]{2,1,0:T(8,128)(2,1)S(1)} %constant_dynamic-slice_fusion.refs_6_), channel_id=1, source_target_pairs={{0,4},{4,8},{8,12},{12,16},{16,20},{20,24},{24,28},{28,0},{1,5},{5... | collective-permute-start | bytes 491528 | tf_op jit(solution)/shard_map/ppermute | solution.py:21
  35.9 9.8 %collective-permute-start.12 = (bf16[80,8,128]{2,1,0:T(8,128)(2,1)S(1)}, bf16[80,8,128]{2,1,0:T(8,128)(2,1)}, u32[]{:S(2)}, u32[]{:S(2)}) collective-permute-start(bf16[80,8,128]{2,1,0:T(8,128)(2,1)S(1)} %constant_dynamic-slice_fusion.refs_6_), channel_id=1, source_target_pairs={{0,24},{4,28},{8,0},{12,4},{16,8},{20,12},{24,16},{28,20},{1,25},{... | collective-permute-start | bytes 491528 | tf_op jit(solution)/shard_map/ppermute | solution.py:21
  60.4 5.9 %collective-permute-start.13 = (f32[3,32,96]{2,1,0:T(8,128)S(1)}, f32[3,32,96]{2,1,0:T(8,128)S(1)}, u32[]{:S(2)}, u32[]{:S(2)}) collective-permute-start(f32[3,32,96]{2,1,0:T(8,128)S(1)} %get-tuple-element.60), channel_id=1, source_target_pairs={{0,16},{4,20},{8,24},{12,28},{16,0},{20,4},{24,8},{28,12},{1,17},{... | collective-permute-start | bytes 110600 | tf_op jit(solution)/shard_map/ppermute | solution.py:266
  66.3 7.7 %collective-permute-start.16 = (f32[3,32,96]{2,1,0:T(8,128)S(1)}, f32[3,32,96]{2,1,0:T(8,128)S(1)}, u32[]{:S(2)}, u32[]{:S(2)}) collective-permute-start(f32[3,32,96]{2,1,0:T(8,128)S(1)} %add.64), channel_id=1, source_target_pairs={{0,8},{4,12},{8,0},{12,4},{16,24},{20,28},{24,16},{28,20},{1,9},{5... | collective-permute-start | bytes 110600 | tf_op jit(solution)/shard_map/ppermute | solution.py:266
  67.7 9.0 %collective-permute-start.14 = (bf16[80,8,128]{2,1,0:T(8,128)(2,1)S(1)}, bf16[80,8,128]{2,1,0:T(8,128)(2,1)S(1)}, u32[]{:S(2)}, u32[]{:S(2)}) collective-permute-start(bf16[80,8,128]{2,1,0:T(8,128)(2,1)S(1)} %get-tuple-element.67), channel_id=1, source_target_pairs={{0,8},{4,12},{8,16},{12,20},{16,24},{20,28},{24,0},{28,4},{1,9},{5... | collective-permute-start | bytes 491528 | tf_op jit(solution)/shard_map/ppermute | solution.py:21
  68.4 9.2 %collective-permute-start.15 = (bf16[80,8,128]{2,1,0:T(8,128)(2,1)S(1)}, bf16[80,8,128]{2,1,0:T(8,128)(2,1)S(1)}, u32[]{:S(2)}, u32[]{:S(2)}) collective-permute-start(bf16[80,8,128]{2,1,0:T(8,128)(2,1)S(1)} %get-tuple-element.68), channel_id=1, source_target_pairs={{0,12},{4,16},{8,20},{12,24},{16,28},{20,0},{24,4},{28,8},{1,13},{... | collective-permute-start | bytes 491528 | tf_op jit(solution)/shard_map/ppermute | solution.py:21
  77.6 11.5 %collective-permute-start.18 = (bf16[80,8,128]{2,1,0:T(8,128)(2,1)S(1)}, bf16[80,8,128]{2,1,0:T(8,128)(2,1)S(1)}, u32[]{:S(2)}, u32[]{:S(2)}) collective-permute-start(bf16[80,8,128]{2,1,0:T(8,128)(2,1)S(1)} %get-tuple-element.71), channel_id=1, source_target_pairs={{0,28},{4,0},{8,4},{12,8},{16,12},{20,16},{24,20},{28,24},{1,29},{... | collective-permute-start | bytes 491528 | tf_op jit(solution)/shard_map/ppermute | solution.py:21
  83.3 10.0 %collective-permute-start.21 = (bf16[80,8,128]{2,1,0:T(8,128)(2,1)S(1)}, bf16[80,8,128]{2,1,0:T(8,128)(2,1)S(1)}, u32[]{:S(2)}, u32[]{:S(2)}) collective-permute-start(bf16[80,8,128]{2,1,0:T(8,128)(2,1)S(1)} %get-tuple-element.75), channel_id=1, source_target_pairs={{0,16},{4,20},{8,24},{12,28},{16,0},{20,4},{24,8},{28,12},{1,17},{... | collective-permute-start | bytes 491528 | tf_op jit(solution)/shard_map/ppermute | solution.py:21
  83.3 5.9 %collective-permute-start.17 = (f32[3,32,96]{2,1,0:T(8,128)S(1)}, f32[3,32,96]{2,1,0:T(8,128)S(1)}, u32[]{:S(2)}, u32[]{:S(2)}) collective-permute-start(f32[3,32,96]{2,1,0:T(8,128)S(1)} %add.66), channel_id=1, source_target_pairs={{0,4},{4,0},{8,12},{12,8},{16,20},{20,16},{24,28},{28,24},{1,5},{5... | collective-permute-start | bytes 110600 | tf_op jit(solution)/shard_map/ppermute | solution.py:266
  83.3 10.0 %collective-permute-start.19 = (bf16[80,8,128]{2,1,0:T(8,128)(2,1)S(1)}, bf16[80,8,128]{2,1,0:T(8,128)(2,1)S(1)}, u32[]{:S(2)}, u32[]{:S(2)}) collective-permute-start(bf16[80,8,128]{2,1,0:T(8,128)(2,1)S(1)} %get-tuple-element.73), channel_id=1, source_target_pairs={{0,24},{4,28},{8,0},{12,4},{16,8},{20,12},{24,16},{28,20},{1,25},{... | collective-permute-start | bytes 491528 | tf_op jit(solution)/shard_map/ppermute | solution.py:21
  84.4 15.9 %collective-permute-start.20 = (bf16[80,8,128]{2,1,0:T(8,128)(2,1)S(1)}, bf16[80,8,128]{2,1,0:T(8,128)(2,1)S(1)}, u32[]{:S(2)}, u32[]{:S(2)}) collective-permute-start(bf16[80,8,128]{2,1,0:T(8,128)(2,1)S(1)} %get-tuple-element.74), channel_id=1, source_target_pairs={{0,20},{4,24},{8,28},{12,0},{16,4},{20,8},{24,12},{28,16},{1,21},{... | collective-permute-start | bytes 491528 | tf_op jit(solution)/shard_map/ppermute | solution.py:21
  89.2 4.2 %collective-permute-start.23 = (f32[3,32,96]{2,1,0:T(8,128)S(1)}, f32[3,32,96]{2,1,0:T(8,128)S(1)}, u32[]{:S(2)}, u32[]{:S(2)}) collective-permute-start(f32[3,32,96]{2,1,0:T(8,128)S(1)} %add.67), channel_id=1, source_target_pairs={{0,2},{1,3},{2,0},{3,1},{4,6},{5,7},{6,4},{7,5},{8,10},{9,11},{10,... | collective-permute-start | bytes 110600 | tf_op jit(solution)/shard_map/ppermute | solution.py:266
  89.8 11.4 %collective-permute-start.22 = (f32[3,32,96]{2,1,0:T(8,128)S(1)}, f32[3,32,96]{2,1,0:T(8,128)S(1)}, u32[]{:S(2)}, u32[]{:S(2)}) collective-permute-start(f32[3,32,96]{2,1,0:T(8,128)S(1)} %add.67), channel_id=1, source_target_pairs={{0,1},{1,0},{2,3},{3,2},{4,5},{5,4},{6,7},{7,6},{8,9},{9,8},{10,11... | collective-permute-start | bytes 110600 | tf_op jit(solution)/shard_map/ppermute | solution.py:266
  93.3 7.9 %collective-permute-start.24 = (f32[3,32,96]{2,1,0:T(8,128)S(1)}, f32[3,32,96]{2,1,0:T(8,128)S(1)}, u32[]{:S(2)}, u32[]{:S(2)}) collective-permute-start(f32[3,32,96]{2,1,0:T(8,128)S(1)} %collective-permute-done.23), channel_id=1, source_target_pairs={{0,1},{1,0},{2,3},{3,2},{4,5},{5,4},{6,7},{7,6},{8,9},{9,8},{10,11... | collective-permute-start | bytes 110600 | tf_op jit(solution)/shard_map/ppermute | solution.py:266
  (6 other events, 20.4 us)

commit v8 on v7

v8 whole, which is shorter than its diff:
```python
import functools
import math

import jax
import jax.numpy as jnp
import numpy as np
from jax import lax
from jax.experimental import pallas as pl
from jax.experimental.pallas import tpu as pltpu
from jax.sharding import PartitionSpec as P

C = 320
G = 40
D = 48
GROUP = C // G
HIGHEST = lax.Precision.HIGHEST


def shifted(value, axis, steps):
    count = lax.axis_size(axis)
    return lax.ppermute(value, axis, [(source, (source + steps) % count) for source in range(count)])


def conv_rows(outs, width):
    main = np.tile(np.arange(width), outs)
    return np.concatenate([main, np.full(outs, -1), np.full(outs, width)])


def toeplitz(kernel_local, width):
    outs, groups = kernel_local.shape[3:]
    row_col = conv_rows(outs, width)
    row_out = np.concatenate([np.repeat(np.arange(outs), width), np.tile(np.arange(outs), 2)])
    spread = np.zeros((outs, row_col.size), np.float32)
    spread[row_out, np.arange(row_col.size)] = 1
    taps = jnp.transpose(kernel_local[::-1], (1, 2, 4, 0, 3))
    wide = jnp.einsum(
        "qrgpo,ok->qrgpk", taps, jnp.asarray(spread, jnp.bfloat16),
        preferred_element_type=jnp.float32,
    ).astype(jnp.bfloat16)
    out_col = np.arange(width)
    column_tap = out_col[:, None] - row_col[None, :] + 1
    total = jnp.zeros((3, groups, width, 3, row_col.size), jnp.bfloat16)
    for tap in range(3):
        mask = jnp.asarray(column_tap == tap)[None, None, :, None, :]
        total = jnp.where(mask, wide[tap][:, :, None], total)
    return total.reshape(3 * groups * width, 3 * row_col.size)


def roll_zero(value, steps):
    size = value.shape[-1]
    lane = lax.broadcasted_iota(jnp.int32, value.shape, value.ndim - 1)
    moved = pltpu.roll(value, steps % size, value.ndim - 1)
    return jnp.where(lane == (0 if steps > 0 else size - 1), 0.0, moved)


def pack(cot_ref, halo_ref, packed_ref):
    outs, levels, width, rows = cot_ref.shape
    main = outs * width

    def step(level, carry):
        packed_ref[level, 0:main] = cot_ref[:, level].reshape(main, rows)
        packed_ref[level, main:] = halo_ref[level]
        return carry

    lax.fori_loop(0, levels, step, 0)


def add_grads(first_level, count, reach, skipped, cot_s, weight_ref, left_s, right_s, left_sum, grad_s):
    channels, width, rows = left_s.shape
    groups = channels // GROUP
    size = groups * width
    span = cot_s.shape[1]
    f32, bf16 = jnp.float32, jnp.bfloat16

    def pair_values(at):
        near = cot_s[pl.ds(at, 3)].reshape(3 * span, rows)
        far = cot_s[pl.ds(at + 1, 3)].reshape(3 * span, rows)
        result = jnp.dot(
            weight_ref[...], jnp.concatenate([near, far], axis=1), preferred_element_type=f32
        )
        values = []
        for half in range(2):
            part = result[:, half * rows : (half + 1) * rows]
            total = (
                part[size : 2 * size]
                + roll_zero(part[:size], -1)
                + roll_zero(part[2 * size :], 1)
            )
            values.append(total.astype(bf16).astype(f32))
        return values

    def step(number, carry):
        level = first_level + number * width
        base = reach - first_level - width - number * width
        rights = right_s.at[:, pl.ds(pl.multiple_of(base, width), 2 * width)]
        grads = grad_s.at[:, pl.ds(pl.multiple_of(base - skipped, width), 2 * width)]

        def use(pair, values):
            at = width - 2 * pair
            for group in range(groups):
                ones = [value[group * width : (group + 1) * width] for value in values]
                for c in range(group * GROUP, (group + 1) * GROUP):
                    left = left_s[c]
                    left_sum[c] += (
                        ones[0] * rights[c, at : at + width]
                        + ones[1] * rights[c, at - 1 : at - 1 + width]
                    )
                    grads[c, at : at + width] += ones[0] * left
                    grads[c, at - 1 : at - 1 + width] += ones[1] * left

        waiting = pair_values(level)
        for pair in range(1, width // 2):
            later = pair_values(level + 2 * pair)
            use(pair - 1, waiting)
            waiting = later
        use(width // 2 - 1, waiting)
        return carry

    lax.fori_loop(0, count // width, step, 0)


def upper_grads(keys, reach, far, places, *refs):
    block_refs, refs = refs[: len(keys)], refs[len(keys) :]
    right_refs, refs = refs[: far + 1], refs[far + 1 :]
    left_ref, weight_ref, cot_s, left_sum, grad_out = refs[:5]
    sent_refs, (left_s, right_s, grad_s, sems) = refs[5 : 5 + far], refs[5 + far :]
    channels, width, rows = left_ref.shape
    levels, span = block_refs[0].shape[:2]
    f32, bf16 = jnp.float32, jnp.bfloat16

    copies = []
    for at, (key, source) in enumerate(zip(keys, block_refs)):
        start = (places[0] ^ key) * levels + 1
        copies.append(pltpu.make_async_copy(source, cot_s.at[pl.ds(start, levels)], sems.at[at]))
    for copy in copies:
        copy.start()
    cot_s[0] = jnp.zeros((span, rows), bf16)
    cot_s[D + 1] = jnp.zeros((span, rows), bf16)
    left_s[...] = left_ref[...].astype(f32)
    left_sum[...] = jnp.zeros(left_sum.shape, f32)
    grad_s[...] = jnp.zeros(grad_s.shape, f32)
    hops = reach // width
    for at in range(far + 1):
        block = right_refs[at][...].astype(f32)
        right_s[:, at * width : (at + 1) * width] = jnp.where(places[1] >= hops - at, block, 0.0)
    for copy in copies:
        copy.wait()
    add_grads(
        D // 2, D // 2, reach, 0, cot_s, weight_ref, left_s, right_s, left_sum, grad_s
    )
    grad_out[...] = grad_s[:, far * width :]
    for at in range(far):
        sent_refs[at][...] = (
            grad_s[:, at * width : (at + 1) * width] * (1.0 / GROUP)
        ).astype(bf16)


def lower_grads(
    first_level, count, reach, skipped, left_ref, weight_ref, cot_s, right_s, left_part, grad_part,
    left_out, grad_out, *rest
):
    sent_refs, (left_s, left_sum, grad_s) = rest[:-3], rest[-3:]
    channels, width, rows = left_ref.shape
    f32, bf16 = jnp.float32, jnp.bfloat16
    last = first_level == 0
    scale = 1.0 / GROUP if last else 1.0
    left_s[...] = left_ref[...].astype(f32)
    left_sum[...] = left_part[...]
    grad_s[...] = grad_part[...]
    add_grads(
        first_level, count, reach, skipped, cot_s, weight_ref, left_s, right_s, left_sum, grad_s
    )
    left_out[...] = (left_sum[...] * scale).astype(left_out.dtype)
    grad_out[...] = grad_s[:, len(sent_refs) * width :] * scale
    for at, sent_ref in enumerate(sent_refs):
        sent_ref[...] = (grad_s[:, at * width : (at + 1) * width] * (1.0 / GROUP)).astype(bf16)


def kernel_sums(hops, places, *refs):
    right_refs, (left_ref, cot_s, fold_ref, right_s, sums_ref, left_s, prod_s) = (
        refs[: hops + 1], refs[hops + 1 :],
    )
    channels, width, rows = left_ref.shape
    groups = channels // GROUP
    span = cot_s.shape[1]
    outs = span // (width + 2)
    main = outs * width
    size = groups * width
    reach = hops * width
    f32, bf16 = jnp.float32, jnp.bfloat16

    left_s[...] = left_ref[...].astype(f32)
    for hop in range(hops + 1):
        at = reach - hop * width
        block = right_refs[hop][...].astype(f32)
        right_s[:, at : at + width] = jnp.where(places[1] >= hop, block, 0.0)
    prod_s[...] = jnp.zeros(prod_s.shape, f32)
    chunk = width // 2

    def step(number, carry):
        level = number * width
        base = pl.multiple_of(reach - width - level, width)
        rights = right_s.at[:, pl.ds(base, 2 * width)]

        def volume_at(d):
            at = width - d
            shifts = ([], [], [])
            for group in range(groups):
                total = None
                for c in range(group * GROUP, (group + 1) * GROUP):
                    term = left_s[c] * rights[c, at : at + width]
                    total = term if total is None else total + term
                value = (total * (1.0 / GROUP)).astype(bf16).astype(f32)
                shifts[0].append(roll_zero(value, 1))
                shifts[1].append(value)
                shifts[2].append(roll_zero(value, -1))
            return jnp.concatenate(shifts[0] + shifts[1] + shifts[2], axis=0).astype(bf16)

        for half in range(2):
            first = half * chunk
            volume = jnp.concatenate([volume_at(first + k) for k in range(chunk)], axis=1)
            for tap in range(3):
                value = jnp.concatenate(
                    [cot_s[level + first + k + tap] for k in range(chunk)], axis=1
                )
                prod_s[tap] += lax.dot_general(
                    value, volume, (((1,), (1,)), ((), ())), preferred_element_type=f32
                )
        return carry

    lax.fori_loop(0, D // width, step, 0)

    col_in = lax.broadcasted_iota(jnp.int32, (width, 3 * size), 0)
    col_out = lax.broadcasted_iota(jnp.int32, (width, 3 * size), 1) % width
    edge = lax.broadcasted_iota(jnp.int32, (outs, 3 * size), 1) % width
    for column_tap in range(3):
        mask = col_out - col_in + 1 == column_tap
        taps = []
        for tap in range(3):
            value = prod_s[tap, 0:main].reshape(outs, width, 3 * size)
            total = jnp.sum(jnp.where(mask[None], value, 0.0), axis=1)
            if column_tap == 2:
                total = total + jnp.where(edge == 0, prod_s[tap, main : main + outs], 0.0)
            if column_tap == 0:
                total = total + jnp.where(edge == width - 1, prod_s[tap, main + outs : span], 0.0)
            taps.append(total)
        gathered = jnp.concatenate(taps, axis=0)
        sums_ref[column_tap] = lax.dot_general(
            fold_ref[...], gathered, (((1,), (1,)), ((), ())),
            precision=HIGHEST, preferred_element_type=f32,
        )


VMEM = pl.BlockSpec(memory_space=pltpu.VMEM)
SMEM = pl.BlockSpec(memory_space=pltpu.SMEM)
ANY = pl.BlockSpec(memory_space=pl.ANY)
MIB = 1024 * 1024


def run(function, operands, outs, scratch, limit, flops):
    return pl.pallas_call(
        function,
        out_shape=[jax.ShapeDtypeStruct(shape, kind) for shape, kind in outs],
        in_specs=[space for space, array in operands],
        out_specs=[VMEM] * len(outs),
        scratch_shapes=scratch,
        compiler_params=pltpu.CompilerParams(vmem_limit_bytes=limit * MIB),
        cost_estimate=pl.CostEstimate(flops=flops, bytes_accessed=1024, transcendentals=0),
    )(*[array for space, array in operands])


def swapped(value, axis, bit):
    count = lax.axis_size(axis)
    return lax.ppermute(value, axis, [(source, source ^ bit) for source in range(count)])


def gather_swapping(value, axis, last_bit=1):
    held = {0: value}
    bit = lax.axis_size(axis) // 2
    while bit >= last_bit:
        held.update({key | bit: swapped(item, axis, bit) for key, item in list(held.items())})
        bit //= 2
    return held


def total_swapping(value, bit):
    return value + swapped(value, "col", bit)


def body(left, right, kernel, cotangent):
    outs, levels, width, rows = cotangent.shape
    parts = lax.axis_size("disp")
    columns = lax.axis_size("col")
    channels = C // parts
    groups = G // parts
    size = groups * width
    span = outs * (width + 2)
    hops = (D + width - 2) // width
    far = D // 2 // width
    first = (hops // 2, hops // 2 + 1)
    near = hops - far
    part, column = lax.axis_index("disp"), lax.axis_index("col")
    places = jnp.stack([part, column]).astype(jnp.int32)
    f32, bf16 = jnp.float32, jnp.bfloat16

    low = jnp.transpose(cotangent[:, :, width - 1], (1, 0, 2))
    high = jnp.transpose(cotangent[:, :, 0], (1, 0, 2))
    low, high, right = lax.optimization_barrier((low, high, right))
    low, high = shifted(low, "col", 1), shifted(high, "col", -1)
    cots = gather_swapping(cotangent, "disp", 2)
    right_own = lax.dynamic_slice_in_dim(right, part * channels, channels, 0)
    left_own = lax.dynamic_slice_in_dim(left, part * channels, channels, 0)
    weights = toeplitz(lax.dynamic_slice_in_dim(kernel, part * groups, groups, 4), width)
    rights = [right_own] + [None] * hops
    for hop in (4, 3):
        rights[hop] = shifted(right_own, "col", hop)
    right_late, low, high, left_own, weights, *rights[3:5] = lax.optimization_barrier(
        (right_own, low, high, left_own, weights, *rights[3:5])
    )
    low = jnp.where(column > 0, low, 0).astype(bf16)
    high = jnp.where(column < columns - 1, high, 0).astype(bf16)
    halos = gather_swapping(jnp.concatenate([low, high], axis=1), "disp", 2)
    for hop in (5, 6):
        rights[hop] = shifted(right_late, "col", hop)
    blocks = {}
    across = parts // 2
    cots[across], *rights[5:] = lax.optimization_barrier((cots[across], *rights[5:]))
    for key in cots:
        (block,) = run(
            pack, [(VMEM, cots[key]), (VMEM, halos[key])],
            [((levels, span, rows), bf16)], [], 4, 1000000000,
        )
        if key == across:
            right_last = lax.optimization_barrier((right_own, block))[0]
        blocks[key] = block
        blocks[key | 1] = swapped(block, "disp", 1)
    for hop in (2, 1):
        rights[hop] = shifted(right_last, "col", hop)

    pad_rows = -(-3 * groups // 8) * 8
    fold = np.zeros((pad_rows, 3 * size), np.float32)
    fold[np.arange(3 * size) // width, np.arange(3 * size)] = 1

    block = (channels, width, rows)
    wide = (channels, (hops + 1) * width, rows)
    f32_block, bf16_block = (block, f32), (block, bf16)
    reach = hops * width
    keys = sorted(blocks)
    cot_wide, left_part, grad_part, *sent = run(
        functools.partial(upper_grads, keys, reach, far),
        [(SMEM, places)]
        + [(ANY, blocks[key]) for key in keys]
        + [(VMEM, rights[hop]) for hop in range(hops, near - 1, -1)]
        + [(VMEM, left_own), (VMEM, weights)],
        [
            ((D + 2, span, rows), bf16),
            f32_block,
            ((channels, (near + 1) * width, rows), f32),
            *[bf16_block] * far,
        ],
        [
            pltpu.VMEM(block, f32),
            pltpu.VMEM((channels, (far + 1) * width, rows), f32),
            pltpu.VMEM(wide, f32),
            pltpu.SemaphoreType.DMA((parts,)),
        ],
        12, 8000000000,
    )
    arrived = {
        hop: shifted(value, "col", -hop) for hop, value in zip(range(hops, near, -1), sent)
    }
    right_wide, total = run(
        functools.partial(kernel_sums, hops),
        [(SMEM, places)]
        + [(VMEM, item) for item in (*rights, left_own, cot_wide, jnp.asarray(fold))],
        [(wide, f32), ((3, pad_rows, 3 * outs), f32)],
        [pltpu.VMEM(block, f32), pltpu.VMEM((3, span, 3 * size), f32)],
        12, 8000000000,
    )
    bits = [1 << k for k in reversed(range(columns.bit_length() - 1))]
    middle = near - 1

    def lower(first_level, count, done, kind, left_part, grad_part):
        skipped = (far + done) * width
        rest = near + 1 - done
        complete = rest - 1 if first_level == 0 else rest - 2
        return run(
            functools.partial(lower_grads, first_level, count, reach, skipped),
            [
                (VMEM, item)
                for item in (left_own, weights, cot_wide, right_wide, left_part, grad_part)
            ],
            [
                (block, kind),
                ((channels, (rest - complete) * width, rows), f32),
                *[bf16_block] * complete,
            ],
            [
                pltpu.VMEM(block, f32),
                pltpu.VMEM(block, f32),
                pltpu.VMEM((channels, rest * width, rows), f32),
            ],
            8, 4000000000,
        )

    grad_part, total, arrived[hops], arrived[hops - 1] = lax.optimization_barrier(
        (grad_part, total, arrived[hops], arrived[hops - 1])
    )
    left_part, grad_part, *sent = lower(width, D // 2 - width, 0, f32, left_part, grad_part)
    total = total_swapping(total, bits[0])
    sent, grad_part, total, arrived[hops - 2] = lax.optimization_barrier(
        (sent, grad_part, total, arrived[hops - 2])
    )
    arrived.update(
        {hop: shifted(value, "col", -hop) for hop, value in zip(range(near, 1, -1), sent)}
    )
    grad_left, own, *sent = lower(0, width, middle, bf16, left_part, grad_part)
    total = total_swapping(total, bits[1])
    arrived[1] = shifted(sent[0], "col", -1)
    for bit in bits[2:]:
        total = total_swapping(total, bit)
    total, arrived[1] = lax.optimization_barrier((total, arrived[1]))

    total_right = own
    for hop in range(1, hops + 1):
        total_right = total_right + jnp.where(
            column + hop < columns, arrived[hop].astype(f32), 0.0
        )

    held = gather_swapping(total, "disp")
    pieces = jnp.stack([held[key] for key in sorted(held)])
    pieces = pieces[jnp.arange(parts) ^ part][:, :, : 3 * groups]
    total = pieces.reshape(parts, 3, 3, groups, 3, outs)
    cell_count = D * width * columns * rows
    grad_kernel = jnp.transpose(total, (4, 1, 2, 5, 0, 3))[::-1].reshape(3, 3, 3, outs, G)
    grad_kernel = grad_kernel * (1.0 / math.sqrt(cell_count))
    return (grad_left, total_right.astype(bf16), grad_kernel)


def solution(mesh):
    return jax.shard_map(
        body,
        mesh=mesh,
        in_specs=(P(None, "col", None), P(None, "col", None), P(), P(None, "disp", "col", None)),
        out_specs=(P("disp", "col", None), P("disp", "col", None), P()),
        check_vma=False,
    )
```

time: 104 us -> 97.9 us (0.941)
  the two profiles are of different devices: /device:TPU:6 before, /device:TPU:0 now
where the time goes in v8:
time: 97.9 us; the launch traced here: 97.7 us
  starting transfers between devices  40.4 us (41%)
  waiting for transfers between devices  24.9 us (25%)
  Pallas kernels  19 us (19%)
  local copies, waits for them, and re-layouts  8.52 us (9%)
  other arithmetic  3.49 us (4%)
  between operations  1 us (1%)
    ppermute x14, starting transfers between devices, shifted(): lax.ppermute(value, axis, [(source, (source + steps) % count) for source...  34.2 us
    pallas_call x6, Pallas kernels, run(): pl.pallas_call(function, out_shape=[jax.ShapeDtypeStruct(shape, kind) for...  19 us
    ppermute x10, waiting for transfers between devices, swapped(): lax.ppermute(value, axis, [(source, source ^ bit) for source in range(cou...  13.6 us
    ppermute x14, waiting for transfers between devices, shifted(): lax.ppermute(value, axis, [(source, (source + steps) % count) for source...  11.3 us
    ppermute x10, starting transfers between devices, swapped(): lax.ppermute(value, axis, [(source, source ^ bit) for source in range(cou...  6.2 us
  transfers between devices with their start and end apart: 24, of which 9 were waited for; matrix products, arithmetic and copies ran while one was open for 8% of the time, Pallas kernels for 17%

profile of v8, /device:TPU:0, one launch (start us, length us, event | category | flops | bytes accessed | tf_op | source)
XLA Modules:
  0.0 97.7 jit_solution(2566796689205416610)
XLA Ops:
  0.7 1.9 %fusion.2 = (bf16[32,12,1,128]{3,2,1,0:T(2,128)(2,1)S(1)}, bf16[32,12,1,128]{3,2,1,0:T(2,128)(2,1)S(1)}) fusion(bf16[32,12,8,128]{3,2,1,0:T(8,128)(2,1)} %cot_ref.1), kind=kLoop, calls=%fused_computation.24 | loop fusion | bytes 393216 | tf_op jit(solution)/shard_map/slice | solution.py:307
  3.3 4.0 %collective-permute-start.2 = (bf16[80,8,128]{2,1,0:T(8,128)(2,1)S(1)}, bf16[80,8,128]{2,1,0:T(8,128)(2,1)S(1)}, u32[]{:S(2)}, u32[]{:S(2)}) collective-permute-start(bf16[80,8,128]{2,1,0:T(8,128)(2,1)S(1)} %constant_dynamic-slice_fusion.2.refs_0_), channel_id=1, source_target_pairs={{0,12},{4,16},{8,20},{12,24},{16,28},{20,0},{24,4},{28,8},{1,13},{... | collective-permute-start | bytes 491528 | tf_op jit(solution)/shard_map/ppermute | solution.py:21
  7.3 2.6 %collective-permute-start.3 = (bf16[80,8,128]{2,1,0:T(8,128)(2,1)S(1)}, bf16[80,8,128]{2,1,0:T(8,128)(2,1)S(1)}, u32[]{:S(2)}, u32[]{:S(2)}) collective-permute-start(bf16[80,8,128]{2,1,0:T(8,128)(2,1)S(1)} %constant_dynamic-slice_fusion.2.refs_0_), channel_id=1, source_target_pairs={{0,16},{4,20},{8,24},{12,28},{16,0},{20,4},{24,8},{28,12},{1,17},{... | collective-permute-start | bytes 491528 | tf_op jit(solution)/shard_map/ppermute | solution.py:21
  9.9 1.5 %collective-permute-start.5 = (bf16[32,12,8,128]{3,2,1,0:T(8,128)(2,1)}, bf16[32,12,8,128]{3,2,1,0:T(8,128)(2,1)S(1)}, u32[]{:S(2)}, u32[]{:S(2)}) collective-permute-start(bf16[32,12,8,128]{3,2,1,0:T(8,128)(2,1)} %cot_ref.1), channel_id=1, source_target_pairs={{0,2},{1,3},{2,0},{3,1},{4,6},{5,7},{6,4},{7,5},{8,10},{9,11},{10,... | collective-permute-start | bytes 2359304 | tf_op jit(solution)/shard_map/ppermute | solution.py:274
  11.4 4.7 %collective-permute-start.1 = (bf16[12,32,128]{2,1,0:T(8,128)(2,1)S(1)}, bf16[12,32,128]{2,1,0:T(8,128)(2,1)}, u32[]{:S(2)}, u32[]{:S(2)}) collective-permute-start(bf16[12,32,128]{2,1,0:T(8,128)(2,1)S(1)} %get-tuple-element.45), channel_id=1, source_target_pairs={{0,28},{4,0},{8,4},{12,8},{16,12},{20,16},{24,20},{28,24},{1,29},{... | collective-permute-start | bytes 294920 | tf_op jit(solution)/shard_map/ppermute | solution.py:21
  16.1 1.1 %constant_dynamic-slice_fusion = bf16[3,3,3,32,10]{4,3,2,1,0:T(8,128)(2,1)S(1)} fusion(bf16[3,3,3,32,40]{4,3,2,1,0:T(8,128)(2,1)} %param.11, s32[]{:T(128)S(6)} %select_n.88), kind=kLoop, calls=%fused_computation.19 | loop fusion | bytes 34564 | tf_op jit(solution)/shard_map/dynamic_slice | solution.py:313
  17.7 1.4 %select_select_fusion = bf16[3,10,8,3,320]{4,3,2,1,0:T(4,128)(2,1)} fusion(pred[8,320]{1,0:T(8,128)(4,1)S(1)} %copy-done.4, pred[8,320]{1,0:T(8,128)(4,1)S(1)} %copy-done.5, pred[8,320]{1,0:T(8,128)(4,1)S(1)} %copy-done.6, bf16[3,10,3,320]{3,2,1,0:T(4,128)(2,1)S(1)} %copy.33, bf16[3,10,3,320]{3,2,1,0:T(4,128)(2,1)S(1)} %copy.32, ...), kind=kLoop, calls=%fused_computation.2 | loop fusion | flops 691200 | bytes 641280 | tf_op jit(solution)/shard_map/jit(_where)/select_n | solution.py:45
  19.1 0.9 constant_dynamic-slice_fusion.1.refs_8_.refs_7_.left_ref
  20.0 1.7 %select_n.92.refs_9_.weight_ref = bf16[240,960]{1,0:T(8,128)(2,1)S(1)} reshape(bf16[3,10,8,3,320]{4,3,2,1,0:T(4,128)(2,1)} %select_select_fusion) | data formatting | bytes 921600 | tf_op jit(solution)/shard_map/jit(_where)/select_n | solution.py:45
  21.8 0.7 collective-permute-done.2.refs_7_.refs_3_
  22.5 0.9 broadcast_select_fusion
  23.4 1.9 %collective-permute-start.8 = (bf16[12,64,128]{2,1,0:T(8,128)(2,1)S(1)}, bf16[12,64,128]{2,1,0:T(8,128)(2,1)S(1)}, u32[]{:S(2)}, u32[]{:S(2)}) collective-permute-start(bf16[12,64,128]{2,1,0:T(8,128)(2,1)S(1)} %pad_maximum_fusion.halo_ref), channel_id=1, source_target_pairs={{0,2},{1,3},{2,0},{3,1},{4,6},{5,7},{6,4},{7,5},{8,10},{9,11},{10,... | collective-permute-start | bytes 589832 | tf_op jit(solution)/shard_map/ppermute | solution.py:274
  25.3 2.8 %collective-permute-start.6 = (bf16[80,8,128]{2,1,0:T(8,128)(2,1)S(1)}, bf16[80,8,128]{2,1,0:T(8,128)(2,1)S(1)}, u32[]{:S(2)}, u32[]{:S(2)}) collective-permute-start(bf16[80,8,128]{2,1,0:T(8,128)(2,1)S(1)} %constant_dynamic-slice_fusion.2.refs_0_), channel_id=1, source_target_pairs={{0,20},{4,24},{8,28},{12,0},{16,4},{20,8},{24,12},{28,16},{1,21},{... | collective-permute-start | bytes 491528 | tf_op jit(solution)/shard_map/ppermute | solution.py:21
  28.1 3.6 %collective-permute-start.7 = (bf16[80,8,128]{2,1,0:T(8,128)(2,1)S(1)}, bf16[80,8,128]{2,1,0:T(8,128)(2,1)S(1)}, u32[]{:S(2)}, u32[]{:S(2)}) collective-permute-start(bf16[80,8,128]{2,1,0:T(8,128)(2,1)S(1)} %constant_dynamic-slice_fusion.2.refs_0_), channel_id=1, source_target_pairs={{0,24},{4,28},{8,0},{12,4},{16,8},{20,12},{24,16},{28,20},{1,25},{... | collective-permute-start | bytes 491528 | tf_op jit(solution)/shard_map/ppermute | solution.py:21
  32.0 2.4 %collective-permute-done.6.refs_5_ = bf16[80,8,128]{2,1,0:T(8,128)(2,1)S(1)} collective-permute-done((bf16[80,8,128]{2,1,0:T(8,128)(2,1)S(1)}, bf16[80,8,128]{2,1,0:T(8,128)(2,1)S(1)}, u32[]{:S(2)}, u32[]{:S(2)}) %collective-permute-start.6) | collective-permute-done | bytes 163872 | tf_op jit(solution)/shard_map/ppermute | solution.py:21
  35.2 5.8 %collective-permute-start.10 = (bf16[80,8,128]{2,1,0:T(8,128)(2,1)S(1)}, bf16[80,8,128]{2,1,0:T(8,128)(2,1)S(1)}, u32[]{:S(2)}, u32[]{:S(2)}) collective-permute-start(bf16[80,8,128]{2,1,0:T(8,128)(2,1)S(1)} %constant_dynamic-slice_fusion.2.refs_0_), channel_id=1, source_target_pairs={{0,4},{4,8},{8,12},{12,16},{16,20},{20,24},{24,28},{28,0},{1,5},{5... | collective-permute-start | bytes 491528 | tf_op jit(solution)/shard_map/ppermute | solution.py:21
  41.0 2.4 %collective-permute-start.11 = (bf16[80,8,128]{2,1,0:T(8,128)(2,1)S(1)}, bf16[80,8,128]{2,1,0:T(8,128)(2,1)S(1)}, u32[]{:S(2)}, u32[]{:S(2)}) collective-permute-start(bf16[80,8,128]{2,1,0:T(8,128)(2,1)S(1)} %constant_dynamic-slice_fusion.2.refs_0_), channel_id=1, source_target_pairs={{0,8},{4,12},{8,16},{12,20},{16,24},{20,28},{24,0},{28,4},{1,9},{5... | collective-permute-start | bytes 491528 | tf_op jit(solution)/shard_map/ppermute | solution.py:21
  43.4 6.5 %shard_map.114 = (bf16[50,320,128]{2,1,0:T(8,128)(2,1)S(1)}, f32[80,8,128]{2,1,0:T(8,128)S(1)}, f32[80,32,128]{2,1,0:T(8,128)S(1)}, bf16[80,8,128]{2,1,0:T(8,128...) custom-call(s32[2]{0:T(128)S(1)} %pad_add_fusion.places, ...), custom_call_target="tpu_custom_call" | custom-call | flops 8000000000 | bytes 1024 | tf_op jit(solution)/shard_map/pallas_call | solution.py:261
  49.9 2.4 %collective-permute-start.12 = (bf16[80,8,128]{2,1,0:T(8,128)(2,1)S(1)}, bf16[80,8,128]{2,1,0:T(8,128)(2,1)S(1)}, u32[]{:S(2)}, u32[]{:S(2)}) collective-permute-start(bf16[80,8,128]{2,1,0:T(8,128)(2,1)S(1)} %get-tuple-element.62), channel_id=1, source_target_pairs={{0,8},{4,12},{8,16},{12,20},{16,24},{20,28},{24,0},{28,4},{1,9},{5... | collective-permute-start | bytes 491528 | tf_op jit(solution)/shard_map/ppermute | solution.py:21
  52.3 2.9 %collective-permute-start.15 = (bf16[80,8,128]{2,1,0:T(8,128)(2,1)S(1)}, bf16[80,8,128]{2,1,0:T(8,128)(2,1)S(1)}, u32[]{:S(2)}, u32[]{:S(2)}) collective-permute-start(bf16[80,8,128]{2,1,0:T(8,128)(2,1)S(1)} %get-tuple-element.70), channel_id=1, source_target_pairs={{0,16},{4,20},{8,24},{12,28},{16,0},{20,4},{24,8},{28,12},{1,17},{... | collective-permute-start | bytes 491528 | tf_op jit(solution)/shard_map/ppermute | solution.py:21
  55.2 7.0 %shard_map.115 = (f32[80,56,128]{2,1,0:T(8,128)S(1)}, f32[3,32,96]{2,1,0:T(8,128)S(1)}) custom-call(s32[2]{0:T(128)S(1)} %pad_add_fusion.places, bf16[80,8,128]{2,1,0:T(8,128)(2,1)S(1)} %constant_dynamic-slice_fusion.2.refs_0_, bf16[80,8,128]{2,1,0:T(8,128)(2,1)S(1)} %collective-permute-done.10.refs_1_, ...), custom_call_target="tpu_custom_call" | custom-call | flops 8000000000 | bytes 1024 | tf_op jit(solution)/shard_map/pallas_call | solution.py:261
  62.2 7.8 %collective-permute-done.13 = bf16[80,8,128]{2,1,0:T(8,128)(2,1)S(1)} collective-permute-done((bf16[80,8,128]{2,1,0:T(8,128)(2,1)S(1)}, bf16[80,8,128]{2,1,0:T(8,128)(2,1)S(1)}, u32[]{:S(2)}, u32[]{:S(2)}) %collective-permute-start.13) | collective-permute-done | bytes 163872 | tf_op jit(solution)/shard_map/ppermute | solution.py:21
  70.0 3.1 %shard_map.116 = (f32[80,8,128]{2,1,0:T(8,128)S(1)}, f32[80,16,128]{2,1,0:T(8,128)S(1)}, bf16[80,8,128]{2,1,0:T(8,128)(2,1)S(1)}, bf16[80,8,128]{2,1,0:T(8,128)(2,1)S(1)}) custom-call(bf16[80,8,128]{2,1,0:T(8,128)(2,1)S(1)} %constant_dynamic-slice_fusion.1.refs_8_.refs_7_.left_ref, bf16[240,960]{1,0:T(8,128)(2,1)S(1)} %select_n.92.refs_9_.weight_ref, ...), custom_call_target="tpu_custom_call" | custom-call | flops 4000000000 | bytes 1024 | tf_op jit(solution)/shard_map/pallas_call | solution.py:261
  73.1 1.9 %collective-permute-done.14 = f32[3,32,96]{2,1,0:T(8,128)S(1)} collective-permute-done((f32[3,32,96]{2,1,0:T(8,128)S(1)}, f32[3,32,96]{2,1,0:T(8,128)S(1)}, u32[]{:S(2)}, u32[]{:S(2)}) %collective-permute-start.14) | collective-permute-done | bytes 36896 | tf_op jit(solution)/shard_map/ppermute | solution.py:274
  75.0 2.0 %shard_map.117 = (bf16[80,8,128]{2,1,0:T(8,128)(2,1)}, f32[80,8,128]{2,1,0:T(8,128)S(1)}, bf16[80,8,128]{2,1,0:T(8,128)(2,1)S(1)}) custom-call(bf16[80,8,128]{2,1,0:T(8,128)(2,1)S(1)} %constant_dynamic-slice_fusion.1.refs_8_.refs_7_.left_ref, bf16[240,960]{1,0:T(8,128)(2,1)S(1)} %select_n.92.refs_9_.weight_ref, ...), custom_call_target="tpu_custom_call" | custom-call | flops 4000000000 | bytes 1024 | tf_op jit(solution)/shard_map/pallas_call | solution.py:261
  77.1 2.0 %collective-permute-start.16 = (f32[3,32,96]{2,1,0:T(8,128)S(1)}, f32[3,32,96]{2,1,0:T(8,128)S(1)}, u32[]{:S(2)}, u32[]{:S(2)}) collective-permute-start(f32[3,32,96]{2,1,0:T(8,128)S(1)} %add.64), channel_id=1, source_target_pairs={{0,8},{4,12},{8,0},{12,4},{16,24},{20,28},{24,16},{28,20},{1,9},{5... | collective-permute-start | bytes 110600 | tf_op jit(solution)/shard_map/ppermute | solution.py:274
  79.6 2.4 %collective-permute-start.20 = (bf16[80,8,128]{2,1,0:T(8,128)(2,1)S(1)}, bf16[80,8,128]{2,1,0:T(8,128)(2,1)S(1)}, u32[]{:S(2)}, u32[]{:S(2)}) collective-permute-start(bf16[80,8,128]{2,1,0:T(8,128)(2,1)S(1)} %get-tuple-element.78), channel_id=1, source_target_pairs={{0,20},{4,24},{8,28},{12,0},{16,4},{20,8},{24,12},{28,16},{1,21},{... | collective-permute-start | bytes 491528 | tf_op jit(solution)/shard_map/ppermute | solution.py:21
  82.0 3.8 %collective-permute-done.16 = f32[3,32,96]{2,1,0:T(8,128)S(1)} collective-permute-done((f32[3,32,96]{2,1,0:T(8,128)S(1)}, f32[3,32,96]{2,1,0:T(8,128)S(1)}, u32[]{:S(2)}, u32[]{:S(2)}) %collective-permute-start.16) | collective-permute-done | bytes 36896 | tf_op jit(solution)/shard_map/ppermute | solution.py:274
  85.9 4.1 %collective-permute-done.17 = f32[3,32,96]{2,1,0:T(8,128)S(1)} collective-permute-done((f32[3,32,96]{2,1,0:T(8,128)S(1)}, f32[3,32,96]{2,1,0:T(8,128)S(1)}, u32[]{:S(2)}, u32[]{:S(2)}) %collective-permute-start.17) | collective-permute-done | bytes 36896 | tf_op jit(solution)/shard_map/ppermute | solution.py:274
  90.6 3.5 %collective-permute-done.22 = f32[3,32,96]{2,1,0:T(8,128)S(1)} collective-permute-done((f32[3,32,96]{2,1,0:T(8,128)S(1)}, f32[3,32,96]{2,1,0:T(8,128)S(1)}, u32[]{:S(2)}, u32[]{:S(2)}) %collective-permute-start.22) | collective-permute-done | bytes 36896 | tf_op jit(solution)/shard_map/ppermute | solution.py:274
  94.1 0.9 add_convert_fusion
  96.7 1.0 copy.37
  (67 shorter events, 5.2 us)
Async XLA Ops:
  0.6 2.6 %copy-start = (bf16[320,8,128]{2,1,0:T(8,128)(2,1)S(1)}, bf16[320,8,128]{2,1,0:T(8,128)(2,1)}, u32[]{:S(2)}) copy-start(bf16[320,8,128]{2,1,0:T(8,128)(2,1)} %param.10) | copy-start | bytes 1966084
  0.6 16.5 %copy-start.3 = (bf16[32,320,1,1,1]{1,0,4,3,2:T(8,128)(2,1)S(1)}, bf16[32,320,1,1,1]{1,0,4,3,2:T(8,128)(2,1)}, u32[]{:S(2)}) copy-start(bf16[32,320,1,1,1]{1,0,4,3,2:T(8,128)(2,1)} %constant.59) | copy-start | bytes 61444
  0.7 17.0 %copy-start.4 = (pred[8,320]{1,0:T(8,128)(4,1)S(1)}, pred[8,320]{1,0:T(8,128)(4,1)}, u32[]{:S(2)}) copy-start(pred[8,320]{1,0:T(8,128)(4,1)} %constant.55.clone) | copy-start | bytes 7684
  0.7 17.0 %copy-start.5 = (pred[8,320]{1,0:T(8,128)(4,1)S(1)}, pred[8,320]{1,0:T(8,128)(4,1)}, u32[]{:S(2)}) copy-start(pred[8,320]{1,0:T(8,128)(4,1)} %constant.56.clone) | copy-start | bytes 7684
  0.7 17.0 %copy-start.6 = (pred[8,320]{1,0:T(8,128)(4,1)S(1)}, pred[8,320]{1,0:T(8,128)(4,1)}, u32[]{:S(2)}) copy-start(pred[8,320]{1,0:T(8,128)(4,1)} %constant.57.clone) | copy-start | bytes 7684
  3.3 19.2 %collective-permute-start.2 = (bf16[80,8,128]{2,1,0:T(8,128)(2,1)S(1)}, bf16[80,8,128]{2,1,0:T(8,128)(2,1)S(1)}, u32[]{:S(2)}, u32[]{:S(2)}) collective-permute-start(bf16[80,8,128]{2,1,0:T(8,128)(2,1)S(1)} %constant_dynamic-slice_fusion.2.refs_0_), channel_id=1, source_target_pairs={{0,12},{4,16},{8,20},{12,24},{16,28},{20,0},{24,4},{28,8},{1,13},{... | collective-permute-start | bytes 491528 | tf_op jit(solution)/shard_map/ppermute | solution.py:21
  7.3 15.2 %collective-permute-start.3 = (bf16[80,8,128]{2,1,0:T(8,128)(2,1)S(1)}, bf16[80,8,128]{2,1,0:T(8,128)(2,1)S(1)}, u32[]{:S(2)}, u32[]{:S(2)}) collective-permute-start(bf16[80,8,128]{2,1,0:T(8,128)(2,1)S(1)} %constant_dynamic-slice_fusion.2.refs_0_), channel_id=1, source_target_pairs={{0,16},{4,20},{8,24},{12,28},{16,0},{20,4},{24,8},{28,12},{1,17},{... | collective-permute-start | bytes 491528 | tf_op jit(solution)/shard_map/ppermute | solution.py:21
  9.9 24.9 %collective-permute-start.5 = (bf16[32,12,8,128]{3,2,1,0:T(8,128)(2,1)}, bf16[32,12,8,128]{3,2,1,0:T(8,128)(2,1)S(1)}, u32[]{:S(2)}, u32[]{:S(2)}) collective-permute-start(bf16[32,12,8,128]{3,2,1,0:T(8,128)(2,1)} %cot_ref.1), channel_id=1, source_target_pairs={{0,2},{1,3},{2,0},{3,1},{4,6},{5,7},{6,4},{7,5},{8,10},{9,11},{10,... | collective-permute-start | bytes 2359304 | tf_op jit(solution)/shard_map/ppermute | solution.py:274
  11.4 10.4 %collective-permute-start = (bf16[12,32,128]{2,1,0:T(8,128)(2,1)}, bf16[12,32,128]{2,1,0:T(8,128)(2,1)}, u32[]{:S(2)}, u32[]{:S(2)}) collective-permute-start(bf16[12,32,128]{2,1,0:T(8,128)(2,1)} %get-tuple-element.44), channel_id=1, source_target_pairs={{0,4},{4,8},{8,12},{12,16},{16,20},{20,24},{24,28},{28,0},{1,5},{5... | collective-permute-start | bytes 294920 | tf_op jit(solution)/shard_map/ppermute | solution.py:21
  11.4 10.4 %collective-permute-start.1 = (bf16[12,32,128]{2,1,0:T(8,128)(2,1)S(1)}, bf16[12,32,128]{2,1,0:T(8,128)(2,1)}, u32[]{:S(2)}, u32[]{:S(2)}) collective-permute-start(bf16[12,32,128]{2,1,0:T(8,128)(2,1)S(1)} %get-tuple-element.45), channel_id=1, source_target_pairs={{0,28},{4,0},{8,4},{12,8},{16,12},{20,16},{24,20},{28,24},{1,29},{... | collective-permute-start | bytes 294920 | tf_op jit(solution)/shard_map/ppermute | solution.py:21
  17.5 14.2 %copy-start.1 = (bf16[32,12,8,128]{3,2,1,0:T(8,128)(2,1)S(1)}, bf16[32,12,8,128]{3,2,1,0:T(8,128)(2,1)}, u32[]{:S(2)}) copy-start(bf16[32,12,8,128]{3,2,1,0:T(8,128)(2,1)} %cot_ref.1) | copy-start | bytes 2359300
  23.4 11.4 %collective-permute-start.8 = (bf16[12,64,128]{2,1,0:T(8,128)(2,1)S(1)}, bf16[12,64,128]{2,1,0:T(8,128)(2,1)S(1)}, u32[]{:S(2)}, u32[]{:S(2)}) collective-permute-start(bf16[12,64,128]{2,1,0:T(8,128)(2,1)S(1)} %pad_maximum_fusion.halo_ref), channel_id=1, source_target_pairs={{0,2},{1,3},{2,0},{3,1},{4,6},{5,7},{6,4},{7,5},{8,10},{9,11},{10,... | collective-permute-start | bytes 589832 | tf_op jit(solution)/shard_map/ppermute | solution.py:274
  25.3 9.1 %collective-permute-start.6 = (bf16[80,8,128]{2,1,0:T(8,128)(2,1)S(1)}, bf16[80,8,128]{2,1,0:T(8,128)(2,1)S(1)}, u32[]{:S(2)}, u32[]{:S(2)}) collective-permute-start(bf16[80,8,128]{2,1,0:T(8,128)(2,1)S(1)} %constant_dynamic-slice_fusion.2.refs_0_), channel_id=1, source_target_pairs={{0,20},{4,24},{8,28},{12,0},{16,4},{20,8},{24,12},{28,16},{1,21},{... | collective-permute-start | bytes 491528 | tf_op jit(solution)/shard_map/ppermute | solution.py:21
  28.1 6.7 %collective-permute-start.7 = (bf16[80,8,128]{2,1,0:T(8,128)(2,1)S(1)}, bf16[80,8,128]{2,1,0:T(8,128)(2,1)S(1)}, u32[]{:S(2)}, u32[]{:S(2)}) collective-permute-start(bf16[80,8,128]{2,1,0:T(8,128)(2,1)S(1)} %constant_dynamic-slice_fusion.2.refs_0_), channel_id=1, source_target_pairs={{0,24},{4,28},{8,0},{12,4},{16,8},{20,12},{24,16},{28,20},{1,25},{... | collective-permute-start | bytes 491528 | tf_op jit(solution)/shard_map/ppermute | solution.py:21
  31.9 11.5 %collective-permute-start.4 = (bf16[12,320,128]{2,1,0:T(8,128)(2,1)S(1)}, bf16[12,320,128]{2,1,0:T(8,128)(2,1)S(1)}, u32[]{:S(2)}, u32[]{:S(2)}) collective-permute-start(bf16[12,320,128]{2,1,0:T(8,128)(2,1)S(1)} %shard_map.112.refs_0_), channel_id=1, source_target_pairs={{0,1},{1,0},{2,3},{3,2},{4,5},{5,4},{6,7},{7,6},{8,9},{9,8},{10,11... | collective-permute-start | bytes 2949128 | tf_op jit(solution)/shard_map/ppermute | solution.py:274
  35.0 8.4 %collective-permute-start.9 = (bf16[12,320,128]{2,1,0:T(8,128)(2,1)S(1)}, bf16[12,320,128]{2,1,0:T(8,128)(2,1)S(1)}, u32[]{:S(2)}, u32[]{:S(2)}) collective-permute-start(bf16[12,320,128]{2,1,0:T(8,128)(2,1)S(1)} %shard_map.113.refs_2_), channel_id=1, source_target_pairs={{0,1},{1,0},{2,3},{3,2},{4,5},{5,4},{6,7},{7,6},{8,9},{9,8},{10,11... | collective-permute-start | bytes 2949128 | tf_op jit(solution)/shard_map/ppermute | solution.py:274
  35.2 20.1 %copy-start.2 = (f32[32,240]{1,0:T(8,128)S(1)}, f32[32,240]{1,0:T(8,128)}, u32[]{:S(2)}) copy-start(f32[32,240]{1,0:T(8,128)} %constant.58.clone.refs_9_) | copy-start | bytes 92164
  35.2 20.0 %collective-permute-start.10 = (bf16[80,8,128]{2,1,0:T(8,128)(2,1)S(1)}, bf16[80,8,128]{2,1,0:T(8,128)(2,1)S(1)}, u32[]{:S(2)}, u32[]{:S(2)}) collective-permute-start(bf16[80,8,128]{2,1,0:T(8,128)(2,1)S(1)} %constant_dynamic-slice_fusion.2.refs_0_), channel_id=1, source_target_pairs={{0,4},{4,8},{8,12},{12,16},{16,20},{20,24},{24,28},{28,0},{1,5},{5... | collective-permute-start | bytes 491528 | tf_op jit(solution)/shard_map/ppermute | solution.py:21
  41.0 14.2 %collective-permute-start.11 = (bf16[80,8,128]{2,1,0:T(8,128)(2,1)S(1)}, bf16[80,8,128]{2,1,0:T(8,128)(2,1)S(1)}, u32[]{:S(2)}, u32[]{:S(2)}) collective-permute-start(bf16[80,8,128]{2,1,0:T(8,128)(2,1)S(1)} %constant_dynamic-slice_fusion.2.refs_0_), channel_id=1, source_target_pairs={{0,8},{4,12},{8,16},{12,20},{16,24},{20,28},{24,0},{28,4},{1,9},{5... | collective-permute-start | bytes 491528 | tf_op jit(solution)/shard_map/ppermute | solution.py:21
  49.9 12.3 %collective-permute-start.12 = (bf16[80,8,128]{2,1,0:T(8,128)(2,1)S(1)}, bf16[80,8,128]{2,1,0:T(8,128)(2,1)S(1)}, u32[]{:S(2)}, u32[]{:S(2)}) collective-permute-start(bf16[80,8,128]{2,1,0:T(8,128)(2,1)S(1)} %get-tuple-element.62), channel_id=1, source_target_pairs={{0,8},{4,12},{8,16},{12,20},{16,24},{20,28},{24,0},{28,4},{1,9},{5... | collective-permute-start | bytes 491528 | tf_op jit(solution)/shard_map/ppermute | solution.py:21
  52.3 17.7 %collective-permute-start.13 = (bf16[80,8,128]{2,1,0:T(8,128)(2,1)S(1)}, bf16[80,8,128]{2,1,0:T(8,128)(2,1)S(1)}, u32[]{:S(2)}, u32[]{:S(2)}) collective-permute-start(bf16[80,8,128]{2,1,0:T(8,128)(2,1)S(1)} %get-tuple-element.63), channel_id=1, source_target_pairs={{0,12},{4,16},{8,20},{12,24},{16,28},{20,0},{24,4},{28,8},{1,13},{... | collective-permute-start | bytes 491528 | tf_op jit(solution)/shard_map/ppermute | solution.py:21
  52.3 22.7 %collective-permute-start.15 = (bf16[80,8,128]{2,1,0:T(8,128)(2,1)S(1)}, bf16[80,8,128]{2,1,0:T(8,128)(2,1)S(1)}, u32[]{:S(2)}, u32[]{:S(2)}) collective-permute-start(bf16[80,8,128]{2,1,0:T(8,128)(2,1)S(1)} %get-tuple-element.70), channel_id=1, source_target_pairs={{0,16},{4,20},{8,24},{12,28},{16,0},{20,4},{24,8},{28,12},{1,17},{... | collective-permute-start | bytes 491528 | tf_op jit(solution)/shard_map/ppermute | solution.py:21
  70.0 5.0 %collective-permute-start.14 = (f32[3,32,96]{2,1,0:T(8,128)S(1)}, f32[3,32,96]{2,1,0:T(8,128)S(1)}, u32[]{:S(2)}, u32[]{:S(2)}) collective-permute-start(f32[3,32,96]{2,1,0:T(8,128)S(1)} %get-tuple-element.69), channel_id=1, source_target_pairs={{0,16},{4,20},{8,24},{12,28},{16,0},{20,4},{24,8},{28,12},{1,17},{... | collective-permute-start | bytes 110600 | tf_op jit(solution)/shard_map/ppermute | solution.py:274
  77.0 12.9 %collective-permute-start.18 = (bf16[80,8,128]{2,1,0:T(8,128)(2,1)S(1)}, bf16[80,8,128]{2,1,0:T(8,128)(2,1)S(1)}, u32[]{:S(2)}, u32[]{:S(2)}) collective-permute-start(bf16[80,8,128]{2,1,0:T(8,128)(2,1)S(1)} %get-tuple-element.75), channel_id=1, source_target_pairs={{0,28},{4,0},{8,4},{12,8},{16,12},{20,16},{24,20},{28,24},{1,29},{... | collective-permute-start | bytes 491528 | tf_op jit(solution)/shard_map/ppermute | solution.py:21
  77.1 8.7 %collective-permute-start.16 = (f32[3,32,96]{2,1,0:T(8,128)S(1)}, f32[3,32,96]{2,1,0:T(8,128)S(1)}, u32[]{:S(2)}, u32[]{:S(2)}) collective-permute-start(f32[3,32,96]{2,1,0:T(8,128)S(1)} %add.64), channel_id=1, source_target_pairs={{0,8},{4,12},{8,0},{12,4},{16,24},{20,28},{24,16},{28,20},{1,9},{5... | collective-permute-start | bytes 110600 | tf_op jit(solution)/shard_map/ppermute | solution.py:274
  79.1 15.0 %collective-permute-start.19 = (bf16[80,8,128]{2,1,0:T(8,128)(2,1)S(1)}, bf16[80,8,128]{2,1,0:T(8,128)(2,1)S(1)}, u32[]{:S(2)}, u32[]{:S(2)}) collective-permute-start(bf16[80,8,128]{2,1,0:T(8,128)(2,1)S(1)} %get-tuple-element.77), channel_id=1, source_target_pairs={{0,24},{4,28},{8,0},{12,4},{16,8},{20,12},{24,16},{28,20},{1,25},{... | collective-permute-start | bytes 491528 | tf_op jit(solution)/shard_map/ppermute | solution.py:21
  79.6 14.6 %collective-permute-start.20 = (bf16[80,8,128]{2,1,0:T(8,128)(2,1)S(1)}, bf16[80,8,128]{2,1,0:T(8,128)(2,1)S(1)}, u32[]{:S(2)}, u32[]{:S(2)}) collective-permute-start(bf16[80,8,128]{2,1,0:T(8,128)(2,1)S(1)} %get-tuple-element.78), channel_id=1, source_target_pairs={{0,20},{4,24},{8,28},{12,0},{16,4},{20,8},{24,12},{28,16},{1,21},{... | collective-permute-start | bytes 491528 | tf_op jit(solution)/shard_map/ppermute | solution.py:21
  85.8 4.2 %collective-permute-start.17 = (f32[3,32,96]{2,1,0:T(8,128)S(1)}, f32[3,32,96]{2,1,0:T(8,128)S(1)}, u32[]{:S(2)}, u32[]{:S(2)}) collective-permute-start(f32[3,32,96]{2,1,0:T(8,128)S(1)} %add.66), channel_id=1, source_target_pairs={{0,4},{4,0},{8,12},{12,8},{16,20},{20,16},{24,28},{28,24},{1,5},{5... | collective-permute-start | bytes 110600 | tf_op jit(solution)/shard_map/ppermute | solution.py:274
  90.0 4.2 %collective-permute-start.22 = (f32[3,32,96]{2,1,0:T(8,128)S(1)}, f32[3,32,96]{2,1,0:T(8,128)S(1)}, u32[]{:S(2)}, u32[]{:S(2)}) collective-permute-start(f32[3,32,96]{2,1,0:T(8,128)S(1)} %add.67), channel_id=1, source_target_pairs={{0,2},{1,3},{2,0},{3,1},{4,6},{5,7},{6,4},{7,5},{8,10},{9,11},{10,... | collective-permute-start | bytes 110600 | tf_op jit(solution)/shard_map/ppermute | solution.py:274
  90.6 4.4 %collective-permute-start.21 = (f32[3,32,96]{2,1,0:T(8,128)S(1)}, f32[3,32,96]{2,1,0:T(8,128)S(1)}, u32[]{:S(2)}, u32[]{:S(2)}) collective-permute-start(f32[3,32,96]{2,1,0:T(8,128)S(1)} %add.67), channel_id=1, source_target_pairs={{0,1},{1,0},{2,3},{3,2},{4,5},{5,4},{6,7},{7,6},{8,9},{9,8},{10,11... | collective-permute-start | bytes 110600 | tf_op jit(solution)/shard_map/ppermute | solution.py:274
  94.1 1.2 %collective-permute-start.23 = (f32[3,32,96]{2,1,0:T(8,128)S(1)}, f32[3,32,96]{2,1,0:T(8,128)S(1)}, u32[]{:S(2)}, u32[]{:S(2)}) collective-permute-start(f32[3,32,96]{2,1,0:T(8,128)S(1)} %collective-permute-done.22), channel_id=1, source_target_pairs={{0,1},{1,0},{2,3},{3,2},{4,5},{5,4},{6,7},{7,6},{8,9},{9,8},{10,11... | collective-permute-start | bytes 110600 | tf_op jit(solution)/shard_map/ppermute | solution.py:274

commit v9 on v8

--- a/solution.py
+++ b/solution.py
@@ -314,28 +314,23 @@
     rights = [right_own] + [None] * hops
     for hop in (4, 3):
         rights[hop] = shifted(right_own, "col", hop)
-    right_late, low, high, left_own, weights, *rights[3:5] = lax.optimization_barrier(
-        (right_own, low, high, left_own, weights, *rights[3:5])
-    )
+    right_late, rights[4] = lax.optimization_barrier((right_own, rights[4]))
+    low, high, left_own, weights = lax.optimization_barrier((low, high, left_own, weights))
     low = jnp.where(column > 0, low, 0).astype(bf16)
     high = jnp.where(column < columns - 1, high, 0).astype(bf16)
     halos = gather_swapping(jnp.concatenate([low, high], axis=1), "disp", 2)
-    for hop in (5, 6):
+    for hop in (5, 6, 2, 1):
         rights[hop] = shifted(right_late, "col", hop)
     blocks = {}
     across = parts // 2
-    cots[across], *rights[5:] = lax.optimization_barrier((cots[across], *rights[5:]))
+    cots[across], *rights[1:] = lax.optimization_barrier((cots[across], *rights[1:]))
     for key in cots:
         (block,) = run(
             pack, [(VMEM, cots[key]), (VMEM, halos[key])],
             [((levels, span, rows), bf16)], [], 4, 1000000000,
         )
-        if key == across:
-            right_last = lax.optimization_barrier((right_own, block))[0]
         blocks[key] = block
         blocks[key | 1] = swapped(block, "disp", 1)
-    for hop in (2, 1):
-        rights[hop] = shifted(right_last, "col", hop)
 
     pad_rows = -(-3 * groups // 8) * 8
     fold = np.zeros((pad_rows, 3 * size), np.float32)
@@ -400,22 +395,23 @@
                 pltpu.VMEM(block, f32),
                 pltpu.VMEM((channels, rest * width, rows), f32),
             ],
-            8, 4000000000,
+            8, 1000000,
         )
 
-    grad_part, total, arrived[hops], arrived[hops - 1] = lax.optimization_barrier(
-        (grad_part, total, arrived[hops], arrived[hops - 1])
-    )
+    grad_part, total = lax.optimization_barrier((grad_part, total))
     left_part, grad_part, *sent = lower(width, D // 2 - width, 0, f32, left_part, grad_part)
     total = total_swapping(total, bits[0])
-    sent, grad_part, total, arrived[hops - 2] = lax.optimization_barrier(
-        (sent, grad_part, total, arrived[hops - 2])
-    )
+    sent, grad_part, total, arrived[near + 1] = lax.optimization_barrier(
+        (sent, grad_part, total, arrived[near + 1])
+    )
+    sent, *items = lax.optimization_barrier((sent, *[arrived[hop] for hop in sorted(arrived)]))
+    arrived = dict(zip(sorted(arrived), items))
     arrived.update(
         {hop: shifted(value, "col", -hop) for hop, value in zip(range(near, 1, -1), sent)}
     )
     grad_left, own, *sent = lower(0, width, middle, bf16, left_part, grad_part)
     total = total_swapping(total, bits[1])
+    sent, total = lax.optimization_barrier((sent, total))
     arrived[1] = shifted(sent[0], "col", -1)
     for bit in bits[2:]:
         total = total_swapping(total, bit)
@@ -427,8 +423,7 @@
             column + hop < columns, arrived[hop].astype(f32), 0.0
         )
 
-    held = gather_swapping(total, "disp")
-    pieces = jnp.stack([held[key] for key in sorted(held)])
+    pieces = jnp.stack([total] + [swapped(total, "disp", key) for key in range(1, parts)])
     pieces = pieces[jnp.arange(parts) ^ part][:, :, : 3 * groups]
     total = pieces.reshape(parts, 3, 3, groups, 3, outs)
     cell_count = D * width * columns * rows

time: 97.9 us -> 101 us (1.032)
  the two profiles are of different devices: /device:TPU:0 before, /device:TPU:13 now
where the time goes in v9:
time: 101 us; the launch traced here: 98.9 us
  starting transfers between devices  33.1 us (33%)
  waiting for transfers between devices  32.7 us (32%)
  Pallas kernels  19 us (19%)
  local copies, waits for them, and re-layouts  8.52 us (8%)
  other arithmetic  4.37 us (4%)
    ppermute x14, starting transfers between devices, shifted(): lax.ppermute(value, axis, [(source, (source + steps) % count) for source...  21.1 us
    ppermute x10, waiting for transfers between devices, swapped(): lax.ppermute(value, axis, [(source, source ^ bit) for source in range(cou...  19.3 us
    pallas_call x6, Pallas kernels, run(): pl.pallas_call(function, out_shape=[jax.ShapeDtypeStruct(shape, kind) for...  19 us
    ppermute x14, waiting for transfers between devices, shifted(): lax.ppermute(value, axis, [(source, (source + steps) % count) for source...  13.4 us
    ppermute x10, starting transfers between devices, swapped(): lax.ppermute(value, axis, [(source, source ^ bit) for source in range(cou...  12 us
  transfers between devices with their start and end apart: 24, of which 9 were waited for; matrix products, arithmetic and copies ran while one was open for 8% of the time, Pallas kernels for 13%

profile of v9, /device:TPU:13, one launch (start us, length us, event | category | flops | bytes accessed | tf_op | source)
XLA Modules:
  0.0 98.9 jit_solution(10406068595371020313)
XLA Ops:
  0.7 1.9 %fusion.2 = (bf16[32,12,1,128]{3,2,1,0:T(2,128)(2,1)S(1)}, bf16[32,12,1,128]{3,2,1,0:T(2,128)(2,1)S(1)}) fusion(bf16[32,12,8,128]{3,2,1,0:T(8,128)(2,1)} %cot_ref.1), kind=kLoop, calls=%fused_computation.24 | loop fusion | bytes 393216 | tf_op jit(solution)/shard_map/slice | solution.py:307
  3.3 2.4 %collective-permute-start.4 = (bf16[80,8,128]{2,1,0:T(8,128)(2,1)S(1)}, bf16[80,8,128]{2,1,0:T(8,128)(2,1)S(1)}, u32[]{:S(2)}, u32[]{:S(2)}) collective-permute-start(bf16[80,8,128]{2,1,0:T(8,128)(2,1)S(1)} %constant_dynamic-slice_fusion.refs_0_), channel_id=1, source_target_pairs={{0,16},{4,20},{8,24},{12,28},{16,0},{20,4},{24,8},{28,12},{1,17},{... | collective-permute-start | bytes 491528 | tf_op jit(solution)/shard_map/ppermute | solution.py:21
  5.6 1.2 %collective-permute-start.3 = (bf16[32,12,8,128]{3,2,1,0:T(8,128)(2,1)}, bf16[32,12,8,128]{3,2,1,0:T(8,128)(2,1)S(1)}, u32[]{:S(2)}, u32[]{:S(2)}) collective-permute-start(bf16[32,12,8,128]{3,2,1,0:T(8,128)(2,1)} %cot_ref.1), channel_id=1, source_target_pairs={{0,2},{1,3},{2,0},{3,1},{4,6},{5,7},{6,4},{7,5},{8,10},{9,11},{10,... | collective-permute-start | bytes 2359304 | tf_op jit(solution)/shard_map/ppermute | solution.py:274
  6.8 1.2 %collective-permute-start = (bf16[12,32,128]{2,1,0:T(8,128)(2,1)}, bf16[12,32,128]{2,1,0:T(8,128)(2,1)}, u32[]{:S(2)}, u32[]{:S(2)}) collective-permute-start(bf16[12,32,128]{2,1,0:T(8,128)(2,1)} %get-tuple-element.50), channel_id=1, source_target_pairs={{0,4},{4,8},{8,12},{12,16},{16,20},{20,24},{24,28},{28,0},{1,5},{5... | collective-permute-start | bytes 294920 | tf_op jit(solution)/shard_map/ppermute | solution.py:21
  8.3 1.1 %constant_dynamic-slice_fusion.1 = bf16[3,3,3,32,10]{4,3,2,1,0:T(8,128)(2,1)S(1)} fusion(bf16[3,3,3,32,40]{4,3,2,1,0:T(8,128)(2,1)} %param.11, s32[]{:T(128)S(6)} %select_n.88), kind=kLoop, calls=%fused_computation.20 | loop fusion | bytes 34564 | tf_op jit(solution)/shard_map/dynamic_slice | solution.py:313
  9.9 1.4 %select_select_fusion = bf16[3,10,8,3,320]{4,3,2,1,0:T(4,128)(2,1)} fusion(pred[8,320]{1,0:T(8,128)(4,1)S(1)} %copy-done.4, pred[8,320]{1,0:T(8,128)(4,1)S(1)} %copy-done.5, pred[8,320]{1,0:T(8,128)(4,1)S(1)} %copy-done.6, bf16[3,10,3,320]{3,2,1,0:T(4,128)(2,1)S(1)} %copy.33, bf16[3,10,3,320]{3,2,1,0:T(4,128)(2,1)S(1)} %copy.32, ...), kind=kLoop, calls=%fused_computation.2 | loop fusion | flops 691200 | bytes 641280 | tf_op jit(solution)/shard_map/jit(_where)/select_n | solution.py:45
  11.3 0.9 constant_dynamic-slice_fusion.2.refs_8_.refs_7_.left_ref
  12.3 1.7 %select_n.92.refs_9_.weight_ref = bf16[240,960]{1,0:T(8,128)(2,1)S(1)} reshape(bf16[3,10,8,3,320]{4,3,2,1,0:T(4,128)(2,1)} %select_select_fusion) | data formatting | bytes 921600 | tf_op jit(solution)/shard_map/jit(_where)/select_n | solution.py:45
  14.0 8.2 %collective-permute-done = bf16[12,32,128]{2,1,0:T(8,128)(2,1)} collective-permute-done((bf16[12,32,128]{2,1,0:T(8,128)(2,1)}, bf16[12,32,128]{2,1,0:T(8,128)(2,1)}, u32[]{:S(2)}, u32[]{:S(2)}) %collective-permute-start) | collective-permute-done | bytes 98336 | tf_op jit(solution)/shard_map/ppermute | solution.py:21
  22.2 0.9 broadcast_select_fusion
  23.1 3.2 %collective-permute-start.5 = (bf16[80,8,128]{2,1,0:T(8,128)(2,1)S(1)}, bf16[80,8,128]{2,1,0:T(8,128)(2,1)S(1)}, u32[]{:S(2)}, u32[]{:S(2)}) collective-permute-start(bf16[80,8,128]{2,1,0:T(8,128)(2,1)S(1)} %constant_dynamic-slice_fusion.refs_0_), channel_id=1, source_target_pairs={{0,4},{4,8},{8,12},{12,16},{16,20},{20,24},{24,28},{28,0},{1,5},{5... | collective-permute-start | bytes 491528 | tf_op jit(solution)/shard_map/ppermute | solution.py:21
  26.3 0.9 broadcast_select_fusion.1
  27.2 1.3 %collective-permute-start.10 = (bf16[12,64,128]{2,1,0:T(8,128)(2,1)S(1)}, bf16[12,64,128]{2,1,0:T(8,128)(2,1)S(1)}, u32[]{:S(2)}, u32[]{:S(2)}) collective-permute-start(bf16[12,64,128]{2,1,0:T(8,128)(2,1)S(1)} %pad_maximum_fusion.halo_ref), channel_id=1, source_target_pairs={{0,2},{1,3},{2,0},{3,1},{4,6},{5,7},{6,4},{7,5},{8,10},{9,11},{10,... | collective-permute-start | bytes 589832 | tf_op jit(solution)/shard_map/ppermute | solution.py:274
  28.5 0.9 collective-permute-done.5.refs_1_
  30.2 2.9 %collective-permute-done.6.refs_2_ = bf16[80,8,128]{2,1,0:T(8,128)(2,1)S(1)} collective-permute-done((bf16[80,8,128]{2,1,0:T(8,128)(2,1)S(1)}, bf16[80,8,128]{2,1,0:T(8,128)(2,1)S(1)}, u32[]{:S(2)}, u32[]{:S(2)}) %collective-permute-start.6) | collective-permute-done | bytes 163872 | tf_op jit(solution)/shard_map/ppermute | solution.py:21
  33.1 3.5 %collective-permute-start.2 = (bf16[12,320,128]{2,1,0:T(8,128)(2,1)S(1)}, bf16[12,320,128]{2,1,0:T(8,128)(2,1)S(1)}, u32[]{:S(2)}, u32[]{:S(2)}) collective-permute-start(bf16[12,320,128]{2,1,0:T(8,128)(2,1)S(1)} %shard_map.112.refs_0_), channel_id=1, source_target_pairs={{0,1},{1,0},{2,3},{3,2},{4,5},{5,4},{6,7},{7,6},{8,9},{9,8},{10,11... | collective-permute-start | bytes 2949128 | tf_op jit(solution)/shard_map/ppermute | solution.py:274
  36.9 2.0 %collective-permute-start.11 = (bf16[12,320,128]{2,1,0:T(8,128)(2,1)S(1)}, bf16[12,320,128]{2,1,0:T(8,128)(2,1)S(1)}, u32[]{:S(2)}, u32[]{:S(2)}) collective-permute-start(bf16[12,320,128]{2,1,0:T(8,128)(2,1)S(1)} %shard_map.113.refs_2_), channel_id=1, source_target_pairs={{0,1},{1,0},{2,3},{3,2},{4,5},{5,4},{6,7},{7,6},{8,9},{9,8},{10,11... | collective-permute-start | bytes 2949128 | tf_op jit(solution)/shard_map/ppermute | solution.py:274
  39.0 2.1 %collective-permute-done.11.refs_3_ = bf16[12,320,128]{2,1,0:T(8,128)(2,1)S(1)} collective-permute-done((bf16[12,320,128]{2,1,0:T(8,128)(2,1)S(1)}, bf16[12,320,128]{2,1,0:T(8,128)(2,1)S(1)}, u32[]{:S(2)}, u32[]{:S(2)}) %collective-permute-start.11) | collective-permute-done | bytes 983072 | tf_op jit(solution)/shard_map/ppermute | solution.py:274
  41.1 6.5 %shard_map.114 = (bf16[50,320,128]{2,1,0:T(8,128)(2,1)S(1)}, f32[80,8,128]{2,1,0:T(8,128)S(1)}, f32[80,32,128]{2,1,0:T(8,128)S(1)}, bf16[80,8,128]{2,1,0:T(8,128...) custom-call(s32[2]{0:T(128)S(1)} %pad_add_fusion.places, ...), custom_call_target="tpu_custom_call" | custom-call | flops 8000000000 | bytes 1024 | tf_op jit(solution)/shard_map/pallas_call | solution.py:261
  47.6 8.0 %collective-permute-start.13 = (bf16[80,8,128]{2,1,0:T(8,128)(2,1)S(1)}, bf16[80,8,128]{2,1,0:T(8,128)(2,1)S(1)}, u32[]{:S(2)}, u32[]{:S(2)}) collective-permute-start(bf16[80,8,128]{2,1,0:T(8,128)(2,1)S(1)} %get-tuple-element.77), channel_id=1, source_target_pairs={{0,16},{4,20},{8,24},{12,28},{16,0},{20,4},{24,8},{28,12},{1,17},{... | collective-permute-start | bytes 491528 | tf_op jit(solution)/shard_map/ppermute | solution.py:21
  55.9 7.0 %shard_map.115 = (f32[80,56,128]{2,1,0:T(8,128)S(1)}, f32[3,32,96]{2,1,0:T(8,128)S(1)}) custom-call(s32[2]{0:T(128)S(1)} %pad_add_fusion.places, bf16[80,8,128]{2,1,0:T(8,128)(2,1)S(1)} %constant_dynamic-slice_fusion.refs_0_, bf16[80,8,128]{2,1,0:T(8,128)(2,1)S(1)} %collective-permute-done.5.refs_1_, bf16[80,8,128]{2,1,0:T(8,128)(2,1)S(1)} %collective-permute-done.6.refs_2_, ...), custom_call_target="tpu_custom_call" | custom-call | flops 8000000000 | bytes 1024 | tf_op jit(solution)/shard_map/pallas_call | solution.py:261
  62.8 1.0 %collective-permute-start.12 = (f32[3,32,96]{2,1,0:T(8,128)S(1)}, f32[3,32,96]{2,1,0:T(8,128)S(1)}, u32[]{:S(2)}, u32[]{:S(2)}) collective-permute-start(f32[3,32,96]{2,1,0:T(8,128)S(1)} %get-tuple-element.76), channel_id=1, source_target_pairs={{0,16},{4,20},{8,24},{12,28},{16,0},{20,4},{24,8},{28,12},{1,17},{... | collective-permute-start | bytes 110600 | tf_op jit(solution)/shard_map/ppermute | solution.py:274
  63.8 3.1 %shard_map.116 = (f32[80,8,128]{2,1,0:T(8,128)S(1)}, f32[80,16,128]{2,1,0:T(8,128)S(1)}, bf16[80,8,128]{2,1,0:T(8,128)(2,1)S(1)}, bf16[80,8,128]{2,1,0:T(8,128)(2,1)S(1)}) custom-call(bf16[80,8,128]{2,1,0:T(8,128)(2,1)S(1)} %constant_dynamic-slice_fusion.2.refs_8_.refs_7_.left_ref, bf16[240,960]{1,0:T(8,128)(2,1)S(1)} %select_n.92.refs_9_.weight_ref, ...), custom_call_target="tpu_custom_call" | custom-call | flops 1000000 | bytes 1024 | tf_op jit(solution)/shard_map/pallas_call | solution.py:261
  66.9 7.6 %collective-permute-done.12 = f32[3,32,96]{2,1,0:T(8,128)S(1)} collective-permute-done((f32[3,32,96]{2,1,0:T(8,128)S(1)}, f32[3,32,96]{2,1,0:T(8,128)S(1)}, u32[]{:S(2)}, u32[]{:S(2)}) %collective-permute-start.12) | collective-permute-done | bytes 36896 | tf_op jit(solution)/shard_map/ppermute | solution.py:274
  76.1 2.0 %shard_map.117 = (bf16[80,8,128]{2,1,0:T(8,128)(2,1)}, f32[80,8,128]{2,1,0:T(8,128)S(1)}, bf16[80,8,128]{2,1,0:T(8,128)(2,1)S(1)}) custom-call(bf16[80,8,128]{2,1,0:T(8,128)(2,1)S(1)} %constant_dynamic-slice_fusion.2.refs_8_.refs_7_.left_ref, bf16[240,960]{1,0:T(8,128)(2,1)S(1)} %select_n.92.refs_9_.weight_ref, ...), custom_call_target="tpu_custom_call" | custom-call | flops 1000000 | bytes 1024 | tf_op jit(solution)/shard_map/pallas_call | solution.py:261
  78.1 4.3 %collective-permute-start.16 = (bf16[80,8,128]{2,1,0:T(8,128)(2,1)S(1)}, bf16[80,8,128]{2,1,0:T(8,128)(2,1)S(1)}, u32[]{:S(2)}, u32[]{:S(2)}) collective-permute-start(bf16[80,8,128]{2,1,0:T(8,128)(2,1)S(1)} %get-tuple-element.84), channel_id=1, source_target_pairs={{0,28},{4,0},{8,4},{12,8},{16,12},{20,16},{24,20},{28,24},{1,29},{... | collective-permute-start | bytes 491528 | tf_op jit(solution)/shard_map/ppermute | solution.py:21
  82.5 7.2 %collective-permute-done.15 = f32[3,32,96]{2,1,0:T(8,128)S(1)} collective-permute-done((f32[3,32,96]{2,1,0:T(8,128)S(1)}, f32[3,32,96]{2,1,0:T(8,128)S(1)}, u32[]{:S(2)}, u32[]{:S(2)}) %collective-permute-start.15) | collective-permute-done | bytes 36896 | tf_op jit(solution)/shard_map/ppermute | solution.py:274
  89.7 1.4 %collective-permute-done.16 = bf16[80,8,128]{2,1,0:T(8,128)(2,1)S(1)} collective-permute-done((bf16[80,8,128]{2,1,0:T(8,128)(2,1)S(1)}, bf16[80,8,128]{2,1,0:T(8,128)(2,1)S(1)}, u32[]{:S(2)}, u32[]{:S(2)}) %collective-permute-start.16) | collective-permute-done | bytes 163872 | tf_op jit(solution)/shard_map/ppermute | solution.py:21
  91.7 1.3 %collective-permute-start.22 = (f32[3,32,96]{2,1,0:T(8,128)S(1)}, f32[3,32,96]{2,1,0:T(8,128)S(1)}, u32[]{:S(2)}, u32[]{:S(2)}) collective-permute-start(f32[3,32,96]{2,1,0:T(8,128)S(1)} %add.67), channel_id=1, source_target_pairs={{0,2},{1,3},{2,0},{3,1},{4,6},{5,7},{6,4},{7,5},{8,10},{9,11},{10,... | collective-permute-start | bytes 110600 | tf_op jit(solution)/shard_map/ppermute | solution.py:274
  93.3 0.9 add_convert_fusion
  95.0 1.6 %collective-permute-done.23 = f32[3,32,96]{2,1,0:T(8,128)S(1)} collective-permute-done((f32[3,32,96]{2,1,0:T(8,128)S(1)}, f32[3,32,96]{2,1,0:T(8,128)S(1)}, u32[]{:S(2)}, u32[]{:S(2)}) %collective-permute-start.23) | collective-permute-done | bytes 36896 | tf_op jit(solution)/shard_map/ppermute | solution.py:274
  97.9 1.0 copy.37
  (67 shorter events, 7.6 us)
Async XLA Ops:
  0.6 2.6 %copy-start = (bf16[320,8,128]{2,1,0:T(8,128)(2,1)S(1)}, bf16[320,8,128]{2,1,0:T(8,128)(2,1)}, u32[]{:S(2)}) copy-start(bf16[320,8,128]{2,1,0:T(8,128)(2,1)} %param.10) | copy-start | bytes 1966084
  0.6 8.8 %copy-start.3 = (bf16[32,320,1,1,1]{1,0,4,3,2:T(8,128)(2,1)S(1)}, bf16[32,320,1,1,1]{1,0,4,3,2:T(8,128)(2,1)}, u32[]{:S(2)}) copy-start(bf16[32,320,1,1,1]{1,0,4,3,2:T(8,128)(2,1)} %constant.59) | copy-start | bytes 61444
  0.7 9.2 %copy-start.4 = (pred[8,320]{1,0:T(8,128)(4,1)S(1)}, pred[8,320]{1,0:T(8,128)(4,1)}, u32[]{:S(2)}) copy-start(pred[8,320]{1,0:T(8,128)(4,1)} %constant.55.clone) | copy-start | bytes 7684
  0.7 9.2 %copy-start.5 = (pred[8,320]{1,0:T(8,128)(4,1)S(1)}, pred[8,320]{1,0:T(8,128)(4,1)}, u32[]{:S(2)}) copy-start(pred[8,320]{1,0:T(8,128)(4,1)} %constant.56.clone) | copy-start | bytes 7684
  0.7 9.2 %copy-start.6 = (pred[8,320]{1,0:T(8,128)(4,1)S(1)}, pred[8,320]{1,0:T(8,128)(4,1)}, u32[]{:S(2)}) copy-start(pred[8,320]{1,0:T(8,128)(4,1)} %constant.57.clone) | copy-start | bytes 7684
  3.3 19.8 %collective-permute-start.4 = (bf16[80,8,128]{2,1,0:T(8,128)(2,1)S(1)}, bf16[80,8,128]{2,1,0:T(8,128)(2,1)S(1)}, u32[]{:S(2)}, u32[]{:S(2)}) collective-permute-start(bf16[80,8,128]{2,1,0:T(8,128)(2,1)S(1)} %constant_dynamic-slice_fusion.refs_0_), channel_id=1, source_target_pairs={{0,16},{4,20},{8,24},{12,28},{16,0},{20,4},{24,8},{28,12},{1,17},{... | collective-permute-start | bytes 491528 | tf_op jit(solution)/shard_map/ppermute | solution.py:21
  5.6 22.8 %collective-permute-start.7 = (bf16[80,8,128]{2,1,0:T(8,128)(2,1)S(1)}, bf16[80,8,128]{2,1,0:T(8,128)(2,1)S(1)}, u32[]{:S(2)}, u32[]{:S(2)}) collective-permute-start(bf16[80,8,128]{2,1,0:T(8,128)(2,1)S(1)} %constant_dynamic-slice_fusion.refs_0_), channel_id=1, source_target_pairs={{0,12},{4,16},{8,20},{12,24},{16,28},{20,0},{24,4},{28,8},{1,13},{... | collective-permute-start | bytes 491528 | tf_op jit(solution)/shard_map/ppermute | solution.py:21
  5.6 31.0 %collective-permute-start.3 = (bf16[32,12,8,128]{3,2,1,0:T(8,128)(2,1)}, bf16[32,12,8,128]{3,2,1,0:T(8,128)(2,1)S(1)}, u32[]{:S(2)}, u32[]{:S(2)}) collective-permute-start(bf16[32,12,8,128]{3,2,1,0:T(8,128)(2,1)} %cot_ref.1), channel_id=1, source_target_pairs={{0,2},{1,3},{2,0},{3,1},{4,6},{5,7},{6,4},{7,5},{8,10},{9,11},{10,... | collective-permute-start | bytes 2359304 | tf_op jit(solution)/shard_map/ppermute | solution.py:274
  6.8 15.3 %collective-permute-start = (bf16[12,32,128]{2,1,0:T(8,128)(2,1)}, bf16[12,32,128]{2,1,0:T(8,128)(2,1)}, u32[]{:S(2)}, u32[]{:S(2)}) collective-permute-start(bf16[12,32,128]{2,1,0:T(8,128)(2,1)} %get-tuple-element.50), channel_id=1, source_target_pairs={{0,4},{4,8},{8,12},{12,16},{16,20},{20,24},{24,28},{28,0},{1,5},{5... | collective-permute-start | bytes 294920 | tf_op jit(solution)/shard_map/ppermute | solution.py:21
  8.1 14.1 %collective-permute-start.1 = (bf16[12,32,128]{2,1,0:T(8,128)(2,1)S(1)}, bf16[12,32,128]{2,1,0:T(8,128)(2,1)}, u32[]{:S(2)}, u32[]{:S(2)}) collective-permute-start(bf16[12,32,128]{2,1,0:T(8,128)(2,1)S(1)} %get-tuple-element.51), channel_id=1, source_target_pairs={{0,28},{4,0},{8,4},{12,8},{16,12},{20,16},{24,20},{28,24},{1,29},{... | collective-permute-start | bytes 294920 | tf_op jit(solution)/shard_map/ppermute | solution.py:21
  9.7 20.3 %copy-start.1 = (bf16[32,12,8,128]{3,2,1,0:T(8,128)(2,1)S(1)}, bf16[32,12,8,128]{3,2,1,0:T(8,128)(2,1)}, u32[]{:S(2)}) copy-start(bf16[32,12,8,128]{3,2,1,0:T(8,128)(2,1)} %cot_ref.1) | copy-start | bytes 2359300
  23.1 6.2 %collective-permute-start.5 = (bf16[80,8,128]{2,1,0:T(8,128)(2,1)S(1)}, bf16[80,8,128]{2,1,0:T(8,128)(2,1)S(1)}, u32[]{:S(2)}, u32[]{:S(2)}) collective-permute-start(bf16[80,8,128]{2,1,0:T(8,128)(2,1)S(1)} %constant_dynamic-slice_fusion.refs_0_), channel_id=1, source_target_pairs={{0,4},{4,8},{8,12},{12,16},{16,20},{20,24},{24,28},{28,0},{1,5},{5... | collective-permute-start | bytes 491528 | tf_op jit(solution)/shard_map/ppermute | solution.py:21
  27.2 9.5 %collective-permute-start.10 = (bf16[12,64,128]{2,1,0:T(8,128)(2,1)S(1)}, bf16[12,64,128]{2,1,0:T(8,128)(2,1)S(1)}, u32[]{:S(2)}, u32[]{:S(2)}) collective-permute-start(bf16[12,64,128]{2,1,0:T(8,128)(2,1)S(1)} %pad_maximum_fusion.halo_ref), channel_id=1, source_target_pairs={{0,2},{1,3},{2,0},{3,1},{4,6},{5,7},{6,4},{7,5},{8,10},{9,11},{10,... | collective-permute-start | bytes 589832 | tf_op jit(solution)/shard_map/ppermute | solution.py:274
  28.5 4.6 %collective-permute-start.6 = (bf16[80,8,128]{2,1,0:T(8,128)(2,1)S(1)}, bf16[80,8,128]{2,1,0:T(8,128)(2,1)S(1)}, u32[]{:S(2)}, u32[]{:S(2)}) collective-permute-start(bf16[80,8,128]{2,1,0:T(8,128)(2,1)S(1)} %constant_dynamic-slice_fusion.refs_0_), channel_id=1, source_target_pairs={{0,8},{4,12},{8,16},{12,20},{16,24},{20,28},{24,0},{28,4},{1,9},{5... | collective-permute-start | bytes 491528 | tf_op jit(solution)/shard_map/ppermute | solution.py:21
  28.5 8.2 %collective-permute-start.8 = (bf16[80,8,128]{2,1,0:T(8,128)(2,1)S(1)}, bf16[80,8,128]{2,1,0:T(8,128)(2,1)S(1)}, u32[]{:S(2)}, u32[]{:S(2)}) collective-permute-start(bf16[80,8,128]{2,1,0:T(8,128)(2,1)S(1)} %constant_dynamic-slice_fusion.refs_0_), channel_id=1, source_target_pairs={{0,20},{4,24},{8,28},{12,0},{16,4},{20,8},{24,12},{28,16},{1,21},{... | collective-permute-start | bytes 491528 | tf_op jit(solution)/shard_map/ppermute | solution.py:21
  29.3 7.3 %collective-permute-start.9 = (bf16[80,8,128]{2,1,0:T(8,128)(2,1)S(1)}, bf16[80,8,128]{2,1,0:T(8,128)(2,1)S(1)}, u32[]{:S(2)}, u32[]{:S(2)}) collective-permute-start(bf16[80,8,128]{2,1,0:T(8,128)(2,1)S(1)} %constant_dynamic-slice_fusion.refs_0_), channel_id=1, source_target_pairs={{0,24},{4,28},{8,0},{12,4},{16,8},{20,12},{24,16},{28,20},{1,25},{... | collective-permute-start | bytes 491528 | tf_op jit(solution)/shard_map/ppermute | solution.py:21
  33.1 5.9 %collective-permute-start.2 = (bf16[12,320,128]{2,1,0:T(8,128)(2,1)S(1)}, bf16[12,320,128]{2,1,0:T(8,128)(2,1)S(1)}, u32[]{:S(2)}, u32[]{:S(2)}) collective-permute-start(bf16[12,320,128]{2,1,0:T(8,128)(2,1)S(1)} %shard_map.112.refs_0_), channel_id=1, source_target_pairs={{0,1},{1,0},{2,3},{3,2},{4,5},{5,4},{6,7},{7,6},{8,9},{9,8},{10,11... | collective-permute-start | bytes 2949128 | tf_op jit(solution)/shard_map/ppermute | solution.py:274
  36.9 4.2 %collective-permute-start.11 = (bf16[12,320,128]{2,1,0:T(8,128)(2,1)S(1)}, bf16[12,320,128]{2,1,0:T(8,128)(2,1)S(1)}, u32[]{:S(2)}, u32[]{:S(2)}) collective-permute-start(bf16[12,320,128]{2,1,0:T(8,128)(2,1)S(1)} %shard_map.113.refs_2_), channel_id=1, source_target_pairs={{0,1},{1,0},{2,3},{3,2},{4,5},{5,4},{6,7},{7,6},{8,9},{9,8},{10,11... | collective-permute-start | bytes 2949128 | tf_op jit(solution)/shard_map/ppermute | solution.py:274
  39.0 16.9 %copy-start.2 = (f32[32,240]{1,0:T(8,128)S(1)}, f32[32,240]{1,0:T(8,128)}, u32[]{:S(2)}) copy-start(f32[32,240]{1,0:T(8,128)} %constant.58.clone.refs_9_) | copy-start | bytes 92164
  47.6 27.0 %collective-permute-start.13 = (bf16[80,8,128]{2,1,0:T(8,128)(2,1)S(1)}, bf16[80,8,128]{2,1,0:T(8,128)(2,1)S(1)}, u32[]{:S(2)}, u32[]{:S(2)}) collective-permute-start(bf16[80,8,128]{2,1,0:T(8,128)(2,1)S(1)} %get-tuple-element.77), channel_id=1, source_target_pairs={{0,16},{4,20},{8,24},{12,28},{16,0},{20,4},{24,8},{28,12},{1,17},{... | collective-permute-start | bytes 491528 | tf_op jit(solution)/shard_map/ppermute | solution.py:21
  55.6 19.7 %collective-permute-start.17 = (bf16[80,8,128]{2,1,0:T(8,128)(2,1)S(1)}, bf16[80,8,128]{2,1,0:T(8,128)(2,1)S(1)}, u32[]{:S(2)}, u32[]{:S(2)}) collective-permute-start(bf16[80,8,128]{2,1,0:T(8,128)(2,1)S(1)} %get-tuple-element.89), channel_id=1, source_target_pairs={{0,12},{4,16},{8,20},{12,24},{16,28},{20,0},{24,4},{28,8},{1,13},{... | collective-permute-start | bytes 491528 | tf_op jit(solution)/shard_map/ppermute | solution.py:21
  55.6 19.7 %collective-permute-start.18 = (bf16[80,8,128]{2,1,0:T(8,128)(2,1)S(1)}, bf16[80,8,128]{2,1,0:T(8,128)(2,1)S(1)}, u32[]{:S(2)}, u32[]{:S(2)}) collective-permute-start(bf16[80,8,128]{2,1,0:T(8,128)(2,1)S(1)} %get-tuple-element.90), channel_id=1, source_target_pairs={{0,8},{4,12},{8,16},{12,20},{16,24},{20,28},{24,0},{28,4},{1,9},{5... | collective-permute-start | bytes 491528 | tf_op jit(solution)/shard_map/ppermute | solution.py:21
  62.8 11.7 %collective-permute-start.12 = (f32[3,32,96]{2,1,0:T(8,128)S(1)}, f32[3,32,96]{2,1,0:T(8,128)S(1)}, u32[]{:S(2)}, u32[]{:S(2)}) collective-permute-start(f32[3,32,96]{2,1,0:T(8,128)S(1)} %get-tuple-element.76), channel_id=1, source_target_pairs={{0,16},{4,20},{8,24},{12,28},{16,0},{20,4},{24,8},{28,12},{1,17},{... | collective-permute-start | bytes 110600 | tf_op jit(solution)/shard_map/ppermute | solution.py:274
  74.5 3.6 %collective-permute-start.14 = (f32[3,32,96]{2,1,0:T(8,128)S(1)}, f32[3,32,96]{2,1,0:T(8,128)S(1)}, u32[]{:S(2)}, u32[]{:S(2)}) collective-permute-start(f32[3,32,96]{2,1,0:T(8,128)S(1)} %add.64), channel_id=1, source_target_pairs={{0,8},{4,12},{8,0},{12,4},{16,24},{20,28},{24,16},{28,20},{1,9},{5... | collective-permute-start | bytes 110600 | tf_op jit(solution)/shard_map/ppermute | solution.py:274
  75.2 18.1 %collective-permute-start.19 = (bf16[80,8,128]{2,1,0:T(8,128)(2,1)S(1)}, bf16[80,8,128]{2,1,0:T(8,128)(2,1)S(1)}, u32[]{:S(2)}, u32[]{:S(2)}) collective-permute-start(bf16[80,8,128]{2,1,0:T(8,128)(2,1)S(1)} %get-tuple-element.91), channel_id=1, source_target_pairs={{0,24},{4,28},{8,0},{12,4},{16,8},{20,12},{24,16},{28,20},{1,25},{... | collective-permute-start | bytes 491528 | tf_op jit(solution)/shard_map/ppermute | solution.py:21
  76.1 17.2 %collective-permute-start.20 = (bf16[80,8,128]{2,1,0:T(8,128)(2,1)S(1)}, bf16[80,8,128]{2,1,0:T(8,128)(2,1)S(1)}, u32[]{:S(2)}, u32[]{:S(2)}) collective-permute-start(bf16[80,8,128]{2,1,0:T(8,128)(2,1)S(1)} %get-tuple-element.92), channel_id=1, source_target_pairs={{0,20},{4,24},{8,28},{12,0},{16,4},{20,8},{24,12},{28,16},{1,21},{... | collective-permute-start | bytes 491528 | tf_op jit(solution)/shard_map/ppermute | solution.py:21
  78.1 13.0 %collective-permute-start.16 = (bf16[80,8,128]{2,1,0:T(8,128)(2,1)S(1)}, bf16[80,8,128]{2,1,0:T(8,128)(2,1)S(1)}, u32[]{:S(2)}, u32[]{:S(2)}) collective-permute-start(bf16[80,8,128]{2,1,0:T(8,128)(2,1)S(1)} %get-tuple-element.84), channel_id=1, source_target_pairs={{0,28},{4,0},{8,4},{12,8},{16,12},{20,16},{24,20},{28,24},{1,29},{... | collective-permute-start | bytes 491528 | tf_op jit(solution)/shard_map/ppermute | solution.py:21
  82.5 7.3 %collective-permute-start.15 = (f32[3,32,96]{2,1,0:T(8,128)S(1)}, f32[3,32,96]{2,1,0:T(8,128)S(1)}, u32[]{:S(2)}, u32[]{:S(2)}) collective-permute-start(f32[3,32,96]{2,1,0:T(8,128)S(1)} %add.66), channel_id=1, source_target_pairs={{0,4},{4,0},{8,12},{12,8},{16,20},{20,16},{24,28},{28,24},{1,5},{5... | collective-permute-start | bytes 110600 | tf_op jit(solution)/shard_map/ppermute | solution.py:274
  91.1 3.1 %collective-permute-start.21 = (f32[3,32,96]{2,1,0:T(8,128)S(1)}, f32[3,32,96]{2,1,0:T(8,128)S(1)}, u32[]{:S(2)}, u32[]{:S(2)}) collective-permute-start(f32[3,32,96]{2,1,0:T(8,128)S(1)} %add.67), channel_id=1, source_target_pairs={{0,1},{1,0},{2,3},{3,2},{4,5},{5,4},{6,7},{7,6},{8,9},{9,8},{10,11... | collective-permute-start | bytes 110600 | tf_op jit(solution)/shard_map/ppermute | solution.py:274
  91.7 3.4 %collective-permute-start.22 = (f32[3,32,96]{2,1,0:T(8,128)S(1)}, f32[3,32,96]{2,1,0:T(8,128)S(1)}, u32[]{:S(2)}, u32[]{:S(2)}) collective-permute-start(f32[3,32,96]{2,1,0:T(8,128)S(1)} %add.67), channel_id=1, source_target_pairs={{0,2},{1,3},{2,0},{3,1},{4,6},{5,7},{6,4},{7,5},{8,10},{9,11},{10,... | collective-permute-start | bytes 110600 | tf_op jit(solution)/shard_map/ppermute | solution.py:274
  92.9 3.6 %collective-permute-start.23 = (f32[3,32,96]{2,1,0:T(8,128)S(1)}, f32[3,32,96]{2,1,0:T(8,128)S(1)}, u32[]{:S(2)}, u32[]{:S(2)}) collective-permute-start(f32[3,32,96]{2,1,0:T(8,128)S(1)} %add.67), channel_id=1, source_target_pairs={{0,3},{1,2},{2,1},{3,0},{4,7},{5,6},{6,5},{7,4},{8,11},{9,10},{10,... | collective-permute-start | bytes 110600 | tf_op jit(solution)/shard_map/ppermute | solution.py:274

commit v10 on v9

--- a/solution.py
+++ b/solution.py
@@ -53,6 +53,26 @@
     return jnp.where(lane == (0 if steps > 0 else size - 1), 0.0, moved)
 
 
+def join(*refs):
+    for at, ref in enumerate(refs[:-1]):
+        refs[-1][at] = ref[...]
+
+
+def right_block(places, hop, even_refs, odd_refs):
+    if hop % 2 == 0:
+        block = even_refs[hop // 2][...]
+    else:
+        second = places[1] & 1
+        at = (hop + 1) // 2 - second
+        count = odd_refs[1].shape[0]
+        block = odd_refs[1][jnp.clip(at - 1, 0, count - 1)]
+        if hop == 1:
+            block = jnp.where(at > 0, block, odd_refs[0][...])
+        if hop == 2 * count + 1:
+            block = jnp.where(at <= count, block, odd_refs[2][...])
+    return jnp.where(places[1] >= hop, block.astype(jnp.float32), 0.0)
+
+
 def pack(cot_ref, halo_ref, packed_ref):
     outs, levels, width, rows = cot_ref.shape
     main = outs * width
@@ -119,9 +139,9 @@
     lax.fori_loop(0, count // width, step, 0)
 
 
-def upper_grads(keys, reach, far, places, *refs):
+def upper_grads(keys, reach, far, pairs, places, *refs):
     block_refs, refs = refs[: len(keys)], refs[len(keys) :]
-    right_refs, refs = refs[: far + 1], refs[far + 1 :]
+    even_refs, odd_refs, refs = refs[:pairs], refs[pairs : pairs + 2], refs[pairs + 2 :]
     left_ref, weight_ref, cot_s, left_sum, grad_out = refs[:5]
     sent_refs, (left_s, right_s, grad_s, sems) = refs[5 : 5 + far], refs[5 + far :]
     channels, width, rows = left_ref.shape
@@ -141,8 +161,8 @@
     grad_s[...] = jnp.zeros(grad_s.shape, f32)
     hops = reach // width
     for at in range(far + 1):
-        block = right_refs[at][...].astype(f32)
-        right_s[:, at * width : (at + 1) * width] = jnp.where(places[1] >= hops - at, block, 0.0)
+        block = right_block(places, hops - at, (None, *even_refs), (None, *odd_refs))
+        right_s[:, at * width : (at + 1) * width] = block
     for copy in copies:
         copy.wait()
     add_grads(
@@ -177,9 +197,9 @@
 
 
 def kernel_sums(hops, places, *refs):
-    right_refs, (left_ref, cot_s, fold_ref, right_s, sums_ref, left_s, prod_s) = (
-        refs[: hops + 1], refs[hops + 1 :],
-    )
+    pairs = hops // 2
+    even_refs, odd_refs, refs = refs[: pairs + 1], refs[pairs + 1 : pairs + 4], refs[pairs + 4 :]
+    left_ref, cot_s, fold_ref, right_s, sums_ref, left_s, prod_s = refs
     channels, width, rows = left_ref.shape
     groups = channels // GROUP
     span = cot_s.shape[1]
@@ -192,8 +212,7 @@
     left_s[...] = left_ref[...].astype(f32)
     for hop in range(hops + 1):
         at = reach - hop * width
-        block = right_refs[hop][...].astype(f32)
-        right_s[:, at : at + width] = jnp.where(places[1] >= hop, block, 0.0)
+        right_s[:, at : at + width] = right_block(places, hop, even_refs, odd_refs)
     prod_s[...] = jnp.zeros(prod_s.shape, f32)
     chunk = width // 2
 
@@ -311,23 +330,26 @@
     right_own = lax.dynamic_slice_in_dim(right, part * channels, channels, 0)
     left_own = lax.dynamic_slice_in_dim(left, part * channels, channels, 0)
     weights = toeplitz(lax.dynamic_slice_in_dim(kernel, part * groups, groups, 4), width)
-    rights = [right_own] + [None] * hops
-    for hop in (4, 3):
-        rights[hop] = shifted(right_own, "col", hop)
-    right_late, rights[4] = lax.optimization_barrier((right_own, rights[4]))
-    low, high, left_own, weights = lax.optimization_barrier((low, high, left_own, weights))
+    pairs = hops // 2
+    evens = [right_own] + [shifted(right_own, "col", 2 * k) for k in range(1, pairs + 1)]
+    low, high, left_own, weights, *evens[1:pairs] = lax.optimization_barrier(
+        (low, high, left_own, weights, *evens[1:pairs])
+    )
     low = jnp.where(column > 0, low, 0).astype(bf16)
     high = jnp.where(column < columns - 1, high, 0).astype(bf16)
     halos = gather_swapping(jnp.concatenate([low, high], axis=1), "disp", 2)
-    for hop in (5, 6, 2, 1):
-        rights[hop] = shifted(right_late, "col", hop)
+    (joined,) = run(
+        join, [(VMEM, item) for item in evens[1:pairs]],
+        [((pairs - 1, channels, width, rows), bf16)], [], 4, 1000000,
+    )
+    odds = [swapped(item, "col", 1) for item in (right_own, joined, evens[pairs])]
     blocks = {}
     across = parts // 2
-    cots[across], *rights[1:] = lax.optimization_barrier((cots[across], *rights[1:]))
+    cots[across], *odds = lax.optimization_barrier((cots[across], *odds))
     for key in cots:
         (block,) = run(
             pack, [(VMEM, cots[key]), (VMEM, halos[key])],
-            [((levels, span, rows), bf16)], [], 4, 1000000000,
+            [((levels, span, rows), bf16)], [], 4, 1000000,
         )
         blocks[key] = block
         blocks[key | 1] = swapped(block, "disp", 1)
@@ -342,10 +364,10 @@
     reach = hops * width
     keys = sorted(blocks)
     cot_wide, left_part, grad_part, *sent = run(
-        functools.partial(upper_grads, keys, reach, far),
+        functools.partial(upper_grads, keys, reach, far, pairs),
         [(SMEM, places)]
         + [(ANY, blocks[key]) for key in keys]
-        + [(VMEM, rights[hop]) for hop in range(hops, near - 1, -1)]
+        + [(VMEM, item) for item in (*evens[1:], *odds[1:])]
         + [(VMEM, left_own), (VMEM, weights)],
         [
             ((D + 2, span, rows), bf16),
@@ -367,7 +389,7 @@
     right_wide, total = run(
         functools.partial(kernel_sums, hops),
         [(SMEM, places)]
-        + [(VMEM, item) for item in (*rights, left_own, cot_wide, jnp.asarray(fold))],
+        + [(VMEM, item) for item in (*evens, *odds, left_own, cot_wide, jnp.asarray(fold))],
         [(wide, f32), ((3, pad_rows, 3 * outs), f32)],
         [pltpu.VMEM(block, f32), pltpu.VMEM((3, span, 3 * size), f32)],
         12, 8000000000,

time: 101 us -> 94.9 us (0.940)
  the two profiles are of different devices: /device:TPU:13 before, /device:TPU:0 now
where the time goes in v10:
time: 94.9 us; the launch traced here: 94.7 us
  starting transfers between devices  32.3 us (34%)
  waiting for transfers between devices  29.9 us (32%)
  Pallas kernels  19.1 us (20%)
  local copies, waits for them, and re-layouts  8.52 us (9%)
  other arithmetic  3.49 us (4%)
  between operations  1.03 us (1%)
    ppermute x13, waiting for transfers between devices, swapped(): lax.ppermute(value, axis, [(source, source ^ bit) for source in range(cou...  26.2 us
    ppermute x11, starting transfers between devices, shifted(): lax.ppermute(value, axis, [(source, (source + steps) % count) for source...  19.7 us
    pallas_call x7, Pallas kernels, run(): pl.pallas_call(function, out_shape=[jax.ShapeDtypeStruct(shape, kind) for...  19.1 us
    ppermute x13, starting transfers between devices, swapped(): lax.ppermute(value, axis, [(source, source ^ bit) for source in range(cou...  12.6 us
    ppermute x11, waiting for transfers between devices, shifted(): lax.ppermute(value, axis, [(source, (source + steps) % count) for source...  3.72 us
  transfers between devices with their start and end apart: 24, of which 8 were waited for; matrix products, arithmetic and copies ran while one was open for 8% of the time, Pallas kernels for 13%

profile of v10, /device:TPU:0, one launch (start us, length us, event | category | flops | bytes accessed | tf_op | source)
XLA Modules:
  0.0 94.7 jit_solution(11258242104324611648)
XLA Ops:
  0.7 1.9 %fusion.2 = (bf16[32,12,1,128]{3,2,1,0:T(2,128)(2,1)S(1)}, bf16[32,12,1,128]{3,2,1,0:T(2,128)(2,1)S(1)}) fusion(bf16[32,12,8,128]{3,2,1,0:T(8,128)(2,1)} %cot_ref.1), kind=kLoop, calls=%fused_computation.24 | loop fusion | bytes 393216 | tf_op jit(solution)/shard_map/slice | solution.py:326
  3.3 3.1 %collective-permute-start.2 = (bf16[80,8,128]{2,1,0:T(8,128)(2,1)S(1)}, bf16[80,8,128]{2,1,0:T(8,128)(2,1)S(1)}, u32[]{:S(2)}, u32[]{:S(2)}) collective-permute-start(bf16[80,8,128]{2,1,0:T(8,128)(2,1)S(1)} %constant_dynamic-slice_fusion.refs_0_), channel_id=1, source_target_pairs={{0,8},{4,12},{8,16},{12,20},{16,24},{20,28},{24,0},{28,4},{1,9},{5... | collective-permute-start | bytes 491528 | tf_op jit(solution)/shard_map/ppermute | solution.py:21
  6.3 2.6 %collective-permute-start.3 = (bf16[80,8,128]{2,1,0:T(8,128)(2,1)S(1)}, bf16[80,8,128]{2,1,0:T(8,128)(2,1)S(1)}, u32[]{:S(2)}, u32[]{:S(2)}) collective-permute-start(bf16[80,8,128]{2,1,0:T(8,128)(2,1)S(1)} %constant_dynamic-slice_fusion.refs_0_), channel_id=1, source_target_pairs={{0,16},{4,20},{8,24},{12,28},{16,0},{20,4},{24,8},{28,12},{1,17},{... | collective-permute-start | bytes 491528 | tf_op jit(solution)/shard_map/ppermute | solution.py:21
  8.9 1.5 %collective-permute-start.5 = (bf16[32,12,8,128]{3,2,1,0:T(8,128)(2,1)}, bf16[32,12,8,128]{3,2,1,0:T(8,128)(2,1)S(1)}, u32[]{:S(2)}, u32[]{:S(2)}) collective-permute-start(bf16[32,12,8,128]{3,2,1,0:T(8,128)(2,1)} %cot_ref.1), channel_id=1, source_target_pairs={{0,2},{1,3},{2,0},{3,1},{4,6},{5,7},{6,4},{7,5},{8,10},{9,11},{10,... | collective-permute-start | bytes 2359304 | tf_op jit(solution)/shard_map/ppermute | solution.py:293
  10.4 1.5 %collective-permute-start = (bf16[12,32,128]{2,1,0:T(8,128)(2,1)}, bf16[12,32,128]{2,1,0:T(8,128)(2,1)}, u32[]{:S(2)}, u32[]{:S(2)}) collective-permute-start(bf16[12,32,128]{2,1,0:T(8,128)(2,1)} %get-tuple-element.47), channel_id=1, source_target_pairs={{0,4},{4,8},{8,12},{12,16},{16,20},{20,24},{24,28},{28,0},{1,5},{5... | collective-permute-start | bytes 294920 | tf_op jit(solution)/shard_map/ppermute | solution.py:21
  11.9 3.2 %collective-permute-start.1 = (bf16[12,32,128]{2,1,0:T(8,128)(2,1)S(1)}, bf16[12,32,128]{2,1,0:T(8,128)(2,1)}, u32[]{:S(2)}, u32[]{:S(2)}) collective-permute-start(bf16[12,32,128]{2,1,0:T(8,128)(2,1)S(1)} %get-tuple-element.48), channel_id=1, source_target_pairs={{0,28},{4,0},{8,4},{12,8},{16,12},{20,16},{24,20},{28,24},{1,29},{... | collective-permute-start | bytes 294920 | tf_op jit(solution)/shard_map/ppermute | solution.py:21
  15.1 1.1 %constant_dynamic-slice_fusion.1 = bf16[3,3,3,32,10]{4,3,2,1,0:T(8,128)(2,1)S(1)} fusion(bf16[3,3,3,32,40]{4,3,2,1,0:T(8,128)(2,1)} %param.11, s32[]{:T(128)S(6)} %select_n.88), kind=kLoop, calls=%fused_computation.20 | loop fusion | bytes 34564 | tf_op jit(solution)/shard_map/dynamic_slice | solution.py:332
  16.8 1.4 %select_select_fusion = bf16[3,10,8,3,320]{4,3,2,1,0:T(4,128)(2,1)} fusion(pred[8,320]{1,0:T(8,128)(4,1)S(1)} %copy-done.4, pred[8,320]{1,0:T(8,128)(4,1)S(1)} %copy-done.5, pred[8,320]{1,0:T(8,128)(4,1)S(1)} %copy-done.6, bf16[3,10,3,320]{3,2,1,0:T(4,128)(2,1)S(1)} %copy.33, bf16[3,10,3,320]{3,2,1,0:T(4,128)(2,1)S(1)} %copy.32, ...), kind=kLoop, calls=%fused_computation.2 | loop fusion | flops 691200 | bytes 641280 | tf_op jit(solution)/shard_map/jit(_where)/select_n | solution.py:45
  19.1 1.7 %select_n.92.refs_10_.weight_ref = bf16[240,960]{1,0:T(8,128)(2,1)S(1)} reshape(bf16[3,10,8,3,320]{4,3,2,1,0:T(4,128)(2,1)} %select_select_fusion) | data formatting | bytes 921600 | tf_op jit(solution)/shard_map/jit(_where)/select_n | solution.py:45
  20.9 2.5 %collective-permute-start.7 = (bf16[2,80,8,128]{3,2,1,0:T(8,128)(2,1)S(1)}, bf16[2,80,8,128]{3,2,1,0:T(8,128)(2,1)S(1)}, u32[]{:S(2)}, u32[]{:S(2)}) collective-permute-start(bf16[2,80,8,128]{3,2,1,0:T(8,128)(2,1)S(1)} %shard_map.113), channel_id=1, source_target_pairs={{0,4},{4,0},{8,12},{12,8},{16,20},{20,16},{24,28},{28,24},{1,5},{5... | collective-permute-start | bytes 983048 | tf_op jit(solution)/shard_map/ppermute | solution.py:293
  24.4 1.6 %collective-permute-start.10 = (bf16[12,64,128]{2,1,0:T(8,128)(2,1)S(1)}, bf16[12,64,128]{2,1,0:T(8,128)(2,1)S(1)}, u32[]{:S(2)}, u32[]{:S(2)}) collective-permute-start(bf16[12,64,128]{2,1,0:T(8,128)(2,1)S(1)} %pad_maximum_fusion.halo_ref), channel_id=1, source_target_pairs={{0,2},{1,3},{2,0},{3,1},{4,6},{5,7},{6,4},{7,5},{8,10},{9,11},{10,... | collective-permute-start | bytes 589832 | tf_op jit(solution)/shard_map/ppermute | solution.py:293
  26.8 1.1 %collective-permute-start.9 = (bf16[80,8,128]{2,1,0:T(8,128)(2,1)S(1)}, bf16[80,8,128]{2,1,0:T(8,128)(2,1)S(1)}, u32[]{:S(2)}, u32[]{:S(2)}) collective-permute-start(bf16[80,8,128]{2,1,0:T(8,128)(2,1)S(1)} %collective-permute-done.8.refs_6_.refs_3_), channel_id=1, source_target_pairs={{0,4},{4,0},{8,12},{12,8},{16,20},{20,16},{24,28},{28,24},{1,5},{5... | collective-permute-start | bytes 491528 | tf_op jit(solution)/shard_map/ppermute | solution.py:293
  28.2 7.3 %collective-permute-done.6.refs_4_ = bf16[80,8,128]{2,1,0:T(8,128)(2,1)S(1)} collective-permute-done((bf16[80,8,128]{2,1,0:T(8,128)(2,1)S(1)}, bf16[80,8,128]{2,1,0:T(8,128)(2,1)S(1)}, u32[]{:S(2)}, u32[]{:S(2)}) %collective-permute-start.6) | collective-permute-done | bytes 163872 | tf_op jit(solution)/shard_map/ppermute | solution.py:293
  35.4 2.8 %collective-permute-done.9.refs_8_.refs_6_ = bf16[80,8,128]{2,1,0:T(8,128)(2,1)S(1)} collective-permute-done((bf16[80,8,128]{2,1,0:T(8,128)(2,1)S(1)}, bf16[80,8,128]{2,1,0:T(8,128)(2,1)S(1)}, u32[]{:S(2)}, u32[]{:S(2)}) %collective-permute-start.9) | collective-permute-done | bytes 163872 | tf_op jit(solution)/shard_map/ppermute | solution.py:293
  38.6 2.5 %collective-permute-done.11.refs_3_ = bf16[12,320,128]{2,1,0:T(8,128)(2,1)S(1)} collective-permute-done((bf16[12,320,128]{2,1,0:T(8,128)(2,1)S(1)}, bf16[12,320,128]{2,1,0:T(8,128)(2,1)S(1)}, u32[]{:S(2)}, u32[]{:S(2)}) %collective-permute-start.11) | collective-permute-done | bytes 983072 | tf_op jit(solution)/shard_map/ppermute | solution.py:293
  41.1 6.5 %shard_map.115 = (bf16[50,320,128]{2,1,0:T(8,128)(2,1)S(1)}, f32[80,8,128]{2,1,0:T(8,128)S(1)}, f32[80,32,128]{2,1,0:T(8,128)S(1)}, bf16[80,8,128]{2,1,0:T(8,128...) custom-call(s32[2]{0:T(128)S(1)} %pad_add_fusion.places, ...), custom_call_target="tpu_custom_call" | custom-call | flops 8000000000 | bytes 1024 | tf_op jit(solution)/shard_map/pallas_call | solution.py:280
  47.6 1.4 %collective-permute-start.13 = (bf16[80,8,128]{2,1,0:T(8,128)(2,1)S(1)}, bf16[80,8,128]{2,1,0:T(8,128)(2,1)S(1)}, u32[]{:S(2)}, u32[]{:S(2)}) collective-permute-start(bf16[80,8,128]{2,1,0:T(8,128)(2,1)S(1)} %get-tuple-element.71), channel_id=1, source_target_pairs={{0,16},{4,20},{8,24},{12,28},{16,0},{20,4},{24,8},{28,12},{1,17},{... | collective-permute-start | bytes 491528 | tf_op jit(solution)/shard_map/ppermute | solution.py:21
  49.0 1.5 %collective-permute-start.17 = (bf16[80,8,128]{2,1,0:T(8,128)(2,1)S(1)}, bf16[80,8,128]{2,1,0:T(8,128)(2,1)S(1)}, u32[]{:S(2)}, u32[]{:S(2)}) collective-permute-start(bf16[80,8,128]{2,1,0:T(8,128)(2,1)S(1)} %get-tuple-element.83), channel_id=1, source_target_pairs={{0,12},{4,16},{8,20},{12,24},{16,28},{20,0},{24,4},{28,8},{1,13},{... | collective-permute-start | bytes 491528 | tf_op jit(solution)/shard_map/ppermute | solution.py:21
  50.5 1.9 %collective-permute-start.18 = (bf16[80,8,128]{2,1,0:T(8,128)(2,1)S(1)}, bf16[80,8,128]{2,1,0:T(8,128)(2,1)S(1)}, u32[]{:S(2)}, u32[]{:S(2)}) collective-permute-start(bf16[80,8,128]{2,1,0:T(8,128)(2,1)S(1)} %get-tuple-element.84), channel_id=1, source_target_pairs={{0,8},{4,12},{8,16},{12,20},{16,24},{20,28},{24,0},{28,4},{1,9},{5... | collective-permute-start | bytes 491528 | tf_op jit(solution)/shard_map/ppermute | solution.py:21
  52.3 7.0 %shard_map.116 = (f32[80,56,128]{2,1,0:T(8,128)S(1)}, f32[3,32,96]{2,1,0:T(8,128)S(1)}) custom-call(s32[2]{0:T(128)S(1)} %pad_add_fusion.places, bf16[80,8,128]{2,1,0:T(8,128)(2,1)S(1)} %constant_dynamic-slice_fusion.refs_0_, bf16[80,8,128]{2,1,0:T(8,128)(2,1)S(1)} %collective-permute-done.2.refs_0_.refs_4_.refs_1_, ...), custom_call_target="tpu_custom_call" | custom-call | flops 8000000000 | bytes 1024 | tf_op jit(solution)/shard_map/pallas_call | solution.py:280
  59.4 1.0 %collective-permute-start.12 = (f32[3,32,96]{2,1,0:T(8,128)S(1)}, f32[3,32,96]{2,1,0:T(8,128)S(1)}, u32[]{:S(2)}, u32[]{:S(2)}) collective-permute-start(f32[3,32,96]{2,1,0:T(8,128)S(1)} %get-tuple-element.70), channel_id=1, source_target_pairs={{0,16},{4,20},{8,24},{12,28},{16,0},{20,4},{24,8},{28,12},{1,17},{... | collective-permute-start | bytes 110600 | tf_op jit(solution)/shard_map/ppermute | solution.py:293
  60.4 3.1 %shard_map.117 = (f32[80,8,128]{2,1,0:T(8,128)S(1)}, f32[80,16,128]{2,1,0:T(8,128)S(1)}, bf16[80,8,128]{2,1,0:T(8,128)(2,1)S(1)}, bf16[80,8,128]{2,1,0:T(8,128)(2,1)S(1)}) custom-call(bf16[80,8,128]{2,1,0:T(8,128)(2,1)S(1)} %constant_dynamic-slice_fusion.2.refs_9_.refs_7_.left_ref, bf16[240,960]{1,0:T(8,128)(2,1)S(1)} %select_n.92.refs_10_.weight_ref, ...), custom_call_target="tpu_custom_call" | custom-call | flops 1000000 | bytes 1024 | tf_op jit(solution)/shard_map/pallas_call | solution.py:280
  63.5 4.0 %collective-permute-done.12 = f32[3,32,96]{2,1,0:T(8,128)S(1)} collective-permute-done((f32[3,32,96]{2,1,0:T(8,128)S(1)}, f32[3,32,96]{2,1,0:T(8,128)S(1)}, u32[]{:S(2)}, u32[]{:S(2)}) %collective-permute-start.12) | collective-permute-done | bytes 36896 | tf_op jit(solution)/shard_map/ppermute | solution.py:293
  67.5 3.7 %collective-permute-done.17 = bf16[80,8,128]{2,1,0:T(8,128)(2,1)S(1)} collective-permute-done((bf16[80,8,128]{2,1,0:T(8,128)(2,1)S(1)}, bf16[80,8,128]{2,1,0:T(8,128)(2,1)S(1)}, u32[]{:S(2)}, u32[]{:S(2)}) %collective-permute-start.17) | collective-permute-done | bytes 163872 | tf_op jit(solution)/shard_map/ppermute | solution.py:21
  71.2 4.5 %collective-permute-start.20 = (bf16[80,8,128]{2,1,0:T(8,128)(2,1)S(1)}, bf16[80,8,128]{2,1,0:T(8,128)(2,1)S(1)}, u32[]{:S(2)}, u32[]{:S(2)}) collective-permute-start(bf16[80,8,128]{2,1,0:T(8,128)(2,1)S(1)} %get-tuple-element.86), channel_id=1, source_target_pairs={{0,20},{4,24},{8,28},{12,0},{16,4},{20,8},{24,12},{28,16},{1,21},{... | collective-permute-start | bytes 491528 | tf_op jit(solution)/shard_map/ppermute | solution.py:21
  75.7 2.0 %shard_map.118 = (bf16[80,8,128]{2,1,0:T(8,128)(2,1)}, f32[80,8,128]{2,1,0:T(8,128)S(1)}, bf16[80,8,128]{2,1,0:T(8,128)(2,1)S(1)}) custom-call(bf16[80,8,128]{2,1,0:T(8,128)(2,1)S(1)} %constant_dynamic-slice_fusion.2.refs_9_.refs_7_.left_ref, bf16[240,960]{1,0:T(8,128)(2,1)S(1)} %select_n.92.refs_10_.weight_ref, ...), custom_call_target="tpu_custom_call" | custom-call | flops 1000000 | bytes 1024 | tf_op jit(solution)/shard_map/pallas_call | solution.py:280
  77.8 2.0 %collective-permute-start.15 = (f32[3,32,96]{2,1,0:T(8,128)S(1)}, f32[3,32,96]{2,1,0:T(8,128)S(1)}, u32[]{:S(2)}, u32[]{:S(2)}) collective-permute-start(f32[3,32,96]{2,1,0:T(8,128)S(1)} %add.66), channel_id=1, source_target_pairs={{0,4},{4,0},{8,12},{12,8},{16,20},{20,16},{24,28},{28,24},{1,5},{5... | collective-permute-start | bytes 110600 | tf_op jit(solution)/shard_map/ppermute | solution.py:293
  79.8 7.1 %collective-permute-done.15 = f32[3,32,96]{2,1,0:T(8,128)S(1)} collective-permute-done((f32[3,32,96]{2,1,0:T(8,128)S(1)}, f32[3,32,96]{2,1,0:T(8,128)S(1)}, u32[]{:S(2)}, u32[]{:S(2)}) %collective-permute-start.15) | collective-permute-done | bytes 36896 | tf_op jit(solution)/shard_map/ppermute | solution.py:293
  87.1 1.6 %collective-permute-start.22 = (f32[3,32,96]{2,1,0:T(8,128)S(1)}, f32[3,32,96]{2,1,0:T(8,128)S(1)}, u32[]{:S(2)}, u32[]{:S(2)}) collective-permute-start(f32[3,32,96]{2,1,0:T(8,128)S(1)} %add.67), channel_id=1, source_target_pairs={{0,2},{1,3},{2,0},{3,1},{4,6},{5,7},{6,4},{7,5},{8,10},{9,11},{10,... | collective-permute-start | bytes 110600 | tf_op jit(solution)/shard_map/ppermute | solution.py:293
  89.8 1.4 %collective-permute-done.22 = f32[3,32,96]{2,1,0:T(8,128)S(1)} collective-permute-done((f32[3,32,96]{2,1,0:T(8,128)S(1)}, f32[3,32,96]{2,1,0:T(8,128)S(1)}, u32[]{:S(2)}, u32[]{:S(2)}) %collective-permute-start.22) | collective-permute-done | bytes 36896 | tf_op jit(solution)/shard_map/ppermute | solution.py:293
  91.2 1.1 %collective-permute-done.23 = f32[3,32,96]{2,1,0:T(8,128)S(1)} collective-permute-done((f32[3,32,96]{2,1,0:T(8,128)S(1)}, f32[3,32,96]{2,1,0:T(8,128)S(1)}, u32[]{:S(2)}, u32[]{:S(2)}) %collective-permute-start.23) | collective-permute-done | bytes 36896 | tf_op jit(solution)/shard_map/ppermute | solution.py:293
  93.7 1.0 %copy.37 = f32[3,3,3,32,40]{4,3,2,1,0:T(8,128)} copy(f32[3,3,3,32,40]{3,4,2,1,0:T(8,128)S(1)} %mul.20) | data formatting | bytes 276480
  (68 shorter events, 7.4 us)
Async XLA Ops:
  0.6 2.6 %copy-start = (bf16[320,8,128]{2,1,0:T(8,128)(2,1)S(1)}, bf16[320,8,128]{2,1,0:T(8,128)(2,1)}, u32[]{:S(2)}) copy-start(bf16[320,8,128]{2,1,0:T(8,128)(2,1)} %param.10) | copy-start | bytes 1966084
  0.6 15.6 %copy-start.3 = (bf16[32,320,1,1,1]{1,0,4,3,2:T(8,128)(2,1)S(1)}, bf16[32,320,1,1,1]{1,0,4,3,2:T(8,128)(2,1)}, u32[]{:S(2)}) copy-start(bf16[32,320,1,1,1]{1,0,4,3,2:T(8,128)(2,1)} %constant.59) | copy-start | bytes 61444
  0.7 16.1 %copy-start.4 = (pred[8,320]{1,0:T(8,128)(4,1)S(1)}, pred[8,320]{1,0:T(8,128)(4,1)}, u32[]{:S(2)}) copy-start(pred[8,320]{1,0:T(8,128)(4,1)} %constant.55.clone) | copy-start | bytes 7684
  0.7 16.1 %copy-start.5 = (pred[8,320]{1,0:T(8,128)(4,1)S(1)}, pred[8,320]{1,0:T(8,128)(4,1)}, u32[]{:S(2)}) copy-start(pred[8,320]{1,0:T(8,128)(4,1)} %constant.56.clone) | copy-start | bytes 7684
  0.7 16.1 %copy-start.6 = (pred[8,320]{1,0:T(8,128)(4,1)S(1)}, pred[8,320]{1,0:T(8,128)(4,1)}, u32[]{:S(2)}) copy-start(pred[8,320]{1,0:T(8,128)(4,1)} %constant.57.clone) | copy-start | bytes 7684
  3.3 17.6 %collective-permute-start.2 = (bf16[80,8,128]{2,1,0:T(8,128)(2,1)S(1)}, bf16[80,8,128]{2,1,0:T(8,128)(2,1)S(1)}, u32[]{:S(2)}, u32[]{:S(2)}) collective-permute-start(bf16[80,8,128]{2,1,0:T(8,128)(2,1)S(1)} %constant_dynamic-slice_fusion.refs_0_), channel_id=1, source_target_pairs={{0,8},{4,12},{8,16},{12,20},{16,24},{20,28},{24,0},{28,4},{1,9},{5... | collective-permute-start | bytes 491528 | tf_op jit(solution)/shard_map/ppermute | solution.py:21
  6.3 14.5 %collective-permute-start.3 = (bf16[80,8,128]{2,1,0:T(8,128)(2,1)S(1)}, bf16[80,8,128]{2,1,0:T(8,128)(2,1)S(1)}, u32[]{:S(2)}, u32[]{:S(2)}) collective-permute-start(bf16[80,8,128]{2,1,0:T(8,128)(2,1)S(1)} %constant_dynamic-slice_fusion.refs_0_), channel_id=1, source_target_pairs={{0,16},{4,20},{8,24},{12,28},{16,0},{20,4},{24,8},{28,12},{1,17},{... | collective-permute-start | bytes 491528 | tf_op jit(solution)/shard_map/ppermute | solution.py:21
  8.9 29.3 %collective-permute-start.5 = (bf16[32,12,8,128]{3,2,1,0:T(8,128)(2,1)}, bf16[32,12,8,128]{3,2,1,0:T(8,128)(2,1)S(1)}, u32[]{:S(2)}, u32[]{:S(2)}) collective-permute-start(bf16[32,12,8,128]{3,2,1,0:T(8,128)(2,1)} %cot_ref.1), channel_id=1, source_target_pairs={{0,2},{1,3},{2,0},{3,1},{4,6},{5,7},{6,4},{7,5},{8,10},{9,11},{10,... | collective-permute-start | bytes 2359304 | tf_op jit(solution)/shard_map/ppermute | solution.py:293
  10.4 10.4 %collective-permute-start = (bf16[12,32,128]{2,1,0:T(8,128)(2,1)}, bf16[12,32,128]{2,1,0:T(8,128)(2,1)}, u32[]{:S(2)}, u32[]{:S(2)}) collective-permute-start(bf16[12,32,128]{2,1,0:T(8,128)(2,1)} %get-tuple-element.47), channel_id=1, source_target_pairs={{0,4},{4,8},{8,12},{12,16},{16,20},{20,24},{24,28},{28,0},{1,5},{5... | collective-permute-start | bytes 294920 | tf_op jit(solution)/shard_map/ppermute | solution.py:21
  11.9 8.9 %collective-permute-start.1 = (bf16[12,32,128]{2,1,0:T(8,128)(2,1)S(1)}, bf16[12,32,128]{2,1,0:T(8,128)(2,1)}, u32[]{:S(2)}, u32[]{:S(2)}) collective-permute-start(bf16[12,32,128]{2,1,0:T(8,128)(2,1)S(1)} %get-tuple-element.48), channel_id=1, source_target_pairs={{0,28},{4,0},{8,4},{12,8},{16,12},{20,16},{24,20},{28,24},{1,29},{... | collective-permute-start | bytes 294920 | tf_op jit(solution)/shard_map/ppermute | solution.py:21
  16.6 11.4 %copy-start.1 = (bf16[32,12,8,128]{3,2,1,0:T(8,128)(2,1)S(1)}, bf16[32,12,8,128]{3,2,1,0:T(8,128)(2,1)}, u32[]{:S(2)}) copy-start(bf16[32,12,8,128]{3,2,1,0:T(8,128)(2,1)} %cot_ref.1) | copy-start | bytes 2359300
  20.8 6.0 %collective-permute-start.8 = (bf16[80,8,128]{2,1,0:T(8,128)(2,1)S(1)}, bf16[80,8,128]{2,1,0:T(8,128)(2,1)S(1)}, u32[]{:S(2)}, u32[]{:S(2)}) collective-permute-start(bf16[80,8,128]{2,1,0:T(8,128)(2,1)S(1)} %constant_dynamic-slice_fusion.refs_0_), channel_id=1, source_target_pairs={{0,24},{4,28},{8,0},{12,4},{16,8},{20,12},{24,16},{28,20},{1,25},{... | collective-permute-start | bytes 491528 | tf_op jit(solution)/shard_map/ppermute | solution.py:21
  20.9 17.3 %collective-permute-start.7 = (bf16[2,80,8,128]{3,2,1,0:T(8,128)(2,1)S(1)}, bf16[2,80,8,128]{3,2,1,0:T(8,128)(2,1)S(1)}, u32[]{:S(2)}, u32[]{:S(2)}) collective-permute-start(bf16[2,80,8,128]{3,2,1,0:T(8,128)(2,1)S(1)} %shard_map.113), channel_id=1, source_target_pairs={{0,4},{4,0},{8,12},{12,8},{16,20},{20,16},{24,28},{28,24},{1,5},{5... | collective-permute-start | bytes 983048 | tf_op jit(solution)/shard_map/ppermute | solution.py:293
  24.4 13.9 %collective-permute-start.10 = (bf16[12,64,128]{2,1,0:T(8,128)(2,1)S(1)}, bf16[12,64,128]{2,1,0:T(8,128)(2,1)S(1)}, u32[]{:S(2)}, u32[]{:S(2)}) collective-permute-start(bf16[12,64,128]{2,1,0:T(8,128)(2,1)S(1)} %pad_maximum_fusion.halo_ref), channel_id=1, source_target_pairs={{0,2},{1,3},{2,0},{3,1},{4,6},{5,7},{6,4},{7,5},{8,10},{9,11},{10,... | collective-permute-start | bytes 589832 | tf_op jit(solution)/shard_map/ppermute | solution.py:293
  25.9 9.5 %collective-permute-start.6 = (bf16[80,8,128]{2,1,0:T(8,128)(2,1)S(1)}, bf16[80,8,128]{2,1,0:T(8,128)(2,1)S(1)}, u32[]{:S(2)}, u32[]{:S(2)}) collective-permute-start(bf16[80,8,128]{2,1,0:T(8,128)(2,1)S(1)} %constant_dynamic-slice_fusion.refs_0_), channel_id=1, source_target_pairs={{0,4},{4,0},{8,12},{12,8},{16,20},{20,16},{24,28},{28,24},{1,5},{5... | collective-permute-start | bytes 491528 | tf_op jit(solution)/shard_map/ppermute | solution.py:293
  26.8 11.4 %collective-permute-start.9 = (bf16[80,8,128]{2,1,0:T(8,128)(2,1)S(1)}, bf16[80,8,128]{2,1,0:T(8,128)(2,1)S(1)}, u32[]{:S(2)}, u32[]{:S(2)}) collective-permute-start(bf16[80,8,128]{2,1,0:T(8,128)(2,1)S(1)} %collective-permute-done.8.refs_6_.refs_3_), channel_id=1, source_target_pairs={{0,4},{4,0},{8,12},{12,8},{16,20},{20,16},{24,28},{28,24},{1,5},{5... | collective-permute-start | bytes 491528 | tf_op jit(solution)/shard_map/ppermute | solution.py:293
  35.4 3.2 %collective-permute-start.4 = (bf16[12,320,128]{2,1,0:T(8,128)(2,1)S(1)}, bf16[12,320,128]{2,1,0:T(8,128)(2,1)S(1)}, u32[]{:S(2)}, u32[]{:S(2)}) collective-permute-start(bf16[12,320,128]{2,1,0:T(8,128)(2,1)S(1)} %shard_map.112.refs_0_), channel_id=1, source_target_pairs={{0,1},{1,0},{2,3},{3,2},{4,5},{5,4},{6,7},{7,6},{8,9},{9,8},{10,11... | collective-permute-start | bytes 2949128 | tf_op jit(solution)/shard_map/ppermute | solution.py:293
  38.4 2.6 %collective-permute-start.11 = (bf16[12,320,128]{2,1,0:T(8,128)(2,1)S(1)}, bf16[12,320,128]{2,1,0:T(8,128)(2,1)S(1)}, u32[]{:S(2)}, u32[]{:S(2)}) collective-permute-start(bf16[12,320,128]{2,1,0:T(8,128)(2,1)S(1)} %shard_map.114.refs_2_), channel_id=1, source_target_pairs={{0,1},{1,0},{2,3},{3,2},{4,5},{5,4},{6,7},{7,6},{8,9},{9,8},{10,11... | collective-permute-start | bytes 2949128 | tf_op jit(solution)/shard_map/ppermute | solution.py:293
  38.6 13.7 %copy-start.2 = (f32[32,240]{1,0:T(8,128)S(1)}, f32[32,240]{1,0:T(8,128)}, u32[]{:S(2)}) copy-start(f32[32,240]{1,0:T(8,128)} %constant.58.clone.refs_9_) | copy-start | bytes 92164
  47.6 19.9 %collective-permute-start.13 = (bf16[80,8,128]{2,1,0:T(8,128)(2,1)S(1)}, bf16[80,8,128]{2,1,0:T(8,128)(2,1)S(1)}, u32[]{:S(2)}, u32[]{:S(2)}) collective-permute-start(bf16[80,8,128]{2,1,0:T(8,128)(2,1)S(1)} %get-tuple-element.71), channel_id=1, source_target_pairs={{0,16},{4,20},{8,24},{12,28},{16,0},{20,4},{24,8},{28,12},{1,17},{... | collective-permute-start | bytes 491528 | tf_op jit(solution)/shard_map/ppermute | solution.py:21
  49.0 22.2 %collective-permute-start.17 = (bf16[80,8,128]{2,1,0:T(8,128)(2,1)S(1)}, bf16[80,8,128]{2,1,0:T(8,128)(2,1)S(1)}, u32[]{:S(2)}, u32[]{:S(2)}) collective-permute-start(bf16[80,8,128]{2,1,0:T(8,128)(2,1)S(1)} %get-tuple-element.83), channel_id=1, source_target_pairs={{0,12},{4,16},{8,20},{12,24},{16,28},{20,0},{24,4},{28,8},{1,13},{... | collective-permute-start | bytes 491528 | tf_op jit(solution)/shard_map/ppermute | solution.py:21
  50.5 20.8 %collective-permute-start.18 = (bf16[80,8,128]{2,1,0:T(8,128)(2,1)S(1)}, bf16[80,8,128]{2,1,0:T(8,128)(2,1)S(1)}, u32[]{:S(2)}, u32[]{:S(2)}) collective-permute-start(bf16[80,8,128]{2,1,0:T(8,128)(2,1)S(1)} %get-tuple-element.84), channel_id=1, source_target_pairs={{0,8},{4,12},{8,16},{12,20},{16,24},{20,28},{24,0},{28,4},{1,9},{5... | collective-permute-start | bytes 491528 | tf_op jit(solution)/shard_map/ppermute | solution.py:21
  59.4 8.1 %collective-permute-start.12 = (f32[3,32,96]{2,1,0:T(8,128)S(1)}, f32[3,32,96]{2,1,0:T(8,128)S(1)}, u32[]{:S(2)}, u32[]{:S(2)}) collective-permute-start(f32[3,32,96]{2,1,0:T(8,128)S(1)} %get-tuple-element.70), channel_id=1, source_target_pairs={{0,16},{4,20},{8,24},{12,28},{16,0},{20,4},{24,8},{28,12},{1,17},{... | collective-permute-start | bytes 110600 | tf_op jit(solution)/shard_map/ppermute | solution.py:293
  67.5 10.3 %collective-permute-start.14 = (f32[3,32,96]{2,1,0:T(8,128)S(1)}, f32[3,32,96]{2,1,0:T(8,128)S(1)}, u32[]{:S(2)}, u32[]{:S(2)}) collective-permute-start(f32[3,32,96]{2,1,0:T(8,128)S(1)} %add.64), channel_id=1, source_target_pairs={{0,8},{4,12},{8,0},{12,4},{16,24},{20,28},{24,16},{28,20},{1,9},{5... | collective-permute-start | bytes 110600 | tf_op jit(solution)/shard_map/ppermute | solution.py:293
  71.2 17.7 %collective-permute-start.19 = (bf16[80,8,128]{2,1,0:T(8,128)(2,1)S(1)}, bf16[80,8,128]{2,1,0:T(8,128)(2,1)S(1)}, u32[]{:S(2)}, u32[]{:S(2)}) collective-permute-start(bf16[80,8,128]{2,1,0:T(8,128)(2,1)S(1)} %get-tuple-element.85), channel_id=1, source_target_pairs={{0,24},{4,28},{8,0},{12,4},{16,8},{20,12},{24,16},{28,20},{1,25},{... | collective-permute-start | bytes 491528 | tf_op jit(solution)/shard_map/ppermute | solution.py:21
  71.2 17.7 %collective-permute-start.20 = (bf16[80,8,128]{2,1,0:T(8,128)(2,1)S(1)}, bf16[80,8,128]{2,1,0:T(8,128)(2,1)S(1)}, u32[]{:S(2)}, u32[]{:S(2)}) collective-permute-start(bf16[80,8,128]{2,1,0:T(8,128)(2,1)S(1)} %get-tuple-element.86), channel_id=1, source_target_pairs={{0,20},{4,24},{8,28},{12,0},{16,4},{20,8},{24,12},{28,16},{1,21},{... | collective-permute-start | bytes 491528 | tf_op jit(solution)/shard_map/ppermute | solution.py:21
  77.7 9.3 %collective-permute-start.16 = (bf16[80,8,128]{2,1,0:T(8,128)(2,1)S(1)}, bf16[80,8,128]{2,1,0:T(8,128)(2,1)S(1)}, u32[]{:S(2)}, u32[]{:S(2)}) collective-permute-start(bf16[80,8,128]{2,1,0:T(8,128)(2,1)S(1)} %get-tuple-element.78), channel_id=1, source_target_pairs={{0,28},{4,0},{8,4},{12,8},{16,12},{20,16},{24,20},{28,24},{1,29},{... | collective-permute-start | bytes 491528 | tf_op jit(solution)/shard_map/ppermute | solution.py:21
  77.8 9.2 %collective-permute-start.15 = (f32[3,32,96]{2,1,0:T(8,128)S(1)}, f32[3,32,96]{2,1,0:T(8,128)S(1)}, u32[]{:S(2)}, u32[]{:S(2)}) collective-permute-start(f32[3,32,96]{2,1,0:T(8,128)S(1)} %add.66), channel_id=1, source_target_pairs={{0,4},{4,0},{8,12},{12,8},{16,20},{20,16},{24,28},{28,24},{1,5},{5... | collective-permute-start | bytes 110600 | tf_op jit(solution)/shard_map/ppermute | solution.py:293
  87.0 2.8 %collective-permute-start.21 = (f32[3,32,96]{2,1,0:T(8,128)S(1)}, f32[3,32,96]{2,1,0:T(8,128)S(1)}, u32[]{:S(2)}, u32[]{:S(2)}) collective-permute-start(f32[3,32,96]{2,1,0:T(8,128)S(1)} %add.67), channel_id=1, source_target_pairs={{0,1},{1,0},{2,3},{3,2},{4,5},{5,4},{6,7},{7,6},{8,9},{9,8},{10,11... | collective-permute-start | bytes 110600 | tf_op jit(solution)/shard_map/ppermute | solution.py:293
  87.1 4.2 %collective-permute-start.22 = (f32[3,32,96]{2,1,0:T(8,128)S(1)}, f32[3,32,96]{2,1,0:T(8,128)S(1)}, u32[]{:S(2)}, u32[]{:S(2)}) collective-permute-start(f32[3,32,96]{2,1,0:T(8,128)S(1)} %add.67), channel_id=1, source_target_pairs={{0,2},{1,3},{2,0},{3,1},{4,6},{5,7},{6,4},{7,5},{8,10},{9,11},{10,... | collective-permute-start | bytes 110600 | tf_op jit(solution)/shard_map/ppermute | solution.py:293
  88.6 3.7 %collective-permute-start.23 = (f32[3,32,96]{2,1,0:T(8,128)S(1)}, f32[3,32,96]{2,1,0:T(8,128)S(1)}, u32[]{:S(2)}, u32[]{:S(2)}) collective-permute-start(f32[3,32,96]{2,1,0:T(8,128)S(1)} %add.67), channel_id=1, source_target_pairs={{0,3},{1,2},{2,1},{3,0},{4,7},{5,6},{6,5},{7,4},{8,11},{9,10},{10,... | collective-permute-start | bytes 110600 | tf_op jit(solution)/shard_map/ppermute | solution.py:293

commit v11 on v10

--- a/solution.py
+++ b/solution.py
@@ -139,32 +139,13 @@
     lax.fori_loop(0, count // width, step, 0)
 
 
-def upper_grads(keys, reach, far, pairs, places, *refs):
-    block_refs, refs = refs[: len(keys)], refs[len(keys) :]
-    even_refs, odd_refs, refs = refs[:pairs], refs[pairs : pairs + 2], refs[pairs + 2 :]
-    left_ref, weight_ref, cot_s, left_sum, grad_out = refs[:5]
-    sent_refs, (left_s, right_s, grad_s, sems) = refs[5 : 5 + far], refs[5 + far :]
-    channels, width, rows = left_ref.shape
-    levels, span = block_refs[0].shape[:2]
+def upper_grads(reach, far, left_ref, weight_ref, cot_s, right_s, left_sum, grad_out, *rest):
+    sent_refs, (left_s, grad_s) = rest[:far], rest[far:]
+    width = left_ref.shape[1]
     f32, bf16 = jnp.float32, jnp.bfloat16
-
-    copies = []
-    for at, (key, source) in enumerate(zip(keys, block_refs)):
-        start = (places[0] ^ key) * levels + 1
-        copies.append(pltpu.make_async_copy(source, cot_s.at[pl.ds(start, levels)], sems.at[at]))
-    for copy in copies:
-        copy.start()
-    cot_s[0] = jnp.zeros((span, rows), bf16)
-    cot_s[D + 1] = jnp.zeros((span, rows), bf16)
     left_s[...] = left_ref[...].astype(f32)
     left_sum[...] = jnp.zeros(left_sum.shape, f32)
     grad_s[...] = jnp.zeros(grad_s.shape, f32)
-    hops = reach // width
-    for at in range(far + 1):
-        block = right_block(places, hops - at, (None, *even_refs), (None, *odd_refs))
-        right_s[:, at * width : (at + 1) * width] = block
-    for copy in copies:
-        copy.wait()
     add_grads(
         D // 2, D // 2, reach, 0, cot_s, weight_ref, left_s, right_s, left_sum, grad_s
     )
@@ -196,23 +177,34 @@
         sent_ref[...] = (grad_s[:, at * width : (at + 1) * width] * (1.0 / GROUP)).astype(bf16)
 
 
-def kernel_sums(hops, places, *refs):
+def kernel_sums(keys, hops, places, *refs):
+    block_refs, refs = refs[: len(keys)], refs[len(keys) :]
     pairs = hops // 2
     even_refs, odd_refs, refs = refs[: pairs + 1], refs[pairs + 1 : pairs + 4], refs[pairs + 4 :]
-    left_ref, cot_s, fold_ref, right_s, sums_ref, left_s, prod_s = refs
+    left_ref, fold_ref, cot_s, right_s, sums_ref, left_s, prod_s, sems = refs
     channels, width, rows = left_ref.shape
     groups = channels // GROUP
-    span = cot_s.shape[1]
+    levels, span = block_refs[0].shape[:2]
     outs = span // (width + 2)
     main = outs * width
     size = groups * width
     reach = hops * width
     f32, bf16 = jnp.float32, jnp.bfloat16
 
+    copies = []
+    for at, (key, source) in enumerate(zip(keys, block_refs)):
+        start = (places[0] ^ key) * levels + 1
+        copies.append(pltpu.make_async_copy(source, cot_s.at[pl.ds(start, levels)], sems.at[at]))
+    for copy in copies:
+        copy.start()
+    cot_s[0] = jnp.zeros((span, rows), bf16)
+    cot_s[D + 1] = jnp.zeros((span, rows), bf16)
     left_s[...] = left_ref[...].astype(f32)
     for hop in range(hops + 1):
         at = reach - hop * width
         right_s[:, at : at + width] = right_block(places, hop, even_refs, odd_refs)
+    for copy in copies:
+        copy.wait()
     prod_s[...] = jnp.zeros(prod_s.shape, f32)
     chunk = width // 2
 
@@ -363,38 +355,32 @@
     f32_block, bf16_block = (block, f32), (block, bf16)
     reach = hops * width
     keys = sorted(blocks)
-    cot_wide, left_part, grad_part, *sent = run(
-        functools.partial(upper_grads, keys, reach, far, pairs),
+    cot_wide, right_wide, total = run(
+        functools.partial(kernel_sums, keys, hops),
         [(SMEM, places)]
         + [(ANY, blocks[key]) for key in keys]
-        + [(VMEM, item) for item in (*evens[1:], *odds[1:])]
-        + [(VMEM, left_own), (VMEM, weights)],
-        [
-            ((D + 2, span, rows), bf16),
-            f32_block,
-            ((channels, (near + 1) * width, rows), f32),
-            *[bf16_block] * far,
-        ],
+        + [(VMEM, item) for item in (*evens, *odds, left_own, jnp.asarray(fold))],
+        [((D + 2, span, rows), bf16), (wide, f32), ((3, pad_rows, 3 * outs), f32)],
         [
             pltpu.VMEM(block, f32),
-            pltpu.VMEM((channels, (far + 1) * width, rows), f32),
-            pltpu.VMEM(wide, f32),
+            pltpu.VMEM((3, span, 3 * size), f32),
             pltpu.SemaphoreType.DMA((parts,)),
         ],
         12, 8000000000,
     )
+    bits = [1 << k for k in reversed(range(columns.bit_length() - 1))]
+    left_part, grad_part, *sent = run(
+        functools.partial(upper_grads, reach, far),
+        [(VMEM, item) for item in (left_own, weights, cot_wide, right_wide)],
+        [f32_block, ((channels, (near + 1) * width, rows), f32), *[bf16_block] * far],
+        [pltpu.VMEM(block, f32), pltpu.VMEM(wide, f32)],
+        12, 8000000000,
+    )
+    total = total_swapping(total, bits[0])
+    sent, grad_part, total = lax.optimization_barrier((sent, grad_part, total))
     arrived = {
         hop: shifted(value, "col", -hop) for hop, value in zip(range(hops, near, -1), sent)
     }
-    right_wide, total = run(
-        functools.partial(kernel_sums, hops),
-        [(SMEM, places)]
-        + [(VMEM, item) for item in (*evens, *odds, left_own, cot_wide, jnp.asarray(fold))],
-        [(wide, f32), ((3, pad_rows, 3 * outs), f32)],
-        [pltpu.VMEM(block, f32), pltpu.VMEM((3, span, 3 * size), f32)],
-        12, 8000000000,
-    )
-    bits = [1 << k for k in reversed(range(columns.bit_length() - 1))]
     middle = near - 1
 
     def lower(first_level, count, done, kind, left_part, grad_part):
@@ -420,24 +406,20 @@
             8, 1000000,
         )
 
+    left_part, grad_part, *sent = lower(width, D // 2 - width, 0, f32, left_part, grad_part)
+    total = total_swapping(total, bits[1])
     grad_part, total = lax.optimization_barrier((grad_part, total))
-    left_part, grad_part, *sent = lower(width, D // 2 - width, 0, f32, left_part, grad_part)
-    total = total_swapping(total, bits[0])
-    sent, grad_part, total, arrived[near + 1] = lax.optimization_barrier(
-        (sent, grad_part, total, arrived[near + 1])
-    )
-    sent, *items = lax.optimization_barrier((sent, *[arrived[hop] for hop in sorted(arrived)]))
-    arrived = dict(zip(sorted(arrived), items))
-    arrived.update(
-        {hop: shifted(value, "col", -hop) for hop, value in zip(range(near, 1, -1), sent)}
-    )
-    grad_left, own, *sent = lower(0, width, middle, bf16, left_part, grad_part)
-    total = total_swapping(total, bits[1])
-    sent, total = lax.optimization_barrier((sent, total))
-    arrived[1] = shifted(sent[0], "col", -1)
+    grad_left, own, *last = lower(0, width, middle, bf16, left_part, grad_part)
     for bit in bits[2:]:
         total = total_swapping(total, bit)
-    total, arrived[1] = lax.optimization_barrier((total, arrived[1]))
+    distant = sorted(arrived)
+    pieces = [total] + [swapped(total, "disp", key) for key in range(1, parts)]
+    sent, last, pieces, *items = lax.optimization_barrier(
+        (sent, last, pieces, *[arrived[hop] for hop in distant])
+    )
+    arrived = dict(zip(distant, items))
+    for hop, value in zip(range(near, 0, -1), [*sent, *last]):
+        arrived[hop] = shifted(value, "col", -hop)
 
     total_right = own
     for hop in range(1, hops + 1):
@@ -445,8 +427,7 @@
             column + hop < columns, arrived[hop].astype(f32), 0.0
         )
 
-    pieces = jnp.stack([total] + [swapped(total, "disp", key) for key in range(1, parts)])
-    pieces = pieces[jnp.arange(parts) ^ part][:, :, : 3 * groups]
+    pieces = jnp.stack(pieces)[jnp.arange(parts) ^ part][:, :, : 3 * groups]
     total = pieces.reshape(parts, 3, 3, groups, 3, outs)
     cell_count = D * width * columns * rows
     grad_kernel = jnp.transpose(total, (4, 1, 2, 5, 0, 3))[::-1].reshape(3, 3, 3, outs, G)

time: 94.9 us -> 99.5 us (1.048)
  the two profiles are of different devices: /device:TPU:0 before, /device:TPU:13 now
where the time goes in v11:
time: 99.5 us; the launch traced here: 97.7 us
  waiting for transfers between devices  28 us (28%)
  starting transfers between devices  26.9 us (27%)
  Pallas kernels  19.9 us (20%)
  local copies, waits for them, and re-layouts  17.1 us (17%)
  other arithmetic  4.48 us (5%)
  between operations  1.02 us (1%)
    pallas_call x7, Pallas kernels, run(): pl.pallas_call(function, out_shape=[jax.ShapeDtypeStruct(shape, kind) for...  19.9 us
    ppermute x11, waiting for transfers between devices, shifted(): lax.ppermute(value, axis, [(source, (source + steps) % count) for source...  15.9 us
    ppermute x13, starting transfers between devices, swapped(): lax.ppermute(value, axis, [(source, source ^ bit) for source in range(cou...  14 us
    ppermute x11, starting transfers between devices, shifted(): lax.ppermute(value, axis, [(source, (source + steps) % count) for source...  12.9 us
    ppermute x13, waiting for transfers between devices, swapped(): lax.ppermute(value, axis, [(source, source ^ bit) for source in range(cou...  12 us
    unnamed x43, local copies, waits for them, and re-layouts  9 us
  transfers between devices with their start and end apart: 24, of which 8 were waited for; matrix products, arithmetic and copies ran while one was open for 10% of the time, Pallas kernels for 11%

profile of v11, /device:TPU:13, one launch (start us, length us, event | category | flops | bytes accessed | tf_op | source)
XLA Modules:
  0.0 97.7 jit_solution(5040820389566782975)
XLA Ops:
  0.7 1.7 %fusion.2 = (bf16[32,12,1,128]{3,2,1,0:T(2,128)(2,1)S(1)}, bf16[32,12,1,128]{3,2,1,0:T(2,128)(2,1)S(1)}) fusion(bf16[32,12,8,128]{3,2,1,0:T(8,128)(2,1)} %cot_ref.1), kind=kLoop, calls=%fused_computation.24 | loop fusion | bytes 393216 | tf_op jit(solution)/shard_map/slice | solution.py:318
  3.2 1.3 %collective-permute-start.2 = (bf16[80,8,128]{2,1,0:T(8,128)(2,1)}, bf16[80,8,128]{2,1,0:T(8,128)(2,1)S(1)}, u32[]{:S(2)}, u32[]{:S(2)}) collective-permute-start(bf16[80,8,128]{2,1,0:T(8,128)(2,1)} %constant_dynamic-slice_fusion.refs_4_), channel_id=1, source_target_pairs={{0,8},{4,12},{8,16},{12,20},{16,24},{20,28},{24,0},{28,4},{1,9},{5... | collective-permute-start | bytes 491528 | tf_op jit(solution)/shard_map/ppermute | solution.py:21
  5.5 1.2 %collective-permute-start.5 = (bf16[32,12,8,128]{3,2,1,0:T(8,128)(2,1)}, bf16[32,12,8,128]{3,2,1,0:T(8,128)(2,1)S(1)}, u32[]{:S(2)}, u32[]{:S(2)}) collective-permute-start(bf16[32,12,8,128]{3,2,1,0:T(8,128)(2,1)} %cot_ref.1), channel_id=1, source_target_pairs={{0,2},{1,3},{2,0},{3,1},{4,6},{5,7},{6,4},{7,5},{8,10},{9,11},{10,... | collective-permute-start | bytes 2359304 | tf_op jit(solution)/shard_map/ppermute | solution.py:285
  7.0 1.2 %collective-permute-start.1 = (bf16[12,32,128]{2,1,0:T(8,128)(2,1)S(1)}, bf16[12,32,128]{2,1,0:T(8,128)(2,1)S(1)}, u32[]{:S(2)}, u32[]{:S(2)}) collective-permute-start(bf16[12,32,128]{2,1,0:T(8,128)(2,1)S(1)} %get-tuple-element.49), channel_id=1, source_target_pairs={{0,28},{4,0},{8,4},{12,8},{16,12},{20,16},{24,20},{28,24},{1,29},{... | collective-permute-start | bytes 294920 | tf_op jit(solution)/shard_map/ppermute | solution.py:21
  9.8 1.4 %select_select_fusion = bf16[3,10,8,3,320]{4,3,2,1,0:T(4,128)(2,1)} fusion(pred[8,320]{1,0:T(8,128)(4,1)S(1)} %copy-done.18, pred[8,320]{1,0:T(8,128)(4,1)S(1)} %copy-done.19, pred[8,320]{1,0:T(8,128)(4,1)S(1)} %copy-done.20, bf16[3,10,3,320]{3,2,1,0:T(4,128)(2,1)S(1)} %copy.33, bf16[3,10,3,320]{3,2,1,0:T(4,128)(2,1)S(1)} %copy.32, ...), kind=kLoop, calls=%fused_computation.2 | loop fusion | flops 691200 | bytes 641280 | tf_op jit(solution)/shard_map/jit(_where)/select_n | solution.py:45
  11.2 1.6 %constant_dynamic-slice_fusion.2.refs_11_.left_ref = bf16[80,8,128]{2,1,0:T(8,128)(2,1)} fusion(bf16[320,8,128]{2,1,0:T(8,128)(2,1)} %param.9, s32[]{:T(128)S(6)} %select_n.87), kind=kLoop, calls=%fused_computation.21 | loop fusion | bytes 327684 | tf_op jit(solution)/shard_map/dynamic_slice | solution.py:323
  12.8 1.7 %select_n.92.weight_ref = bf16[240,960]{1,0:T(8,128)(2,1)S(1)} reshape(bf16[3,10,8,3,320]{4,3,2,1,0:T(4,128)(2,1)} %select_select_fusion) | data formatting | bytes 921600 | tf_op jit(solution)/shard_map/jit(_where)/select_n | solution.py:45
  14.5 2.2 %collective-permute-done = bf16[12,32,128]{2,1,0:T(8,128)(2,1)S(1)} collective-permute-done((bf16[12,32,128]{2,1,0:T(8,128)(2,1)S(1)}, bf16[12,32,128]{2,1,0:T(8,128)(2,1)S(1)}, u32[]{:S(2)}, u32[]{:S(2)}) %collective-permute-start) | collective-permute-done | bytes 98336 | tf_op jit(solution)/shard_map/ppermute | solution.py:21
  16.7 2.7 %collective-permute-done.1 = bf16[12,32,128]{2,1,0:T(8,128)(2,1)S(1)} collective-permute-done((bf16[12,32,128]{2,1,0:T(8,128)(2,1)S(1)}, bf16[12,32,128]{2,1,0:T(8,128)(2,1)S(1)}, u32[]{:S(2)}, u32[]{:S(2)}) %collective-permute-start.1) | collective-permute-done | bytes 98336 | tf_op jit(solution)/shard_map/ppermute | solution.py:21
  20.2 1.3 %collective-permute-start.10 = (bf16[12,64,128]{2,1,0:T(8,128)(2,1)S(1)}, bf16[12,64,128]{2,1,0:T(8,128)(2,1)S(1)}, u32[]{:S(2)}, u32[]{:S(2)}) collective-permute-start(bf16[12,64,128]{2,1,0:T(8,128)(2,1)S(1)} %pad_maximum_fusion.halo_ref), channel_id=1, source_target_pairs={{0,2},{1,3},{2,0},{3,1},{4,6},{5,7},{6,4},{7,5},{8,10},{9,11},{10,... | collective-permute-start | bytes 589832 | tf_op jit(solution)/shard_map/ppermute | solution.py:285
  23.2 8.6 %collective-permute-done.6.refs_8_ = bf16[80,8,128]{2,1,0:T(8,128)(2,1)S(1)} collective-permute-done((bf16[80,8,128]{2,1,0:T(8,128)(2,1)}, bf16[80,8,128]{2,1,0:T(8,128)(2,1)S(1)}, u32[]{:S(2)}, u32[]{:S(2)}) %collective-permute-start.6) | collective-permute-done | bytes 163872 | tf_op jit(solution)/shard_map/ppermute | solution.py:285
  31.8 2.3 %collective-permute-start.4 = (bf16[12,320,128]{2,1,0:T(8,128)(2,1)S(1)}, bf16[12,320,128]{2,1,0:T(8,128)(2,1)S(1)}, u32[]{:S(2)}, u32[]{:S(2)}) collective-permute-start(bf16[12,320,128]{2,1,0:T(8,128)(2,1)S(1)} %shard_map.112.refs_0_), channel_id=1, source_target_pairs={{0,1},{1,0},{2,3},{3,2},{4,5},{5,4},{6,7},{7,6},{8,9},{9,8},{10,11... | collective-permute-start | bytes 2949128 | tf_op jit(solution)/shard_map/ppermute | solution.py:285
  34.1 1.2 %collective-permute-done.9.refs_10_ = bf16[80,8,128]{2,1,0:T(8,128)(2,1)S(1)} collective-permute-done((bf16[80,8,128]{2,1,0:T(8,128)(2,1)S(1)}, bf16[80,8,128]{2,1,0:T(8,128)(2,1)S(1)}, u32[]{:S(2)}, u32[]{:S(2)}) %collective-permute-start.9) | collective-permute-done | bytes 163872 | tf_op jit(solution)/shard_map/ppermute | solution.py:285
  35.6 1.4 %collective-permute-start.11 = (bf16[12,320,128]{2,1,0:T(8,128)(2,1)S(1)}, bf16[12,320,128]{2,1,0:T(8,128)(2,1)S(1)}, u32[]{:S(2)}, u32[]{:S(2)}) collective-permute-start(bf16[12,320,128]{2,1,0:T(8,128)(2,1)S(1)} %shard_map.114.refs_2_), channel_id=1, source_target_pairs={{0,1},{1,0},{2,3},{3,2},{4,5},{5,4},{6,7},{7,6},{8,9},{9,8},{10,11... | collective-permute-start | bytes 2949128 | tf_op jit(solution)/shard_map/ppermute | solution.py:285
  37.1 2.1 %collective-permute-done.11.refs_3_ = bf16[12,320,128]{2,1,0:T(8,128)(2,1)S(1)} collective-permute-done((bf16[12,320,128]{2,1,0:T(8,128)(2,1)S(1)}, bf16[12,320,128]{2,1,0:T(8,128)(2,1)S(1)}, u32[]{:S(2)}, u32[]{:S(2)}) %collective-permute-start.11) | collective-permute-done | bytes 983072 | tf_op jit(solution)/shard_map/ppermute | solution.py:285
  39.2 8.7 %shard_map.115 = (bf16[50,320,128]{2,1,0:T(8,128)(2,1)S(1)}, f32[80,56,128]{2,1,0:T(8,128)S(1)}, f32[3,32,96]{2,1,0:T(8,128)S(1)}) custom-call(s32[2]{0:T(128)S(1)} %pad_add_fusion.places, bf16[12,320,128]{2,1,0:T(8,128)(2,1)S(1)} %shard_map.112.refs_0_, bf16[12,320,128]{2,1,0:T(8,128)(2,1)S(1)} %collective-permute-done.4.refs_1_, ...), custom_call_target="tpu_custom_call" | custom-call | flops 8000000000 | bytes 1024 | tf_op jit(solution)/shard_map/pallas_call | solution.py:272
  48.1 5.0 %shard_map.116 = (f32[80,8,128]{2,1,0:T(8,128)S(1)}, f32[80,32,128]{2,1,0:T(8,128)S(1)}, bf16[80,8,128]{2,1,0:T(8,128)(2,1)}, bf16[80,8,128]{2,1,0:T(8,128)(2,1)}, bf16[80,8,128]{2,1,0:T(8,128)(2,1)}) custom-call(bf16[80,8,128]{2,1,0:T(8,128)(2,1)S(1)} %copy-done.4, bf16[240,960]{1,0:T(8,128)(2,1)S(1)} %select_n.92.weight_ref, ...), custom_call_target="tpu_custom_call" | custom-call | flops 8000000000 | bytes 1024 | tf_op jit(solution)/shard_map/pallas_call | solution.py:272
  53.1 1.6 %collective-permute-start.13 = (f32[3,32,96]{2,1,0:T(8,128)S(1)}, f32[3,32,96]{2,1,0:T(8,128)S(1)}, u32[]{:S(2)}, u32[]{:S(2)}) collective-permute-start(f32[3,32,96]{2,1,0:T(8,128)S(1)} %add.64), channel_id=1, source_target_pairs={{0,8},{4,12},{8,0},{12,4},{16,24},{20,28},{24,16},{28,20},{1,9},{5... | collective-permute-start | bytes 110600 | tf_op jit(solution)/shard_map/ppermute | solution.py:285
  54.7 3.7 %shard_map.117 = (f32[80,8,128]{2,1,0:T(8,128)S(1)}, f32[80,16,128]{2,1,0:T(8,128)S(1)}, bf16[80,8,128]{2,1,0:T(8,128)(2,1)}, bf16[80,8,128]{2,1,0:T(8,128)(2,1)}) custom-call(bf16[80,8,128]{2,1,0:T(8,128)(2,1)S(1)} %copy-done.4, bf16[240,960]{1,0:T(8,128)(2,1)S(1)} %select_n.92.weight_ref, bf16[50,320,128]{2,1,0:T(8,128)(2,1)S(1)} %get-tuple-element.61.cot_s, ...), custom_call_target="tpu_custom_call" | custom-call | flops 1000000 | bytes 1024 | tf_op jit(solution)/shard_map/pallas_call | solution.py:272
  60.1 2.0 %collective-permute-start.18 = (bf16[80,8,128]{2,1,0:T(8,128)(2,1)}, bf16[80,8,128]{2,1,0:T(8,128)(2,1)}, u32[]{:S(2)}, u32[]{:S(2)}) collective-permute-start(bf16[80,8,128]{2,1,0:T(8,128)(2,1)} %get-tuple-element.80), channel_id=1, source_target_pairs={{0,16},{4,20},{8,24},{12,28},{16,0},{20,4},{24,8},{28,12},{1,17},{... | collective-permute-start | bytes 491528 | tf_op jit(solution)/shard_map/ppermute | solution.py:21
  62.1 1.5 %collective-permute-start.19 = (bf16[80,8,128]{2,1,0:T(8,128)(2,1)}, bf16[80,8,128]{2,1,0:T(8,128)(2,1)}, u32[]{:S(2)}, u32[]{:S(2)}) collective-permute-start(bf16[80,8,128]{2,1,0:T(8,128)(2,1)} %get-tuple-element.81), channel_id=1, source_target_pairs={{0,12},{4,16},{8,20},{12,24},{16,28},{20,0},{24,4},{28,8},{1,13},{... | collective-permute-start | bytes 491528 | tf_op jit(solution)/shard_map/ppermute | solution.py:21
  64.7 2.1 %collective-permute-start.15 = (f32[3,32,96]{2,1,0:T(8,128)S(1)}, f32[3,32,96]{2,1,0:T(8,128)S(1)}, u32[]{:S(2)}, u32[]{:S(2)}) collective-permute-start(f32[3,32,96]{2,1,0:T(8,128)S(1)} %add.67), channel_id=1, source_target_pairs={{0,1},{1,0},{2,3},{3,2},{4,5},{5,4},{6,7},{7,6},{8,9},{9,8},{10,11... | collective-permute-start | bytes 110600 | tf_op jit(solution)/shard_map/ppermute | solution.py:285
  66.8 1.2 %collective-permute-start.16 = (f32[3,32,96]{2,1,0:T(8,128)S(1)}, f32[3,32,96]{2,1,0:T(8,128)}, u32[]{:S(2)}, u32[]{:S(2)}) collective-permute-start(f32[3,32,96]{2,1,0:T(8,128)S(1)} %add.67), channel_id=1, source_target_pairs={{0,2},{1,3},{2,0},{3,1},{4,6},{5,7},{6,4},{7,5},{8,10},{9,11},{10,... | collective-permute-start | bytes 110600 | tf_op jit(solution)/shard_map/ppermute | solution.py:285
  68.0 1.1 %collective-permute-start.17 = (f32[3,32,96]{2,1,0:T(8,128)S(1)}, f32[3,32,96]{2,1,0:T(8,128)}, u32[]{:S(2)}, u32[]{:S(2)}) collective-permute-start(f32[3,32,96]{2,1,0:T(8,128)S(1)} %add.67), channel_id=1, source_target_pairs={{0,3},{1,2},{2,1},{3,0},{4,7},{5,6},{6,5},{7,4},{8,11},{9,10},{10,... | collective-permute-start | bytes 110600 | tf_op jit(solution)/shard_map/ppermute | solution.py:285
  69.1 2.2 %copy-done.2 = bf16[50,320,128]{2,1,0:T(8,128)(2,1)S(1)} copy-done((bf16[50,320,128]{2,1,0:T(8,128)(2,1)S(1)}, bf16[50,320,128]{2,1,0:T(8,128)(2,1)}, u32[]{:S(2)}) %copy-start.2) | copy-done | bytes 4096024
  74.3 2.0 %shard_map.118 = (bf16[80,8,128]{2,1,0:T(8,128)(2,1)}, f32[80,8,128]{2,1,0:T(8,128)S(1)}, bf16[80,8,128]{2,1,0:T(8,128)(2,1)}) custom-call(bf16[80,8,128]{2,1,0:T(8,128)(2,1)S(1)} %copy-done.5, bf16[240,960]{1,0:T(8,128)(2,1)S(1)} %select_n.92.weight_ref, bf16[50,320,128]{2,1,0:T(8,128)(2,1)S(1)} %copy-done.2, f32[80,56,128]{2,1,0:T(8,128)S(1)} %get-tuple-element.62.right_s, ...), custom_call_target="tpu_custom_call" | custom-call | flops 1000000 | bytes 1024 | tf_op jit(solution)/shard_map/pallas_call | solution.py:272
  77.0 3.3 %collective-permute-done.20 = bf16[80,8,128]{2,1,0:T(8,128)(2,1)} collective-permute-done((bf16[80,8,128]{2,1,0:T(8,128)(2,1)}, bf16[80,8,128]{2,1,0:T(8,128)(2,1)}, u32[]{:S(2)}, u32[]{:S(2)}) %collective-permute-start.20) | collective-permute-done | bytes 163872 | tf_op jit(solution)/shard_map/ppermute | solution.py:21
  80.4 3.2 %collective-permute-start.23 = (bf16[80,8,128]{2,1,0:T(8,128)(2,1)}, bf16[80,8,128]{2,1,0:T(8,128)(2,1)S(1)}, u32[]{:S(2)}, u32[]{:S(2)}) collective-permute-start(bf16[80,8,128]{2,1,0:T(8,128)(2,1)} %get-tuple-element.85), channel_id=1, source_target_pairs={{0,20},{4,24},{8,28},{12,0},{16,4},{20,8},{24,12},{28,16},{1,21},{... | collective-permute-start | bytes 491528 | tf_op jit(solution)/shard_map/ppermute | solution.py:21
  83.6 1.3 %collective-permute-start.21 = (bf16[80,8,128]{2,1,0:T(8,128)(2,1)}, bf16[80,8,128]{2,1,0:T(8,128)(2,1)S(1)}, u32[]{:S(2)}, u32[]{:S(2)}) collective-permute-start(bf16[80,8,128]{2,1,0:T(8,128)(2,1)} %get-tuple-element.83), channel_id=1, source_target_pairs={{0,28},{4,0},{8,4},{12,8},{16,12},{20,16},{24,20},{28,24},{1,29},{... | collective-permute-start | bytes 491528 | tf_op jit(solution)/shard_map/ppermute | solution.py:21
  88.1 2.5 %collective-permute-done.22 = bf16[80,8,128]{2,1,0:T(8,128)(2,1)S(1)} collective-permute-done((bf16[80,8,128]{2,1,0:T(8,128)(2,1)}, bf16[80,8,128]{2,1,0:T(8,128)(2,1)S(1)}, u32[]{:S(2)}, u32[]{:S(2)}) %collective-permute-start.22) | collective-permute-done | bytes 163872 | tf_op jit(solution)/shard_map/ppermute | solution.py:21
  90.6 5.2 %collective-permute-done.21 = bf16[80,8,128]{2,1,0:T(8,128)(2,1)S(1)} collective-permute-done((bf16[80,8,128]{2,1,0:T(8,128)(2,1)}, bf16[80,8,128]{2,1,0:T(8,128)(2,1)S(1)}, u32[]{:S(2)}, u32[]{:S(2)}) %collective-permute-start.21) | collective-permute-done | bytes 163872 | tf_op jit(solution)/shard_map/ppermute | solution.py:21
  95.7 1.9 %add_convert_fusion = bf16[80,8,128]{2,1,0:T(8,128)(2,1)} fusion(bf16[80,8,128]{2,1,0:T(8,128)(2,1)} %collective-permute-done.20, bf16[80,8,128]{2,1,0:T(8,128)(2,1)} %collective-permute-done.19, bf16[80,8,128]{2,1,0:T(8,128)(2,1)} %collective-permute-done.18, bf16[80,8,128]{2,1,0:T(8,128)(2,1)S(1)} %collective-permute-done.23, ...), kind=kLoop, calls=%fused_computation.5 | loop fusion | flops 1556480 | bytes 1474566 | tf_op jit(solution)/shard_map/convert_element_type | solution.py:435
  (96 shorter events, 16.0 us)
Async XLA Ops:
  0.7 9.1 %copy-start.18 = (pred[8,320]{1,0:T(8,128)(4,1)S(1)}, pred[8,320]{1,0:T(8,128)(4,1)}, u32[]{:S(2)}) copy-start(pred[8,320]{1,0:T(8,128)(4,1)} %constant.55.clone) | copy-start | bytes 7684
  0.7 9.1 %copy-start.19 = (pred[8,320]{1,0:T(8,128)(4,1)S(1)}, pred[8,320]{1,0:T(8,128)(4,1)}, u32[]{:S(2)}) copy-start(pred[8,320]{1,0:T(8,128)(4,1)} %constant.56.clone) | copy-start | bytes 7684
  0.7 9.1 %copy-start.20 = (pred[8,320]{1,0:T(8,128)(4,1)S(1)}, pred[8,320]{1,0:T(8,128)(4,1)}, u32[]{:S(2)}) copy-start(pred[8,320]{1,0:T(8,128)(4,1)} %constant.57.clone) | copy-start | bytes 7684
  3.2 16.3 %collective-permute-start.2 = (bf16[80,8,128]{2,1,0:T(8,128)(2,1)}, bf16[80,8,128]{2,1,0:T(8,128)(2,1)S(1)}, u32[]{:S(2)}, u32[]{:S(2)}) collective-permute-start(bf16[80,8,128]{2,1,0:T(8,128)(2,1)} %constant_dynamic-slice_fusion.refs_4_), channel_id=1, source_target_pairs={{0,8},{4,12},{8,16},{12,20},{16,24},{20,28},{24,0},{28,4},{1,9},{5... | collective-permute-start | bytes 491528 | tf_op jit(solution)/shard_map/ppermute | solution.py:21
  4.5 15.0 %collective-permute-start.3 = (bf16[80,8,128]{2,1,0:T(8,128)(2,1)}, bf16[80,8,128]{2,1,0:T(8,128)(2,1)S(1)}, u32[]{:S(2)}, u32[]{:S(2)}) collective-permute-start(bf16[80,8,128]{2,1,0:T(8,128)(2,1)} %constant_dynamic-slice_fusion.refs_4_), channel_id=1, source_target_pairs={{0,16},{4,20},{8,24},{12,28},{16,0},{20,4},{24,8},{28,12},{1,17},{... | collective-permute-start | bytes 491528 | tf_op jit(solution)/shard_map/ppermute | solution.py:21
  5.5 29.9 %collective-permute-start.5 = (bf16[32,12,8,128]{3,2,1,0:T(8,128)(2,1)}, bf16[32,12,8,128]{3,2,1,0:T(8,128)(2,1)S(1)}, u32[]{:S(2)}, u32[]{:S(2)}) collective-permute-start(bf16[32,12,8,128]{3,2,1,0:T(8,128)(2,1)} %cot_ref.1), channel_id=1, source_target_pairs={{0,2},{1,3},{2,0},{3,1},{4,6},{5,7},{6,4},{7,5},{8,10},{9,11},{10,... | collective-permute-start | bytes 2359304 | tf_op jit(solution)/shard_map/ppermute | solution.py:285
  6.7 10.0 %collective-permute-start = (bf16[12,32,128]{2,1,0:T(8,128)(2,1)S(1)}, bf16[12,32,128]{2,1,0:T(8,128)(2,1)S(1)}, u32[]{:S(2)}, u32[]{:S(2)}) collective-permute-start(bf16[12,32,128]{2,1,0:T(8,128)(2,1)S(1)} %get-tuple-element.48), channel_id=1, source_target_pairs={{0,4},{4,8},{8,12},{12,16},{16,20},{20,24},{24,28},{28,0},{1,5},{5... | collective-permute-start | bytes 294920 | tf_op jit(solution)/shard_map/ppermute | solution.py:21
  7.0 12.4 %collective-permute-start.1 = (bf16[12,32,128]{2,1,0:T(8,128)(2,1)S(1)}, bf16[12,32,128]{2,1,0:T(8,128)(2,1)S(1)}, u32[]{:S(2)}, u32[]{:S(2)}) collective-permute-start(bf16[12,32,128]{2,1,0:T(8,128)(2,1)S(1)} %get-tuple-element.49), channel_id=1, source_target_pairs={{0,28},{4,0},{8,4},{12,8},{16,12},{20,16},{24,20},{28,24},{1,29},{... | collective-permute-start | bytes 294920 | tf_op jit(solution)/shard_map/ppermute | solution.py:21
  9.6 13.4 %copy-start.3 = (bf16[32,12,8,128]{3,2,1,0:T(8,128)(2,1)S(1)}, bf16[32,12,8,128]{3,2,1,0:T(8,128)(2,1)}, u32[]{:S(2)}) copy-start(bf16[32,12,8,128]{3,2,1,0:T(8,128)(2,1)} %cot_ref.1) | copy-start | bytes 2359300
  16.7 5.7 %collective-permute-start.8 = (bf16[80,8,128]{2,1,0:T(8,128)(2,1)}, bf16[80,8,128]{2,1,0:T(8,128)(2,1)S(1)}, u32[]{:S(2)}, u32[]{:S(2)}) collective-permute-start(bf16[80,8,128]{2,1,0:T(8,128)(2,1)} %constant_dynamic-slice_fusion.refs_4_), channel_id=1, source_target_pairs={{0,24},{4,28},{8,0},{12,4},{16,8},{20,12},{24,16},{28,20},{1,25},{... | collective-permute-start | bytes 491528 | tf_op jit(solution)/shard_map/ppermute | solution.py:21
  19.5 15.9 %collective-permute-start.7 = (bf16[2,80,8,128]{3,2,1,0:T(8,128)(2,1)S(1)}, bf16[2,80,8,128]{3,2,1,0:T(8,128)(2,1)S(1)}, u32[]{:S(2)}, u32[]{:S(2)}) collective-permute-start(bf16[2,80,8,128]{3,2,1,0:T(8,128)(2,1)S(1)} %shard_map.113), channel_id=1, source_target_pairs={{0,4},{4,0},{8,12},{12,8},{16,20},{20,16},{24,28},{28,24},{1,5},{5... | collective-permute-start | bytes 983048 | tf_op jit(solution)/shard_map/ppermute | solution.py:285
  20.1 19.1 %copy-start.4 = (bf16[80,8,128]{2,1,0:T(8,128)(2,1)S(1)}, bf16[80,8,128]{2,1,0:T(8,128)(2,1)}, u32[]{:S(2)}) copy-start(bf16[80,8,128]{2,1,0:T(8,128)(2,1)} %constant_dynamic-slice_fusion.2.refs_11_.left_ref) | copy-start | bytes 491524
  20.1 19.1 %copy-start.16 = (f32[32,240]{1,0:T(8,128)S(1)}, f32[32,240]{1,0:T(8,128)}, u32[]{:S(2)}) copy-start(f32[32,240]{1,0:T(8,128)} %constant.58.clone.refs_12_) | copy-start | bytes 92164
  20.1 19.0 %copy-start.13 = (bf16[80,8,128]{2,1,0:T(8,128)(2,1)S(1)}, bf16[80,8,128]{2,1,0:T(8,128)(2,1)}, u32[]{:S(2)}) copy-start(bf16[80,8,128]{2,1,0:T(8,128)(2,1)} %copy-done.12) | copy-start | bytes 491524
  20.2 19.0 %copy-start.15 = (bf16[80,8,128]{2,1,0:T(8,128)(2,1)S(1)}, bf16[80,8,128]{2,1,0:T(8,128)(2,1)}, u32[]{:S(2)}) copy-start(bf16[80,8,128]{2,1,0:T(8,128)(2,1)} %copy-done.14) | copy-start | bytes 491524
  20.2 15.2 %collective-permute-start.10 = (bf16[12,64,128]{2,1,0:T(8,128)(2,1)S(1)}, bf16[12,64,128]{2,1,0:T(8,128)(2,1)S(1)}, u32[]{:S(2)}, u32[]{:S(2)}) collective-permute-start(bf16[12,64,128]{2,1,0:T(8,128)(2,1)S(1)} %pad_maximum_fusion.halo_ref), channel_id=1, source_target_pairs={{0,2},{1,3},{2,0},{3,1},{4,6},{5,7},{6,4},{7,5},{8,10},{9,11},{10,... | collective-permute-start | bytes 589832 | tf_op jit(solution)/shard_map/ppermute | solution.py:285
  21.5 10.4 %collective-permute-start.6 = (bf16[80,8,128]{2,1,0:T(8,128)(2,1)}, bf16[80,8,128]{2,1,0:T(8,128)(2,1)S(1)}, u32[]{:S(2)}, u32[]{:S(2)}) collective-permute-start(bf16[80,8,128]{2,1,0:T(8,128)(2,1)} %constant_dynamic-slice_fusion.refs_4_), channel_id=1, source_target_pairs={{0,4},{4,0},{8,12},{12,8},{16,20},{20,16},{24,28},{28,24},{1,5},{5... | collective-permute-start | bytes 491528 | tf_op jit(solution)/shard_map/ppermute | solution.py:285
  22.4 12.9 %collective-permute-start.9 = (bf16[80,8,128]{2,1,0:T(8,128)(2,1)S(1)}, bf16[80,8,128]{2,1,0:T(8,128)(2,1)S(1)}, u32[]{:S(2)}, u32[]{:S(2)}) collective-permute-start(bf16[80,8,128]{2,1,0:T(8,128)(2,1)S(1)} %collective-permute-done.8.refs_7_), channel_id=1, source_target_pairs={{0,4},{4,0},{8,12},{12,8},{16,20},{20,16},{24,28},{28,24},{1,5},{5... | collective-permute-start | bytes 491528 | tf_op jit(solution)/shard_map/ppermute | solution.py:285
  31.8 5.2 %collective-permute-start.4 = (bf16[12,320,128]{2,1,0:T(8,128)(2,1)S(1)}, bf16[12,320,128]{2,1,0:T(8,128)(2,1)S(1)}, u32[]{:S(2)}, u32[]{:S(2)}) collective-permute-start(bf16[12,320,128]{2,1,0:T(8,128)(2,1)S(1)} %shard_map.112.refs_0_), channel_id=1, source_target_pairs={{0,1},{1,0},{2,3},{3,2},{4,5},{5,4},{6,7},{7,6},{8,9},{9,8},{10,11... | collective-permute-start | bytes 2949128 | tf_op jit(solution)/shard_map/ppermute | solution.py:285
  35.6 3.6 %collective-permute-start.11 = (bf16[12,320,128]{2,1,0:T(8,128)(2,1)S(1)}, bf16[12,320,128]{2,1,0:T(8,128)(2,1)S(1)}, u32[]{:S(2)}, u32[]{:S(2)}) collective-permute-start(bf16[12,320,128]{2,1,0:T(8,128)(2,1)S(1)} %shard_map.114.refs_2_), channel_id=1, source_target_pairs={{0,1},{1,0},{2,3},{3,2},{4,5},{5,4},{6,7},{7,6},{8,9},{9,8},{10,11... | collective-permute-start | bytes 2949128 | tf_op jit(solution)/shard_map/ppermute | solution.py:285
  48.0 5.1 %collective-permute-start.12 = (f32[3,32,96]{2,1,0:T(8,128)S(1)}, f32[3,32,96]{2,1,0:T(8,128)S(1)}, u32[]{:S(2)}, u32[]{:S(2)}) collective-permute-start(f32[3,32,96]{2,1,0:T(8,128)S(1)} %get-tuple-element.68), channel_id=1, source_target_pairs={{0,16},{4,20},{8,24},{12,28},{16,0},{20,4},{24,8},{28,12},{1,17},{... | collective-permute-start | bytes 110600 | tf_op jit(solution)/shard_map/ppermute | solution.py:285
  53.1 6.9 %collective-permute-start.13 = (f32[3,32,96]{2,1,0:T(8,128)S(1)}, f32[3,32,96]{2,1,0:T(8,128)S(1)}, u32[]{:S(2)}, u32[]{:S(2)}) collective-permute-start(f32[3,32,96]{2,1,0:T(8,128)S(1)} %add.64), channel_id=1, source_target_pairs={{0,8},{4,12},{8,0},{12,4},{16,24},{20,28},{24,16},{28,20},{1,9},{5... | collective-permute-start | bytes 110600 | tf_op jit(solution)/shard_map/ppermute | solution.py:285
  60.0 4.7 %collective-permute-start.14 = (f32[3,32,96]{2,1,0:T(8,128)S(1)}, f32[3,32,96]{2,1,0:T(8,128)S(1)}, u32[]{:S(2)}, u32[]{:S(2)}) collective-permute-start(f32[3,32,96]{2,1,0:T(8,128)S(1)} %add.65), channel_id=1, source_target_pairs={{0,4},{4,0},{8,12},{12,8},{16,20},{20,16},{24,28},{28,24},{1,5},{5... | collective-permute-start | bytes 110600 | tf_op jit(solution)/shard_map/ppermute | solution.py:285
  60.1 16.9 %collective-permute-start.18 = (bf16[80,8,128]{2,1,0:T(8,128)(2,1)}, bf16[80,8,128]{2,1,0:T(8,128)(2,1)}, u32[]{:S(2)}, u32[]{:S(2)}) collective-permute-start(bf16[80,8,128]{2,1,0:T(8,128)(2,1)} %get-tuple-element.80), channel_id=1, source_target_pairs={{0,16},{4,20},{8,24},{12,28},{16,0},{20,4},{24,8},{28,12},{1,17},{... | collective-permute-start | bytes 491528 | tf_op jit(solution)/shard_map/ppermute | solution.py:21
  62.1 14.9 %collective-permute-start.19 = (bf16[80,8,128]{2,1,0:T(8,128)(2,1)}, bf16[80,8,128]{2,1,0:T(8,128)(2,1)}, u32[]{:S(2)}, u32[]{:S(2)}) collective-permute-start(bf16[80,8,128]{2,1,0:T(8,128)(2,1)} %get-tuple-element.81), channel_id=1, source_target_pairs={{0,12},{4,16},{8,20},{12,24},{16,28},{20,0},{24,4},{28,8},{1,13},{... | collective-permute-start | bytes 491528 | tf_op jit(solution)/shard_map/ppermute | solution.py:21
  63.6 16.7 %collective-permute-start.20 = (bf16[80,8,128]{2,1,0:T(8,128)(2,1)}, bf16[80,8,128]{2,1,0:T(8,128)(2,1)}, u32[]{:S(2)}, u32[]{:S(2)}) collective-permute-start(bf16[80,8,128]{2,1,0:T(8,128)(2,1)} %get-tuple-element.82), channel_id=1, source_target_pairs={{0,8},{4,12},{8,16},{12,20},{16,24},{20,28},{24,0},{28,4},{1,9},{5... | collective-permute-start | bytes 491528 | tf_op jit(solution)/shard_map/ppermute | solution.py:21
  64.7 3.4 %collective-permute-start.15 = (f32[3,32,96]{2,1,0:T(8,128)S(1)}, f32[3,32,96]{2,1,0:T(8,128)S(1)}, u32[]{:S(2)}, u32[]{:S(2)}) collective-permute-start(f32[3,32,96]{2,1,0:T(8,128)S(1)} %add.67), channel_id=1, source_target_pairs={{0,1},{1,0},{2,3},{3,2},{4,5},{5,4},{6,7},{7,6},{8,9},{9,8},{10,11... | collective-permute-start | bytes 110600 | tf_op jit(solution)/shard_map/ppermute | solution.py:285
  66.8 10.2 %collective-permute-start.16 = (f32[3,32,96]{2,1,0:T(8,128)S(1)}, f32[3,32,96]{2,1,0:T(8,128)}, u32[]{:S(2)}, u32[]{:S(2)}) collective-permute-start(f32[3,32,96]{2,1,0:T(8,128)S(1)} %add.67), channel_id=1, source_target_pairs={{0,2},{1,3},{2,0},{3,1},{4,6},{5,7},{6,4},{7,5},{8,10},{9,11},{10,... | collective-permute-start | bytes 110600 | tf_op jit(solution)/shard_map/ppermute | solution.py:285
  68.0 9.0 %collective-permute-start.17 = (f32[3,32,96]{2,1,0:T(8,128)S(1)}, f32[3,32,96]{2,1,0:T(8,128)}, u32[]{:S(2)}, u32[]{:S(2)}) collective-permute-start(f32[3,32,96]{2,1,0:T(8,128)S(1)} %add.67), channel_id=1, source_target_pairs={{0,3},{1,2},{2,1},{3,0},{4,7},{5,6},{6,5},{7,4},{8,11},{9,10},{10,... | collective-permute-start | bytes 110600 | tf_op jit(solution)/shard_map/ppermute | solution.py:285
  80.4 7.7 %collective-permute-start.23 = (bf16[80,8,128]{2,1,0:T(8,128)(2,1)}, bf16[80,8,128]{2,1,0:T(8,128)(2,1)S(1)}, u32[]{:S(2)}, u32[]{:S(2)}) collective-permute-start(bf16[80,8,128]{2,1,0:T(8,128)(2,1)} %get-tuple-element.85), channel_id=1, source_target_pairs={{0,20},{4,24},{8,28},{12,0},{16,4},{20,8},{24,12},{28,16},{1,21},{... | collective-permute-start | bytes 491528 | tf_op jit(solution)/shard_map/ppermute | solution.py:21
  83.6 6.9 %collective-permute-start.22 = (bf16[80,8,128]{2,1,0:T(8,128)(2,1)}, bf16[80,8,128]{2,1,0:T(8,128)(2,1)S(1)}, u32[]{:S(2)}, u32[]{:S(2)}) collective-permute-start(bf16[80,8,128]{2,1,0:T(8,128)(2,1)} %get-tuple-element.84), channel_id=1, source_target_pairs={{0,24},{4,28},{8,0},{12,4},{16,8},{20,12},{24,16},{28,20},{1,25},{... | collective-permute-start | bytes 491528 | tf_op jit(solution)/shard_map/ppermute | solution.py:21
  83.6 12.1 %collective-permute-start.21 = (bf16[80,8,128]{2,1,0:T(8,128)(2,1)}, bf16[80,8,128]{2,1,0:T(8,128)(2,1)S(1)}, u32[]{:S(2)}, u32[]{:S(2)}) collective-permute-start(bf16[80,8,128]{2,1,0:T(8,128)(2,1)} %get-tuple-element.83), channel_id=1, source_target_pairs={{0,28},{4,0},{8,4},{12,8},{16,12},{20,16},{24,20},{28,24},{1,29},{... | collective-permute-start | bytes 491528 | tf_op jit(solution)/shard_map/ppermute | solution.py:21
  (13 other events, 34.9 us)

commit v12 on v11

--- a/solution.py
+++ b/solution.py
@@ -413,9 +413,8 @@
     for bit in bits[2:]:
         total = total_swapping(total, bit)
     distant = sorted(arrived)
-    pieces = [total] + [swapped(total, "disp", key) for key in range(1, parts)]
-    sent, last, pieces, *items = lax.optimization_barrier(
-        (sent, last, pieces, *[arrived[hop] for hop in distant])
+    sent, last, total, *items = lax.optimization_barrier(
+        (sent, last, total, *[arrived[hop] for hop in distant])
     )
     arrived = dict(zip(distant, items))
     for hop, value in zip(range(near, 0, -1), [*sent, *last]):
@@ -427,7 +426,8 @@
             column + hop < columns, arrived[hop].astype(f32), 0.0
         )
 
-    pieces = jnp.stack(pieces)[jnp.arange(parts) ^ part][:, :, : 3 * groups]
+    pieces = jnp.stack([total] + [swapped(total, "disp", key) for key in range(1, parts)])
+    pieces = pieces[jnp.arange(parts) ^ part][:, :, : 3 * groups]
     total = pieces.reshape(parts, 3, 3, groups, 3, outs)
     cell_count = D * width * columns * rows
     grad_kernel = jnp.transpose(total, (4, 1, 2, 5, 0, 3))[::-1].reshape(3, 3, 3, outs, G)

time: 99.5 us -> 94.4 us (0.949); the launches traced: 97.7 us -> 93.7 us
  local copies, waits for them, and re-layouts: 17.1 us -> 8.52 us
  waiting for transfers between devices: 28 us -> 34.3 us
  Pallas kernels: 19.9 us -> 18.2 us
    unnamed x43 -> x15, local copies, waits for them, and re-layouts: 9 us -> 1.02 us
    ppermute x13, waiting for transfers between devices: 12 us -> 17.5 us  [swapped(): lax.ppermute(value, axis, [(source, source ^ bit) for source in range(cou...]
    pallas_call x7, Pallas kernels: 19.9 us -> 18.2 us  [run(): pl.pallas_call(function, out_shape=[jax.ShapeDtypeStruct(shape, kind) for...]
  transfers between devices with their start and end apart: 24 -> 24, of which waited for: 8 -> 11; matrix products, arithmetic and copies ran while one was open for 10% -> 10% of each run, Pallas kernels for 11% -> 10%
where the time goes in v12:
time: 94.4 us; the launch traced here: 93.7 us
  waiting for transfers between devices  34.3 us (36%)
  starting transfers between devices  26 us (28%)
  Pallas kernels  18.2 us (19%)
  local copies, waits for them, and re-layouts  8.52 us (9%)
  other arithmetic  5.46 us (6%)
  between operations  1 us (1%)
    pallas_call x7, Pallas kernels, run(): pl.pallas_call(function, out_shape=[jax.ShapeDtypeStruct(shape, kind) for...  18.2 us
    ppermute x13, waiting for transfers between devices, swapped(): lax.ppermute(value, axis, [(source, source ^ bit) for source in range(cou...  17.5 us
    ppermute x11, waiting for transfers between devices, shifted(): lax.ppermute(value, axis, [(source, (source + steps) % count) for source...  16.8 us
    ppermute x13, starting transfers between devices, swapped(): lax.ppermute(value, axis, [(source, source ^ bit) for source in range(cou...  13.7 us
    ppermute x11, starting transfers between devices, shifted(): lax.ppermute(value, axis, [(source, (source + steps) % count) for source...  12.4 us
    convert_element_type x1, other arithmetic, body(): return (grad_left, total_right.astype(bf16), grad_kernel)  1.95 us
  transfers between devices with their start and end apart: 24, of which 11 were waited for; matrix products, arithmetic and copies ran while one was open for 10% of the time, Pallas kernels for 10%

profile of v12, /device:TPU:13, one launch (start us, length us, event | category | flops | bytes accessed | tf_op | source)
XLA Modules:
  0.0 93.7 jit_solution(1186267270049826557)
XLA Ops:
  0.7 1.9 %fusion.2 = (bf16[32,12,1,128]{3,2,1,0:T(2,128)(2,1)S(1)}, bf16[32,12,1,128]{3,2,1,0:T(2,128)(2,1)S(1)}) fusion(bf16[32,12,8,128]{3,2,1,0:T(8,128)(2,1)} %cot_ref.1), kind=kLoop, calls=%fused_computation.24 | loop fusion | bytes 393216 | tf_op jit(solution)/shard_map/slice | solution.py:318
  3.3 1.3 %collective-permute-start.2 = (bf16[80,8,128]{2,1,0:T(8,128)(2,1)S(1)}, bf16[80,8,128]{2,1,0:T(8,128)(2,1)S(1)}, u32[]{:S(2)}, u32[]{:S(2)}) collective-permute-start(bf16[80,8,128]{2,1,0:T(8,128)(2,1)S(1)} %constant_dynamic-slice_fusion.refs_4_), channel_id=1, source_target_pairs={{0,8},{4,12},{8,16},{12,20},{16,24},{20,28},{24,0},{28,4},{1,9},{5... | collective-permute-start | bytes 491528 | tf_op jit(solution)/shard_map/ppermute | solution.py:21
  4.6 1.1 %collective-permute-start.3 = (bf16[80,8,128]{2,1,0:T(8,128)(2,1)S(1)}, bf16[80,8,128]{2,1,0:T(8,128)(2,1)S(1)}, u32[]{:S(2)}, u32[]{:S(2)}) collective-permute-start(bf16[80,8,128]{2,1,0:T(8,128)(2,1)S(1)} %constant_dynamic-slice_fusion.refs_4_), channel_id=1, source_target_pairs={{0,16},{4,20},{8,24},{12,28},{16,0},{20,4},{24,8},{28,12},{1,17},{... | collective-permute-start | bytes 491528 | tf_op jit(solution)/shard_map/ppermute | solution.py:21
  5.7 1.2 %collective-permute-start.5 = (bf16[32,12,8,128]{3,2,1,0:T(8,128)(2,1)}, bf16[32,12,8,128]{3,2,1,0:T(8,128)(2,1)S(1)}, u32[]{:S(2)}, u32[]{:S(2)}) collective-permute-start(bf16[32,12,8,128]{3,2,1,0:T(8,128)(2,1)} %cot_ref.1), channel_id=1, source_target_pairs={{0,2},{1,3},{2,0},{3,1},{4,6},{5,7},{6,4},{7,5},{8,10},{9,11},{10,... | collective-permute-start | bytes 2359304 | tf_op jit(solution)/shard_map/ppermute | solution.py:285
  7.1 1.3 %collective-permute-start.1 = (bf16[12,32,128]{2,1,0:T(8,128)(2,1)S(1)}, bf16[12,32,128]{2,1,0:T(8,128)(2,1)}, u32[]{:S(2)}, u32[]{:S(2)}) collective-permute-start(bf16[12,32,128]{2,1,0:T(8,128)(2,1)S(1)} %get-tuple-element.46), channel_id=1, source_target_pairs={{0,28},{4,0},{8,4},{12,8},{16,12},{20,16},{24,20},{28,24},{1,29},{... | collective-permute-start | bytes 294920 | tf_op jit(solution)/shard_map/ppermute | solution.py:21
  8.4 1.1 %constant_dynamic-slice_fusion.1 = bf16[3,3,3,32,10]{4,3,2,1,0:T(8,128)(2,1)S(1)} fusion(bf16[3,3,3,32,40]{4,3,2,1,0:T(8,128)(2,1)} %param.11, s32[]{:T(128)S(6)} %select_n.88), kind=kLoop, calls=%fused_computation.20 | loop fusion | bytes 34564 | tf_op jit(solution)/shard_map/dynamic_slice | solution.py:324
  10.0 1.4 %select_select_fusion = bf16[3,10,8,3,320]{4,3,2,1,0:T(4,128)(2,1)} fusion(pred[8,320]{1,0:T(8,128)(4,1)S(1)} %copy-done.4, pred[8,320]{1,0:T(8,128)(4,1)S(1)} %copy-done.5, pred[8,320]{1,0:T(8,128)(4,1)S(1)} %copy-done.6, bf16[3,10,3,320]{3,2,1,0:T(4,128)(2,1)S(1)} %copy.33, bf16[3,10,3,320]{3,2,1,0:T(4,128)(2,1)S(1)} %copy.32, ...), kind=kLoop, calls=%fused_computation.2 | loop fusion | flops 691200 | bytes 641280 | tf_op jit(solution)/shard_map/jit(_where)/select_n | solution.py:45
  12.3 1.7 %select_n.92.weight_ref = bf16[240,960]{1,0:T(8,128)(2,1)S(1)} reshape(bf16[3,10,8,3,320]{4,3,2,1,0:T(4,128)(2,1)} %select_select_fusion) | data formatting | bytes 921600 | tf_op jit(solution)/shard_map/jit(_where)/select_n | solution.py:45
  14.0 2.7 %collective-permute-done = bf16[12,32,128]{2,1,0:T(8,128)(2,1)} collective-permute-done((bf16[12,32,128]{2,1,0:T(8,128)(2,1)}, bf16[12,32,128]{2,1,0:T(8,128)(2,1)}, u32[]{:S(2)}, u32[]{:S(2)}) %collective-permute-start) | collective-permute-done | bytes 98336 | tf_op jit(solution)/shard_map/ppermute | solution.py:21
  16.7 2.7 %collective-permute-done.1 = bf16[12,32,128]{2,1,0:T(8,128)(2,1)} collective-permute-done((bf16[12,32,128]{2,1,0:T(8,128)(2,1)S(1)}, bf16[12,32,128]{2,1,0:T(8,128)(2,1)}, u32[]{:S(2)}, u32[]{:S(2)}) %collective-permute-start.1) | collective-permute-done | bytes 98336 | tf_op jit(solution)/shard_map/ppermute | solution.py:21
  21.4 1.3 %collective-permute-start.10 = (bf16[12,64,128]{2,1,0:T(8,128)(2,1)S(1)}, bf16[12,64,128]{2,1,0:T(8,128)(2,1)S(1)}, u32[]{:S(2)}, u32[]{:S(2)}) collective-permute-start(bf16[12,64,128]{2,1,0:T(8,128)(2,1)S(1)} %pad_maximum_fusion.halo_ref), channel_id=1, source_target_pairs={{0,2},{1,3},{2,0},{3,1},{4,6},{5,7},{6,4},{7,5},{8,10},{9,11},{10,... | collective-permute-start | bytes 589832 | tf_op jit(solution)/shard_map/ppermute | solution.py:285
  22.7 1.4 %collective-permute-start.6 = (bf16[80,8,128]{2,1,0:T(8,128)(2,1)S(1)}, bf16[80,8,128]{2,1,0:T(8,128)(2,1)S(1)}, u32[]{:S(2)}, u32[]{:S(2)}) collective-permute-start(bf16[80,8,128]{2,1,0:T(8,128)(2,1)S(1)} %constant_dynamic-slice_fusion.refs_4_), channel_id=1, source_target_pairs={{0,4},{4,0},{8,12},{12,8},{16,20},{20,16},{24,28},{28,24},{1,5},{5... | collective-permute-start | bytes 491528 | tf_op jit(solution)/shard_map/ppermute | solution.py:285
  24.4 7.3 %collective-permute-done.6.refs_8_ = bf16[80,8,128]{2,1,0:T(8,128)(2,1)S(1)} collective-permute-done((bf16[80,8,128]{2,1,0:T(8,128)(2,1)S(1)}, bf16[80,8,128]{2,1,0:T(8,128)(2,1)S(1)}, u32[]{:S(2)}, u32[]{:S(2)}) %collective-permute-start.6) | collective-permute-done | bytes 163872 | tf_op jit(solution)/shard_map/ppermute | solution.py:285
  31.7 2.5 %collective-permute-start.4 = (bf16[12,320,128]{2,1,0:T(8,128)(2,1)S(1)}, bf16[12,320,128]{2,1,0:T(8,128)(2,1)S(1)}, u32[]{:S(2)}, u32[]{:S(2)}) collective-permute-start(bf16[12,320,128]{2,1,0:T(8,128)(2,1)S(1)} %shard_map.112.refs_0_), channel_id=1, source_target_pairs={{0,1},{1,0},{2,3},{3,2},{4,5},{5,4},{6,7},{7,6},{8,9},{9,8},{10,11... | collective-permute-start | bytes 2949128 | tf_op jit(solution)/shard_map/ppermute | solution.py:285
  34.3 1.0 %collective-permute-done.9.refs_10_ = bf16[80,8,128]{2,1,0:T(8,128)(2,1)S(1)} collective-permute-done((bf16[80,8,128]{2,1,0:T(8,128)(2,1)S(1)}, bf16[80,8,128]{2,1,0:T(8,128)(2,1)S(1)}, u32[]{:S(2)}, u32[]{:S(2)}) %collective-permute-start.9) | collective-permute-done | bytes 163872 | tf_op jit(solution)/shard_map/ppermute | solution.py:285
  35.5 1.5 %collective-permute-start.11 = (bf16[12,320,128]{2,1,0:T(8,128)(2,1)S(1)}, bf16[12,320,128]{2,1,0:T(8,128)(2,1)S(1)}, u32[]{:S(2)}, u32[]{:S(2)}) collective-permute-start(bf16[12,320,128]{2,1,0:T(8,128)(2,1)S(1)} %shard_map.114.refs_2_), channel_id=1, source_target_pairs={{0,1},{1,0},{2,3},{3,2},{4,5},{5,4},{6,7},{7,6},{8,9},{9,8},{10,11... | collective-permute-start | bytes 2949128 | tf_op jit(solution)/shard_map/ppermute | solution.py:285
  37.1 2.1 %collective-permute-done.11.refs_3_ = bf16[12,320,128]{2,1,0:T(8,128)(2,1)S(1)} collective-permute-done((bf16[12,320,128]{2,1,0:T(8,128)(2,1)S(1)}, bf16[12,320,128]{2,1,0:T(8,128)(2,1)S(1)}, u32[]{:S(2)}, u32[]{:S(2)}) %collective-permute-start.11) | collective-permute-done | bytes 983072 | tf_op jit(solution)/shard_map/ppermute | solution.py:285
  39.2 8.3 %shard_map.115 = (bf16[50,320,128]{2,1,0:T(8,128)(2,1)S(1)}, f32[80,56,128]{2,1,0:T(8,128)S(1)}, f32[3,32,96]{2,1,0:T(8,128)S(1)}) custom-call(s32[2]{0:T(128)S(1)} %pad_add_fusion.places, bf16[12,320,128]{2,1,0:T(8,128)(2,1)S(1)} %shard_map.112.refs_0_, bf16[12,320,128]{2,1,0:T(8,128)(2,1)S(1)} %collective-permute-done.4.refs_1_, ...), custom_call_target="tpu_custom_call" | custom-call | flops 8000000000 | bytes 1024 | tf_op jit(solution)/shard_map/pallas_call | solution.py:272
  48.3 4.2 %shard_map.116 = (f32[80,8,128]{2,1,0:T(8,128)S(1)}, f32[80,32,128]{2,1,0:T(8,128)S(1)}, bf16[80,8,128]{2,1,0:T(8,128)(2,1)S(1)}, bf16[80,8,128]{2,1,0:T(8,128)(2,1)S(1)}, bf16[80,8,128]{2,1,0:T(8,128)(2,1)S(1)}) custom-call(bf16[80,8,128]{2,1,0:T(8,128)(2,1)S(1)} %constant_dynamic-slice_fusion.2.refs_11_.left_ref, ...), custom_call_target="tpu_custom_call" | custom-call | flops 8000000000 | bytes 1024 | tf_op jit(solution)/shard_map/pallas_call | solution.py:272
  52.6 1.7 %collective-permute-start.15 = (bf16[80,8,128]{2,1,0:T(8,128)(2,1)S(1)}, bf16[80,8,128]{2,1,0:T(8,128)(2,1)S(1)}, u32[]{:S(2)}, u32[]{:S(2)}) collective-permute-start(bf16[80,8,128]{2,1,0:T(8,128)(2,1)S(1)} %get-tuple-element.77), channel_id=1, source_target_pairs={{0,16},{4,20},{8,24},{12,28},{16,0},{20,4},{24,8},{28,12},{1,17},{... | collective-permute-start | bytes 491528 | tf_op jit(solution)/shard_map/ppermute | solution.py:21
  54.3 2.2 %collective-permute-start.16 = (bf16[80,8,128]{2,1,0:T(8,128)(2,1)S(1)}, bf16[80,8,128]{2,1,0:T(8,128)(2,1)S(1)}, u32[]{:S(2)}, u32[]{:S(2)}) collective-permute-start(bf16[80,8,128]{2,1,0:T(8,128)(2,1)S(1)} %get-tuple-element.78), channel_id=1, source_target_pairs={{0,12},{4,16},{8,20},{12,24},{16,28},{20,0},{24,4},{28,8},{1,13},{... | collective-permute-start | bytes 491528 | tf_op jit(solution)/shard_map/ppermute | solution.py:21
  56.5 1.5 %collective-permute-start.13 = (f32[3,32,96]{2,1,0:T(8,128)S(1)}, f32[3,32,96]{2,1,0:T(8,128)S(1)}, u32[]{:S(2)}, u32[]{:S(2)}) collective-permute-start(f32[3,32,96]{2,1,0:T(8,128)S(1)} %add.64), channel_id=1, source_target_pairs={{0,8},{4,12},{8,0},{12,4},{16,24},{20,28},{24,16},{28,20},{1,9},{5... | collective-permute-start | bytes 110600 | tf_op jit(solution)/shard_map/ppermute | solution.py:285
  58.0 3.1 %shard_map.117 = (f32[80,8,128]{2,1,0:T(8,128)S(1)}, f32[80,16,128]{2,1,0:T(8,128)S(1)}, bf16[80,8,128]{2,1,0:T(8,128)(2,1)S(1)}, bf16[80,8,128]{2,1,0:T(8,128)(2,1)S(1)}) custom-call(bf16[80,8,128]{2,1,0:T(8,128)(2,1)S(1)} %constant_dynamic-slice_fusion.2.refs_11_.left_ref, bf16[240,960]{1,0:T(8,128)(2,1)S(1)} %select_n.92.weight_ref, ...), custom_call_target="tpu_custom_call" | custom-call | flops 1000000 | bytes 1024 | tf_op jit(solution)/shard_map/pallas_call | solution.py:272
  61.1 6.2 %collective-permute-done.13 = f32[3,32,96]{2,1,0:T(8,128)S(1)} collective-permute-done((f32[3,32,96]{2,1,0:T(8,128)S(1)}, f32[3,32,96]{2,1,0:T(8,128)S(1)}, u32[]{:S(2)}, u32[]{:S(2)}) %collective-permute-start.13) | collective-permute-done | bytes 36896 | tf_op jit(solution)/shard_map/ppermute | solution.py:285
  67.4 2.0 %shard_map.118 = (bf16[80,8,128]{2,1,0:T(8,128)(2,1)}, f32[80,8,128]{2,1,0:T(8,128)S(1)}, bf16[80,8,128]{2,1,0:T(8,128)(2,1)S(1)}) custom-call(bf16[80,8,128]{2,1,0:T(8,128)(2,1)S(1)} %constant_dynamic-slice_fusion.2.refs_11_.left_ref, bf16[240,960]{1,0:T(8,128)(2,1)S(1)} %select_n.92.weight_ref, bf16[50,320,128]{2,1,0:T(8,128)(2,1)S(1)} %get-tuple-element.58.cot_s, ...), custom_call_target="tpu_custom_call" | custom-call | flops 1000000 | bytes 1024 | tf_op jit(solution)/shard_map/pallas_call | solution.py:272
  70.3 1.1 %collective-permute-done.17 = bf16[80,8,128]{2,1,0:T(8,128)(2,1)S(1)} collective-permute-done((bf16[80,8,128]{2,1,0:T(8,128)(2,1)S(1)}, bf16[80,8,128]{2,1,0:T(8,128)(2,1)S(1)}, u32[]{:S(2)}, u32[]{:S(2)}) %collective-permute-start.17) | collective-permute-done | bytes 163872 | tf_op jit(solution)/shard_map/ppermute | solution.py:21
  71.4 2.8 %collective-permute-start.23 = (f32[3,32,96]{2,1,0:T(8,128)S(1)}, f32[3,32,96]{2,1,0:T(8,128)S(1)}, u32[]{:S(2)}, u32[]{:S(2)}) collective-permute-start(f32[3,32,96]{2,1,0:T(8,128)S(1)} %add.67), channel_id=1, source_target_pairs={{0,3},{1,2},{2,1},{3,0},{4,7},{5,6},{6,5},{7,4},{8,11},{9,10},{10,... | collective-permute-start | bytes 110600 | tf_op jit(solution)/shard_map/ppermute | solution.py:285
  74.6 3.6 %collective-permute-start.20 = (bf16[80,8,128]{2,1,0:T(8,128)(2,1)S(1)}, bf16[80,8,128]{2,1,0:T(8,128)(2,1)}, u32[]{:S(2)}, u32[]{:S(2)}) collective-permute-start(bf16[80,8,128]{2,1,0:T(8,128)(2,1)S(1)} %get-tuple-element.82), channel_id=1, source_target_pairs={{0,20},{4,24},{8,28},{12,0},{16,4},{20,8},{24,12},{28,16},{1,21},{... | collective-permute-start | bytes 491528 | tf_op jit(solution)/shard_map/ppermute | solution.py:21
  80.6 1.0 %copy.37 = f32[3,3,3,32,40]{4,3,2,1,0:T(8,128)} copy(f32[3,3,3,32,40]{3,4,2,1,0:T(8,128)S(1)} %mul.20) | data formatting | bytes 276480
  82.2 3.2 %collective-permute-done.19 = bf16[80,8,128]{2,1,0:T(8,128)(2,1)} collective-permute-done((bf16[80,8,128]{2,1,0:T(8,128)(2,1)S(1)}, bf16[80,8,128]{2,1,0:T(8,128)(2,1)}, u32[]{:S(2)}, u32[]{:S(2)}) %collective-permute-start.19) | collective-permute-done | bytes 163872 | tf_op jit(solution)/shard_map/ppermute | solution.py:21
  85.3 6.4 %collective-permute-done.18 = bf16[80,8,128]{2,1,0:T(8,128)(2,1)} collective-permute-done((bf16[80,8,128]{2,1,0:T(8,128)(2,1)S(1)}, bf16[80,8,128]{2,1,0:T(8,128)(2,1)}, u32[]{:S(2)}, u32[]{:S(2)}) %collective-permute-start.18) | collective-permute-done | bytes 163872 | tf_op jit(solution)/shard_map/ppermute | solution.py:21
  91.8 1.9 %add_convert_fusion = bf16[80,8,128]{2,1,0:T(8,128)(2,1)} fusion(bf16[80,8,128]{2,1,0:T(8,128)(2,1)S(1)} %collective-permute-done.17, bf16[80,8,128]{2,1,0:T(8,128)(2,1)S(1)} %collective-permute-done.16, bf16[80,8,128]{2,1,0:T(8,128)(2,1)S(1)} %collective-permute-done.15, bf16[80,8,128]{2,1,0:T(8,128)(2,1)} %collective-permute-done.20, ...), kind=kLoop, calls=%fused_computation.5 | loop fusion | flops 1556480 | bytes 1474566 | tf_op jit(solution)/shard_map/convert_element_type | solution.py:435
  (68 shorter events, 9.9 us)
Async XLA Ops:
  0.6 2.6 %copy-start = (bf16[320,8,128]{2,1,0:T(8,128)(2,1)S(1)}, bf16[320,8,128]{2,1,0:T(8,128)(2,1)}, u32[]{:S(2)}) copy-start(bf16[320,8,128]{2,1,0:T(8,128)(2,1)} %param.10) | copy-start | bytes 1966084
  0.6 8.8 %copy-start.3 = (bf16[32,320,1,1,1]{1,0,4,3,2:T(8,128)(2,1)S(1)}, bf16[32,320,1,1,1]{1,0,4,3,2:T(8,128)(2,1)}, u32[]{:S(2)}) copy-start(bf16[32,320,1,1,1]{1,0,4,3,2:T(8,128)(2,1)} %constant.59) | copy-start | bytes 61444
  0.7 9.3 %copy-start.4 = (pred[8,320]{1,0:T(8,128)(4,1)S(1)}, pred[8,320]{1,0:T(8,128)(4,1)}, u32[]{:S(2)}) copy-start(pred[8,320]{1,0:T(8,128)(4,1)} %constant.55.clone) | copy-start | bytes 7684
  0.7 9.3 %copy-start.5 = (pred[8,320]{1,0:T(8,128)(4,1)S(1)}, pred[8,320]{1,0:T(8,128)(4,1)}, u32[]{:S(2)}) copy-start(pred[8,320]{1,0:T(8,128)(4,1)} %constant.56.clone) | copy-start | bytes 7684
  0.7 9.3 %copy-start.6 = (pred[8,320]{1,0:T(8,128)(4,1)S(1)}, pred[8,320]{1,0:T(8,128)(4,1)}, u32[]{:S(2)}) copy-start(pred[8,320]{1,0:T(8,128)(4,1)} %constant.57.clone) | copy-start | bytes 7684
  3.3 16.2 %collective-permute-start.2 = (bf16[80,8,128]{2,1,0:T(8,128)(2,1)S(1)}, bf16[80,8,128]{2,1,0:T(8,128)(2,1)S(1)}, u32[]{:S(2)}, u32[]{:S(2)}) collective-permute-start(bf16[80,8,128]{2,1,0:T(8,128)(2,1)S(1)} %constant_dynamic-slice_fusion.refs_4_), channel_id=1, source_target_pairs={{0,8},{4,12},{8,16},{12,20},{16,24},{20,28},{24,0},{28,4},{1,9},{5... | collective-permute-start | bytes 491528 | tf_op jit(solution)/shard_map/ppermute | solution.py:21
  4.6 14.9 %collective-permute-start.3 = (bf16[80,8,128]{2,1,0:T(8,128)(2,1)S(1)}, bf16[80,8,128]{2,1,0:T(8,128)(2,1)S(1)}, u32[]{:S(2)}, u32[]{:S(2)}) collective-permute-start(bf16[80,8,128]{2,1,0:T(8,128)(2,1)S(1)} %constant_dynamic-slice_fusion.refs_4_), channel_id=1, source_target_pairs={{0,16},{4,20},{8,24},{12,28},{16,0},{20,4},{24,8},{28,12},{1,17},{... | collective-permute-start | bytes 491528 | tf_op jit(solution)/shard_map/ppermute | solution.py:21
  5.7 29.5 %collective-permute-start.5 = (bf16[32,12,8,128]{3,2,1,0:T(8,128)(2,1)}, bf16[32,12,8,128]{3,2,1,0:T(8,128)(2,1)S(1)}, u32[]{:S(2)}, u32[]{:S(2)}) collective-permute-start(bf16[32,12,8,128]{3,2,1,0:T(8,128)(2,1)} %cot_ref.1), channel_id=1, source_target_pairs={{0,2},{1,3},{2,0},{3,1},{4,6},{5,7},{6,4},{7,5},{8,10},{9,11},{10,... | collective-permute-start | bytes 2359304 | tf_op jit(solution)/shard_map/ppermute | solution.py:285
  6.9 9.8 %collective-permute-start = (bf16[12,32,128]{2,1,0:T(8,128)(2,1)}, bf16[12,32,128]{2,1,0:T(8,128)(2,1)}, u32[]{:S(2)}, u32[]{:S(2)}) collective-permute-start(bf16[12,32,128]{2,1,0:T(8,128)(2,1)} %get-tuple-element.45), channel_id=1, source_target_pairs={{0,4},{4,8},{8,12},{12,16},{16,20},{20,24},{24,28},{28,0},{1,5},{5... | collective-permute-start | bytes 294920 | tf_op jit(solution)/shard_map/ppermute | solution.py:21
  7.1 12.3 %collective-permute-start.1 = (bf16[12,32,128]{2,1,0:T(8,128)(2,1)S(1)}, bf16[12,32,128]{2,1,0:T(8,128)(2,1)}, u32[]{:S(2)}, u32[]{:S(2)}) collective-permute-start(bf16[12,32,128]{2,1,0:T(8,128)(2,1)S(1)} %get-tuple-element.46), channel_id=1, source_target_pairs={{0,28},{4,0},{8,4},{12,8},{16,12},{20,16},{24,20},{28,24},{1,29},{... | collective-permute-start | bytes 294920 | tf_op jit(solution)/shard_map/ppermute | solution.py:21
  9.8 14.4 %copy-start.1 = (bf16[32,12,8,128]{3,2,1,0:T(8,128)(2,1)S(1)}, bf16[32,12,8,128]{3,2,1,0:T(8,128)(2,1)}, u32[]{:S(2)}) copy-start(bf16[32,12,8,128]{3,2,1,0:T(8,128)(2,1)} %cot_ref.1) | copy-start | bytes 2359300
  16.7 7.5 %collective-permute-start.8 = (bf16[80,8,128]{2,1,0:T(8,128)(2,1)S(1)}, bf16[80,8,128]{2,1,0:T(8,128)(2,1)S(1)}, u32[]{:S(2)}, u32[]{:S(2)}) collective-permute-start(bf16[80,8,128]{2,1,0:T(8,128)(2,1)S(1)} %constant_dynamic-slice_fusion.refs_4_), channel_id=1, source_target_pairs={{0,24},{4,28},{8,0},{12,4},{16,8},{20,12},{24,16},{28,20},{1,25},{... | collective-permute-start | bytes 491528 | tf_op jit(solution)/shard_map/ppermute | solution.py:21
  19.5 15.7 %collective-permute-start.7 = (bf16[2,80,8,128]{3,2,1,0:T(8,128)(2,1)S(1)}, bf16[2,80,8,128]{3,2,1,0:T(8,128)(2,1)S(1)}, u32[]{:S(2)}, u32[]{:S(2)}) collective-permute-start(bf16[2,80,8,128]{3,2,1,0:T(8,128)(2,1)S(1)} %shard_map.113), channel_id=1, source_target_pairs={{0,4},{4,0},{8,12},{12,8},{16,20},{20,16},{24,28},{28,24},{1,5},{5... | collective-permute-start | bytes 983048 | tf_op jit(solution)/shard_map/ppermute | solution.py:285
  20.5 18.7 %copy-start.2 = (f32[32,240]{1,0:T(8,128)S(1)}, f32[32,240]{1,0:T(8,128)}, u32[]{:S(2)}) copy-start(f32[32,240]{1,0:T(8,128)} %constant.58.clone.refs_12_) | copy-start | bytes 92164
  21.4 13.8 %collective-permute-start.10 = (bf16[12,64,128]{2,1,0:T(8,128)(2,1)S(1)}, bf16[12,64,128]{2,1,0:T(8,128)(2,1)S(1)}, u32[]{:S(2)}, u32[]{:S(2)}) collective-permute-start(bf16[12,64,128]{2,1,0:T(8,128)(2,1)S(1)} %pad_maximum_fusion.halo_ref), channel_id=1, source_target_pairs={{0,2},{1,3},{2,0},{3,1},{4,6},{5,7},{6,4},{7,5},{8,10},{9,11},{10,... | collective-permute-start | bytes 589832 | tf_op jit(solution)/shard_map/ppermute | solution.py:285
  22.7 9.0 %collective-permute-start.6 = (bf16[80,8,128]{2,1,0:T(8,128)(2,1)S(1)}, bf16[80,8,128]{2,1,0:T(8,128)(2,1)S(1)}, u32[]{:S(2)}, u32[]{:S(2)}) collective-permute-start(bf16[80,8,128]{2,1,0:T(8,128)(2,1)S(1)} %constant_dynamic-slice_fusion.refs_4_), channel_id=1, source_target_pairs={{0,4},{4,0},{8,12},{12,8},{16,20},{20,16},{24,28},{28,24},{1,5},{5... | collective-permute-start | bytes 491528 | tf_op jit(solution)/shard_map/ppermute | solution.py:285
  24.2 11.1 %collective-permute-start.9 = (bf16[80,8,128]{2,1,0:T(8,128)(2,1)S(1)}, bf16[80,8,128]{2,1,0:T(8,128)(2,1)S(1)}, u32[]{:S(2)}, u32[]{:S(2)}) collective-permute-start(bf16[80,8,128]{2,1,0:T(8,128)(2,1)S(1)} %collective-permute-done.8.refs_7_), channel_id=1, source_target_pairs={{0,4},{4,0},{8,12},{12,8},{16,20},{20,16},{24,28},{28,24},{1,5},{5... | collective-permute-start | bytes 491528 | tf_op jit(solution)/shard_map/ppermute | solution.py:285
  31.7 5.4 %collective-permute-start.4 = (bf16[12,320,128]{2,1,0:T(8,128)(2,1)S(1)}, bf16[12,320,128]{2,1,0:T(8,128)(2,1)S(1)}, u32[]{:S(2)}, u32[]{:S(2)}) collective-permute-start(bf16[12,320,128]{2,1,0:T(8,128)(2,1)S(1)} %shard_map.112.refs_0_), channel_id=1, source_target_pairs={{0,1},{1,0},{2,3},{3,2},{4,5},{5,4},{6,7},{7,6},{8,9},{9,8},{10,11... | collective-permute-start | bytes 2949128 | tf_op jit(solution)/shard_map/ppermute | solution.py:285
  35.5 3.7 %collective-permute-start.11 = (bf16[12,320,128]{2,1,0:T(8,128)(2,1)S(1)}, bf16[12,320,128]{2,1,0:T(8,128)(2,1)S(1)}, u32[]{:S(2)}, u32[]{:S(2)}) collective-permute-start(bf16[12,320,128]{2,1,0:T(8,128)(2,1)S(1)} %shard_map.114.refs_2_), channel_id=1, source_target_pairs={{0,1},{1,0},{2,3},{3,2},{4,5},{5,4},{6,7},{7,6},{8,9},{9,8},{10,11... | collective-permute-start | bytes 2949128 | tf_op jit(solution)/shard_map/ppermute | solution.py:285
  47.6 5.0 %collective-permute-start.12 = (f32[3,32,96]{2,1,0:T(8,128)S(1)}, f32[3,32,96]{2,1,0:T(8,128)S(1)}, u32[]{:S(2)}, u32[]{:S(2)}) collective-permute-start(f32[3,32,96]{2,1,0:T(8,128)S(1)} %get-tuple-element.65), channel_id=1, source_target_pairs={{0,16},{4,20},{8,24},{12,28},{16,0},{20,4},{24,8},{28,12},{1,17},{... | collective-permute-start | bytes 110600 | tf_op jit(solution)/shard_map/ppermute | solution.py:285
  52.6 17.7 %collective-permute-start.15 = (bf16[80,8,128]{2,1,0:T(8,128)(2,1)S(1)}, bf16[80,8,128]{2,1,0:T(8,128)(2,1)S(1)}, u32[]{:S(2)}, u32[]{:S(2)}) collective-permute-start(bf16[80,8,128]{2,1,0:T(8,128)(2,1)S(1)} %get-tuple-element.77), channel_id=1, source_target_pairs={{0,16},{4,20},{8,24},{12,28},{16,0},{20,4},{24,8},{28,12},{1,17},{... | collective-permute-start | bytes 491528 | tf_op jit(solution)/shard_map/ppermute | solution.py:21
  54.3 16.0 %collective-permute-start.16 = (bf16[80,8,128]{2,1,0:T(8,128)(2,1)S(1)}, bf16[80,8,128]{2,1,0:T(8,128)(2,1)S(1)}, u32[]{:S(2)}, u32[]{:S(2)}) collective-permute-start(bf16[80,8,128]{2,1,0:T(8,128)(2,1)S(1)} %get-tuple-element.78), channel_id=1, source_target_pairs={{0,12},{4,16},{8,20},{12,24},{16,28},{20,0},{24,4},{28,8},{1,13},{... | collective-permute-start | bytes 491528 | tf_op jit(solution)/shard_map/ppermute | solution.py:21
  56.5 14.9 %collective-permute-start.17 = (bf16[80,8,128]{2,1,0:T(8,128)(2,1)S(1)}, bf16[80,8,128]{2,1,0:T(8,128)(2,1)S(1)}, u32[]{:S(2)}, u32[]{:S(2)}) collective-permute-start(bf16[80,8,128]{2,1,0:T(8,128)(2,1)S(1)} %get-tuple-element.79), channel_id=1, source_target_pairs={{0,8},{4,12},{8,16},{12,20},{16,24},{20,28},{24,0},{28,4},{1,9},{5... | collective-permute-start | bytes 491528 | tf_op jit(solution)/shard_map/ppermute | solution.py:21
  56.5 10.7 %collective-permute-start.13 = (f32[3,32,96]{2,1,0:T(8,128)S(1)}, f32[3,32,96]{2,1,0:T(8,128)S(1)}, u32[]{:S(2)}, u32[]{:S(2)}) collective-permute-start(f32[3,32,96]{2,1,0:T(8,128)S(1)} %add.64), channel_id=1, source_target_pairs={{0,8},{4,12},{8,0},{12,4},{16,24},{20,28},{24,16},{28,20},{1,9},{5... | collective-permute-start | bytes 110600 | tf_op jit(solution)/shard_map/ppermute | solution.py:285
  67.3 3.0 %collective-permute-start.14 = (f32[3,32,96]{2,1,0:T(8,128)S(1)}, f32[3,32,96]{2,1,0:T(8,128)S(1)}, u32[]{:S(2)}, u32[]{:S(2)}) collective-permute-start(f32[3,32,96]{2,1,0:T(8,128)S(1)} %add.65), channel_id=1, source_target_pairs={{0,4},{4,0},{8,12},{12,8},{16,20},{20,16},{24,28},{28,24},{1,5},{5... | collective-permute-start | bytes 110600 | tf_op jit(solution)/shard_map/ppermute | solution.py:285
  71.4 7.4 %collective-permute-start.23 = (f32[3,32,96]{2,1,0:T(8,128)S(1)}, f32[3,32,96]{2,1,0:T(8,128)S(1)}, u32[]{:S(2)}, u32[]{:S(2)}) collective-permute-start(f32[3,32,96]{2,1,0:T(8,128)S(1)} %add.67), channel_id=1, source_target_pairs={{0,3},{1,2},{2,1},{3,0},{4,7},{5,6},{6,5},{7,4},{8,11},{9,10},{10,... | collective-permute-start | bytes 110600 | tf_op jit(solution)/shard_map/ppermute | solution.py:285
  74.2 5.0 %collective-permute-start.22 = (f32[3,32,96]{2,1,0:T(8,128)S(1)}, f32[3,32,96]{2,1,0:T(8,128)S(1)}, u32[]{:S(2)}, u32[]{:S(2)}) collective-permute-start(f32[3,32,96]{2,1,0:T(8,128)S(1)} %add.67), channel_id=1, source_target_pairs={{0,2},{1,3},{2,0},{3,1},{4,6},{5,7},{6,4},{7,5},{8,10},{9,11},{10,... | collective-permute-start | bytes 110600 | tf_op jit(solution)/shard_map/ppermute | solution.py:285
  74.3 4.9 %collective-permute-start.21 = (f32[3,32,96]{2,1,0:T(8,128)S(1)}, f32[3,32,96]{2,1,0:T(8,128)S(1)}, u32[]{:S(2)}, u32[]{:S(2)}) collective-permute-start(f32[3,32,96]{2,1,0:T(8,128)S(1)} %add.67), channel_id=1, source_target_pairs={{0,1},{1,0},{2,3},{3,2},{4,5},{5,4},{6,7},{7,6},{8,9},{9,8},{10,11... | collective-permute-start | bytes 110600 | tf_op jit(solution)/shard_map/ppermute | solution.py:285
  74.6 7.5 %collective-permute-start.20 = (bf16[80,8,128]{2,1,0:T(8,128)(2,1)S(1)}, bf16[80,8,128]{2,1,0:T(8,128)(2,1)}, u32[]{:S(2)}, u32[]{:S(2)}) collective-permute-start(bf16[80,8,128]{2,1,0:T(8,128)(2,1)S(1)} %get-tuple-element.82), channel_id=1, source_target_pairs={{0,20},{4,24},{8,28},{12,0},{16,4},{20,8},{24,12},{28,16},{1,21},{... | collective-permute-start | bytes 491528 | tf_op jit(solution)/shard_map/ppermute | solution.py:21
  78.2 7.1 %collective-permute-start.19 = (bf16[80,8,128]{2,1,0:T(8,128)(2,1)S(1)}, bf16[80,8,128]{2,1,0:T(8,128)(2,1)}, u32[]{:S(2)}, u32[]{:S(2)}) collective-permute-start(bf16[80,8,128]{2,1,0:T(8,128)(2,1)S(1)} %get-tuple-element.81), channel_id=1, source_target_pairs={{0,24},{4,28},{8,0},{12,4},{16,8},{20,12},{24,16},{28,20},{1,25},{... | collective-permute-start | bytes 491528 | tf_op jit(solution)/shard_map/ppermute | solution.py:21
  78.8 13.0 %collective-permute-start.18 = (bf16[80,8,128]{2,1,0:T(8,128)(2,1)S(1)}, bf16[80,8,128]{2,1,0:T(8,128)(2,1)}, u32[]{:S(2)}, u32[]{:S(2)}) collective-permute-start(bf16[80,8,128]{2,1,0:T(8,128)(2,1)S(1)} %get-tuple-element.80), channel_id=1, source_target_pairs={{0,28},{4,0},{8,4},{12,8},{16,12},{20,16},{24,20},{28,24},{1,29},{... | collective-permute-start | bytes 491528 | tf_op jit(solution)/shard_map/ppermute | solution.py:21

commit v13 on v12

--- a/solution.py
+++ b/solution.py
@@ -147,7 +147,7 @@
     left_sum[...] = jnp.zeros(left_sum.shape, f32)
     grad_s[...] = jnp.zeros(grad_s.shape, f32)
     add_grads(
-        D // 2, D // 2, reach, 0, cot_s, weight_ref, left_s, right_s, left_sum, grad_s
+        reach - far * width, D - reach + far * width, reach, 0, cot_s, weight_ref, left_s, right_s, left_sum, grad_s
     )
     grad_out[...] = grad_s[:, far * width :]
     for at in range(far):
@@ -307,7 +307,7 @@
     size = groups * width
     span = outs * (width + 2)
     hops = (D + width - 2) // width
-    far = D // 2 // width
+    far = 2
     first = (hops // 2, hops // 2 + 1)
     near = hops - far
     part, column = lax.axis_index("disp"), lax.axis_index("col")
@@ -324,8 +324,9 @@
     weights = toeplitz(lax.dynamic_slice_in_dim(kernel, part * groups, groups, 4), width)
     pairs = hops // 2
     evens = [right_own] + [shifted(right_own, "col", 2 * k) for k in range(1, pairs + 1)]
-    low, high, left_own, weights, *evens[1:pairs] = lax.optimization_barrier(
-        (low, high, left_own, weights, *evens[1:pairs])
+    swap_own = swapped(right_own, "col", 1)
+    low, high, left_own, weights, swap_own, *evens[1:pairs] = lax.optimization_barrier(
+        (low, high, left_own, weights, swap_own, *evens[1:pairs])
     )
     low = jnp.where(column > 0, low, 0).astype(bf16)
     high = jnp.where(column < columns - 1, high, 0).astype(bf16)
@@ -334,7 +335,7 @@
         join, [(VMEM, item) for item in evens[1:pairs]],
         [((pairs - 1, channels, width, rows), bf16)], [], 4, 1000000,
     )
-    odds = [swapped(item, "col", 1) for item in (right_own, joined, evens[pairs])]
+    odds = [swap_own] + [swapped(item, "col", 1) for item in (joined, evens[pairs])]
     blocks = {}
     across = parts // 2
     cots[across], *odds = lax.optimization_barrier((cots[across], *odds))
@@ -406,19 +407,24 @@
             8, 1000000,
         )
 
-    left_part, grad_part, *sent = lower(width, D // 2 - width, 0, f32, left_part, grad_part)
+    left_part, grad_part, *sent = lower(
+        width, reach - (far + 1) * width, 0, f32, left_part, grad_part
+    )
     total = total_swapping(total, bits[1])
     grad_part, total = lax.optimization_barrier((grad_part, total))
     grad_left, own, *last = lower(0, width, middle, bf16, left_part, grad_part)
     for bit in bits[2:]:
         total = total_swapping(total, bit)
-    distant = sorted(arrived)
-    sent, last, total, *items = lax.optimization_barrier(
-        (sent, last, total, *[arrived[hop] for hop in distant])
-    )
-    arrived = dict(zip(distant, items))
-    for hop, value in zip(range(near, 0, -1), [*sent, *last]):
+    for hop, value in zip(range(near, 2, -1), sent):
         arrived[hop] = shifted(value, "col", -hop)
+    waiting, arrived[hops], arrived[hops - 1] = lax.optimization_barrier(
+        (sent[-1], arrived[hops], arrived[hops - 1])
+    )
+    arrived[2] = shifted(waiting, "col", -2)
+    waiting, arrived[4], arrived[3] = lax.optimization_barrier(
+        (last[0], arrived[4], arrived[3])
+    )
+    arrived[1] = shifted(waiting, "col", -1)
 
     total_right = own
     for hop in range(1, hops + 1):

time: 94.4 us -> 96.4 us (1.021)
  waiting for transfers between devices: 34.3 us -> 19.5 us
  local copies, waits for them, and re-layouts: 8.52 us -> 18.8 us
  starting transfers between devices: 26 us -> 31.6 us
  other arithmetic: 5.46 us -> 4.4 us
  Pallas kernels: 18.2 us -> 19.2 us
    ppermute x13, waiting for transfers between devices: 17.5 us -> 5.67 us  [swapped(): lax.ppermute(value, axis, [(source, source ^ bit) for source in range(cou...]
    unnamed x15 -> x55, local copies, waits for them, and re-layouts: 1.02 us -> 10.8 us
    ppermute x13, starting transfers between devices: 13.7 us -> 21.4 us  [swapped(): lax.ppermute(value, axis, [(source, source ^ bit) for source in range(cou...]
    ppermute x11, waiting for transfers between devices: 16.8 us -> 13.9 us  [shifted(): lax.ppermute(value, axis, [(source, (source + steps) % count) for source...]
    ppermute x11, starting transfers between devices: 12.4 us -> 10.2 us  [shifted(): lax.ppermute(value, axis, [(source, (source + steps) % count) for source...]
    pallas_call x7, Pallas kernels: 18.2 us -> 19.2 us  [run(): pl.pallas_call(function, out_shape=[jax.ShapeDtypeStruct(shape, kind) for...]
  transfers between devices with their start and end apart: 24 -> 24, of which waited for: 11 -> 8; matrix products, arithmetic and copies ran while one was open for 10% -> 10% of each run, Pallas kernels for 10% -> 11%
where the time goes in v13:
time: 96.4 us; the launch traced here: 94.8 us
  starting transfers between devices  31.6 us (33%)
  waiting for transfers between devices  19.5 us (20%)
  Pallas kernels  19.2 us (20%)
  local copies, waits for them, and re-layouts  18.8 us (20%)
  other arithmetic  4.4 us (5%)
  between operations  1.06 us (1%)
    ppermute x13, starting transfers between devices, swapped(): lax.ppermute(value, axis, [(source, source ^ bit) for source in range(cou...  21.4 us
    pallas_call x7, Pallas kernels, run(): pl.pallas_call(function, out_shape=[jax.ShapeDtypeStruct(shape, kind) for...  19.2 us
    ppermute x11, waiting for transfers between devices, shifted(): lax.ppermute(value, axis, [(source, (source + steps) % count) for source...  13.9 us
    unnamed x55, local copies, waits for them, and re-layouts  10.8 us
    ppermute x11, starting transfers between devices, shifted(): lax.ppermute(value, axis, [(source, (source + steps) % count) for source...  10.2 us
    ppermute x13, waiting for transfers between devices, swapped(): lax.ppermute(value, axis, [(source, source ^ bit) for source in range(cou...  5.67 us
  transfers between devices with their start and end apart: 24, of which 8 were waited for; matrix products, arithmetic and copies ran while one was open for 10% of the time, Pallas kernels for 11%

profile of v13, /device:TPU:13, one launch (start us, length us, event | category | flops | bytes accessed | tf_op | source)
XLA Modules:
  0.0 94.8 jit_solution(10978668738852755835)
XLA Ops:
  0.7 1.7 %fusion.2 = (bf16[32,12,1,128]{3,2,1,0:T(2,128)(2,1)S(1)}, bf16[32,12,1,128]{3,2,1,0:T(2,128)(2,1)S(1)}) fusion(bf16[32,12,8,128]{3,2,1,0:T(8,128)(2,1)} %cot_ref.1), kind=kLoop, calls=%fused_computation.24 | loop fusion | bytes 393216 | tf_op jit(solution)/shard_map/slice | solution.py:318
  3.4 1.3 %collective-permute-start.3 = (bf16[80,8,128]{2,1,0:T(8,128)(2,1)}, bf16[80,8,128]{2,1,0:T(8,128)(2,1)S(1)}, u32[]{:S(2)}, u32[]{:S(2)}) collective-permute-start(bf16[80,8,128]{2,1,0:T(8,128)(2,1)} %constant_dynamic-slice_fusion.refs_4_), channel_id=1, source_target_pairs={{0,8},{4,12},{8,16},{12,20},{16,24},{20,28},{24,0},{28,4},{1,9},{5... | collective-permute-start | bytes 491528 | tf_op jit(solution)/shard_map/ppermute | solution.py:21
  5.7 1.2 %collective-permute-start.6 = (bf16[32,12,8,128]{3,2,1,0:T(8,128)(2,1)}, bf16[32,12,8,128]{3,2,1,0:T(8,128)(2,1)S(1)}, u32[]{:S(2)}, u32[]{:S(2)}) collective-permute-start(bf16[32,12,8,128]{3,2,1,0:T(8,128)(2,1)} %cot_ref.1), channel_id=1, source_target_pairs={{0,2},{1,3},{2,0},{3,1},{4,6},{5,7},{6,4},{7,5},{8,10},{9,11},{10,... | collective-permute-start | bytes 2359304 | tf_op jit(solution)/shard_map/ppermute | solution.py:285
  6.9 1.3 %collective-permute-start = (bf16[12,32,128]{2,1,0:T(8,128)(2,1)S(1)}, bf16[12,32,128]{2,1,0:T(8,128)(2,1)S(1)}, u32[]{:S(2)}, u32[]{:S(2)}) collective-permute-start(bf16[12,32,128]{2,1,0:T(8,128)(2,1)S(1)} %get-tuple-element.44), channel_id=1, source_target_pairs={{0,4},{4,8},{8,12},{12,16},{16,20},{20,24},{24,28},{28,0},{1,5},{5... | collective-permute-start | bytes 294920 | tf_op jit(solution)/shard_map/ppermute | solution.py:21
  9.8 1.4 %select_select_fusion = bf16[3,10,8,3,320]{4,3,2,1,0:T(4,128)(2,1)} fusion(pred[8,320]{1,0:T(8,128)(4,1)S(1)} %copy-done.24, pred[8,320]{1,0:T(8,128)(4,1)S(1)} %copy-done.25, pred[8,320]{1,0:T(8,128)(4,1)S(1)} %copy-done.26, bf16[3,10,3,320]{3,2,1,0:T(4,128)(2,1)S(1)} %copy.33, bf16[3,10,3,320]{3,2,1,0:T(4,128)(2,1)S(1)} %copy.32, ...), kind=kLoop, calls=%fused_computation.2 | loop fusion | flops 691200 | bytes 641280 | tf_op jit(solution)/shard_map/jit(_where)/select_n | solution.py:45
  11.2 5.4 %collective-permute-done = bf16[12,32,128]{2,1,0:T(8,128)(2,1)S(1)} collective-permute-done((bf16[12,32,128]{2,1,0:T(8,128)(2,1)S(1)}, bf16[12,32,128]{2,1,0:T(8,128)(2,1)S(1)}, u32[]{:S(2)}, u32[]{:S(2)}) %collective-permute-start) | collective-permute-done | bytes 98336 | tf_op jit(solution)/shard_map/ppermute | solution.py:21
  16.6 1.6 %constant_dynamic-slice_fusion.2.refs_11_.left_ref = bf16[80,8,128]{2,1,0:T(8,128)(2,1)} fusion(bf16[320,8,128]{2,1,0:T(8,128)(2,1)} %param.9, s32[]{:T(128)S(6)} %select_n.87), kind=kLoop, calls=%fused_computation.21 | loop fusion | bytes 327684 | tf_op jit(solution)/shard_map/dynamic_slice | solution.py:323
  18.2 1.7 %select_n.92.weight_ref = bf16[240,960]{1,0:T(8,128)(2,1)S(1)} reshape(bf16[3,10,8,3,320]{4,3,2,1,0:T(4,128)(2,1)} %select_select_fusion) | data formatting | bytes 921600 | tf_op jit(solution)/shard_map/jit(_where)/select_n | solution.py:45
  19.9 1.5 %collective-permute-done.1 = bf16[12,32,128]{2,1,0:T(8,128)(2,1)S(1)} collective-permute-done((bf16[12,32,128]{2,1,0:T(8,128)(2,1)S(1)}, bf16[12,32,128]{2,1,0:T(8,128)(2,1)S(1)}, u32[]{:S(2)}, u32[]{:S(2)}) %collective-permute-start.1) | collective-permute-done | bytes 98336 | tf_op jit(solution)/shard_map/ppermute | solution.py:21
  23.3 1.3 %collective-permute-start.10 = (bf16[12,64,128]{2,1,0:T(8,128)(2,1)S(1)}, bf16[12,64,128]{2,1,0:T(8,128)(2,1)S(1)}, u32[]{:S(2)}, u32[]{:S(2)}) collective-permute-start(bf16[12,64,128]{2,1,0:T(8,128)(2,1)S(1)} %pad_maximum_fusion.halo_ref), channel_id=1, source_target_pairs={{0,2},{1,3},{2,0},{3,1},{4,6},{5,7},{6,4},{7,5},{8,10},{9,11},{10,... | collective-permute-start | bytes 589832 | tf_op jit(solution)/shard_map/ppermute | solution.py:285
  24.6 1.4 %collective-permute-done.8.refs_7_ = bf16[80,8,128]{2,1,0:T(8,128)(2,1)S(1)} collective-permute-done((bf16[80,8,128]{2,1,0:T(8,128)(2,1)}, bf16[80,8,128]{2,1,0:T(8,128)(2,1)S(1)}, u32[]{:S(2)}, u32[]{:S(2)}) %collective-permute-start.8) | collective-permute-done | bytes 163872 | tf_op jit(solution)/shard_map/ppermute | solution.py:21
  26.9 3.9 %collective-permute-start.5 = (bf16[12,320,128]{2,1,0:T(8,128)(2,1)S(1)}, bf16[12,320,128]{2,1,0:T(8,128)(2,1)S(1)}, u32[]{:S(2)}, u32[]{:S(2)}) collective-permute-start(bf16[12,320,128]{2,1,0:T(8,128)(2,1)S(1)} %shard_map.112.refs_0_), channel_id=1, source_target_pairs={{0,1},{1,0},{2,3},{3,2},{4,5},{5,4},{6,7},{7,6},{8,9},{9,8},{10,11... | collective-permute-start | bytes 2949128 | tf_op jit(solution)/shard_map/ppermute | solution.py:285
  30.8 2.0 %collective-permute-done.9.refs_10_ = bf16[80,8,128]{2,1,0:T(8,128)(2,1)S(1)} collective-permute-done((bf16[80,8,128]{2,1,0:T(8,128)(2,1)S(1)}, bf16[80,8,128]{2,1,0:T(8,128)(2,1)S(1)}, u32[]{:S(2)}, u32[]{:S(2)}) %collective-permute-start.9) | collective-permute-done | bytes 163872 | tf_op jit(solution)/shard_map/ppermute | solution.py:285
  33.1 3.5 %collective-permute-start.11 = (bf16[12,320,128]{2,1,0:T(8,128)(2,1)S(1)}, bf16[12,320,128]{2,1,0:T(8,128)(2,1)S(1)}, u32[]{:S(2)}, u32[]{:S(2)}) collective-permute-start(bf16[12,320,128]{2,1,0:T(8,128)(2,1)S(1)} %shard_map.114.refs_2_), channel_id=1, source_target_pairs={{0,1},{1,0},{2,3},{3,2},{4,5},{5,4},{6,7},{7,6},{8,9},{9,8},{10,11... | collective-permute-start | bytes 2949128 | tf_op jit(solution)/shard_map/ppermute | solution.py:285
  36.7 2.1 %collective-permute-done.11.refs_3_ = bf16[12,320,128]{2,1,0:T(8,128)(2,1)S(1)} collective-permute-done((bf16[12,320,128]{2,1,0:T(8,128)(2,1)S(1)}, bf16[12,320,128]{2,1,0:T(8,128)(2,1)S(1)}, u32[]{:S(2)}, u32[]{:S(2)}) %collective-permute-start.11) | collective-permute-done | bytes 983072 | tf_op jit(solution)/shard_map/ppermute | solution.py:285
  38.8 8.7 %shard_map.115 = (bf16[50,320,128]{2,1,0:T(8,128)(2,1)S(1)}, f32[80,56,128]{2,1,0:T(8,128)S(1)}, f32[3,32,96]{2,1,0:T(8,128)S(1)}) custom-call(s32[2]{0:T(128)S(1)} %pad_add_fusion.places, bf16[12,320,128]{2,1,0:T(8,128)(2,1)S(1)} %shard_map.112.refs_0_, bf16[12,320,128]{2,1,0:T(8,128)(2,1)S(1)} %collective-permute-done.5.refs_1_, ...), custom_call_target="tpu_custom_call" | custom-call | flops 8000000000 | bytes 1024 | tf_op jit(solution)/shard_map/pallas_call | solution.py:272
  47.6 2.4 %collective-permute-start.12 = (f32[3,32,96]{2,1,0:T(8,128)S(1)}, f32[3,32,96]{2,1,0:T(8,128)S(1)}, u32[]{:S(2)}, u32[]{:S(2)}) collective-permute-start(f32[3,32,96]{2,1,0:T(8,128)S(1)} %get-tuple-element.64), channel_id=1, source_target_pairs={{0,16},{4,20},{8,24},{12,28},{16,0},{20,4},{24,8},{28,12},{1,17},{... | collective-permute-start | bytes 110600 | tf_op jit(solution)/shard_map/ppermute | solution.py:285
  50.0 2.9 %shard_map.116 = (f32[80,8,128]{2,1,0:T(8,128)S(1)}, f32[80,40,128]{2,1,0:T(8,128)S(1)}, bf16[80,8,128]{2,1,0:T(8,128)(2,1)S(1)}, bf16[80,8,128]{2,1,0:T(8,128)(2,1)S(1)}) custom-call(bf16[80,8,128]{2,1,0:T(8,128)(2,1)S(1)} %copy-done.4, bf16[240,960]{1,0:T(8,128)(2,1)S(1)} %select_n.92.weight_ref, bf16[50,320,128]{2,1,0:T(8,128)(2,1)S(1)} %get-tuple-element.58.cot_s, ...), custom_call_target="tpu_custom_call" | custom-call | flops 8000000000 | bytes 1024 | tf_op jit(solution)/shard_map/pallas_call | solution.py:272
  53.0 2.4 %collective-permute-start.18 = (bf16[80,8,128]{2,1,0:T(8,128)(2,1)S(1)}, bf16[80,8,128]{2,1,0:T(8,128)(2,1)S(1)}, u32[]{:S(2)}, u32[]{:S(2)}) collective-permute-start(bf16[80,8,128]{2,1,0:T(8,128)(2,1)S(1)} %get-tuple-element.78), channel_id=1, source_target_pairs={{0,12},{4,16},{8,20},{12,24},{16,28},{20,0},{24,4},{28,8},{1,13},{... | collective-permute-start | bytes 491528 | tf_op jit(solution)/shard_map/ppermute | solution.py:21
  55.4 1.4 %collective-permute-start.13 = (f32[3,32,96]{2,1,0:T(8,128)S(1)}, f32[3,32,96]{2,1,0:T(8,128)S(1)}, u32[]{:S(2)}, u32[]{:S(2)}) collective-permute-start(f32[3,32,96]{2,1,0:T(8,128)S(1)} %add.64), channel_id=1, source_target_pairs={{0,8},{4,12},{8,0},{12,4},{16,24},{20,28},{24,16},{28,20},{1,9},{5... | collective-permute-start | bytes 110600 | tf_op jit(solution)/shard_map/ppermute | solution.py:285
  56.8 5.0 %shard_map.117 = (f32[80,8,128]{2,1,0:T(8,128)S(1)}, f32[80,16,128]{2,1,0:T(8,128)S(1)}, bf16[80,8,128]{2,1,0:T(8,128)(2,1)}, bf16[80,8,128]{2,1,0:T(8,128)(2,1)}, bf16[80,8,128]{2,1,0:T(8,128)(2,1)}) custom-call(bf16[80,8,128]{2,1,0:T(8,128)(2,1)S(1)} %copy-done.4, bf16[240,960]{1,0:T(8,128)(2,1)S(1)} %select_n.92.weight_ref, ...), custom_call_target="tpu_custom_call" | custom-call | flops 1000000 | bytes 1024 | tf_op jit(solution)/shard_map/pallas_call | solution.py:272
  63.5 2.0 %collective-permute-start.15 = (bf16[80,8,128]{2,1,0:T(8,128)(2,1)}, bf16[80,8,128]{2,1,0:T(8,128)(2,1)}, u32[]{:S(2)}, u32[]{:S(2)}) collective-permute-start(bf16[80,8,128]{2,1,0:T(8,128)(2,1)} %get-tuple-element.74), channel_id=1, source_target_pairs={{0,20},{4,24},{8,28},{12,0},{16,4},{20,8},{24,12},{28,16},{1,21},{... | collective-permute-start | bytes 491528 | tf_op jit(solution)/shard_map/ppermute | solution.py:21
  65.5 1.5 %collective-permute-start.20 = (f32[3,32,96]{2,1,0:T(8,128)S(1)}, f32[3,32,96]{2,1,0:T(8,128)S(1)}, u32[]{:S(2)}, u32[]{:S(2)}) collective-permute-start(f32[3,32,96]{2,1,0:T(8,128)S(1)} %add.65), channel_id=1, source_target_pairs={{0,4},{4,0},{8,12},{12,8},{16,20},{20,16},{24,28},{28,24},{1,5},{5... | collective-permute-start | bytes 110600 | tf_op jit(solution)/shard_map/ppermute | solution.py:285
  67.0 1.5 %collective-permute-done.20 = f32[3,32,96]{2,1,0:T(8,128)S(1)} collective-permute-done((f32[3,32,96]{2,1,0:T(8,128)S(1)}, f32[3,32,96]{2,1,0:T(8,128)S(1)}, u32[]{:S(2)}, u32[]{:S(2)}) %collective-permute-start.20) | collective-permute-done | bytes 36896 | tf_op jit(solution)/shard_map/ppermute | solution.py:285
  68.5 4.9 %collective-permute-start.23 = (f32[3,32,96]{2,1,0:T(8,128)S(1)}, f32[3,32,96]{2,1,0:T(8,128)S(1)}, u32[]{:S(2)}, u32[]{:S(2)}) collective-permute-start(f32[3,32,96]{2,1,0:T(8,128)S(1)} %add.78), channel_id=1, source_target_pairs={{0,3},{1,2},{2,1},{3,0},{4,7},{5,6},{6,5},{7,4},{8,11},{9,10},{10,... | collective-permute-start | bytes 110600 | tf_op jit(solution)/shard_map/ppermute | solution.py:285
  74.7 2.2 %copy-done.2 = bf16[50,320,128]{2,1,0:T(8,128)(2,1)S(1)} copy-done((bf16[50,320,128]{2,1,0:T(8,128)(2,1)S(1)}, bf16[50,320,128]{2,1,0:T(8,128)(2,1)}, u32[]{:S(2)}) %copy-start.2) | copy-done | bytes 4096024
  77.8 1.1 %copy-done.7 = f32[80,16,128]{2,1,0:T(8,128)S(1)} copy-done((f32[80,16,128]{2,1,0:T(8,128)S(1)}, f32[80,16,128]{2,1,0:T(8,128)}, u32[]{:S(2)}) %copy-start.7) | copy-done | bytes 655384
  79.9 2.0 %shard_map.118 = (bf16[80,8,128]{2,1,0:T(8,128)(2,1)}, f32[80,8,128]{2,1,0:T(8,128)S(1)}, bf16[80,8,128]{2,1,0:T(8,128)(2,1)}) custom-call(bf16[80,8,128]{2,1,0:T(8,128)(2,1)S(1)} %copy-done.5, bf16[240,960]{1,0:T(8,128)(2,1)S(1)} %select_n.92.weight_ref, bf16[50,320,128]{2,1,0:T(8,128)(2,1)S(1)} %copy-done.2, f32[80,56,128]{2,1,0:T(8,128)S(1)} %get-tuple-element.59.right_s, ...), custom_call_target="tpu_custom_call" | custom-call | flops 1000000 | bytes 1024 | tf_op jit(solution)/shard_map/pallas_call | solution.py:272
  83.0 1.1 %collective-permute-start.16 = (bf16[80,8,128]{2,1,0:T(8,128)(2,1)}, bf16[80,8,128]{2,1,0:T(8,128)(2,1)S(1)}, u32[]{:S(2)}, u32[]{:S(2)}) collective-permute-start(bf16[80,8,128]{2,1,0:T(8,128)(2,1)} %get-tuple-element.75), channel_id=1, source_target_pairs={{0,28},{4,0},{8,4},{12,8},{16,12},{20,16},{24,20},{28,24},{1,29},{... | collective-permute-start | bytes 491528 | tf_op jit(solution)/shard_map/ppermute | solution.py:21
  87.3 1.4 %collective-permute-done.19 = bf16[80,8,128]{2,1,0:T(8,128)(2,1)S(1)} collective-permute-done((bf16[80,8,128]{2,1,0:T(8,128)(2,1)}, bf16[80,8,128]{2,1,0:T(8,128)(2,1)S(1)}, u32[]{:S(2)}, u32[]{:S(2)}) %collective-permute-start.19) | collective-permute-done | bytes 163872 | tf_op jit(solution)/shard_map/ppermute | solution.py:21
  88.7 4.2 %collective-permute-done.16 = bf16[80,8,128]{2,1,0:T(8,128)(2,1)S(1)} collective-permute-done((bf16[80,8,128]{2,1,0:T(8,128)(2,1)}, bf16[80,8,128]{2,1,0:T(8,128)(2,1)S(1)}, u32[]{:S(2)}, u32[]{:S(2)}) %collective-permute-start.16) | collective-permute-done | bytes 163872 | tf_op jit(solution)/shard_map/ppermute | solution.py:21
  93.0 1.9 %add_convert_fusion = bf16[80,8,128]{2,1,0:T(8,128)(2,1)} fusion(bf16[80,8,128]{2,1,0:T(8,128)(2,1)S(1)} %copy-done.20, bf16[80,8,128]{2,1,0:T(8,128)(2,1)S(1)} %copy-done.22, bf16[80,8,128]{2,1,0:T(8,128)(2,1)} %collective-permute-done.14, bf16[80,8,128]{2,1,0:T(8,128)(2,1)} %collective-permute-done.15, bf16[80,8,128]{2,1,0:T(8,128)(2,1)S(1)} %collective-permute-done.19, ...), kind=kLoop, calls=%fused_computation.5 | loop fusion | flops 1556480 | bytes 1474566 | tf_op jit(solution)/shard_map/convert_element_type | solution.py:441
  (108 shorter events, 15.9 us)
Async XLA Ops:
  0.7 9.2 %copy-start.24 = (pred[8,320]{1,0:T(8,128)(4,1)S(1)}, pred[8,320]{1,0:T(8,128)(4,1)}, u32[]{:S(2)}) copy-start(pred[8,320]{1,0:T(8,128)(4,1)} %constant.55.clone) | copy-start | bytes 7684
  3.2 18.7 %collective-permute-start.2 = (bf16[80,8,128]{2,1,0:T(8,128)(2,1)}, bf16[80,8,128]{2,1,0:T(8,128)(2,1)S(1)}, u32[]{:S(2)}, u32[]{:S(2)}) collective-permute-start(bf16[80,8,128]{2,1,0:T(8,128)(2,1)} %constant_dynamic-slice_fusion.refs_4_), channel_id=1, source_target_pairs={{0,4},{4,0},{8,12},{12,8},{16,20},{20,16},{24,28},{28,24},{1,5},{5... | collective-permute-start | bytes 491528 | tf_op jit(solution)/shard_map/ppermute | solution.py:285
  3.4 19.1 %collective-permute-start.3 = (bf16[80,8,128]{2,1,0:T(8,128)(2,1)}, bf16[80,8,128]{2,1,0:T(8,128)(2,1)S(1)}, u32[]{:S(2)}, u32[]{:S(2)}) collective-permute-start(bf16[80,8,128]{2,1,0:T(8,128)(2,1)} %constant_dynamic-slice_fusion.refs_4_), channel_id=1, source_target_pairs={{0,8},{4,12},{8,16},{12,20},{16,24},{20,28},{24,0},{28,4},{1,9},{5... | collective-permute-start | bytes 491528 | tf_op jit(solution)/shard_map/ppermute | solution.py:21
  4.7 17.9 %collective-permute-start.4 = (bf16[80,8,128]{2,1,0:T(8,128)(2,1)}, bf16[80,8,128]{2,1,0:T(8,128)(2,1)S(1)}, u32[]{:S(2)}, u32[]{:S(2)}) collective-permute-start(bf16[80,8,128]{2,1,0:T(8,128)(2,1)} %constant_dynamic-slice_fusion.refs_4_), channel_id=1, source_target_pairs={{0,16},{4,20},{8,24},{12,28},{16,0},{20,4},{24,8},{28,12},{1,17},{... | collective-permute-start | bytes 491528 | tf_op jit(solution)/shard_map/ppermute | solution.py:21
  5.7 27.1 %collective-permute-start.6 = (bf16[32,12,8,128]{3,2,1,0:T(8,128)(2,1)}, bf16[32,12,8,128]{3,2,1,0:T(8,128)(2,1)S(1)}, u32[]{:S(2)}, u32[]{:S(2)}) collective-permute-start(bf16[32,12,8,128]{3,2,1,0:T(8,128)(2,1)} %cot_ref.1), channel_id=1, source_target_pairs={{0,2},{1,3},{2,0},{3,1},{4,6},{5,7},{6,4},{7,5},{8,10},{9,11},{10,... | collective-permute-start | bytes 2359304 | tf_op jit(solution)/shard_map/ppermute | solution.py:285
  6.9 9.7 %collective-permute-start = (bf16[12,32,128]{2,1,0:T(8,128)(2,1)S(1)}, bf16[12,32,128]{2,1,0:T(8,128)(2,1)S(1)}, u32[]{:S(2)}, u32[]{:S(2)}) collective-permute-start(bf16[12,32,128]{2,1,0:T(8,128)(2,1)S(1)} %get-tuple-element.44), channel_id=1, source_target_pairs={{0,4},{4,8},{8,12},{12,16},{16,20},{20,24},{24,28},{28,0},{1,5},{5... | collective-permute-start | bytes 294920 | tf_op jit(solution)/shard_map/ppermute | solution.py:21
  9.7 17.0 %copy-start.3 = (bf16[32,12,8,128]{3,2,1,0:T(8,128)(2,1)S(1)}, bf16[32,12,8,128]{3,2,1,0:T(8,128)(2,1)}, u32[]{:S(2)}) copy-start(bf16[32,12,8,128]{3,2,1,0:T(8,128)(2,1)} %cot_ref.1) | copy-start | bytes 2359300
  16.6 4.8 %collective-permute-start.1 = (bf16[12,32,128]{2,1,0:T(8,128)(2,1)S(1)}, bf16[12,32,128]{2,1,0:T(8,128)(2,1)S(1)}, u32[]{:S(2)}, u32[]{:S(2)}) collective-permute-start(bf16[12,32,128]{2,1,0:T(8,128)(2,1)S(1)} %get-tuple-element.45), channel_id=1, source_target_pairs={{0,28},{4,0},{8,4},{12,8},{16,12},{20,16},{24,20},{28,24},{1,29},{... | collective-permute-start | bytes 294920 | tf_op jit(solution)/shard_map/ppermute | solution.py:21
  21.4 4.5 %collective-permute-start.8 = (bf16[80,8,128]{2,1,0:T(8,128)(2,1)}, bf16[80,8,128]{2,1,0:T(8,128)(2,1)S(1)}, u32[]{:S(2)}, u32[]{:S(2)}) collective-permute-start(bf16[80,8,128]{2,1,0:T(8,128)(2,1)} %constant_dynamic-slice_fusion.refs_4_), channel_id=1, source_target_pairs={{0,24},{4,28},{8,0},{12,4},{16,8},{20,12},{24,16},{28,20},{1,25},{... | collective-permute-start | bytes 491528 | tf_op jit(solution)/shard_map/ppermute | solution.py:21
  22.6 10.2 %collective-permute-start.7 = (bf16[2,80,8,128]{3,2,1,0:T(8,128)(2,1)S(1)}, bf16[2,80,8,128]{3,2,1,0:T(8,128)(2,1)S(1)}, u32[]{:S(2)}, u32[]{:S(2)}) collective-permute-start(bf16[2,80,8,128]{3,2,1,0:T(8,128)(2,1)S(1)} %shard_map.113), channel_id=1, source_target_pairs={{0,4},{4,0},{8,12},{12,8},{16,20},{20,16},{24,28},{28,24},{1,5},{5... | collective-permute-start | bytes 983048 | tf_op jit(solution)/shard_map/ppermute | solution.py:285
  23.2 15.6 %copy-start.4 = (bf16[80,8,128]{2,1,0:T(8,128)(2,1)S(1)}, bf16[80,8,128]{2,1,0:T(8,128)(2,1)}, u32[]{:S(2)}) copy-start(bf16[80,8,128]{2,1,0:T(8,128)(2,1)} %constant_dynamic-slice_fusion.2.refs_11_.left_ref) | copy-start | bytes 491524
  23.2 15.6 %copy-start.17 = (bf16[80,8,128]{2,1,0:T(8,128)(2,1)S(1)}, bf16[80,8,128]{2,1,0:T(8,128)(2,1)}, u32[]{:S(2)}) copy-start(bf16[80,8,128]{2,1,0:T(8,128)(2,1)} %copy-done.16) | copy-start | bytes 491524
  23.2 15.6 %copy-start.18 = (f32[32,240]{1,0:T(8,128)S(1)}, f32[32,240]{1,0:T(8,128)}, u32[]{:S(2)}) copy-start(f32[32,240]{1,0:T(8,128)} %constant.58.clone.refs_12_) | copy-start | bytes 92164
  23.3 15.5 %copy-start.13 = (bf16[80,8,128]{2,1,0:T(8,128)(2,1)S(1)}, bf16[80,8,128]{2,1,0:T(8,128)(2,1)}, u32[]{:S(2)}) copy-start(bf16[80,8,128]{2,1,0:T(8,128)(2,1)} %copy-done.12) | copy-start | bytes 491524
  23.3 15.5 %copy-start.15 = (bf16[80,8,128]{2,1,0:T(8,128)(2,1)S(1)}, bf16[80,8,128]{2,1,0:T(8,128)(2,1)}, u32[]{:S(2)}) copy-start(bf16[80,8,128]{2,1,0:T(8,128)(2,1)} %copy-done.14) | copy-start | bytes 491524
  23.3 9.5 %collective-permute-start.10 = (bf16[12,64,128]{2,1,0:T(8,128)(2,1)S(1)}, bf16[12,64,128]{2,1,0:T(8,128)(2,1)S(1)}, u32[]{:S(2)}, u32[]{:S(2)}) collective-permute-start(bf16[12,64,128]{2,1,0:T(8,128)(2,1)S(1)} %pad_maximum_fusion.halo_ref), channel_id=1, source_target_pairs={{0,2},{1,3},{2,0},{3,1},{4,6},{5,7},{6,4},{7,5},{8,10},{9,11},{10,... | collective-permute-start | bytes 589832 | tf_op jit(solution)/shard_map/ppermute | solution.py:285
  25.9 6.9 %collective-permute-start.9 = (bf16[80,8,128]{2,1,0:T(8,128)(2,1)S(1)}, bf16[80,8,128]{2,1,0:T(8,128)(2,1)S(1)}, u32[]{:S(2)}, u32[]{:S(2)}) collective-permute-start(bf16[80,8,128]{2,1,0:T(8,128)(2,1)S(1)} %collective-permute-done.8.refs_7_), channel_id=1, source_target_pairs={{0,4},{4,0},{8,12},{12,8},{16,20},{20,16},{24,28},{28,24},{1,5},{5... | collective-permute-start | bytes 491528 | tf_op jit(solution)/shard_map/ppermute | solution.py:285
  26.9 9.8 %collective-permute-start.5 = (bf16[12,320,128]{2,1,0:T(8,128)(2,1)S(1)}, bf16[12,320,128]{2,1,0:T(8,128)(2,1)S(1)}, u32[]{:S(2)}, u32[]{:S(2)}) collective-permute-start(bf16[12,320,128]{2,1,0:T(8,128)(2,1)S(1)} %shard_map.112.refs_0_), channel_id=1, source_target_pairs={{0,1},{1,0},{2,3},{3,2},{4,5},{5,4},{6,7},{7,6},{8,9},{9,8},{10,11... | collective-permute-start | bytes 2949128 | tf_op jit(solution)/shard_map/ppermute | solution.py:285
  33.1 5.7 %collective-permute-start.11 = (bf16[12,320,128]{2,1,0:T(8,128)(2,1)S(1)}, bf16[12,320,128]{2,1,0:T(8,128)(2,1)S(1)}, u32[]{:S(2)}, u32[]{:S(2)}) collective-permute-start(bf16[12,320,128]{2,1,0:T(8,128)(2,1)S(1)} %shard_map.114.refs_2_), channel_id=1, source_target_pairs={{0,1},{1,0},{2,3},{3,2},{4,5},{5,4},{6,7},{7,6},{8,9},{9,8},{10,11... | collective-permute-start | bytes 2949128 | tf_op jit(solution)/shard_map/ppermute | solution.py:285
  47.6 9.2 %copy-start.1 = (bf16[50,320,128]{2,1,0:T(8,128)(2,1)}, bf16[50,320,128]{2,1,0:T(8,128)(2,1)S(1)}, u32[]{:S(2)}) copy-start(bf16[50,320,128]{2,1,0:T(8,128)(2,1)S(1)} %get-tuple-element.58.cot_s) | copy-start | bytes 12288004
  47.6 5.3 %collective-permute-start.12 = (f32[3,32,96]{2,1,0:T(8,128)S(1)}, f32[3,32,96]{2,1,0:T(8,128)S(1)}, u32[]{:S(2)}, u32[]{:S(2)}) collective-permute-start(f32[3,32,96]{2,1,0:T(8,128)S(1)} %get-tuple-element.64), channel_id=1, source_target_pairs={{0,16},{4,20},{8,24},{12,28},{16,0},{20,4},{24,8},{28,12},{1,17},{... | collective-permute-start | bytes 110600 | tf_op jit(solution)/shard_map/ppermute | solution.py:285
  52.9 20.5 %collective-permute-start.17 = (bf16[80,8,128]{2,1,0:T(8,128)(2,1)S(1)}, bf16[80,8,128]{2,1,0:T(8,128)(2,1)S(1)}, u32[]{:S(2)}, u32[]{:S(2)}) collective-permute-start(bf16[80,8,128]{2,1,0:T(8,128)(2,1)S(1)} %get-tuple-element.77), channel_id=1, source_target_pairs={{0,8},{4,12},{8,16},{12,20},{16,24},{20,28},{24,0},{28,4},{1,9},{5... | collective-permute-start | bytes 491528 | tf_op jit(solution)/shard_map/ppermute | solution.py:21
  53.0 20.7 %collective-permute-start.18 = (bf16[80,8,128]{2,1,0:T(8,128)(2,1)S(1)}, bf16[80,8,128]{2,1,0:T(8,128)(2,1)S(1)}, u32[]{:S(2)}, u32[]{:S(2)}) collective-permute-start(bf16[80,8,128]{2,1,0:T(8,128)(2,1)S(1)} %get-tuple-element.78), channel_id=1, source_target_pairs={{0,12},{4,16},{8,20},{12,24},{16,28},{20,0},{24,4},{28,8},{1,13},{... | collective-permute-start | bytes 491528 | tf_op jit(solution)/shard_map/ppermute | solution.py:21
  55.4 10.1 %collective-permute-start.13 = (f32[3,32,96]{2,1,0:T(8,128)S(1)}, f32[3,32,96]{2,1,0:T(8,128)S(1)}, u32[]{:S(2)}, u32[]{:S(2)}) collective-permute-start(f32[3,32,96]{2,1,0:T(8,128)S(1)} %add.64), channel_id=1, source_target_pairs={{0,8},{4,12},{8,0},{12,4},{16,24},{20,28},{24,16},{28,20},{1,9},{5... | collective-permute-start | bytes 110600 | tf_op jit(solution)/shard_map/ppermute | solution.py:285
  63.4 19.3 %collective-permute-start.14 = (bf16[80,8,128]{2,1,0:T(8,128)(2,1)}, bf16[80,8,128]{2,1,0:T(8,128)(2,1)}, u32[]{:S(2)}, u32[]{:S(2)}) collective-permute-start(bf16[80,8,128]{2,1,0:T(8,128)(2,1)} %get-tuple-element.73), channel_id=1, source_target_pairs={{0,16},{4,20},{8,24},{12,28},{16,0},{20,4},{24,8},{28,12},{1,17},{... | collective-permute-start | bytes 491528 | tf_op jit(solution)/shard_map/ppermute | solution.py:21
  63.5 19.1 %collective-permute-start.15 = (bf16[80,8,128]{2,1,0:T(8,128)(2,1)}, bf16[80,8,128]{2,1,0:T(8,128)(2,1)}, u32[]{:S(2)}, u32[]{:S(2)}) collective-permute-start(bf16[80,8,128]{2,1,0:T(8,128)(2,1)} %get-tuple-element.74), channel_id=1, source_target_pairs={{0,20},{4,24},{8,28},{12,0},{16,4},{20,8},{24,12},{28,16},{1,21},{... | collective-permute-start | bytes 491528 | tf_op jit(solution)/shard_map/ppermute | solution.py:21
  65.5 3.0 %collective-permute-start.20 = (f32[3,32,96]{2,1,0:T(8,128)S(1)}, f32[3,32,96]{2,1,0:T(8,128)S(1)}, u32[]{:S(2)}, u32[]{:S(2)}) collective-permute-start(f32[3,32,96]{2,1,0:T(8,128)S(1)} %add.65), channel_id=1, source_target_pairs={{0,4},{4,0},{8,12},{12,8},{16,20},{20,16},{24,28},{28,24},{1,5},{5... | collective-permute-start | bytes 110600 | tf_op jit(solution)/shard_map/ppermute | solution.py:285
  68.5 15.6 %collective-permute-start.23 = (f32[3,32,96]{2,1,0:T(8,128)S(1)}, f32[3,32,96]{2,1,0:T(8,128)S(1)}, u32[]{:S(2)}, u32[]{:S(2)}) collective-permute-start(f32[3,32,96]{2,1,0:T(8,128)S(1)} %add.78), channel_id=1, source_target_pairs={{0,3},{1,2},{2,1},{3,0},{4,7},{5,6},{6,5},{7,4},{8,11},{9,10},{10,... | collective-permute-start | bytes 110600 | tf_op jit(solution)/shard_map/ppermute | solution.py:285
  73.4 10.8 %collective-permute-start.22 = (f32[3,32,96]{2,1,0:T(8,128)S(1)}, f32[3,32,96]{2,1,0:T(8,128)}, u32[]{:S(2)}, u32[]{:S(2)}) collective-permute-start(f32[3,32,96]{2,1,0:T(8,128)S(1)} %add.78), channel_id=1, source_target_pairs={{0,2},{1,3},{2,0},{3,1},{4,6},{5,7},{6,4},{7,5},{8,10},{9,11},{10,... | collective-permute-start | bytes 110600 | tf_op jit(solution)/shard_map/ppermute | solution.py:285
  74.1 10.1 %collective-permute-start.21 = (f32[3,32,96]{2,1,0:T(8,128)S(1)}, f32[3,32,96]{2,1,0:T(8,128)}, u32[]{:S(2)}, u32[]{:S(2)}) collective-permute-start(f32[3,32,96]{2,1,0:T(8,128)S(1)} %add.78), channel_id=1, source_target_pairs={{0,1},{1,0},{2,3},{3,2},{4,5},{5,4},{6,7},{7,6},{8,9},{9,8},{10,11... | collective-permute-start | bytes 110600 | tf_op jit(solution)/shard_map/ppermute | solution.py:285
  82.7 6.1 %collective-permute-start.19 = (bf16[80,8,128]{2,1,0:T(8,128)(2,1)}, bf16[80,8,128]{2,1,0:T(8,128)(2,1)S(1)}, u32[]{:S(2)}, u32[]{:S(2)}) collective-permute-start(bf16[80,8,128]{2,1,0:T(8,128)(2,1)} %get-tuple-element.79), channel_id=1, source_target_pairs={{0,24},{4,28},{8,0},{12,4},{16,8},{20,12},{24,16},{28,20},{1,25},{... | collective-permute-start | bytes 491528 | tf_op jit(solution)/shard_map/ppermute | solution.py:21
  83.0 9.9 %collective-permute-start.16 = (bf16[80,8,128]{2,1,0:T(8,128)(2,1)}, bf16[80,8,128]{2,1,0:T(8,128)(2,1)S(1)}, u32[]{:S(2)}, u32[]{:S(2)}) collective-permute-start(bf16[80,8,128]{2,1,0:T(8,128)(2,1)} %get-tuple-element.75), channel_id=1, source_target_pairs={{0,28},{4,0},{8,4},{12,8},{16,12},{20,16},{24,20},{28,24},{1,29},{... | collective-permute-start | bytes 491528 | tf_op jit(solution)/shard_map/ppermute | solution.py:21
  (19 other events, 60.4 us)

commit v14 on v13

--- a/solution.py
+++ b/solution.py
@@ -382,7 +382,6 @@
     arrived = {
         hop: shifted(value, "col", -hop) for hop, value in zip(range(hops, near, -1), sent)
     }
-    middle = near - 1
 
     def lower(first_level, count, done, kind, left_part, grad_part):
         skipped = (far + done) * width
@@ -407,24 +406,16 @@
             8, 1000000,
         )
 
-    left_part, grad_part, *sent = lower(
-        width, reach - (far + 1) * width, 0, f32, left_part, grad_part
-    )
+    grad_left, own, *sent = lower(0, reach - far * width, 0, bf16, left_part, grad_part)
     total = total_swapping(total, bits[1])
-    grad_part, total = lax.optimization_barrier((grad_part, total))
-    grad_left, own, *last = lower(0, width, middle, bf16, left_part, grad_part)
+    own, total = lax.optimization_barrier((own, total))
+    sent[2:], arrived[hops], arrived[hops - 1] = lax.optimization_barrier(
+        (sent[2:], arrived[hops], arrived[hops - 1])
+    )
+    for hop, value in zip(range(near, 0, -1), sent):
+        arrived[hop] = shifted(value, "col", -hop)
     for bit in bits[2:]:
         total = total_swapping(total, bit)
-    for hop, value in zip(range(near, 2, -1), sent):
-        arrived[hop] = shifted(value, "col", -hop)
-    waiting, arrived[hops], arrived[hops - 1] = lax.optimization_barrier(
-        (sent[-1], arrived[hops], arrived[hops - 1])
-    )
-    arrived[2] = shifted(waiting, "col", -2)
-    waiting, arrived[4], arrived[3] = lax.optimization_barrier(
-        (last[0], arrived[4], arrived[3])
-    )
-    arrived[1] = shifted(waiting, "col", -1)
 
     total_right = own
     for hop in range(1, hops + 1):

time: 96.4 us -> 96.5 us (level); the launches traced: 94.8 us -> 96.3 us
  waiting for transfers between devices: 19.5 us -> 33.1 us
  local copies, waits for them, and re-layouts: 18.8 us -> 8.57 us
  starting transfers between devices: 31.6 us -> 29.5 us
  other arithmetic: 4.4 us -> 5.53 us
    ppermute x11, waiting for transfers between devices: 13.9 us -> 26.7 us  [shifted(): lax.ppermute(value, axis, [(source, (source + steps) % count) for source...]
    unnamed x55 -> x19, local copies, waits for them, and re-layouts: 10.8 us -> 1.03 us
    ppermute x13, starting transfers between devices: 21.4 us -> 19 us  [swapped(): lax.ppermute(value, axis, [(source, source ^ bit) for source in range(cou...]
    pallas_call x7 -> x6, Pallas kernels: 19.2 us -> 18.3 us  [run(): pl.pallas_call(function, out_shape=[jax.ShapeDtypeStruct(shape, kind) for...]
  transfers between devices with their start and end apart: 24 -> 24, of which waited for: 8 -> 10; matrix products, arithmetic and copies ran while one was open for 10% -> 10% of each run, Pallas kernels for 11% -> 10%
where the time goes in v14:
time: 96.5 us; the launch traced here: 96.3 us
  waiting for transfers between devices  33.1 us (34%)
  starting transfers between devices  29.5 us (31%)
  Pallas kernels  18.3 us (19%)
  local copies, waits for them, and re-layouts  8.57 us (9%)
  other arithmetic  5.53 us (6%)
  between operations  1 us (1%)
    ppermute x11, waiting for transfers between devices, shifted(): lax.ppermute(value, axis, [(source, (source + steps) % count) for source...  26.7 us
    ppermute x13, starting transfers between devices, swapped(): lax.ppermute(value, axis, [(source, source ^ bit) for source in range(cou...  19 us
    pallas_call x6, Pallas kernels, run(): pl.pallas_call(function, out_shape=[jax.ShapeDtypeStruct(shape, kind) for...  18.3 us
    ppermute x11, starting transfers between devices, shifted(): lax.ppermute(value, axis, [(source, (source + steps) % count) for source...  10.5 us
    ppermute x13, waiting for transfers between devices, swapped(): lax.ppermute(value, axis, [(source, source ^ bit) for source in range(cou...  6.34 us
    convert_element_type x1, other arithmetic, body(): return (grad_left, total_right.astype(bf16), grad_kernel)  2.03 us
  transfers between devices with their start and end apart: 24, of which 10 were waited for; matrix products, arithmetic and copies ran while one was open for 10% of the time, Pallas kernels for 10%

profile of v14, /device:TPU:13, one launch (start us, length us, event | category | flops | bytes accessed | tf_op | source)
XLA Modules:
  0.0 96.3 jit_solution(15995253373623766069)
XLA Ops:
  0.7 1.9 %fusion.2 = (bf16[32,12,1,128]{3,2,1,0:T(2,128)(2,1)S(1)}, bf16[32,12,1,128]{3,2,1,0:T(2,128)(2,1)S(1)}) fusion(bf16[32,12,8,128]{3,2,1,0:T(8,128)(2,1)} %cot_ref.1), kind=kLoop, calls=%fused_computation.24 | loop fusion | bytes 393216 | tf_op jit(solution)/shard_map/slice | solution.py:318
  3.6 1.3 %collective-permute-start.3 = (bf16[80,8,128]{2,1,0:T(8,128)(2,1)S(1)}, bf16[80,8,128]{2,1,0:T(8,128)(2,1)S(1)}, u32[]{:S(2)}, u32[]{:S(2)}) collective-permute-start(bf16[80,8,128]{2,1,0:T(8,128)(2,1)S(1)} %constant_dynamic-slice_fusion.refs_4_), channel_id=1, source_target_pairs={{0,8},{4,12},{8,16},{12,20},{16,24},{20,28},{24,0},{28,4},{1,9},{5... | collective-permute-start | bytes 491528 | tf_op jit(solution)/shard_map/ppermute | solution.py:21
  4.9 1.0 %collective-permute-start.4 = (bf16[80,8,128]{2,1,0:T(8,128)(2,1)S(1)}, bf16[80,8,128]{2,1,0:T(8,128)(2,1)S(1)}, u32[]{:S(2)}, u32[]{:S(2)}) collective-permute-start(bf16[80,8,128]{2,1,0:T(8,128)(2,1)S(1)} %constant_dynamic-slice_fusion.refs_4_), channel_id=1, source_target_pairs={{0,16},{4,20},{8,24},{12,28},{16,0},{20,4},{24,8},{28,12},{1,17},{... | collective-permute-start | bytes 491528 | tf_op jit(solution)/shard_map/ppermute | solution.py:21
  5.9 1.2 %collective-permute-start.6 = (bf16[32,12,8,128]{3,2,1,0:T(8,128)(2,1)}, bf16[32,12,8,128]{3,2,1,0:T(8,128)(2,1)S(1)}, u32[]{:S(2)}, u32[]{:S(2)}) collective-permute-start(bf16[32,12,8,128]{3,2,1,0:T(8,128)(2,1)} %cot_ref.1), channel_id=1, source_target_pairs={{0,2},{1,3},{2,0},{3,1},{4,6},{5,7},{6,4},{7,5},{8,10},{9,11},{10,... | collective-permute-start | bytes 2359304 | tf_op jit(solution)/shard_map/ppermute | solution.py:285
  7.1 1.3 %collective-permute-start = (bf16[12,32,128]{2,1,0:T(8,128)(2,1)}, bf16[12,32,128]{2,1,0:T(8,128)(2,1)}, u32[]{:S(2)}, u32[]{:S(2)}) collective-permute-start(bf16[12,32,128]{2,1,0:T(8,128)(2,1)} %get-tuple-element.40), channel_id=1, source_target_pairs={{0,4},{4,8},{8,12},{12,16},{16,20},{20,24},{24,28},{28,0},{1,5},{5... | collective-permute-start | bytes 294920 | tf_op jit(solution)/shard_map/ppermute | solution.py:21
  8.4 1.1 %constant_dynamic-slice_fusion.1 = bf16[3,3,3,32,10]{4,3,2,1,0:T(8,128)(2,1)S(1)} fusion(bf16[3,3,3,32,40]{4,3,2,1,0:T(8,128)(2,1)} %param.11, s32[]{:T(128)S(6)} %select_n.88), kind=kLoop, calls=%fused_computation.20 | loop fusion | bytes 34564 | tf_op jit(solution)/shard_map/dynamic_slice | solution.py:324
  10.0 1.4 %select_select_fusion = bf16[3,10,8,3,320]{4,3,2,1,0:T(4,128)(2,1)} fusion(pred[8,320]{1,0:T(8,128)(4,1)S(1)} %copy-done.6, pred[8,320]{1,0:T(8,128)(4,1)S(1)} %copy-done.7, pred[8,320]{1,0:T(8,128)(4,1)S(1)} %copy-done.8, bf16[3,10,3,320]{3,2,1,0:T(4,128)(2,1)S(1)} %copy.33, bf16[3,10,3,320]{3,2,1,0:T(4,128)(2,1)S(1)} %copy.32, ...), kind=kLoop, calls=%fused_computation.2 | loop fusion | flops 691200 | bytes 641280 | tf_op jit(solution)/shard_map/jit(_where)/select_n | solution.py:45
  11.4 5.2 %collective-permute-done = bf16[12,32,128]{2,1,0:T(8,128)(2,1)} collective-permute-done((bf16[12,32,128]{2,1,0:T(8,128)(2,1)}, bf16[12,32,128]{2,1,0:T(8,128)(2,1)}, u32[]{:S(2)}, u32[]{:S(2)}) %collective-permute-start) | collective-permute-done | bytes 98336 | tf_op jit(solution)/shard_map/ppermute | solution.py:21
  16.7 0.9 constant_dynamic-slice_fusion.2.refs_11_.left_ref
  17.6 1.7 %select_n.92.weight_ref = bf16[240,960]{1,0:T(8,128)(2,1)S(1)} reshape(bf16[3,10,8,3,320]{4,3,2,1,0:T(4,128)(2,1)} %select_select_fusion) | data formatting | bytes 921600 | tf_op jit(solution)/shard_map/jit(_where)/select_n | solution.py:45
  19.3 2.5 %collective-permute-done.1 = bf16[12,32,128]{2,1,0:T(8,128)(2,1)} collective-permute-done((bf16[12,32,128]{2,1,0:T(8,128)(2,1)}, bf16[12,32,128]{2,1,0:T(8,128)(2,1)}, u32[]{:S(2)}, u32[]{:S(2)}) %collective-permute-start.1) | collective-permute-done | bytes 98336 | tf_op jit(solution)/shard_map/ppermute | solution.py:21
  22.0 0.9 broadcast_select_fusion
  23.0 0.9 broadcast_select_fusion.1
  23.9 1.3 %collective-permute-start.10 = (bf16[12,64,128]{2,1,0:T(8,128)(2,1)S(1)}, bf16[12,64,128]{2,1,0:T(8,128)(2,1)S(1)}, u32[]{:S(2)}, u32[]{:S(2)}) collective-permute-start(bf16[12,64,128]{2,1,0:T(8,128)(2,1)S(1)} %pad_maximum_fusion.halo_ref), channel_id=1, source_target_pairs={{0,2},{1,3},{2,0},{3,1},{4,6},{5,7},{6,4},{7,5},{8,10},{9,11},{10,... | collective-permute-start | bytes 589832 | tf_op jit(solution)/shard_map/ppermute | solution.py:285
  26.9 4.0 %collective-permute-start.5 = (bf16[12,320,128]{2,1,0:T(8,128)(2,1)S(1)}, bf16[12,320,128]{2,1,0:T(8,128)(2,1)S(1)}, u32[]{:S(2)}, u32[]{:S(2)}) collective-permute-start(bf16[12,320,128]{2,1,0:T(8,128)(2,1)S(1)} %shard_map.112.refs_0_), channel_id=1, source_target_pairs={{0,1},{1,0},{2,3},{3,2},{4,5},{5,4},{6,7},{7,6},{8,9},{9,8},{10,11... | collective-permute-start | bytes 2949128 | tf_op jit(solution)/shard_map/ppermute | solution.py:285
  31.0 1.1 %collective-permute-done.9.refs_10_ = bf16[80,8,128]{2,1,0:T(8,128)(2,1)S(1)} collective-permute-done((bf16[80,8,128]{2,1,0:T(8,128)(2,1)S(1)}, bf16[80,8,128]{2,1,0:T(8,128)(2,1)S(1)}, u32[]{:S(2)}, u32[]{:S(2)}) %collective-permute-start.9) | collective-permute-done | bytes 163872 | tf_op jit(solution)/shard_map/ppermute | solution.py:285
  32.3 3.6 %collective-permute-start.11 = (bf16[12,320,128]{2,1,0:T(8,128)(2,1)S(1)}, bf16[12,320,128]{2,1,0:T(8,128)(2,1)S(1)}, u32[]{:S(2)}, u32[]{:S(2)}) collective-permute-start(bf16[12,320,128]{2,1,0:T(8,128)(2,1)S(1)} %shard_map.114.refs_2_), channel_id=1, source_target_pairs={{0,1},{1,0},{2,3},{3,2},{4,5},{5,4},{6,7},{7,6},{8,9},{9,8},{10,11... | collective-permute-start | bytes 2949128 | tf_op jit(solution)/shard_map/ppermute | solution.py:285
  36.0 2.1 %collective-permute-done.11.refs_3_ = bf16[12,320,128]{2,1,0:T(8,128)(2,1)S(1)} collective-permute-done((bf16[12,320,128]{2,1,0:T(8,128)(2,1)S(1)}, bf16[12,320,128]{2,1,0:T(8,128)(2,1)S(1)}, u32[]{:S(2)}, u32[]{:S(2)}) %collective-permute-start.11) | collective-permute-done | bytes 983072 | tf_op jit(solution)/shard_map/ppermute | solution.py:285
  38.1 8.5 %shard_map.115 = (bf16[50,320,128]{2,1,0:T(8,128)(2,1)S(1)}, f32[80,56,128]{2,1,0:T(8,128)S(1)}, f32[3,32,96]{2,1,0:T(8,128)S(1)}) custom-call(s32[2]{0:T(128)S(1)} %pad_add_fusion.places, bf16[12,320,128]{2,1,0:T(8,128)(2,1)S(1)} %shard_map.112.refs_0_, bf16[12,320,128]{2,1,0:T(8,128)(2,1)S(1)} %collective-permute-done.5.refs_1_, ...), custom_call_target="tpu_custom_call" | custom-call | flops 8000000000 | bytes 1024 | tf_op jit(solution)/shard_map/pallas_call | solution.py:272
  46.7 1.8 %collective-permute-start.12 = (f32[3,32,96]{2,1,0:T(8,128)S(1)}, f32[3,32,96]{2,1,0:T(8,128)S(1)}, u32[]{:S(2)}, u32[]{:S(2)}) collective-permute-start(f32[3,32,96]{2,1,0:T(8,128)S(1)} %get-tuple-element.60), channel_id=1, source_target_pairs={{0,16},{4,20},{8,24},{12,28},{16,0},{20,4},{24,8},{28,12},{1,17},{... | collective-permute-start | bytes 110600 | tf_op jit(solution)/shard_map/ppermute | solution.py:285
  48.5 2.9 %shard_map.116 = (f32[80,8,128]{2,1,0:T(8,128)S(1)}, f32[80,40,128]{2,1,0:T(8,128)S(1)}, bf16[80,8,128]{2,1,0:T(8,128)(2,1)S(1)}, bf16[80,8,128]{2,1,0:T(8,128)(2,1)S(1)}) custom-call(bf16[80,8,128]{2,1,0:T(8,128)(2,1)S(1)} %constant_dynamic-slice_fusion.2.refs_11_.left_ref, bf16[240,960]{1,0:T(8,128)(2,1)S(1)} %select_n.92.weight_ref, ...), custom_call_target="tpu_custom_call" | custom-call | flops 8000000000 | bytes 1024 | tf_op jit(solution)/shard_map/pallas_call | solution.py:272
  51.4 1.6 %collective-permute-start.13 = (f32[3,32,96]{2,1,0:T(8,128)S(1)}, f32[3,32,96]{2,1,0:T(8,128)S(1)}, u32[]{:S(2)}, u32[]{:S(2)}) collective-permute-start(f32[3,32,96]{2,1,0:T(8,128)S(1)} %add.64), channel_id=1, source_target_pairs={{0,8},{4,12},{8,0},{12,4},{16,24},{20,28},{24,16},{28,20},{1,9},{5... | collective-permute-start | bytes 110600 | tf_op jit(solution)/shard_map/ppermute | solution.py:285
  53.0 3.0 %collective-permute-start.15 = (bf16[80,8,128]{2,1,0:T(8,128)(2,1)S(1)}, bf16[80,8,128]{2,1,0:T(8,128)(2,1)S(1)}, u32[]{:S(2)}, u32[]{:S(2)}) collective-permute-start(bf16[80,8,128]{2,1,0:T(8,128)(2,1)S(1)} %get-tuple-element.69), channel_id=1, source_target_pairs={{0,12},{4,16},{8,20},{12,24},{16,28},{20,0},{24,4},{28,8},{1,13},{... | collective-permute-start | bytes 491528 | tf_op jit(solution)/shard_map/ppermute | solution.py:21
  56.0 6.4 %shard_map.117 = (bf16[80,8,128]{2,1,0:T(8,128)(2,1)}, f32[80,8,128]{2,1,0:T(8,128)S(1)}, bf16[80,8,128]{2,1,0:T(8,128)(2,1)S(1)}, bf16[80,8,128]{2,1,0:T(8,128)...) custom-call(bf16[80,8,128]{2,1,0:T(8,128)(2,1)S(1)} %constant_dynamic-slice_fusion.2.refs_11_.left_ref, ...), custom_call_target="tpu_custom_call" | custom-call | flops 1000000 | bytes 1024 | tf_op jit(solution)/shard_map/pallas_call | solution.py:272
  62.5 2.9 %collective-permute-done.20 = f32[3,32,96]{2,1,0:T(8,128)S(1)} collective-permute-done((f32[3,32,96]{2,1,0:T(8,128)S(1)}, f32[3,32,96]{2,1,0:T(8,128)S(1)}, u32[]{:S(2)}, u32[]{:S(2)}) %collective-permute-start.20) | collective-permute-done | bytes 36896 | tf_op jit(solution)/shard_map/ppermute | solution.py:285
  65.4 3.8 %collective-permute-start.23 = (f32[3,32,96]{2,1,0:T(8,128)S(1)}, f32[3,32,96]{2,1,0:T(8,128)S(1)}, u32[]{:S(2)}, u32[]{:S(2)}) collective-permute-start(f32[3,32,96]{2,1,0:T(8,128)S(1)} %add.78), channel_id=1, source_target_pairs={{0,3},{1,2},{2,1},{3,0},{4,7},{5,6},{6,5},{7,4},{8,11},{9,10},{10,... | collective-permute-start | bytes 110600 | tf_op jit(solution)/shard_map/ppermute | solution.py:285
  69.7 1.5 %collective-permute-start.19 = (bf16[80,8,128]{2,1,0:T(8,128)(2,1)S(1)}, bf16[80,8,128]{2,1,0:T(8,128)(2,1)}, u32[]{:S(2)}, u32[]{:S(2)}) collective-permute-start(bf16[80,8,128]{2,1,0:T(8,128)(2,1)S(1)} %get-tuple-element.73), channel_id=1, source_target_pairs={{0,16},{4,20},{8,24},{12,28},{16,0},{20,4},{24,8},{28,12},{1,17},{... | collective-permute-start | bytes 491528 | tf_op jit(solution)/shard_map/ppermute | solution.py:21
  71.7 1.4 %collective-permute-start.17 = (bf16[80,8,128]{2,1,0:T(8,128)(2,1)S(1)}, bf16[80,8,128]{2,1,0:T(8,128)(2,1)}, u32[]{:S(2)}, u32[]{:S(2)}) collective-permute-start(bf16[80,8,128]{2,1,0:T(8,128)(2,1)S(1)} %get-tuple-element.71), channel_id=1, source_target_pairs={{0,24},{4,28},{8,0},{12,4},{16,8},{20,12},{24,16},{28,20},{1,25},{... | collective-permute-start | bytes 491528 | tf_op jit(solution)/shard_map/ppermute | solution.py:21
  75.1 1.0 %copy.37 = f32[3,3,3,32,40]{4,3,2,1,0:T(8,128)} copy(f32[3,3,3,32,40]{3,4,2,1,0:T(8,128)S(1)} %mul.20) | data formatting | bytes 276480
  76.1 8.7 %collective-permute-done.19 = bf16[80,8,128]{2,1,0:T(8,128)(2,1)} collective-permute-done((bf16[80,8,128]{2,1,0:T(8,128)(2,1)S(1)}, bf16[80,8,128]{2,1,0:T(8,128)(2,1)}, u32[]{:S(2)}, u32[]{:S(2)}) %collective-permute-start.19) | collective-permute-done | bytes 163872 | tf_op jit(solution)/shard_map/ppermute | solution.py:21
  85.7 8.6 %collective-permute-done.16 = bf16[80,8,128]{2,1,0:T(8,128)(2,1)} collective-permute-done((bf16[80,8,128]{2,1,0:T(8,128)(2,1)S(1)}, bf16[80,8,128]{2,1,0:T(8,128)(2,1)}, u32[]{:S(2)}, u32[]{:S(2)}) %collective-permute-start.16) | collective-permute-done | bytes 163872 | tf_op jit(solution)/shard_map/ppermute | solution.py:21
  94.2 2.0 %add_convert_fusion = bf16[80,8,128]{2,1,0:T(8,128)(2,1)} fusion(bf16[80,8,128]{2,1,0:T(8,128)(2,1)S(1)} %collective-permute-done.14, bf16[80,8,128]{2,1,0:T(8,128)(2,1)S(1)} %copy-done.4, bf16[80,8,128]{2,1,0:T(8,128)(2,1)} %collective-permute-done.19, bf16[80,8,128]{2,1,0:T(8,128)(2,1)} %collective-permute-done.18, ...), kind=kLoop, calls=%fused_computation.5 | loop fusion | flops 1556480 | bytes 1474566 | tf_op jit(solution)/shard_map/convert_element_type | solution.py:432
  (71 shorter events, 7.7 us)
Async XLA Ops:
  0.6 8.8 %copy-start.5 = (bf16[32,320,1,1,1]{1,0,4,3,2:T(8,128)(2,1)S(1)}, bf16[32,320,1,1,1]{1,0,4,3,2:T(8,128)(2,1)}, u32[]{:S(2)}) copy-start(bf16[32,320,1,1,1]{1,0,4,3,2:T(8,128)(2,1)} %constant.59) | copy-start | bytes 61444
  0.7 9.3 %copy-start.6 = (pred[8,320]{1,0:T(8,128)(4,1)S(1)}, pred[8,320]{1,0:T(8,128)(4,1)}, u32[]{:S(2)}) copy-start(pred[8,320]{1,0:T(8,128)(4,1)} %constant.55.clone) | copy-start | bytes 7684
  0.7 9.3 %copy-start.7 = (pred[8,320]{1,0:T(8,128)(4,1)S(1)}, pred[8,320]{1,0:T(8,128)(4,1)}, u32[]{:S(2)}) copy-start(pred[8,320]{1,0:T(8,128)(4,1)} %constant.56.clone) | copy-start | bytes 7684
  0.7 9.3 %copy-start.8 = (pred[8,320]{1,0:T(8,128)(4,1)S(1)}, pred[8,320]{1,0:T(8,128)(4,1)}, u32[]{:S(2)}) copy-start(pred[8,320]{1,0:T(8,128)(4,1)} %constant.57.clone) | copy-start | bytes 7684
  3.3 18.6 %collective-permute-start.2 = (bf16[80,8,128]{2,1,0:T(8,128)(2,1)S(1)}, bf16[80,8,128]{2,1,0:T(8,128)(2,1)S(1)}, u32[]{:S(2)}, u32[]{:S(2)}) collective-permute-start(bf16[80,8,128]{2,1,0:T(8,128)(2,1)S(1)} %constant_dynamic-slice_fusion.refs_4_), channel_id=1, source_target_pairs={{0,4},{4,0},{8,12},{12,8},{16,20},{20,16},{24,28},{28,24},{1,5},{5... | collective-permute-start | bytes 491528 | tf_op jit(solution)/shard_map/ppermute | solution.py:285
  3.6 18.3 %collective-permute-start.3 = (bf16[80,8,128]{2,1,0:T(8,128)(2,1)S(1)}, bf16[80,8,128]{2,1,0:T(8,128)(2,1)S(1)}, u32[]{:S(2)}, u32[]{:S(2)}) collective-permute-start(bf16[80,8,128]{2,1,0:T(8,128)(2,1)S(1)} %constant_dynamic-slice_fusion.refs_4_), channel_id=1, source_target_pairs={{0,8},{4,12},{8,16},{12,20},{16,24},{20,28},{24,0},{28,4},{1,9},{5... | collective-permute-start | bytes 491528 | tf_op jit(solution)/shard_map/ppermute | solution.py:21
  4.9 17.0 %collective-permute-start.4 = (bf16[80,8,128]{2,1,0:T(8,128)(2,1)S(1)}, bf16[80,8,128]{2,1,0:T(8,128)(2,1)S(1)}, u32[]{:S(2)}, u32[]{:S(2)}) collective-permute-start(bf16[80,8,128]{2,1,0:T(8,128)(2,1)S(1)} %constant_dynamic-slice_fusion.refs_4_), channel_id=1, source_target_pairs={{0,16},{4,20},{8,24},{12,28},{16,0},{20,4},{24,8},{28,12},{1,17},{... | collective-permute-start | bytes 491528 | tf_op jit(solution)/shard_map/ppermute | solution.py:21
  5.9 26.2 %collective-permute-start.6 = (bf16[32,12,8,128]{3,2,1,0:T(8,128)(2,1)}, bf16[32,12,8,128]{3,2,1,0:T(8,128)(2,1)S(1)}, u32[]{:S(2)}, u32[]{:S(2)}) collective-permute-start(bf16[32,12,8,128]{3,2,1,0:T(8,128)(2,1)} %cot_ref.1), channel_id=1, source_target_pairs={{0,2},{1,3},{2,0},{3,1},{4,6},{5,7},{6,4},{7,5},{8,10},{9,11},{10,... | collective-permute-start | bytes 2359304 | tf_op jit(solution)/shard_map/ppermute | solution.py:285
  7.1 9.6 %collective-permute-start = (bf16[12,32,128]{2,1,0:T(8,128)(2,1)}, bf16[12,32,128]{2,1,0:T(8,128)(2,1)}, u32[]{:S(2)}, u32[]{:S(2)}) collective-permute-start(bf16[12,32,128]{2,1,0:T(8,128)(2,1)} %get-tuple-element.40), channel_id=1, source_target_pairs={{0,4},{4,8},{8,12},{12,16},{16,20},{20,24},{24,28},{28,0},{1,5},{5... | collective-permute-start | bytes 294920 | tf_op jit(solution)/shard_map/ppermute | solution.py:21
  9.8 16.9 %copy-start.1 = (bf16[32,12,8,128]{3,2,1,0:T(8,128)(2,1)S(1)}, bf16[32,12,8,128]{3,2,1,0:T(8,128)(2,1)}, u32[]{:S(2)}) copy-start(bf16[32,12,8,128]{3,2,1,0:T(8,128)(2,1)} %cot_ref.1) | copy-start | bytes 2359300
  16.7 5.1 %collective-permute-start.1 = (bf16[12,32,128]{2,1,0:T(8,128)(2,1)}, bf16[12,32,128]{2,1,0:T(8,128)(2,1)}, u32[]{:S(2)}, u32[]{:S(2)}) collective-permute-start(bf16[12,32,128]{2,1,0:T(8,128)(2,1)} %get-tuple-element.41), channel_id=1, source_target_pairs={{0,28},{4,0},{8,4},{12,8},{16,12},{20,16},{24,20},{28,24},{1,29},{... | collective-permute-start | bytes 294920 | tf_op jit(solution)/shard_map/ppermute | solution.py:21
  21.8 4.2 %collective-permute-start.8 = (bf16[80,8,128]{2,1,0:T(8,128)(2,1)S(1)}, bf16[80,8,128]{2,1,0:T(8,128)(2,1)S(1)}, u32[]{:S(2)}, u32[]{:S(2)}) collective-permute-start(bf16[80,8,128]{2,1,0:T(8,128)(2,1)S(1)} %constant_dynamic-slice_fusion.refs_4_), channel_id=1, source_target_pairs={{0,24},{4,28},{8,0},{12,4},{16,8},{20,12},{24,16},{28,20},{1,25},{... | collective-permute-start | bytes 491528 | tf_op jit(solution)/shard_map/ppermute | solution.py:21
  21.9 10.2 %collective-permute-start.7 = (bf16[2,80,8,128]{3,2,1,0:T(8,128)(2,1)S(1)}, bf16[2,80,8,128]{3,2,1,0:T(8,128)(2,1)S(1)}, u32[]{:S(2)}, u32[]{:S(2)}) collective-permute-start(bf16[2,80,8,128]{3,2,1,0:T(8,128)(2,1)S(1)} %shard_map.113), channel_id=1, source_target_pairs={{0,4},{4,0},{8,12},{12,8},{16,20},{20,16},{24,28},{28,24},{1,5},{5... | collective-permute-start | bytes 983048 | tf_op jit(solution)/shard_map/ppermute | solution.py:285
  22.9 15.2 %copy-start.2 = (f32[32,240]{1,0:T(8,128)S(1)}, f32[32,240]{1,0:T(8,128)}, u32[]{:S(2)}) copy-start(f32[32,240]{1,0:T(8,128)} %constant.58.clone.refs_12_) | copy-start | bytes 92164
  23.9 8.2 %collective-permute-start.10 = (bf16[12,64,128]{2,1,0:T(8,128)(2,1)S(1)}, bf16[12,64,128]{2,1,0:T(8,128)(2,1)S(1)}, u32[]{:S(2)}, u32[]{:S(2)}) collective-permute-start(bf16[12,64,128]{2,1,0:T(8,128)(2,1)S(1)} %pad_maximum_fusion.halo_ref), channel_id=1, source_target_pairs={{0,2},{1,3},{2,0},{3,1},{4,6},{5,7},{6,4},{7,5},{8,10},{9,11},{10,... | collective-permute-start | bytes 589832 | tf_op jit(solution)/shard_map/ppermute | solution.py:285
  26.0 6.1 %collective-permute-start.9 = (bf16[80,8,128]{2,1,0:T(8,128)(2,1)S(1)}, bf16[80,8,128]{2,1,0:T(8,128)(2,1)S(1)}, u32[]{:S(2)}, u32[]{:S(2)}) collective-permute-start(bf16[80,8,128]{2,1,0:T(8,128)(2,1)S(1)} %collective-permute-done.8.refs_7_), channel_id=1, source_target_pairs={{0,4},{4,0},{8,12},{12,8},{16,20},{20,16},{24,28},{28,24},{1,5},{5... | collective-permute-start | bytes 491528 | tf_op jit(solution)/shard_map/ppermute | solution.py:285
  26.9 9.1 %collective-permute-start.5 = (bf16[12,320,128]{2,1,0:T(8,128)(2,1)S(1)}, bf16[12,320,128]{2,1,0:T(8,128)(2,1)S(1)}, u32[]{:S(2)}, u32[]{:S(2)}) collective-permute-start(bf16[12,320,128]{2,1,0:T(8,128)(2,1)S(1)} %shard_map.112.refs_0_), channel_id=1, source_target_pairs={{0,1},{1,0},{2,3},{3,2},{4,5},{5,4},{6,7},{7,6},{8,9},{9,8},{10,11... | collective-permute-start | bytes 2949128 | tf_op jit(solution)/shard_map/ppermute | solution.py:285
  32.3 5.8 %collective-permute-start.11 = (bf16[12,320,128]{2,1,0:T(8,128)(2,1)S(1)}, bf16[12,320,128]{2,1,0:T(8,128)(2,1)S(1)}, u32[]{:S(2)}, u32[]{:S(2)}) collective-permute-start(bf16[12,320,128]{2,1,0:T(8,128)(2,1)S(1)} %shard_map.114.refs_2_), channel_id=1, source_target_pairs={{0,1},{1,0},{2,3},{3,2},{4,5},{5,4},{6,7},{7,6},{8,9},{9,8},{10,11... | collective-permute-start | bytes 2949128 | tf_op jit(solution)/shard_map/ppermute | solution.py:285
  46.7 4.7 %collective-permute-start.12 = (f32[3,32,96]{2,1,0:T(8,128)S(1)}, f32[3,32,96]{2,1,0:T(8,128)S(1)}, u32[]{:S(2)}, u32[]{:S(2)}) collective-permute-start(f32[3,32,96]{2,1,0:T(8,128)S(1)} %get-tuple-element.60), channel_id=1, source_target_pairs={{0,16},{4,20},{8,24},{12,28},{16,0},{20,4},{24,8},{28,12},{1,17},{... | collective-permute-start | bytes 110600 | tf_op jit(solution)/shard_map/ppermute | solution.py:285
  51.4 11.0 %collective-permute-start.13 = (f32[3,32,96]{2,1,0:T(8,128)S(1)}, f32[3,32,96]{2,1,0:T(8,128)S(1)}, u32[]{:S(2)}, u32[]{:S(2)}) collective-permute-start(f32[3,32,96]{2,1,0:T(8,128)S(1)} %add.64), channel_id=1, source_target_pairs={{0,8},{4,12},{8,0},{12,4},{16,24},{20,28},{24,16},{28,20},{1,9},{5... | collective-permute-start | bytes 110600 | tf_op jit(solution)/shard_map/ppermute | solution.py:285
  53.0 16.7 %collective-permute-start.14 = (bf16[80,8,128]{2,1,0:T(8,128)(2,1)S(1)}, bf16[80,8,128]{2,1,0:T(8,128)(2,1)S(1)}, u32[]{:S(2)}, u32[]{:S(2)}) collective-permute-start(bf16[80,8,128]{2,1,0:T(8,128)(2,1)S(1)} %get-tuple-element.68), channel_id=1, source_target_pairs={{0,8},{4,12},{8,16},{12,20},{16,24},{20,28},{24,0},{28,4},{1,9},{5... | collective-permute-start | bytes 491528 | tf_op jit(solution)/shard_map/ppermute | solution.py:21
  53.0 18.2 %collective-permute-start.15 = (bf16[80,8,128]{2,1,0:T(8,128)(2,1)S(1)}, bf16[80,8,128]{2,1,0:T(8,128)(2,1)S(1)}, u32[]{:S(2)}, u32[]{:S(2)}) collective-permute-start(bf16[80,8,128]{2,1,0:T(8,128)(2,1)S(1)} %get-tuple-element.69), channel_id=1, source_target_pairs={{0,12},{4,16},{8,20},{12,24},{16,28},{20,0},{24,4},{28,8},{1,13},{... | collective-permute-start | bytes 491528 | tf_op jit(solution)/shard_map/ppermute | solution.py:21
  62.4 3.0 %collective-permute-start.20 = (f32[3,32,96]{2,1,0:T(8,128)S(1)}, f32[3,32,96]{2,1,0:T(8,128)S(1)}, u32[]{:S(2)}, u32[]{:S(2)}) collective-permute-start(f32[3,32,96]{2,1,0:T(8,128)S(1)} %add.65), channel_id=1, source_target_pairs={{0,4},{4,0},{8,12},{12,8},{16,20},{20,16},{24,28},{28,24},{1,5},{5... | collective-permute-start | bytes 110600 | tf_op jit(solution)/shard_map/ppermute | solution.py:285
  65.4 6.3 %collective-permute-start.23 = (f32[3,32,96]{2,1,0:T(8,128)S(1)}, f32[3,32,96]{2,1,0:T(8,128)S(1)}, u32[]{:S(2)}, u32[]{:S(2)}) collective-permute-start(f32[3,32,96]{2,1,0:T(8,128)S(1)} %add.78), channel_id=1, source_target_pairs={{0,3},{1,2},{2,1},{3,0},{4,7},{5,6},{6,5},{7,4},{8,11},{9,10},{10,... | collective-permute-start | bytes 110600 | tf_op jit(solution)/shard_map/ppermute | solution.py:285
  69.2 3.9 %collective-permute-start.22 = (f32[3,32,96]{2,1,0:T(8,128)S(1)}, f32[3,32,96]{2,1,0:T(8,128)S(1)}, u32[]{:S(2)}, u32[]{:S(2)}) collective-permute-start(f32[3,32,96]{2,1,0:T(8,128)S(1)} %add.78), channel_id=1, source_target_pairs={{0,2},{1,3},{2,0},{3,1},{4,6},{5,7},{6,4},{7,5},{8,10},{9,11},{10,... | collective-permute-start | bytes 110600 | tf_op jit(solution)/shard_map/ppermute | solution.py:285
  69.5 4.2 %collective-permute-start.21 = (f32[3,32,96]{2,1,0:T(8,128)S(1)}, f32[3,32,96]{2,1,0:T(8,128)S(1)}, u32[]{:S(2)}, u32[]{:S(2)}) collective-permute-start(f32[3,32,96]{2,1,0:T(8,128)S(1)} %add.78), channel_id=1, source_target_pairs={{0,1},{1,0},{2,3},{3,2},{4,5},{5,4},{6,7},{7,6},{8,9},{9,8},{10,11... | collective-permute-start | bytes 110600 | tf_op jit(solution)/shard_map/ppermute | solution.py:285
  69.7 15.1 %collective-permute-start.19 = (bf16[80,8,128]{2,1,0:T(8,128)(2,1)S(1)}, bf16[80,8,128]{2,1,0:T(8,128)(2,1)}, u32[]{:S(2)}, u32[]{:S(2)}) collective-permute-start(bf16[80,8,128]{2,1,0:T(8,128)(2,1)S(1)} %get-tuple-element.73), channel_id=1, source_target_pairs={{0,16},{4,20},{8,24},{12,28},{16,0},{20,4},{24,8},{28,12},{1,17},{... | collective-permute-start | bytes 491528 | tf_op jit(solution)/shard_map/ppermute | solution.py:21
  71.2 3.5 %copy-start.3 = (bf16[80,8,128]{2,1,0:T(8,128)(2,1)}, bf16[80,8,128]{2,1,0:T(8,128)(2,1)S(1)}, u32[]{:S(2)}) copy-start(bf16[80,8,128]{2,1,0:T(8,128)(2,1)S(1)} %collective-permute-done.15) | copy-start | bytes 491524
  71.2 13.6 %collective-permute-start.18 = (bf16[80,8,128]{2,1,0:T(8,128)(2,1)S(1)}, bf16[80,8,128]{2,1,0:T(8,128)(2,1)}, u32[]{:S(2)}, u32[]{:S(2)}) collective-permute-start(bf16[80,8,128]{2,1,0:T(8,128)(2,1)S(1)} %get-tuple-element.72), channel_id=1, source_target_pairs={{0,20},{4,24},{8,28},{12,0},{16,4},{20,8},{24,12},{28,16},{1,21},{... | collective-permute-start | bytes 491528 | tf_op jit(solution)/shard_map/ppermute | solution.py:21
  71.7 13.9 %collective-permute-start.17 = (bf16[80,8,128]{2,1,0:T(8,128)(2,1)S(1)}, bf16[80,8,128]{2,1,0:T(8,128)(2,1)}, u32[]{:S(2)}, u32[]{:S(2)}) collective-permute-start(bf16[80,8,128]{2,1,0:T(8,128)(2,1)S(1)} %get-tuple-element.71), channel_id=1, source_target_pairs={{0,24},{4,28},{8,0},{12,4},{16,8},{20,12},{24,16},{28,20},{1,25},{... | collective-permute-start | bytes 491528 | tf_op jit(solution)/shard_map/ppermute | solution.py:21
  73.1 21.1 %collective-permute-start.16 = (bf16[80,8,128]{2,1,0:T(8,128)(2,1)S(1)}, bf16[80,8,128]{2,1,0:T(8,128)(2,1)}, u32[]{:S(2)}, u32[]{:S(2)}) collective-permute-start(bf16[80,8,128]{2,1,0:T(8,128)(2,1)S(1)} %get-tuple-element.70), channel_id=1, source_target_pairs={{0,28},{4,0},{8,4},{12,8},{16,12},{20,16},{24,20},{28,24},{1,29},{... | collective-permute-start | bytes 491528 | tf_op jit(solution)/shard_map/ppermute | solution.py:21
  74.9 19.3 %copy-start.4 = (bf16[80,8,128]{2,1,0:T(8,128)(2,1)S(1)}, bf16[80,8,128]{2,1,0:T(8,128)(2,1)}, u32[]{:S(2)}) copy-start(bf16[80,8,128]{2,1,0:T(8,128)(2,1)} %copy-done.3) | copy-start | bytes 491524
  (1 other events, 2.6 us)
